TPU v7x, 32 devices: a whole 2x2x4 slice. The times are simulated.
32 devices in a mesh: rep: 2 (over y), exp: 4 (over z), unit: 4 (over x, core).
Axes of the slice: x: 2, y: 2, z: 4, core: 2. Of those that a mesh axis runs over, the one named last changes fastest.
Arguments:
- tokens: bfloat16 [1024, 4096], P(('rep', 'exp')), parts along dimension 0, may hold values from -6 to 6
- norm_gain: float32 [4096], replicated, may hold values from 0.1 to 1.9
- route_ids: int32 [1024, 2], P(('rep', 'exp')), parts along dimension 0, may hold values from 0 to 7, all different within a row; in each aligned block of 128 rows (0 to 127, 128 to 255, ...) at most 40 rows name the same one
- route_weight: float32 [1024, 2], P(('rep', 'exp')), parts along dimension 0, may hold values from 0.2 to 1
- active_blocks: int32 [4, 8, 48], P('rep'), parts along dimension 0, may hold values from 0 to 112, as said below
- gate_weight: bfloat16 [4096, 57344], P(None, ('exp', 'unit')), may hold values from -0.09375 to 0.09375
- up_weight: bfloat16 [4096, 57344], P(None, ('exp', 'unit')), may hold values from -0.09375 to 0.09375
- down_weight: bfloat16 [57344, 4096], P(('exp', 'unit')), may hold values from -0.1875 to 0.1875
Outputs:
- mixed: bfloat16 [1024, 4096], P(('rep', 'exp'), 'unit'), parts along dimension 0
There are 2 independent parts, one for each index of `rep`. A program takes and returns all parts, laid end to end along the dimension named above; an argument that names none is the same for every part. Nothing has to cross between parts.
Inputs may be any that keep to these rules, and one draw needn't show every extreme that they name: `route_ids`: in each aligned block of 128 tokens (those of one index of exp) no expert is named by more than 40 route entries, a bound that some block reaches; the two experts of a token differ; every expert is named somewhere. `active_blocks`: each list holds 24 to 48 distinct block numbers below 112, followed by 112 as padding; some list is full and some list is padded.
All inputs are finite; a program needn't handle non-finite values.
Results may differ from a plain program's by a relative error of at most 0.0095.
Values may be sent and summed in bfloat16 or wider, within the bound.
No kernel may reach another device: no remote copies, remote signals or barrier semaphores. Data moves between devices by JAX's collectives and lax.ppermute only.
A program may use at most 192 MiB of HBM per device.

v0:
```python
import jax
import jax.numpy as jnp
import numpy as np
from jax import lax
from jax.sharding import PartitionSpec as P

EXPERTS = 8
FF = 7168
BLK = 64
TILE = 256
CAP = 40


EPSILON = 1e-05


def normalize(tokens, norm_gain):
    values = tokens.astype(jnp.float32)
    inv_rms = lax.rsqrt(jnp.mean(values * values, axis=-1, keepdims=True) + EPSILON)
    return (values * inv_rms * norm_gain).astype(jnp.bfloat16)


def slot_numbers(entries, expert_count):
    onehot = (entries[..., None] == jnp.arange(expert_count, dtype=jnp.int32)).astype(jnp.int32)
    before = jnp.cumsum(onehot, axis=-2, dtype=jnp.int32) - onehot
    return jnp.sum(before * onehot, axis=-1)


def per_device(
    tokens, norm_gain, route_ids, route_weight, active_blocks, gate_weight, up_weight, down_weight
):
    exp_count = lax.axis_size("exp")
    unit_count = lax.axis_size("unit")
    tok_count, feature_width = tokens.shape
    unit_width = gate_weight.shape[1]
    row_units = unit_count * unit_width
    per_exp = max(1, row_units // FF)
    part_width = feature_width // unit_count
    block_count = unit_width // BLK
    tile_count = active_blocks.shape[0]
    exp_index = lax.axis_index("exp")
    unit_index = lax.axis_index("unit")
    first_unit = (exp_index * unit_count + unit_index) * unit_width
    own_expert = first_unit // FF
    first_block = first_unit % FF // BLK
    local_expert = own_expert - exp_index * row_units // FF
    normed = normalize(tokens, norm_gain)
    slot_index = slot_numbers(route_ids.reshape(1, -1), EXPERTS).reshape(tok_count, 2)
    positions = jnp.arange(tok_count, dtype=jnp.int32)
    tile_of = (exp_index * tok_count + positions) // TILE
    route_slot = (route_ids * CAP + slot_index).reshape(-1)
    token_source = (
        jnp.full((EXPERTS * CAP,), tok_count, jnp.int32)
        .at[route_slot]
        .set(jnp.repeat(positions, 2))
    )
    row_experts = np.arange(exp_count)[:, None] * row_units // FF + np.arange(per_exp)[None, :]
    slot_source = token_source.reshape(EXPERTS, CAP)[row_experts]
    padded_tiles = jnp.concatenate([tile_of, jnp.zeros((1,), jnp.int32)])
    slot_tiles = padded_tiles[slot_source]
    active_mine = lax.dynamic_index_in_dim(active_blocks, own_expert, 1, keepdims=False)
    local_blocks = first_block + jnp.arange(block_count, dtype=jnp.int32)
    block_on = jnp.any(active_mine[:, :, None] == local_blocks[None, None, :], axis=1).astype(
        jnp.float32
    )
    row_part = lax.dynamic_slice_in_dim(normed, unit_index * part_width, part_width, 1)
    padded_rows = jnp.concatenate([row_part, jnp.zeros((1, part_width), jnp.bfloat16)], 0)
    whole_rows = lax.all_gather(
        lax.all_to_all(padded_rows[slot_source], "exp", split_axis=0, concat_axis=0, tiled=True),
        "unit",
        axis=3,
        tiled=True,
    )
    slot_count = whole_rows.shape[2]
    own_rows = lax.dynamic_index_in_dim(whole_rows, local_expert, 1, keepdims=False).reshape(
        -1, feature_width
    )
    own_tiles = lax.dynamic_index_in_dim(
        lax.all_to_all(slot_tiles, "exp", split_axis=0, concat_axis=0, tiled=True),
        local_expert,
        1,
        keepdims=False,
    ).reshape(-1)
    tile_hot = (own_tiles[:, None] == jnp.arange(tile_count, dtype=jnp.int32)[None, :]).astype(
        jnp.float32
    )
    row_mask = jnp.dot(tile_hot, block_on, precision=lax.Precision.HIGHEST)
    gate_acts = jnp.dot(own_rows, gate_weight, preferred_element_type=jnp.float32)
    up_acts = jnp.dot(own_rows, up_weight, preferred_element_type=jnp.float32)
    hidden = jax.nn.relu(gate_acts) * jax.nn.relu(up_acts)
    hidden = (hidden.reshape(-1, block_count, BLK) * row_mask[:, :, None]).reshape(-1, unit_width)
    hidden = hidden.astype(jnp.bfloat16)
    partial_value = jnp.dot(hidden, down_weight, preferred_element_type=jnp.float32)
    partial_value = partial_value.reshape(exp_count, slot_count, feature_width)
    result = jnp.zeros((exp_count, per_exp, slot_count, feature_width), jnp.float32)
    partial_all = lax.dynamic_update_index_in_dim(result, partial_value, local_expert, 1)

    def by_expert(returned):
        last_width = returned.shape[-1]
        if per_exp == 1:
            grouped = returned.reshape(EXPERTS, exp_count // EXPERTS, CAP, last_width)
            return jnp.sum(grouped, axis=1, dtype=jnp.float32)
        return returned.reshape(EXPERTS, CAP, last_width).astype(jnp.float32)

    summed = lax.psum_scatter(
        partial_all.astype(jnp.bfloat16), "unit", scatter_dimension=3, tiled=True
    ).astype(jnp.float32)
    returned = lax.all_to_all(
        summed.astype(jnp.bfloat16), "exp", split_axis=0, concat_axis=0, tiled=True
    ).astype(summed.dtype)
    per_expert = by_expert(returned)
    last_width = per_expert.shape[-1]
    picked = per_expert.reshape(EXPERTS * CAP, last_width)[route_slot].reshape(
        tok_count, 2, last_width
    )
    mixed = jnp.sum(route_weight[:, :, None] * picked, axis=1)
    return mixed.astype(jnp.bfloat16)


def solution(mesh):
    return jax.shard_map(
        per_device,
        mesh=mesh,
        in_specs=(
            P(("rep", "exp"), None),
            P(),
            P(("rep", "exp"), None),
            P(("rep", "exp"), None),
            P("rep", None, None),
            P(None, ("exp", "unit")),
            P(None, ("exp", "unit")),
            P(("exp", "unit"), None),
        ),
        out_specs=P(("rep", "exp"), "unit"),
        check_vma=False,
    )
```

profile of v0, /device:TPU:0, one launch (start us, length us, event | category | flops | bytes accessed | tf_op | source)
XLA Modules:
  0.0 171.3 jit_solution(6161141406407314963)
XLA Ops:
  6.6 1.5 convert_element_type.31
  8.1 0.0 copy-done.3
  8.1 0.3 multiply_reduce_fusion
  8.4 0.1 copy.27
  8.5 0.1 eq.59
  8.7 0.6 reduce-window.6
  9.2 0.2 slice_reduce_fusion
  9.5 0.1 fusion.16
  9.6 0.1 reshape.211
  9.7 0.1 copy.28
  9.8 0.1 copy.29
  9.9 0.1 reshape.212
  10.1 0.1 reshape.255
  10.3 1.4 scatter_custom_fusion
  11.7 0.1 reshape.214
  11.8 0.6 gather_fusion
  12.3 0.1 reshape.229
  12.4 0.7 dynamic-slice
  13.1 0.1 fusion.12
  13.3 2.1 %gather_fusion.1 = bf16[320,1024]{1,0:T(8,128)(2,1)S(1)} fusion(bf16[129,1024]{1,0:T(8,128)(2,1)S(1)} %concatenate.6, s32[1024]{0:T(1024)S(1)} %pad_clamp_fusion.1), kind=kCustom, calls=%fused_computation.1 | custom fusion | bytes 1312000 | tf_op jit(solution)/shard_map/gather | solution.py:69
  15.4 23.5 %all_to_all.15 = bf16[4,2,40,1024]{3,2,1,0:T(8,128)(2,1)} all-to-all(bf16[4,2,40,1024]{3,2,1,0:T(8,128)(2,1)S(1)} %bitcast.48), channel_id=1, replica_groups=mesh['rep'=2,'exp'=4,'unit'=4] {'exp'}, dimensions={0} | all-to-all | bytes 1310720 | tf_op jit(solution)/shard_map/all_to_all | solution.py:69
  38.9 0.0 all-gather.2.cloned.1.call-update
  39.0 2.4 %gather_fusion.2 = s32[320]{0:T(512)S(1)} fusion(s32[129]{0:T(256)S(1)} %pad_add_fusion, s32[1024]{0:T(1024)S(1)} %pad_clamp_fusion.1), kind=kCustom, calls=%fused_computation.2 | custom fusion | bytes 3840 | tf_op jit(solution)/shard_map/gather | solution.py:60
  41.4 0.7 reshape.236
  42.1 3.2 %all-to-all-start.1 = ((s32[4,2,40]{2,1,0:T(2,128)}), s32[4,2,40]{2,1,0:T(2,128)S(1)}, u32[]{:S(2)}, u32[]{:S(2)}) async-start(s32[4,2,40]{2,1,0:T(2,128)} %reshape.236), calls=%async_computation.1 | async-start | bytes 8192 | tf_op jit(solution)/shard_map/all_to_all | solution.py:79
  45.4 0.2 reduce-scatter.2.cloned.1.call-start
  45.7 0.1 compare_reduce_fusion
  45.8 5.1 %all-to-all-done.1 = s32[4,2,40]{2,1,0:T(2,128)S(1)} async-done(((s32[4,2,40]{2,1,0:T(2,128)}), s32[4,2,40]{2,1,0:T(2,128)S(1)}, u32[]{:S(2)}, u32[]{:S(2)}) %all-to-all-start.1) | async-done | bytes 1312 | tf_op jit(solution)/shard_map/all_to_all | solution.py:79
  50.9 0.1 eq.63
  51.0 0.2 fusion.13
  51.2 3.3 %mul.80 = f32[160,56,64]{2,1,0:T(8,128)} broadcast(f32[160,56]{1,0:T(8,128)S(1)} %fusion.13), dimensions={0,1} | broadcast | bytes 2329600 | tf_op jit(solution)/shard_map/mul | solution.py:91
  54.6 3.5 %mul.81 = f32[160,3584]{1,0:T(8,128)S(1)} reshape(f32[160,56,64]{2,1,0:T(8,128)} %mul.80) | data formatting | bytes 4587520 | tf_op jit(solution)/shard_map/mul | solution.py:91
  58.1 5.6 %all-gather.2.cloned.1.call-done = bf16[4,2,40,4096]{3,2,1,0:T(8,128)(2,1)} async-done(((bf16[4,2,40,1024]{3,2,1,0:T(8,128)(2,1)}), bf16[4,2,40,4096]{3,2,1,0:T(8,128)(2,1)}) %all-gather.2.cloned.1.call-update) | async-done | bytes 2621456 | tf_op jit(solution)/shard_map/all_gather | solution.py:68
  63.7 1.4 constant_dynamic-slice_fusion.1
  65.2 11.9 %convolution_maximum_fusion = f32[160,3584]{1,0:T(8,128)S(1)} fusion(bf16[160,4096]{1,0:T(8,128)(2,1)S(1)} %bitcast.45, bf16[4096,3584]{1,0:T(8,128)(2,1)} %param.16), kind=kOutput, calls=%fused_computation.7 | convolution fusion | flops 4698193920 | bytes 32964608 | tf_op jit(solution)/shard_map/dot_general | solution.py:89
  77.1 12.5 %fusion.10 = bf16[160,3584]{1,0:T(8,128)(2,1)S(1)} fusion(f32[160,3584]{1,0:T(8,128)S(1)} %mul.81, f32[160,3584]{1,0:T(8,128)S(1)} %convolution_maximum_fusion, bf16[160,4096]{1,0:T(8,128)(2,1)S(1)} %bitcast.46, bf16[4096,3584]{1,0:T(8,128)(2,1)} %param.15), kind=kOutput, calls=%fused_computation.13 | convolution fusion | flops 4699914240 | bytes 36405248 | tf_op jit(solution)/shard_map/dot_general | solution.py:88
  89.7 0.3 broadcast_in_dim.9
  90.0 12.2 %fusion.7 = bf16[4,2,40,4096]{3,2,1,0:T(8,128)(2,1)S(1)} fusion(bf16[4,2,40,4096]{3,2,1,0:T(8,128)(2,1)S(1)} %broadcast_in_dim.9, s32[]{:T(128)S(6)} %select_n.68, bf16[4,40,3584]{2,1,0:T(8,128)(2,1)S(1)} %bitcast.47, bf16[3584,4096]{1,0:T(8,128)(2,1)} %param.17), kind=kOutput, calls=%fused_computation.12 | convolution fusion | flops 4697620480 | bytes 33128452 | tf_op jit(solution)/shard_map/dot_general | solution.py:93
  102.2 1.5 copy-done.2
  103.7 0.0 reduce-scatter.2.cloned.1.call-update
  103.7 34.9 %reduce-scatter.2.cloned.1.call-done = bf16[4,2,40,1024]{3,2,1,0:T(8,128)(2,1)} async-done(((bf16[4,2,40,4096]{3,2,1,0:T(8,128)(2,1)}), bf16[4,2,40,1024]{3,2,1,0:T(8,128)(2,1)}) %reduce-scatter.2.cloned.1.call-update) | async-done | bytes 655376 | tf_op jit(solution)/shard_map/reduce_scatter | solution.py:105
  138.6 4.6 %all-to-all-start.2 = ((bf16[4,2,40,1024]{3,2,1,0:T(8,128)(2,1)}), bf16[4,2,40,1024]{3,2,1,0:T(8,128)(2,1)S(1)}, u32[]{:S(2)}, u32[]{:S(2)}) async-start(bf16[4,2,40,1024]{3,2,1,0:T(8,128)(2,1)} %reduce-scatter.2.cloned.1.call-done), calls=%async_computation.3 | async-start | bytes 1310720 | tf_op jit(solution)/shard_map/all_to_all | solution.py:108
  143.1 0.1 copy.26
  143.3 17.2 %all-to-all-done.2 = bf16[4,2,40,1024]{3,2,1,0:T(8,128)(2,1)S(1)} async-done(((bf16[4,2,40,1024]{3,2,1,0:T(8,128)(2,1)}), bf16[4,2,40,1024]{3,2,1,0:T(8,128)(2,1)S(1)}, u32[]{:S(2)}, u32[]{:S(2)}) %all-to-all-start.2) | async-done | bytes 655392 | tf_op jit(solution)/shard_map/all_to_all | solution.py:108
  160.5 0.2 bitcast_convert_fusion
  160.7 1.1 gather_fusion.3
  161.7 0.6 reshape.217
  162.4 2.1 %multiply_reduce_fusion.1 = bf16[128,1024]{1,0:T(8,128)(2,1)} fusion(f32[128,2,1024]{2,1,0:T(2,128)S(1)} %reshape.217, f32[128,2]{1,0:T(8,128)S(1)} %copy.26), kind=kLoop, calls=%fused_computation.15 | loop fusion | flops 393216 | bytes 1311744 | tf_op jit(solution)/shard_map/reduce_sum | solution.py:116
  (29 shorter events, 0.2 us)
Async XLA Ops:
  6.5 39.1 %copy-start = (s32[2,8,48]{2,1,0:T(8,128)S(1)}, s32[2,8,48]{2,1,0:T(8,128)}, u32[]{:S(2)}) copy-start(s32[2,8,48]{2,1,0:T(8,128)} %param.14) | copy-start | bytes 9220
  6.5 1.6 copy-start.3
  6.5 1.8 %copy-start.4 = (s32[128,2]{0,1:T(2,128)S(1)}, s32[128,2]{0,1:T(2,128)}, u32[]{:S(2)}) copy-start(s32[128,2]{0,1:T(2,128)} %param.12) | copy-start | bytes 3076
  6.5 57.2 %all-gather.2.cloned.1.call-start = ((), (), s32[]{:S(2)}) async-start(), calls=%async_computation.4 | async-start | bytes 3276800 | tf_op jit(solution)/shard_map/all_gather | solution.py:68
  42.1 8.8 %all-to-all-start.1 = ((s32[4,2,40]{2,1,0:T(2,128)}), s32[4,2,40]{2,1,0:T(2,128)S(1)}, u32[]{:S(2)}, u32[]{:S(2)}) async-start(s32[4,2,40]{2,1,0:T(2,128)} %reshape.236), calls=%async_computation.1 | async-start | bytes 8192 | tf_op jit(solution)/shard_map/all_to_all | solution.py:79
  45.4 93.2 %reduce-scatter.2.cloned.1.call-start = ((), (), s32[]{:S(2)}) async-start(), calls=%async_computation.5 | async-start | bytes 3276800 | tf_op jit(solution)/shard_map/reduce_scatter | solution.py:105
  102.2 1.5 copy-start.2
  102.2 41.0 %copy-start.5 = (f32[128,2]{0,1:T(2,128)S(1)}, f32[128,2]{0,1:T(2,128)}, u32[]{:S(2)}) copy-start(f32[128,2]{0,1:T(2,128)} %param.13) | copy-start | bytes 3076
  138.6 21.9 %all-to-all-start.2 = ((bf16[4,2,40,1024]{3,2,1,0:T(8,128)(2,1)}), bf16[4,2,40,1024]{3,2,1,0:T(8,128)(2,1)S(1)}, u32[]{:S(2)}, u32[]{:S(2)}) async-start(bf16[4,2,40,1024]{3,2,1,0:T(8,128)(2,1)} %reduce-scatter.2.cloned.1.call-done), calls=%async_computation.3 | async-start | bytes 1310720 | tf_op jit(solution)/shard_map/all_to_all | solution.py:108
  160.6 3.8 %copy-start.1 = (s32[2,8,48]{2,1,0:T(8,128)S(1)}, s32[2,8,48]{2,1,0:T(8,128)}, u32[]{:S(2)}) copy-start(s32[2,8,48]{2,1,0:T(8,128)} %param.14) | copy-start | bytes 9220
Sparse Core Ops, SparseCore 0:
  39.0 24.6 all-gather.1
  103.8 34.6 reduce-scatter.1
where the time goes:
time: 172 us; the launch traced here: 171 us
  waiting for transfers between devices  62.8 us (37%)
  matrix products  36.9 us (21%)
  blocking collectives  23.5 us (14%)
  local copies, waits for them, and re-layouts  21.2 us (12%)
  between operations  13.8 us (8%)
  starting transfers between devices  8.07 us (5%)
  other arithmetic  5.04 us (3%)
    reduce_scatter x1, waiting for transfers between devices, per_device(): lax.psum_scatter(partial_all.astype(jnp.bfloat16), 'unit', scatter_dimens...  34.9 us
    all_to_all x1, blocking collectives, per_device(): lax.all_to_all(padded_rows[slot_source], 'exp', split_axis=0, concat_axis...  23.5 us
    all_to_all x1, waiting for transfers between devices, per_device(): lax.all_to_all(summed.astype(jnp.bfloat16), 'exp', split_axis=0, concat_a...  17.2 us
    dot_general x1, matrix products, per_device(): jnp.dot(own_rows, gate_weight, preferred_element_type=jnp.float32)  12.5 us
    dot_general x1, matrix products, per_device(): jnp.dot(hidden, down_weight, preferred_element_type=jnp.float32)  12.2 us
    dot_general x1, matrix products, per_device(): up_acts = jnp.dot(own_rows, up_weight, preferred_element_type=jnp.float32)  11.9 us
    mul x2, local copies, waits for them, and re-layouts, per_device(): hidden.reshape(-1, block_count, BLK) * row_mask[:, :, None]  6.89 us
    all_gather x1, waiting for transfers between devices, per_device(): lax.all_gather(lax.all_to_all(padded_rows[slot_source], 'exp', split_axis...  5.64 us
  transfers between devices with their start and end apart: 4, of which 4 were waited for; matrix products, arithmetic and copies ran while one was open for 6% of the time, Pallas kernels for 0%

commit v1 on v0

--- a/solution.py
+++ b/solution.py
@@ -1,7 +1,11 @@
+import functools
+
 import jax
 import jax.numpy as jnp
 import numpy as np
 from jax import lax
+from jax.experimental import pallas as pl
+from jax.experimental.pallas import tpu as pltpu
 from jax.sharding import PartitionSpec as P
 
 EXPERTS = 8
@@ -10,8 +14,18 @@
 TILE = 256
 CAP = 40
 
-
 EPSILON = 1e-05
+
+IN_CHUNKS = 2
+OUT_CHUNKS = 2
+K_SLAB = 256
+K_DEPTH = 6
+N_SLAB = 256
+N_DEPTH = 4
+VMEM_LIMIT = 40 * 1024 * 1024
+
+F32 = jnp.float32
+BF16 = jnp.bfloat16
 
 
 def normalize(tokens, norm_gain):
@@ -26,7 +40,7 @@
     return jnp.sum(before * onehot, axis=-1)
 
 
-def per_device(
+def spread_experts(
     tokens, norm_gain, route_ids, route_weight, active_blocks, gate_weight, up_weight, down_weight
 ):
     exp_count = lax.axis_size("exp")
@@ -117,6 +131,378 @@
     return mixed.astype(jnp.bfloat16)
 
 
+def place(sizes):
+    exp_count, groups = sizes
+    return lax.axis_index("exp"), lax.axis_index("unit") // 2, lax.axis_index("unit") % 2
+
+
+def route_kernel(sizes, width, tokens, gain, ids, own, *rest):
+    exp_count, groups = sizes
+    sends, normed = rest[:-1], rest[-1]
+    rows, features = tokens.shape
+    z, g, s = place(sizes)
+    step = 16
+    for first in range(0, rows, step):
+        values = tokens[first : first + step, :].astype(F32)
+        mean = jnp.sum(values * values, axis=1, keepdims=True) * (1.0 / features)
+        inv_rms = lax.rsqrt(mean + EPSILON)
+        normed[first : first + step, :] = (values * inv_rms * gain[...]).astype(BF16)
+    earlier = (
+        lax.broadcasted_iota(jnp.int32, (rows, rows), 0)
+        < lax.broadcasted_iota(jnp.int32, (rows, rows), 1)
+    ).astype(BF16)
+    ids0, ids1 = ids[0:1, :], ids[1:2, :]
+    slots = lax.broadcasted_iota(jnp.int32, (CAP, rows), 0)
+    distance = lax.broadcasted_iota(jnp.int32, (max(8, exp_count), rows), 0)
+    experts = lax.rem(z + distance, exp_count) * groups + g
+    named = (ids0 == experts) | (ids1 == experts)
+    before = jnp.dot(named.astype(BF16), earlier, preferred_element_type=F32).astype(jnp.int32)
+    picks = []
+    for d in range(exp_count):
+        hit = named[d : d + 1, :].astype(jnp.int32)
+        place_of = jnp.where(hit > 0, before[d : d + 1, :], -1)
+        picks.append((place_of == slots).astype(F32))
+    own[...] = jnp.dot(
+        picks[0].astype(BF16), normed[...], preferred_element_type=F32
+    ).astype(BF16)
+    others = jnp.concatenate(picks[1:], axis=0).astype(BF16)
+    half = features // 2
+    for chunk in range(half // width):
+        start = pl.multiple_of(s * half + chunk * width, 128)
+        found = jnp.dot(others, normed[:, pl.ds(start, width)], preferred_element_type=F32)
+        for d in range(1, exp_count):
+            part = found[(d - 1) * CAP : d * CAP, :].astype(BF16)
+            sends[chunk * (exp_count - 1) + d - 1][...] = part
+
+
+def prepare_kernel(sizes, ids, weights, active, combine_high, combine_low, mask):
+    exp_count, groups = sizes
+    rows = ids.shape[1]
+    z, g, s = place(sizes)
+    earlier = (
+        lax.broadcasted_iota(jnp.int32, (rows, rows), 0)
+        < lax.broadcasted_iota(jnp.int32, (rows, rows), 1)
+    ).astype(BF16)
+    ids0, ids1 = ids[0:1, :], ids[1:2, :]
+    slots = lax.broadcasted_iota(jnp.int32, (CAP, rows), 0)
+
+    def expert_at(j):
+        return lax.rem(z + j // groups, exp_count) * groups + lax.rem(
+            g + groups - lax.rem(j, groups), groups
+        )
+
+    experts = expert_at(lax.broadcasted_iota(jnp.int32, (EXPERTS, rows), 0))
+    named = (ids0 == experts) | (ids1 == experts)
+    before = jnp.dot(named.astype(BF16), earlier, preferred_element_type=F32).astype(jnp.int32)
+    zero = jnp.zeros((CAP, rows), F32)
+    parts = []
+    for j in range(EXPERTS):
+        here = before[j : j + 1, :] == slots
+        expert = expert_at(j)
+        first = jnp.where(here & (ids0 == expert), weights[0:1, :], zero)
+        second = jnp.where(here & (ids1 == expert), weights[1:2, :], zero)
+        parts.append(first + second)
+    total = EXPERTS * CAP
+    padded = -(-total // 128) * 128
+    if padded > total:
+        parts.append(jnp.zeros((padded - total, rows), F32))
+    table = jnp.concatenate(parts, axis=0).T
+    high = table.astype(BF16)
+    low = (table - high.astype(F32)).astype(BF16)
+    combine_high[...] = high
+    combine_low[...] = low
+    unit_width = mask.shape[1]
+    blocks = lax.broadcasted_iota(jnp.int32, mask.shape, 1) // BLK + s * (unit_width // BLK)
+    source = lax.broadcasted_iota(jnp.int32, (mask.shape[0], 1), 0)
+    own_expert = z * groups + g
+
+    def add_entry(k, found):
+        entry = jnp.full((mask.shape[0], 1), -1, jnp.int32)
+        for d in range(exp_count):
+            tile = lax.rem(z - d + exp_count, exp_count) * rows // TILE
+            entry = jnp.where(source == d, active[tile, own_expert, k], entry)
+        return jnp.where(blocks == entry, 1.0, found)
+
+    mask[...] = lax.fori_loop(0, active.shape[2], add_entry, jnp.zeros(mask.shape, F32))
+
+
+def hidden_kernel(sizes, chunk, width, first, last, *refs):
+    exp_count, groups = sizes
+    z, g, s = place(sizes)
+    refs = list(refs)
+    own = refs.pop(0)
+    mine = [refs.pop(0) for _ in range(exp_count - 1)]
+    other = [refs.pop(0) for _ in range(exp_count - 1)]
+    gate, up = refs.pop(0), refs.pop(0)
+    gate_in, up_in = (None, None) if first else (refs.pop(0), refs.pop(0))
+    mask = refs.pop(0) if last else None
+    if last:
+        hidden = refs.pop(0)
+        gate_sum, up_sum = refs.pop(0), refs.pop(0)
+    else:
+        gate_sum, up_sum = refs.pop(0), refs.pop(0)
+    rows, slabs, sems = refs
+    half = own.shape[1] // 2
+    slab_count = width // K_SLAB
+    total = 2 * slab_count
+    depth = min(K_DEPTH, 2 * total)
+
+    def copy(index, ref, which):
+        side = jnp.where(index < slab_count, s, 1 - s)
+        row = side * half + chunk * width + lax.rem(index, slab_count) * K_SLAB
+        slot = lax.rem(index * 2 + which, depth)
+        return pltpu.make_async_copy(
+            ref.at[pl.ds(pl.multiple_of(row, K_SLAB), K_SLAB), :], slabs.at[slot], sems.at[slot]
+        )
+
+    for n in range(depth):
+        copy(n // 2, (gate, up)[n % 2], n % 2).start()
+    for side_of in range(2):
+        source = (mine, other)[side_of]
+        side = s if side_of == 0 else 1 - s
+        start = pl.multiple_of(side * half + chunk * width, 128)
+        pieces = [own[:, pl.ds(start, width)].astype(F32)] + [r[...].astype(F32) for r in source]
+        whole = jnp.concatenate(pieces, axis=0).astype(BF16)
+        for n in range(slab_count):
+            rows[side_of * slab_count + n] = whole[:, n * K_SLAB : (n + 1) * K_SLAB]
+    unit_width = gate.shape[1]
+    n_tile = 512
+    if first:
+        gate_sum[...] = jnp.zeros_like(gate_sum)
+        up_sum[...] = jnp.zeros_like(up_sum)
+    else:
+        gate_sum[...] = gate_in[...]
+        up_sum[...] = up_in[...]
+
+    def body(index, carry):
+        left = rows[index]
+        for which, (ref, acc) in enumerate(((gate, gate_sum), (up, up_sum))):
+            copy(index, ref, which).wait()
+            slot = lax.rem(index * 2 + which, depth)
+            for col in range(0, unit_width, n_tile):
+                end = min(col + n_tile, unit_width)
+                acc[:, col:end] += jnp.dot(
+                    left, slabs[slot, :, col:end], preferred_element_type=F32
+                )
+
+            @pl.when(index * 2 + which + depth < 2 * total)
+            def _():
+                copy(index + depth // 2, ref, which).start()
+
+        return carry
+
+    lax.fori_loop(0, total, body, 0)
+    if last:
+        for d in range(exp_count):
+            lines = slice(d * CAP, (d + 1) * CAP)
+            for col in range(0, unit_width, n_tile):
+                cols = slice(col, min(col + n_tile, unit_width))
+                product = jnp.maximum(gate_sum[lines, cols], 0.0) * jnp.maximum(
+                    up_sum[lines, cols], 0.0
+                )
+                gate_sum[lines, cols] = product * mask[d : d + 1, cols]
+        hidden[...] = gate_sum[...].astype(BF16)
+
+
+def output_kernel(sizes, chunk, width, keep, *refs):
+    exp_count, groups = sizes
+    z, g, s = place(sizes)
+    refs = list(refs)
+    hidden, down = refs.pop(0), refs.pop(0)
+    received = [refs.pop(0) for _ in range(groups)] if keep else None
+    count = groups * exp_count if keep else groups
+    outs = [refs.pop(0) for _ in range(count)]
+    slabs, sems = refs
+    side = s if keep else 1 - s
+    part = down.shape[1] // (2 * groups)
+    per_group = width // N_SLAB
+    total = groups * per_group
+    depth = min(N_DEPTH, total)
+
+    def copy(index):
+        group = lax.rem(g + index // per_group, groups)
+        column = (group * 2 + side) * part + chunk * width + index % per_group * N_SLAB
+        return pltpu.make_async_copy(
+            down.at[:, pl.ds(pl.multiple_of(column, 128), N_SLAB)],
+            slabs.at[index % depth],
+            sems.at[index % depth],
+        )
+
+    for index in range(depth):
+        copy(index).start()
+    for index in range(total):
+        copy(index).wait()
+        value = jnp.dot(hidden[...], slabs[index % depth], preferred_element_type=F32)
+        if index + depth < total:
+            copy(index + depth).start()
+        group = index // per_group
+        cols = slice(index % per_group * N_SLAB, (index % per_group + 1) * N_SLAB)
+        if keep:
+            value = value + received[group][:, cols].astype(F32)
+            for d in range(exp_count):
+                lines = value[d * CAP : (d + 1) * CAP, :].astype(BF16)
+                outs[group * exp_count + d][:, cols] = lines
+        else:
+            outs[group][:, cols] = value.astype(BF16)
+
+
+def combine_kernel(sizes, high, low, *refs):
+    refs = list(refs)
+    out = refs.pop()
+    total = EXPERTS * CAP
+    per_chunk = EXPERTS
+    width = refs[0].shape[1]
+    for chunk in range(len(refs) // per_chunk):
+        pieces = [r[...].astype(F32) for r in refs[chunk * per_chunk : (chunk + 1) * per_chunk]]
+        found = jnp.concatenate(pieces, axis=0).astype(BF16)
+        value = jnp.dot(high[:, :total], found, preferred_element_type=F32)
+        value = value + jnp.dot(low[:, :total], found, preferred_element_type=F32)
+        out[:, chunk * width : (chunk + 1) * width] = value.astype(BF16)
+
+
+def call(kernel, outs, ins, scratch=(), flops=0, moved=0, aliases=None):
+    vmem = pl.BlockSpec(memory_space=pltpu.VMEM)
+    arrays = [a for a, _ in ins]
+    specs = [vmem if space is None else pl.BlockSpec(memory_space=space) for _, space in ins]
+    return pl.pallas_call(
+        kernel,
+        out_shape=[jax.ShapeDtypeStruct(shape, kind) for shape, kind in outs],
+        in_specs=specs,
+        out_specs=[vmem] * len(outs),
+        scratch_shapes=list(scratch),
+        compiler_params=pltpu.CompilerParams(vmem_limit_bytes=VMEM_LIMIT),
+        cost_estimate=pl.CostEstimate(flops=flops, bytes_accessed=moved, transcendentals=0),
+    )(*arrays)
+
+
+def paired_experts(
+    tokens, norm_gain, route_ids, route_weight, active_blocks, gate_weight, up_weight, down_weight
+):
+    exp_count, unit_count = lax.axis_size("exp"), lax.axis_size("unit")
+    groups = unit_count // 2
+    sizes = (exp_count, groups)
+    tok_count, features = tokens.shape
+    unit_width = gate_weight.shape[1]
+    slots = exp_count * CAP
+    half = features // 2
+    width = half // IN_CHUNKS
+    ids = route_ids.T
+    weights = route_weight.T
+
+    def shift(value, distance, group_shift=0):
+        pairs = []
+        for z in range(exp_count):
+            for u in range(unit_count):
+                target = (z + distance) % exp_count
+                group = (u // 2 + group_shift) % groups
+                pairs.append((z * unit_count + u, target * unit_count + group * 2 + u % 2))
+        return lax.ppermute(value, ("exp", "unit"), pairs)
+
+    def swap(value):
+        return lax.ppermute(value, "unit", [(u, u ^ 1) for u in range(unit_count)])
+
+    own, *sends = call(
+        functools.partial(route_kernel, sizes, width),
+        [((CAP, features), BF16)] + [((CAP, width), BF16)] * (IN_CHUNKS * (exp_count - 1)),
+        [(tokens, None), (norm_gain.reshape(1, -1), None), (ids, None)],
+        [pltpu.VMEM((tok_count, features), BF16)],
+        flops=2 * tok_count * slots * features,
+        moved=4 * tok_count * features,
+    )
+    padded = -(-EXPERTS * CAP // 128) * 128
+    combine_high, combine_low, mask = call(
+        functools.partial(prepare_kernel, sizes),
+        [
+            ((tok_count, padded), BF16),
+            ((tok_count, padded), BF16),
+            ((max(8, exp_count), unit_width), F32),
+        ],
+        [(ids, None), (weights, None), (active_blocks, pltpu.SMEM)],
+        moved=1 << 20,
+    )
+    mine, other = [], []
+    for chunk in range(IN_CHUNKS):
+        batch = sends[chunk * (exp_count - 1) : (chunk + 1) * (exp_count - 1)]
+        arrived = [shift(value, d + 1) for d, value in enumerate(batch)]
+        mine.append(arrived)
+        other.append([swap(value) for value in arrived])
+    sums = None
+    for chunk in range(IN_CHUNKS):
+        first, last = chunk == 0, chunk == IN_CHUNKS - 1
+        ins = [(own, None)] + [(v, None) for v in mine[chunk] + other[chunk]]
+        ins += [(gate_weight, pl.ANY), (up_weight, pl.ANY)]
+        if not first:
+            ins += [(v, None) for v in sums]
+        if last:
+            ins += [(mask, None)]
+        acc = ((slots, unit_width), F32)
+        scratch = [
+            pltpu.VMEM((2 * width // K_SLAB, slots, K_SLAB), BF16),
+            pltpu.VMEM((K_DEPTH, K_SLAB, unit_width), BF16),
+            pltpu.SemaphoreType.DMA((K_DEPTH,)),
+        ]
+        if last:
+            scratch = [pltpu.VMEM(*acc), pltpu.VMEM(*acc)] + scratch
+        sums = call(
+            functools.partial(hidden_kernel, sizes, chunk, width, first, last),
+            [((slots, unit_width), BF16)] if last else [acc, acc],
+            ins,
+            scratch,
+            flops=2 * 2 * slots * 2 * width * unit_width,
+            moved=2 * 2 * width * unit_width * 2,
+        )
+    hidden = sums[0]
+    part = features // unit_count
+    out_width = part // OUT_CHUNKS
+
+    def output(chunk, keep, received):
+        ins = [(hidden, None), (down_weight, pl.ANY)] + [(v, None) for v in received]
+        outs = [((slots, out_width), BF16)] * groups
+        if keep:
+            outs = [((CAP, out_width), BF16)] * (groups * exp_count)
+        return call(
+            functools.partial(output_kernel, sizes, chunk, out_width, keep),
+            outs,
+            ins,
+            [
+                pltpu.VMEM((N_DEPTH, unit_width, N_SLAB), BF16),
+                pltpu.SemaphoreType.DMA((N_DEPTH,)),
+            ],
+            flops=2 * slots * unit_width * groups * out_width,
+            moved=2 * unit_width * groups * out_width,
+        )
+
+    given = [output(chunk, False, ()) for chunk in range(OUT_CHUNKS)]
+    taken = [[swap(value) for value in values] for values in given]
+    pieces = []
+    for chunk in range(OUT_CHUNKS):
+        kept = output(chunk, True, taken[chunk])
+        for d in range(exp_count):
+            for offset in range(groups):
+                value = kept[offset * exp_count + d]
+                pieces.append(shift(value, -d, offset) if d or offset else value)
+    return call(
+        functools.partial(combine_kernel, sizes),
+        [((tok_count, part), BF16)],
+        [(combine_high, None), (combine_low, None)] + [(v, None) for v in pieces],
+        flops=4 * tok_count * EXPERTS * CAP * part,
+        moved=4 * EXPERTS * CAP * part,
+    )[0]
+
+
+def per_device(*operands):
+    tokens, gate_weight = operands[0], operands[5]
+    exp_count, unit_count = lax.axis_size("exp"), lax.axis_size("unit")
+    unit_width = gate_weight.shape[1]
+    paired = (
+        2 * unit_width == FF
+        and unit_count % 2 == 0
+        and exp_count * unit_count // 2 == EXPERTS
+        and TILE % tokens.shape[0] == 0
+    )
+    return (paired_experts if paired else spread_experts)(*operands)
+
+
 def solution(mesh):
     return jax.shard_map(
         per_device,

time: 172 us -> 96.4 us (0.56)
  waiting for transfers between devices: 62.8 us -> 11.7 us
  Pallas kernels: 0 us -> 43.6 us
  matrix products: 36.9 us -> 0 us
  starting transfers between devices: 8.07 us -> 36.6 us
  blocking collectives: 23.5 us -> 0 us
  local copies, waits for them, and re-layouts: 21.2 us -> 3.99 us
  between operations: 13.8 us -> 0.17 us
  other arithmetic: 5.04 us -> 0 us
    pallas_call x0 -> x9, Pallas kernels: none -> 43.6 us  [call(): pl.pallas_call(kernel, out_shape=[jax.ShapeDtypeStruct(shape, kind) for s...]
    dot_general x4 -> x0, matrix products: 36.9 us -> none  [the longest x1 12.5 us: per_device(): jnp.dot(own_rows, gate_weight, preferred_element_type=jnp.float32)]
    ppermute x0 -> x30, starting transfers between devices: none -> 36.6 us  [the longest x20 34.3 us: shift(): return lax.ppermute(value, ('exp', 'unit'), pairs)]
    reduce_scatter x1 -> x0, waiting for transfers between devices: 34.9 us -> none  [per_device(): lax.psum_scatter(partial_all.astype(jnp.bfloat16), 'unit', scatter_dimens...]
    all_to_all x1 -> x0, blocking collectives: 23.5 us -> none  [per_device(): lax.all_to_all(padded_rows[slot_source], 'exp', split_axis=0, concat_axis...]
    all_to_all x2 -> x0, waiting for transfers between devices: 22.3 us -> none  [the longest x1 17.2 us: per_device(): lax.all_to_all(summed.astype(jnp.bfloat16), 'exp', split_axis=0, concat_a...]
    ppermute x0 -> x30, waiting for transfers between devices: none -> 11.7 us  [the longest x20 11.7 us: shift(): return lax.ppermute(value, ('exp', 'unit'), pairs)]
    all_to_all x2 -> x0, starting transfers between devices: 7.84 us -> none  [the longest x1 4.59 us: per_device(): lax.all_to_all(summed.astype(jnp.bfloat16), 'exp', split_axis=0, concat_a...]
  transfers between devices with their start and end apart: 4 -> 30, of which waited for: 4 -> 6; matrix products, arithmetic and copies ran while one was open for 6% -> 0% of each run, Pallas kernels for 0% -> 28%
where the time goes in v1:
time: 96.4 us; the launch traced here: 96.1 us
  Pallas kernels  43.6 us (45%)
  starting transfers between devices  36.6 us (38%)
  waiting for transfers between devices  11.7 us (12%)
  local copies, waits for them, and re-layouts  3.99 us (4%)
    pallas_call x9, Pallas kernels, call(): pl.pallas_call(kernel, out_shape=[jax.ShapeDtypeStruct(shape, kind) for s...  43.6 us
    ppermute x20, starting transfers between devices, shift(): return lax.ppermute(value, ('exp', 'unit'), pairs)  34.3 us
    ppermute x20, waiting for transfers between devices, shift(): return lax.ppermute(value, ('exp', 'unit'), pairs)  11.7 us
    unnamed x10, local copies, waits for them, and re-layouts  3.99 us
    ppermute x10, starting transfers between devices, swap(): return lax.ppermute(value, 'unit', [(u, u ^ 1) for u in range(unit_count)])  2.31 us
  transfers between devices with their start and end apart: 30, of which 6 were waited for; matrix products, arithmetic and copies ran while one was open for 0% of the time, Pallas kernels for 28%

profile of v1, /device:TPU:0, one launch (start us, length us, event | category | flops | bytes accessed | tf_op | source)
XLA Modules:
  0.0 96.1 jit_solution(15174754184938031281)
XLA Ops:
  0.0 1.2 %copy-done = bf16[128,4096]{1,0:T(8,128)(2,1)S(1)} copy-done((bf16[128,4096]{1,0:T(8,128)(2,1)S(1)}, bf16[128,4096]{1,0:T(8,128)(2,1)}, u32[]{:S(2)}) %copy-start) | copy-done | bytes 1048600
  1.2 0.7 copy-done.1
  1.9 0.7 copy-done.3
  2.6 0.8 shard_map.83
  3.5 3.1 %collective-permute-start = (bf16[40,1024]{1,0:T(8,128)(2,1)S(1)}, bf16[40,1024]{1,0:T(8,128)(2,1)S(1)}, u32[]{:S(2)}, u32[]{:S(2)}) collective-permute-start(bf16[40,1024]{1,0:T(8,128)(2,1)S(1)} %get-tuple-element.40), channel_id=1, source_target_pairs={{0,4},{1,5},{2,6},{3,7},{4,8},{5,9},{6,10},{7,11},{8,12},{9,13},{1... | collective-permute-start | bytes 245768 | tf_op jit(solution)/shard_map/ppermute | solution.py:399
  6.5 1.6 %collective-permute-start.6 = (bf16[40,1024]{1,0:T(8,128)(2,1)S(1)}, bf16[40,1024]{1,0:T(8,128)(2,1)S(1)}, u32[]{:S(2)}, u32[]{:S(2)}) collective-permute-start(bf16[40,1024]{1,0:T(8,128)(2,1)S(1)} %get-tuple-element.43), channel_id=1, source_target_pairs={{0,4},{1,5},{2,6},{3,7},{4,8},{5,9},{6,10},{7,11},{8,12},{9,13},{1... | collective-permute-start | bytes 245768 | tf_op jit(solution)/shard_map/ppermute | solution.py:399
  8.1 1.1 %collective-permute-start.7 = (bf16[40,1024]{1,0:T(8,128)(2,1)S(1)}, bf16[40,1024]{1,0:T(8,128)(2,1)S(1)}, u32[]{:S(2)}, u32[]{:S(2)}) collective-permute-start(bf16[40,1024]{1,0:T(8,128)(2,1)S(1)} %get-tuple-element.44), channel_id=1, source_target_pairs={{0,8},{1,9},{2,10},{3,11},{4,12},{5,13},{6,14},{7,15},{8,0},{9,1},... | collective-permute-start | bytes 245768 | tf_op jit(solution)/shard_map/ppermute | solution.py:399
  9.2 2.9 %collective-permute-start.8 = (bf16[40,1024]{1,0:T(8,128)(2,1)S(1)}, bf16[40,1024]{1,0:T(8,128)(2,1)S(1)}, u32[]{:S(2)}, u32[]{:S(2)}) collective-permute-start(bf16[40,1024]{1,0:T(8,128)(2,1)S(1)} %get-tuple-element.45), channel_id=1, source_target_pairs={{0,12},{1,13},{2,14},{3,15},{4,0},{5,1},{6,2},{7,3},{8,4},{9,5},{1... | collective-permute-start | bytes 245768 | tf_op jit(solution)/shard_map/ppermute | solution.py:399
  12.0 0.3 collective-permute-start.1
  12.4 1.2 %collective-permute-start.2 = (bf16[40,1024]{1,0:T(8,128)(2,1)S(1)}, bf16[40,1024]{1,0:T(8,128)(2,1)S(1)}, u32[]{:S(2)}, u32[]{:S(2)}) collective-permute-start(bf16[40,1024]{1,0:T(8,128)(2,1)S(1)} %get-tuple-element.42), channel_id=1, source_target_pairs={{0,12},{1,13},{2,14},{3,15},{4,0},{5,1},{6,2},{7,3},{8,4},{9,5},{1... | collective-permute-start | bytes 245768 | tf_op jit(solution)/shard_map/ppermute | solution.py:399
  13.6 0.1 collective-permute-done.6.refs_1_
  13.7 3.5 %collective-permute-done.7.refs_2_ = bf16[40,1024]{1,0:T(8,128)(2,1)S(1)} collective-permute-done((bf16[40,1024]{1,0:T(8,128)(2,1)S(1)}, bf16[40,1024]{1,0:T(8,128)(2,1)S(1)}, u32[]{:S(2)}, u32[]{:S(2)}) %collective-permute-start.7) | collective-permute-done | bytes 81952 | tf_op jit(solution)/shard_map/ppermute | solution.py:399
  17.3 0.0 collective-permute-done.8.refs_3_
  17.3 0.5 collective-permute-start.11
  17.8 0.7 copy-done.2
  18.5 0.7 copy-done.4
  19.2 2.8 %shard_map.82 = (bf16[128,384]{1,0:T(8,128)(2,1)S(1)}, bf16[128,384]{1,0:T(8,128)(2,1)S(1)}, f32[8,3584]{1,0:T(8,128)S(1)}) custom-call(s32[2,128]{1,0:T(2,128)S(1)} %bitcast.5, f32[2,128]{1,0:T(2,128)S(1)} %bitcast.6, s32[2,8,48]{2,1,0:T(8,128)S(1)} %copy-done.2), custom_call_target="tpu_custom_call" | custom-call | bytes 1048576 | tf_op jit(solution)/shard_map/pallas_call | solution.py:367
  22.0 0.1 collective-permute-start.3
  22.1 0.5 collective-permute-start.4
  22.6 0.1 collective-permute-start.5
  22.7 10.2 %shard_map.84 = (f32[160,3584]{1,0:T(8,128)S(1)}, f32[160,3584]{1,0:T(8,128)S(1)}) custom-call(bf16[40,4096]{1,0:T(8,128)(2,1)S(1)} %get-tuple-element.39.refs_0_, bf16[40,1024]{1,0:T(8,128)(2,1)S(1)} %collective-permute-done.6.refs_1_, bf16[40,1024]{1,0:T(8,128)(2,1)S(1)} %collective-permute-done.7.refs_2_, ...), custom_call_target="tpu_custom_call" | custom-call | flops 4697620480 | bytes 29360128 | tf_op jit(solution)/shard_map/pallas_call | solution.py:367
  32.9 10.6 %shard_map.85.refs_0_ = bf16[160,3584]{1,0:T(8,128)(2,1)S(1)} custom-call(bf16[40,4096]{1,0:T(8,128)(2,1)S(1)} %get-tuple-element.39.refs_0_, bf16[40,1024]{1,0:T(8,128)(2,1)S(1)} %collective-permute-done.refs_1_, bf16[40,1024]{1,0:T(8,128)(2,1)S(1)} %collective-permute-done.1.refs_2_, bf16[40,1024]{1,0:T(8,128)(2,1)S(1)} %collective-permute-done.2.refs_3_, ...), custom_call_target="tpu_custom_call" | custom-call | flops 4697620480 | bytes 29360128 | tf_op jit(solution)/shard_map/pallas_call | solution.py:367
  43.5 4.5 %shard_map.88 = (bf16[160,512]{1,0:T(8,128)(2,1)S(1)}, bf16[160,512]{1,0:T(8,128)(2,1)S(1)}) custom-call(bf16[160,3584]{1,0:T(8,128)(2,1)S(1)} %shard_map.85.refs_0_, bf16[3584,4096]{1,0:T(8,128)(2,1)} %refs_1_.7), custom_call_target="tpu_custom_call" | custom-call | flops 1174405120 | bytes 7340032 | tf_op jit(solution)/shard_map/pallas_call | solution.py:367
  48.0 0.5 collective-permute-start.21
  48.5 0.1 collective-permute-start.22
  48.6 4.5 %shard_map.86 = (bf16[160,512]{1,0:T(8,128)(2,1)S(1)}, bf16[160,512]{1,0:T(8,128)(2,1)S(1)}) custom-call(bf16[160,3584]{1,0:T(8,128)(2,1)S(1)} %shard_map.85.refs_0_, bf16[3584,4096]{1,0:T(8,128)(2,1)} %refs_1_.7), custom_call_target="tpu_custom_call" | custom-call | flops 1174405120 | bytes 7340032 | tf_op jit(solution)/shard_map/pallas_call | solution.py:367
  53.1 0.5 collective-permute-start.12
  53.6 0.1 collective-permute-start.13
  53.7 4.5 %shard_map.89 = (bf16[40,512]{1,0:T(8,128)(2,1)S(1)}, bf16[40,512]{1,0:T(8,128)(2,1)S(1)}, bf16[40,512]{1,0:T(8,128)(2,1)S(1)}, bf16[40,512]{1,0:T(8,128)(2,1)S(...) custom-call(bf16[160,3584]{1,0:T(8,128)(2,1)S(1)} %shard_map.85.refs, ...), custom_call_target="tpu_custom_call" | custom-call | flops 1174405120 | bytes 7340032 | tf_op jit(solution)/shard_map/pallas_call | solution.py:367
  58.2 1.9 %collective-permute-start.23 = (bf16[40,512]{1,0:T(8,128)(2,1)S(1)}, bf16[40,512]{1,0:T(8,128)(2,1)S(1)}, u32[]{:S(2)}, u32[]{:S(2)}) collective-permute-start(bf16[40,512]{1,0:T(8,128)(2,1)S(1)} %get-tuple-element.62), channel_id=1, source_target_pairs={{0,2},{1,3},{2,0},{3,1},{4,6},{5,7},{6,4},{7,5},{8,10},{9,11},{10,... | collective-permute-start | bytes 122888 | tf_op jit(solution)/shard_map/ppermute | solution.py:399
  60.1 6.5 %collective-permute-start.24 = (bf16[40,512]{1,0:T(8,128)(2,1)S(1)}, bf16[40,512]{1,0:T(8,128)(2,1)S(1)}, u32[]{:S(2)}, u32[]{:S(2)}) collective-permute-start(bf16[40,512]{1,0:T(8,128)(2,1)S(1)} %get-tuple-element.63), channel_id=1, source_target_pairs={{0,12},{1,13},{2,14},{3,15},{4,0},{5,1},{6,2},{7,3},{8,4},{9,5},{1... | collective-permute-start | bytes 122888 | tf_op jit(solution)/shard_map/ppermute | solution.py:399
  66.6 0.0 collective-permute-start.25
  66.7 3.8 %collective-permute-start.27 = (bf16[40,512]{1,0:T(8,128)(2,1)S(1)}, bf16[40,512]{1,0:T(8,128)(2,1)S(1)}, u32[]{:S(2)}, u32[]{:S(2)}) collective-permute-start(bf16[40,512]{1,0:T(8,128)(2,1)S(1)} %get-tuple-element.66), channel_id=1, source_target_pairs={{0,10},{1,11},{2,8},{3,9},{4,14},{5,15},{6,12},{7,13},{8,2},{9,3},... | collective-permute-start | bytes 122888 | tf_op jit(solution)/shard_map/ppermute | solution.py:399
  70.5 4.5 %shard_map.87 = (bf16[40,512]{1,0:T(8,128)(2,1)S(1)}, bf16[40,512]{1,0:T(8,128)(2,1)S(1)}, bf16[40,512]{1,0:T(8,128)(2,1)S(1)}, bf16[40,512]{1,0:T(8,128)(2,1)S(...) custom-call(bf16[160,3584]{1,0:T(8,128)(2,1)S(1)} %shard_map.85.refs, ...), custom_call_target="tpu_custom_call" | custom-call | flops 1174405120 | bytes 7340032 | tf_op jit(solution)/shard_map/pallas_call | solution.py:367
  75.0 2.1 %collective-permute-start.28 = (bf16[40,512]{1,0:T(8,128)(2,1)S(1)}, bf16[40,512]{1,0:T(8,128)(2,1)S(1)}, u32[]{:S(2)}, u32[]{:S(2)}) collective-permute-start(bf16[40,512]{1,0:T(8,128)(2,1)S(1)} %get-tuple-element.67), channel_id=1, source_target_pairs={{0,4},{1,5},{2,6},{3,7},{4,8},{5,9},{6,10},{7,11},{8,12},{9,13},{1... | collective-permute-start | bytes 122888 | tf_op jit(solution)/shard_map/ppermute | solution.py:399
  77.1 0.0 collective-permute-start.29
  77.1 1.5 %collective-permute-start.14 = (bf16[40,512]{1,0:T(8,128)(2,1)S(1)}, bf16[40,512]{1,0:T(8,128)(2,1)S(1)}, u32[]{:S(2)}, u32[]{:S(2)}) collective-permute-start(bf16[40,512]{1,0:T(8,128)(2,1)S(1)} %get-tuple-element.52), channel_id=1, source_target_pairs={{0,2},{1,3},{2,0},{3,1},{4,6},{5,7},{6,4},{7,5},{8,10},{9,11},{10,... | collective-permute-start | bytes 122888 | tf_op jit(solution)/shard_map/ppermute | solution.py:399
  78.6 3.8 %collective-permute-start.15 = (bf16[40,512]{1,0:T(8,128)(2,1)S(1)}, bf16[40,512]{1,0:T(8,128)(2,1)S(1)}, u32[]{:S(2)}, u32[]{:S(2)}) collective-permute-start(bf16[40,512]{1,0:T(8,128)(2,1)S(1)} %get-tuple-element.53), channel_id=1, source_target_pairs={{0,12},{1,13},{2,14},{3,15},{4,0},{5,1},{6,2},{7,3},{8,4},{9,5},{1... | collective-permute-start | bytes 122888 | tf_op jit(solution)/shard_map/ppermute | solution.py:399
  82.4 0.0 collective-permute-start.16
  82.4 0.1 collective-permute-start.17
  82.4 1.3 %collective-permute-done.29.refs_15_ = bf16[40,512]{1,0:T(8,128)(2,1)S(1)} collective-permute-done((bf16[40,512]{1,0:T(8,128)(2,1)S(1)}, bf16[40,512]{1,0:T(8,128)(2,1)S(1)}, u32[]{:S(2)}, u32[]{:S(2)}) %collective-permute-start.29) | collective-permute-done | bytes 40992 | tf_op jit(solution)/shard_map/ppermute | solution.py:399
  83.8 2.5 %collective-permute-start.18 = (bf16[40,512]{1,0:T(8,128)(2,1)S(1)}, bf16[40,512]{1,0:T(8,128)(2,1)S(1)}, u32[]{:S(2)}, u32[]{:S(2)}) collective-permute-start(bf16[40,512]{1,0:T(8,128)(2,1)S(1)} %get-tuple-element.56), channel_id=1, source_target_pairs={{0,10},{1,11},{2,8},{3,9},{4,14},{5,15},{6,12},{7,13},{8,2},{9,3},... | collective-permute-start | bytes 122888 | tf_op jit(solution)/shard_map/ppermute | solution.py:399
  86.2 2.0 %collective-permute-start.19 = (bf16[40,512]{1,0:T(8,128)(2,1)S(1)}, bf16[40,512]{1,0:T(8,128)(2,1)S(1)}, u32[]{:S(2)}, u32[]{:S(2)}) collective-permute-start(bf16[40,512]{1,0:T(8,128)(2,1)S(1)} %get-tuple-element.57), channel_id=1, source_target_pairs={{0,4},{1,5},{2,6},{3,7},{4,8},{5,9},{6,10},{7,11},{8,12},{9,13},{1... | collective-permute-start | bytes 122888 | tf_op jit(solution)/shard_map/ppermute | solution.py:399
  88.2 0.0 collective-permute-start.20
  88.2 2.6 %collective-permute-done.18.refs_5_ = bf16[40,512]{1,0:T(8,128)(2,1)S(1)} collective-permute-done((bf16[40,512]{1,0:T(8,128)(2,1)S(1)}, bf16[40,512]{1,0:T(8,128)(2,1)S(1)}, u32[]{:S(2)}, u32[]{:S(2)}) %collective-permute-start.18) | collective-permute-done | bytes 40992 | tf_op jit(solution)/shard_map/ppermute | solution.py:399
  90.9 1.2 %collective-permute-done.19.refs_6_ = bf16[40,512]{1,0:T(8,128)(2,1)S(1)} collective-permute-done((bf16[40,512]{1,0:T(8,128)(2,1)S(1)}, bf16[40,512]{1,0:T(8,128)(2,1)S(1)}, u32[]{:S(2)}, u32[]{:S(2)}) %collective-permute-start.19) | collective-permute-done | bytes 40992 | tf_op jit(solution)/shard_map/ppermute | solution.py:399
  92.0 2.9 %collective-permute-done.20.refs_7_ = bf16[40,512]{1,0:T(8,128)(2,1)S(1)} collective-permute-done((bf16[40,512]{1,0:T(8,128)(2,1)S(1)}, bf16[40,512]{1,0:T(8,128)(2,1)S(1)}, u32[]{:S(2)}, u32[]{:S(2)}) %collective-permute-start.20) | collective-permute-done | bytes 40992 | tf_op jit(solution)/shard_map/ppermute | solution.py:399
  94.9 1.1 %shard_map.90 = bf16[128,1024]{1,0:T(8,128)(2,1)} custom-call(bf16[128,384]{1,0:T(8,128)(2,1)S(1)} %get-tuple-element.37.high, bf16[128,384]{1,0:T(8,128)(2,1)S(1)} %get-tuple-element.38.low, bf16[40,512]{1,0:T(8,128)(2,1)S(1)} %get-tuple-element.51.refs_0_, bf16[40,512]{1,0:T(8,128)(2,1)S(1)} %collective-permute-done.14.refs_1_, ...), custom_call_target="tpu_custom_call" | custom-call | flops 167772160 | bytes 1310720 | tf_op jit(solution)/shard_map/pallas_call | solution.py:367
  (31 shorter events, 0.1 us)
Async XLA Ops:
  0.0 1.2 %copy-start = (bf16[128,4096]{1,0:T(8,128)(2,1)S(1)}, bf16[128,4096]{1,0:T(8,128)(2,1)}, u32[]{:S(2)}) copy-start(bf16[128,4096]{1,0:T(8,128)(2,1)} %tokens.1) | copy-start | bytes 3145732
  1.2 0.7 copy-start.1
  1.9 0.7 copy-start.3
  3.5 8.9 %collective-permute-start = (bf16[40,1024]{1,0:T(8,128)(2,1)S(1)}, bf16[40,1024]{1,0:T(8,128)(2,1)S(1)}, u32[]{:S(2)}, u32[]{:S(2)}) collective-permute-start(bf16[40,1024]{1,0:T(8,128)(2,1)S(1)} %get-tuple-element.40), channel_id=1, source_target_pairs={{0,4},{1,5},{2,6},{3,7},{4,8},{5,9},{6,10},{7,11},{8,12},{9,13},{1... | collective-permute-start | bytes 245768 | tf_op jit(solution)/shard_map/ppermute | solution.py:399
  6.5 7.2 %collective-permute-start.6 = (bf16[40,1024]{1,0:T(8,128)(2,1)S(1)}, bf16[40,1024]{1,0:T(8,128)(2,1)S(1)}, u32[]{:S(2)}, u32[]{:S(2)}) collective-permute-start(bf16[40,1024]{1,0:T(8,128)(2,1)S(1)} %get-tuple-element.43), channel_id=1, source_target_pairs={{0,4},{1,5},{2,6},{3,7},{4,8},{5,9},{6,10},{7,11},{8,12},{9,13},{1... | collective-permute-start | bytes 245768 | tf_op jit(solution)/shard_map/ppermute | solution.py:399
  8.1 9.2 %collective-permute-start.7 = (bf16[40,1024]{1,0:T(8,128)(2,1)S(1)}, bf16[40,1024]{1,0:T(8,128)(2,1)S(1)}, u32[]{:S(2)}, u32[]{:S(2)}) collective-permute-start(bf16[40,1024]{1,0:T(8,128)(2,1)S(1)} %get-tuple-element.44), channel_id=1, source_target_pairs={{0,8},{1,9},{2,10},{3,11},{4,12},{5,13},{6,14},{7,15},{8,0},{9,1},... | collective-permute-start | bytes 245768 | tf_op jit(solution)/shard_map/ppermute | solution.py:399
  9.2 8.1 %collective-permute-start.8 = (bf16[40,1024]{1,0:T(8,128)(2,1)S(1)}, bf16[40,1024]{1,0:T(8,128)(2,1)S(1)}, u32[]{:S(2)}, u32[]{:S(2)}) collective-permute-start(bf16[40,1024]{1,0:T(8,128)(2,1)S(1)} %get-tuple-element.45), channel_id=1, source_target_pairs={{0,12},{1,13},{2,14},{3,15},{4,0},{5,1},{6,2},{7,3},{8,4},{9,5},{1... | collective-permute-start | bytes 245768 | tf_op jit(solution)/shard_map/ppermute | solution.py:399
  12.0 10.0 %collective-permute-start.1 = (bf16[40,1024]{1,0:T(8,128)(2,1)S(1)}, bf16[40,1024]{1,0:T(8,128)(2,1)S(1)}, u32[]{:S(2)}, u32[]{:S(2)}) collective-permute-start(bf16[40,1024]{1,0:T(8,128)(2,1)S(1)} %get-tuple-element.41), channel_id=1, source_target_pairs={{0,8},{1,9},{2,10},{3,11},{4,12},{5,13},{6,14},{7,15},{8,0},{9,1},... | collective-permute-start | bytes 245768 | tf_op jit(solution)/shard_map/ppermute | solution.py:399
  12.4 9.7 %collective-permute-start.2 = (bf16[40,1024]{1,0:T(8,128)(2,1)S(1)}, bf16[40,1024]{1,0:T(8,128)(2,1)S(1)}, u32[]{:S(2)}, u32[]{:S(2)}) collective-permute-start(bf16[40,1024]{1,0:T(8,128)(2,1)S(1)} %get-tuple-element.42), channel_id=1, source_target_pairs={{0,12},{1,13},{2,14},{3,15},{4,0},{5,1},{6,2},{7,3},{8,4},{9,5},{1... | collective-permute-start | bytes 245768 | tf_op jit(solution)/shard_map/ppermute | solution.py:399
  13.7 8.9 %collective-permute-start.9 = (bf16[40,1024]{1,0:T(8,128)(2,1)S(1)}, bf16[40,1024]{1,0:T(8,128)(2,1)S(1)}, u32[]{:S(2)}, u32[]{:S(2)}) collective-permute-start(bf16[40,1024]{1,0:T(8,128)(2,1)S(1)} %collective-permute-done.6.refs_1_), channel_id=1, source_target_pairs={{0,1},{1,0},{2,3},{3,2},{4,5},{5,4},{6,7},{7,6},{8,9},{9,8},{10,11... | collective-permute-start | bytes 245768 | tf_op jit(solution)/shard_map/ppermute | solution.py:402
  17.3 5.4 %collective-permute-start.10 = (bf16[40,1024]{1,0:T(8,128)(2,1)S(1)}, bf16[40,1024]{1,0:T(8,128)(2,1)S(1)}, u32[]{:S(2)}, u32[]{:S(2)}) collective-permute-start(bf16[40,1024]{1,0:T(8,128)(2,1)S(1)} %collective-permute-done.7.refs_2_), channel_id=1, source_target_pairs={{0,1},{1,0},{2,3},{3,2},{4,5},{5,4},{6,7},{7,6},{8,9},{9,8},{10,11... | collective-permute-start | bytes 245768 | tf_op jit(solution)/shard_map/ppermute | solution.py:402
  17.3 5.4 %collective-permute-start.11 = (bf16[40,1024]{1,0:T(8,128)(2,1)S(1)}, bf16[40,1024]{1,0:T(8,128)(2,1)S(1)}, u32[]{:S(2)}, u32[]{:S(2)}) collective-permute-start(bf16[40,1024]{1,0:T(8,128)(2,1)S(1)} %collective-permute-done.8.refs_3_), channel_id=1, source_target_pairs={{0,1},{1,0},{2,3},{3,2},{4,5},{5,4},{6,7},{7,6},{8,9},{9,8},{10,11... | collective-permute-start | bytes 245768 | tf_op jit(solution)/shard_map/ppermute | solution.py:402
  17.8 0.7 copy-start.2
  18.5 0.7 copy-start.4
  22.0 10.9 %collective-permute-start.3 = (bf16[40,1024]{1,0:T(8,128)(2,1)S(1)}, bf16[40,1024]{1,0:T(8,128)(2,1)S(1)}, u32[]{:S(2)}, u32[]{:S(2)}) collective-permute-start(bf16[40,1024]{1,0:T(8,128)(2,1)S(1)} %collective-permute-done.refs_1_), channel_id=1, source_target_pairs={{0,1},{1,0},{2,3},{3,2},{4,5},{5,4},{6,7},{7,6},{8,9},{9,8},{10,11... | collective-permute-start | bytes 245768 | tf_op jit(solution)/shard_map/ppermute | solution.py:402
  22.1 10.8 %collective-permute-start.4 = (bf16[40,1024]{1,0:T(8,128)(2,1)S(1)}, bf16[40,1024]{1,0:T(8,128)(2,1)S(1)}, u32[]{:S(2)}, u32[]{:S(2)}) collective-permute-start(bf16[40,1024]{1,0:T(8,128)(2,1)S(1)} %collective-permute-done.1.refs_2_), channel_id=1, source_target_pairs={{0,1},{1,0},{2,3},{3,2},{4,5},{5,4},{6,7},{7,6},{8,9},{9,8},{10,11... | collective-permute-start | bytes 245768 | tf_op jit(solution)/shard_map/ppermute | solution.py:402
  22.6 10.3 %collective-permute-start.5 = (bf16[40,1024]{1,0:T(8,128)(2,1)S(1)}, bf16[40,1024]{1,0:T(8,128)(2,1)S(1)}, u32[]{:S(2)}, u32[]{:S(2)}) collective-permute-start(bf16[40,1024]{1,0:T(8,128)(2,1)S(1)} %collective-permute-done.2.refs_3_), channel_id=1, source_target_pairs={{0,1},{1,0},{2,3},{3,2},{4,5},{5,4},{6,7},{7,6},{8,9},{9,8},{10,11... | collective-permute-start | bytes 245768 | tf_op jit(solution)/shard_map/ppermute | solution.py:402
  48.0 5.7 %collective-permute-start.21 = (bf16[160,512]{1,0:T(8,128)(2,1)S(1)}, bf16[160,512]{1,0:T(8,128)(2,1)S(1)}, u32[]{:S(2)}, u32[]{:S(2)}) collective-permute-start(bf16[160,512]{1,0:T(8,128)(2,1)S(1)} %get-tuple-element.59), channel_id=1, source_target_pairs={{0,1},{1,0},{2,3},{3,2},{4,5},{5,4},{6,7},{7,6},{8,9},{9,8},{10,11... | collective-permute-start | bytes 491528 | tf_op jit(solution)/shard_map/ppermute | solution.py:402
  48.5 5.2 %collective-permute-start.22 = (bf16[160,512]{1,0:T(8,128)(2,1)S(1)}, bf16[160,512]{1,0:T(8,128)(2,1)S(1)}, u32[]{:S(2)}, u32[]{:S(2)}) collective-permute-start(bf16[160,512]{1,0:T(8,128)(2,1)S(1)} %get-tuple-element.60), channel_id=1, source_target_pairs={{0,1},{1,0},{2,3},{3,2},{4,5},{5,4},{6,7},{7,6},{8,9},{9,8},{10,11... | collective-permute-start | bytes 491528 | tf_op jit(solution)/shard_map/ppermute | solution.py:402
  53.1 13.5 %collective-permute-start.12 = (bf16[160,512]{1,0:T(8,128)(2,1)S(1)}, bf16[160,512]{1,0:T(8,128)(2,1)S(1)}, u32[]{:S(2)}, u32[]{:S(2)}) collective-permute-start(bf16[160,512]{1,0:T(8,128)(2,1)S(1)} %get-tuple-element.49), channel_id=1, source_target_pairs={{0,1},{1,0},{2,3},{3,2},{4,5},{5,4},{6,7},{7,6},{8,9},{9,8},{10,11... | collective-permute-start | bytes 491528 | tf_op jit(solution)/shard_map/ppermute | solution.py:402
  53.6 13.0 %collective-permute-start.13 = (bf16[160,512]{1,0:T(8,128)(2,1)S(1)}, bf16[160,512]{1,0:T(8,128)(2,1)S(1)}, u32[]{:S(2)}, u32[]{:S(2)}) collective-permute-start(bf16[160,512]{1,0:T(8,128)(2,1)S(1)} %get-tuple-element.50), channel_id=1, source_target_pairs={{0,1},{1,0},{2,3},{3,2},{4,5},{5,4},{6,7},{7,6},{8,9},{9,8},{10,11... | collective-permute-start | bytes 491528 | tf_op jit(solution)/shard_map/ppermute | solution.py:402
  58.2 16.8 %collective-permute-start.23 = (bf16[40,512]{1,0:T(8,128)(2,1)S(1)}, bf16[40,512]{1,0:T(8,128)(2,1)S(1)}, u32[]{:S(2)}, u32[]{:S(2)}) collective-permute-start(bf16[40,512]{1,0:T(8,128)(2,1)S(1)} %get-tuple-element.62), channel_id=1, source_target_pairs={{0,2},{1,3},{2,0},{3,1},{4,6},{5,7},{6,4},{7,5},{8,10},{9,11},{10,... | collective-permute-start | bytes 122888 | tf_op jit(solution)/shard_map/ppermute | solution.py:399
  60.1 16.9 %collective-permute-start.24 = (bf16[40,512]{1,0:T(8,128)(2,1)S(1)}, bf16[40,512]{1,0:T(8,128)(2,1)S(1)}, u32[]{:S(2)}, u32[]{:S(2)}) collective-permute-start(bf16[40,512]{1,0:T(8,128)(2,1)S(1)} %get-tuple-element.63), channel_id=1, source_target_pairs={{0,12},{1,13},{2,14},{3,15},{4,0},{5,1},{6,2},{7,3},{8,4},{9,5},{1... | collective-permute-start | bytes 122888 | tf_op jit(solution)/shard_map/ppermute | solution.py:399
  66.6 10.5 %collective-permute-start.25 = (bf16[40,512]{1,0:T(8,128)(2,1)S(1)}, bf16[40,512]{1,0:T(8,128)(2,1)S(1)}, u32[]{:S(2)}, u32[]{:S(2)}) collective-permute-start(bf16[40,512]{1,0:T(8,128)(2,1)S(1)} %get-tuple-element.64), channel_id=1, source_target_pairs={{0,14},{1,15},{2,12},{3,13},{4,2},{5,3},{6,0},{7,1},{8,6},{9,7},{1... | collective-permute-start | bytes 122888 | tf_op jit(solution)/shard_map/ppermute | solution.py:399
  66.6 12.0 %collective-permute-start.26 = (bf16[40,512]{1,0:T(8,128)(2,1)S(1)}, bf16[40,512]{1,0:T(8,128)(2,1)S(1)}, u32[]{:S(2)}, u32[]{:S(2)}) collective-permute-start(bf16[40,512]{1,0:T(8,128)(2,1)S(1)} %get-tuple-element.65), channel_id=1, source_target_pairs={{0,8},{1,9},{2,10},{3,11},{4,12},{5,13},{6,14},{7,15},{8,0},{9,1},... | collective-permute-start | bytes 122888 | tf_op jit(solution)/shard_map/ppermute | solution.py:399
  66.7 15.7 %collective-permute-start.27 = (bf16[40,512]{1,0:T(8,128)(2,1)S(1)}, bf16[40,512]{1,0:T(8,128)(2,1)S(1)}, u32[]{:S(2)}, u32[]{:S(2)}) collective-permute-start(bf16[40,512]{1,0:T(8,128)(2,1)S(1)} %get-tuple-element.66), channel_id=1, source_target_pairs={{0,10},{1,11},{2,8},{3,9},{4,14},{5,15},{6,12},{7,13},{8,2},{9,3},... | collective-permute-start | bytes 122888 | tf_op jit(solution)/shard_map/ppermute | solution.py:399
  75.0 7.4 %collective-permute-start.28 = (bf16[40,512]{1,0:T(8,128)(2,1)S(1)}, bf16[40,512]{1,0:T(8,128)(2,1)S(1)}, u32[]{:S(2)}, u32[]{:S(2)}) collective-permute-start(bf16[40,512]{1,0:T(8,128)(2,1)S(1)} %get-tuple-element.67), channel_id=1, source_target_pairs={{0,4},{1,5},{2,6},{3,7},{4,8},{5,9},{6,10},{7,11},{8,12},{9,13},{1... | collective-permute-start | bytes 122888 | tf_op jit(solution)/shard_map/ppermute | solution.py:399
  77.1 6.7 %collective-permute-start.29 = (bf16[40,512]{1,0:T(8,128)(2,1)S(1)}, bf16[40,512]{1,0:T(8,128)(2,1)S(1)}, u32[]{:S(2)}, u32[]{:S(2)}) collective-permute-start(bf16[40,512]{1,0:T(8,128)(2,1)S(1)} %get-tuple-element.68), channel_id=1, source_target_pairs={{0,6},{1,7},{2,4},{3,5},{4,10},{5,11},{6,8},{7,9},{8,14},{9,15},{1... | collective-permute-start | bytes 122888 | tf_op jit(solution)/shard_map/ppermute | solution.py:399
  77.1 9.2 %collective-permute-start.14 = (bf16[40,512]{1,0:T(8,128)(2,1)S(1)}, bf16[40,512]{1,0:T(8,128)(2,1)S(1)}, u32[]{:S(2)}, u32[]{:S(2)}) collective-permute-start(bf16[40,512]{1,0:T(8,128)(2,1)S(1)} %get-tuple-element.52), channel_id=1, source_target_pairs={{0,2},{1,3},{2,0},{3,1},{4,6},{5,7},{6,4},{7,5},{8,10},{9,11},{10,... | collective-permute-start | bytes 122888 | tf_op jit(solution)/shard_map/ppermute | solution.py:399
  78.6 9.6 %collective-permute-start.15 = (bf16[40,512]{1,0:T(8,128)(2,1)S(1)}, bf16[40,512]{1,0:T(8,128)(2,1)S(1)}, u32[]{:S(2)}, u32[]{:S(2)}) collective-permute-start(bf16[40,512]{1,0:T(8,128)(2,1)S(1)} %get-tuple-element.53), channel_id=1, source_target_pairs={{0,12},{1,13},{2,14},{3,15},{4,0},{5,1},{6,2},{7,3},{8,4},{9,5},{1... | collective-permute-start | bytes 122888 | tf_op jit(solution)/shard_map/ppermute | solution.py:399
  82.4 5.9 %collective-permute-start.16 = (bf16[40,512]{1,0:T(8,128)(2,1)S(1)}, bf16[40,512]{1,0:T(8,128)(2,1)S(1)}, u32[]{:S(2)}, u32[]{:S(2)}) collective-permute-start(bf16[40,512]{1,0:T(8,128)(2,1)S(1)} %get-tuple-element.54), channel_id=1, source_target_pairs={{0,14},{1,15},{2,12},{3,13},{4,2},{5,3},{6,0},{7,1},{8,6},{9,7},{1... | collective-permute-start | bytes 122888 | tf_op jit(solution)/shard_map/ppermute | solution.py:399
  82.4 5.9 %collective-permute-start.17 = (bf16[40,512]{1,0:T(8,128)(2,1)S(1)}, bf16[40,512]{1,0:T(8,128)(2,1)S(1)}, u32[]{:S(2)}, u32[]{:S(2)}) collective-permute-start(bf16[40,512]{1,0:T(8,128)(2,1)S(1)} %get-tuple-element.55), channel_id=1, source_target_pairs={{0,8},{1,9},{2,10},{3,11},{4,12},{5,13},{6,14},{7,15},{8,0},{9,1},... | collective-permute-start | bytes 122888 | tf_op jit(solution)/shard_map/ppermute | solution.py:399
  83.8 7.1 %collective-permute-start.18 = (bf16[40,512]{1,0:T(8,128)(2,1)S(1)}, bf16[40,512]{1,0:T(8,128)(2,1)S(1)}, u32[]{:S(2)}, u32[]{:S(2)}) collective-permute-start(bf16[40,512]{1,0:T(8,128)(2,1)S(1)} %get-tuple-element.56), channel_id=1, source_target_pairs={{0,10},{1,11},{2,8},{3,9},{4,14},{5,15},{6,12},{7,13},{8,2},{9,3},... | collective-permute-start | bytes 122888 | tf_op jit(solution)/shard_map/ppermute | solution.py:399
  86.2 5.8 %collective-permute-start.19 = (bf16[40,512]{1,0:T(8,128)(2,1)S(1)}, bf16[40,512]{1,0:T(8,128)(2,1)S(1)}, u32[]{:S(2)}, u32[]{:S(2)}) collective-permute-start(bf16[40,512]{1,0:T(8,128)(2,1)S(1)} %get-tuple-element.57), channel_id=1, source_target_pairs={{0,4},{1,5},{2,6},{3,7},{4,8},{5,9},{6,10},{7,11},{8,12},{9,13},{1... | collective-permute-start | bytes 122888 | tf_op jit(solution)/shard_map/ppermute | solution.py:399
  88.2 6.7 %collective-permute-start.20 = (bf16[40,512]{1,0:T(8,128)(2,1)S(1)}, bf16[40,512]{1,0:T(8,128)(2,1)S(1)}, u32[]{:S(2)}, u32[]{:S(2)}) collective-permute-start(bf16[40,512]{1,0:T(8,128)(2,1)S(1)} %get-tuple-element.58), channel_id=1, source_target_pairs={{0,6},{1,7},{2,4},{3,5},{4,10},{5,11},{6,8},{7,9},{8,14},{9,15},{1... | collective-permute-start | bytes 122888 | tf_op jit(solution)/shard_map/ppermute | solution.py:399

commit v2 on v1

--- a/solution.py
+++ b/solution.py
@@ -18,10 +18,9 @@
 
 IN_CHUNKS = 2
 OUT_CHUNKS = 2
-K_SLAB = 256
+K_SLAB = 512
 K_DEPTH = 6
-N_SLAB = 256
-N_DEPTH = 4
+N_ROWS = 512
 VMEM_LIMIT = 40 * 1024 * 1024
 
 F32 = jnp.float32
@@ -136,81 +135,87 @@
     return lax.axis_index("exp"), lax.axis_index("unit") // 2, lax.axis_index("unit") % 2
 
 
-def route_kernel(sizes, width, tokens, gain, ids, own, *rest):
+def pick_rows(named, before, d):
+    rows = named.shape[1]
+    place_of = jnp.where(named[d : d + 1, :] > 0, before[d : d + 1, :], -1)
+    return (place_of == lax.broadcasted_iota(jnp.int32, (CAP, rows), 0)).astype(F32)
+
+
+def count_earlier(ids, experts):
+    rows = ids.shape[1]
+    earlier = (
+        lax.broadcasted_iota(jnp.int32, (rows, rows), 0)
+        < lax.broadcasted_iota(jnp.int32, (rows, rows), 1)
+    ).astype(BF16)
+    named = ((ids[0:1, :] == experts) | (ids[1:2, :] == experts)).astype(jnp.int32)
+    before = jnp.dot(named.astype(BF16), earlier, preferred_element_type=F32)
+    return named, before.astype(jnp.int32)
+
+
+def group_experts(exp_count, groups, z, g, rows):
+    distance = lax.broadcasted_iota(jnp.int32, (max(8, exp_count), rows), 0)
+    return lax.rem(z + distance, exp_count) * groups + g
+
+
+def send_rows(normed, others, start, width, sends):
+    found = jnp.dot(others, normed[:, pl.ds(start, width)], preferred_element_type=F32)
+    for d, send in enumerate(sends):
+        send[...] = found[d * CAP : (d + 1) * CAP, :].astype(BF16)
+
+
+def route_kernel(sizes, width, tokens_hbm, gain_hbm, ids_hbm, normed, others, *rest):
     exp_count, groups = sizes
-    sends, normed = rest[:-1], rest[-1]
+    sends, (tokens, gain, ids, sems) = rest[:-4], rest[-4:]
+    pairs = ((tokens_hbm, tokens), (gain_hbm, gain), (ids_hbm, ids))
+    copies = [pltpu.make_async_copy(a, b, sems.at[n]) for n, (a, b) in enumerate(pairs)]
+    for copy in copies:
+        copy.start()
     rows, features = tokens.shape
     z, g, s = place(sizes)
+    for copy in copies:
+        copy.wait()
     step = 16
     for first in range(0, rows, step):
         values = tokens[first : first + step, :].astype(F32)
         mean = jnp.sum(values * values, axis=1, keepdims=True) * (1.0 / features)
         inv_rms = lax.rsqrt(mean + EPSILON)
         normed[first : first + step, :] = (values * inv_rms * gain[...]).astype(BF16)
-    earlier = (
-        lax.broadcasted_iota(jnp.int32, (rows, rows), 0)
-        < lax.broadcasted_iota(jnp.int32, (rows, rows), 1)
+    named, before = count_earlier(ids, group_experts(exp_count, groups, z, g, rows))
+    picks = [pick_rows(named, before, d) for d in range(1, exp_count)]
+    others[...] = jnp.concatenate(picks, axis=0).astype(BF16)
+    start = pl.multiple_of(s * (features // 2), 128)
+    send_rows(normed, others[...], start, width, sends)
+
+
+def prepare_kernel(sizes, width, normed, others, ids, weights, active, *rest):
+    exp_count, groups = sizes
+    own, combine_high, combine_low, mask = rest[:4]
+    sends = rest[4:]
+    rows, features = normed.shape
+    z, g, s = place(sizes)
+    for n in range(len(sends) // (exp_count - 1)):
+        start = pl.multiple_of(s * (features // 2) + (n + 1) * width, 128)
+        batch = sends[n * (exp_count - 1) : (n + 1) * (exp_count - 1)]
+        send_rows(normed, others[...], start, width, batch)
+    named, before = count_earlier(ids, group_experts(exp_count, groups, z, g, rows))
+    own[...] = jnp.dot(
+        pick_rows(named, before, 0).astype(BF16), normed[...], preferred_element_type=F32
     ).astype(BF16)
-    ids0, ids1 = ids[0:1, :], ids[1:2, :]
-    slots = lax.broadcasted_iota(jnp.int32, (CAP, rows), 0)
-    distance = lax.broadcasted_iota(jnp.int32, (max(8, exp_count), rows), 0)
-    experts = lax.rem(z + distance, exp_count) * groups + g
-    named = (ids0 == experts) | (ids1 == experts)
-    before = jnp.dot(named.astype(BF16), earlier, preferred_element_type=F32).astype(jnp.int32)
-    picks = []
-    for d in range(exp_count):
-        hit = named[d : d + 1, :].astype(jnp.int32)
-        place_of = jnp.where(hit > 0, before[d : d + 1, :], -1)
-        picks.append((place_of == slots).astype(F32))
-    own[...] = jnp.dot(
-        picks[0].astype(BF16), normed[...], preferred_element_type=F32
-    ).astype(BF16)
-    others = jnp.concatenate(picks[1:], axis=0).astype(BF16)
-    half = features // 2
-    for chunk in range(half // width):
-        start = pl.multiple_of(s * half + chunk * width, 128)
-        found = jnp.dot(others, normed[:, pl.ds(start, width)], preferred_element_type=F32)
-        for d in range(1, exp_count):
-            part = found[(d - 1) * CAP : d * CAP, :].astype(BF16)
-            sends[chunk * (exp_count - 1) + d - 1][...] = part
-
-
-def prepare_kernel(sizes, ids, weights, active, combine_high, combine_low, mask):
-    exp_count, groups = sizes
-    rows = ids.shape[1]
-    z, g, s = place(sizes)
-    earlier = (
-        lax.broadcasted_iota(jnp.int32, (rows, rows), 0)
-        < lax.broadcasted_iota(jnp.int32, (rows, rows), 1)
-    ).astype(BF16)
-    ids0, ids1 = ids[0:1, :], ids[1:2, :]
-    slots = lax.broadcasted_iota(jnp.int32, (CAP, rows), 0)
-
-    def expert_at(j):
-        return lax.rem(z + j // groups, exp_count) * groups + lax.rem(
-            g + groups - lax.rem(j, groups), groups
-        )
-
-    experts = expert_at(lax.broadcasted_iota(jnp.int32, (EXPERTS, rows), 0))
-    named = (ids0 == experts) | (ids1 == experts)
-    before = jnp.dot(named.astype(BF16), earlier, preferred_element_type=F32).astype(jnp.int32)
     zero = jnp.zeros((CAP, rows), F32)
     parts = []
-    for j in range(EXPERTS):
-        here = before[j : j + 1, :] == slots
-        expert = expert_at(j)
-        first = jnp.where(here & (ids0 == expert), weights[0:1, :], zero)
-        second = jnp.where(here & (ids1 == expert), weights[1:2, :], zero)
+    for d in range(exp_count):
+        here = pick_rows(named, before, d) > 0
+        expert = lax.rem(z + d, exp_count) * groups + g
+        first = jnp.where(here & (ids[0:1, :] == expert), weights[0:1, :], zero)
+        second = jnp.where(here & (ids[1:2, :] == expert), weights[1:2, :], zero)
         parts.append(first + second)
-    total = EXPERTS * CAP
-    padded = -(-total // 128) * 128
-    if padded > total:
-        parts.append(jnp.zeros((padded - total, rows), F32))
+    padded = combine_high.shape[1]
+    if padded > exp_count * CAP:
+        parts.append(jnp.zeros((padded - exp_count * CAP, rows), F32))
     table = jnp.concatenate(parts, axis=0).T
     high = table.astype(BF16)
-    low = (table - high.astype(F32)).astype(BF16)
     combine_high[...] = high
-    combine_low[...] = low
+    combine_low[...] = (table - high.astype(F32)).astype(BF16)
     unit_width = mask.shape[1]
     blocks = lax.broadcasted_iota(jnp.int32, mask.shape, 1) // BLK + s * (unit_width // BLK)
     source = lax.broadcasted_iota(jnp.int32, (mask.shape[0], 1), 0)
@@ -309,54 +314,65 @@
     z, g, s = place(sizes)
     refs = list(refs)
     hidden, down = refs.pop(0), refs.pop(0)
-    received = [refs.pop(0) for _ in range(groups)] if keep else None
-    count = groups * exp_count if keep else groups
-    outs = [refs.pop(0) for _ in range(count)]
-    slabs, sems = refs
+    received = refs.pop(0) if keep else None
+    total_sum, slabs, sems = refs[-3:]
+    outs = refs[:-3]
     side = s if keep else 1 - s
     part = down.shape[1] // (2 * groups)
-    per_group = width // N_SLAB
-    total = groups * per_group
-    depth = min(N_DEPTH, total)
+    pieces = down.shape[0] // N_ROWS
 
     def copy(index):
-        group = lax.rem(g + index // per_group, groups)
-        column = (group * 2 + side) * part + chunk * width + index % per_group * N_SLAB
+        group = lax.rem(g + index // pieces, groups)
+        column = pl.multiple_of((group * 2 + side) * part + chunk * width, 128)
+        lines = pl.ds(index % pieces * N_ROWS, N_ROWS)
         return pltpu.make_async_copy(
-            down.at[:, pl.ds(pl.multiple_of(column, 128), N_SLAB)],
-            slabs.at[index % depth],
-            sems.at[index % depth],
+            down.at[lines, pl.ds(column, width)], slabs.at[index], sems.at[index]
         )
 
-    for index in range(depth):
+    for index in range(groups * pieces):
         copy(index).start()
-    for index in range(total):
-        copy(index).wait()
-        value = jnp.dot(hidden[...], slabs[index % depth], preferred_element_type=F32)
-        if index + depth < total:
-            copy(index + depth).start()
-        group = index // per_group
-        cols = slice(index % per_group * N_SLAB, (index % per_group + 1) * N_SLAB)
+    for offset in range(groups):
+        for piece in range(pieces):
+            index = offset * pieces + piece
+            copy(index).wait()
+            value = jnp.dot(
+                hidden[:, piece * N_ROWS : (piece + 1) * N_ROWS],
+                slabs[index],
+                preferred_element_type=F32,
+            )
+            total_sum[...] = value if piece == 0 else total_sum[...] + value
+        cols = slice(offset * width, (offset + 1) * width)
         if keep:
-            value = value + received[group][:, cols].astype(F32)
             for d in range(exp_count):
-                lines = value[d * CAP : (d + 1) * CAP, :].astype(BF16)
-                outs[group * exp_count + d][:, cols] = lines
+                lines = slice(d * CAP, (d + 1) * CAP)
+                value = total_sum[lines, :] + received[:, cols].astype(F32)[lines, :]
+                outs[d][:, cols] = value.astype(BF16)
         else:
-            outs[group][:, cols] = value.astype(BF16)
-
-
-def combine_kernel(sizes, high, low, *refs):
-    refs = list(refs)
-    out = refs.pop()
-    total = EXPERTS * CAP
-    per_chunk = EXPERTS
+            outs[0][:, cols] = total_sum[...].astype(BF16)
+
+
+def combine_kernel(exp_count, high, low, *refs):
+    pieces = [r[...].astype(F32) for r in refs[:exp_count]]
+    kept, gives = refs[exp_count], refs[exp_count + 1 :]
+    total = exp_count * CAP
+    width = kept.shape[1]
+    found = jnp.concatenate(pieces, axis=0).astype(BF16)
+    value = jnp.dot(high[:, :total], found, preferred_element_type=F32)
+    value = value + jnp.dot(low[:, :total], found, preferred_element_type=F32)
+    kept[...] = value[:, :width]
+    for n, give in enumerate(gives):
+        give[...] = value[:, (n + 1) * width : (n + 2) * width].astype(BF16)
+
+
+def finish_kernel(chunks, *refs):
+    out = refs[-1]
+    per_chunk = (len(refs) - 1) // chunks
     width = refs[0].shape[1]
-    for chunk in range(len(refs) // per_chunk):
-        pieces = [r[...].astype(F32) for r in refs[chunk * per_chunk : (chunk + 1) * per_chunk]]
-        found = jnp.concatenate(pieces, axis=0).astype(BF16)
-        value = jnp.dot(high[:, :total], found, preferred_element_type=F32)
-        value = value + jnp.dot(low[:, :total], found, preferred_element_type=F32)
+    for chunk in range(chunks):
+        kept, *others = refs[chunk * per_chunk : (chunk + 1) * per_chunk]
+        value = kept[...]
+        for other in others:
+            value = value + other[...].astype(F32)
         out[:, chunk * width : (chunk + 1) * width] = value.astype(BF16)
 
 
@@ -401,36 +417,51 @@
     def swap(value):
         return lax.ppermute(value, "unit", [(u, u ^ 1) for u in range(unit_count)])
 
-    own, *sends = call(
+    batch = exp_count - 1
+    normed, others, *sends = call(
         functools.partial(route_kernel, sizes, width),
-        [((CAP, features), BF16)] + [((CAP, width), BF16)] * (IN_CHUNKS * (exp_count - 1)),
-        [(tokens, None), (norm_gain.reshape(1, -1), None), (ids, None)],
-        [pltpu.VMEM((tok_count, features), BF16)],
-        flops=2 * tok_count * slots * features,
+        [((tok_count, features), BF16), ((batch * CAP, tok_count), BF16)]
+        + [((CAP, width), BF16)] * batch,
+        [
+            (tokens, pltpu.HBM),
+            (norm_gain.reshape(1, -1), pltpu.HBM),
+            (ids, pltpu.HBM),
+        ],
+        [
+            pltpu.VMEM((tok_count, features), BF16),
+            pltpu.VMEM((1, features), F32),
+            pltpu.VMEM(ids.shape, jnp.int32),
+            pltpu.SemaphoreType.DMA((3,)),
+        ],
+        flops=2 * tok_count * slots * width,
         moved=4 * tok_count * features,
     )
-    padded = -(-EXPERTS * CAP // 128) * 128
-    combine_high, combine_low, mask = call(
-        functools.partial(prepare_kernel, sizes),
+    padded = -(-slots // 128) * 128
+    own, combine_high, combine_low, mask, *more = call(
+        functools.partial(prepare_kernel, sizes, width),
         [
+            ((CAP, features), BF16),
             ((tok_count, padded), BF16),
             ((tok_count, padded), BF16),
             ((max(8, exp_count), unit_width), F32),
-        ],
-        [(ids, None), (weights, None), (active_blocks, pltpu.SMEM)],
+        ]
+        + [((CAP, width), BF16)] * (batch * (IN_CHUNKS - 1)),
+        [(normed, None), (others, None), (ids, None), (weights, None), (active_blocks, pltpu.SMEM)],
+        flops=2 * tok_count * slots * features,
         moved=1 << 20,
     )
+    sends = sends + more
     mine, other = [], []
     for chunk in range(IN_CHUNKS):
-        batch = sends[chunk * (exp_count - 1) : (chunk + 1) * (exp_count - 1)]
-        arrived = [shift(value, d + 1) for d, value in enumerate(batch)]
+        ready = sends[chunk * batch : (chunk + 1) * batch]
+        arrived = [shift(value, d + 1) for d, value in enumerate(ready)]
         mine.append(arrived)
         other.append([swap(value) for value in arrived])
     sums = None
     for chunk in range(IN_CHUNKS):
         first, last = chunk == 0, chunk == IN_CHUNKS - 1
         ins = [(own, None)] + [(v, None) for v in mine[chunk] + other[chunk]]
-        ins += [(gate_weight, pl.ANY), (up_weight, pl.ANY)]
+        ins += [(gate_weight, pltpu.HBM), (up_weight, pltpu.HBM)]
         if not first:
             ins += [(v, None) for v in sums]
         if last:
@@ -456,37 +487,41 @@
     out_width = part // OUT_CHUNKS
 
     def output(chunk, keep, received):
-        ins = [(hidden, None), (down_weight, pl.ANY)] + [(v, None) for v in received]
-        outs = [((slots, out_width), BF16)] * groups
-        if keep:
-            outs = [((CAP, out_width), BF16)] * (groups * exp_count)
+        pieces = groups * (unit_width // N_ROWS)
         return call(
             functools.partial(output_kernel, sizes, chunk, out_width, keep),
-            outs,
-            ins,
+            [((CAP, groups * out_width), BF16)] * exp_count
+            if keep
+            else [((slots, groups * out_width), BF16)],
+            [(hidden, None), (down_weight, pltpu.HBM)] + [(v, None) for v in received],
             [
-                pltpu.VMEM((N_DEPTH, unit_width, N_SLAB), BF16),
-                pltpu.SemaphoreType.DMA((N_DEPTH,)),
+                pltpu.VMEM((slots, out_width), F32),
+                pltpu.VMEM((pieces, N_ROWS, out_width), BF16),
+                pltpu.SemaphoreType.DMA((pieces,)),
             ],
             flops=2 * slots * unit_width * groups * out_width,
             moved=2 * unit_width * groups * out_width,
         )
 
-    given = [output(chunk, False, ()) for chunk in range(OUT_CHUNKS)]
-    taken = [[swap(value) for value in values] for values in given]
-    pieces = []
+    given = [output(chunk, False, ())[0] for chunk in range(OUT_CHUNKS)]
+    taken = [swap(value) for value in given]
+    last = []
     for chunk in range(OUT_CHUNKS):
-        kept = output(chunk, True, taken[chunk])
-        for d in range(exp_count):
-            for offset in range(groups):
-                value = kept[offset * exp_count + d]
-                pieces.append(shift(value, -d, offset) if d or offset else value)
+        kept = output(chunk, True, [taken[chunk]])
+        home = [kept[0]] + [shift(kept[d], -d) for d in range(1, exp_count)]
+        stay, *gives = call(
+            functools.partial(combine_kernel, exp_count),
+            [((tok_count, out_width), F32)] + [((tok_count, out_width), BF16)] * (groups - 1),
+            [(combine_high, None), (combine_low, None)] + [(v, None) for v in home],
+            flops=4 * tok_count * slots * groups * out_width,
+            moved=1 << 20,
+        )
+        last += [stay] + [shift(value, 0, n + 1) for n, value in enumerate(gives)]
     return call(
-        functools.partial(combine_kernel, sizes),
+        functools.partial(finish_kernel, OUT_CHUNKS),
         [((tok_count, part), BF16)],
-        [(combine_high, None), (combine_low, None)] + [(v, None) for v in pieces],
-        flops=4 * tok_count * EXPERTS * CAP * part,
-        moved=4 * EXPERTS * CAP * part,
+        [(v, None) for v in last],
+        moved=1 << 20,
     )[0]
 
 

time: 96.4 us -> 85.3 us (0.88)
  starting transfers between devices: 36.6 us -> 23.6 us
  waiting for transfers between devices: 11.7 us -> 16.6 us
  Pallas kernels: 43.6 us -> 40.6 us
    ppermute x20 -> x14, starting transfers between devices: 34.3 us -> 21.9 us  [shift(): return lax.ppermute(value, ('exp', 'unit'), pairs)]
    ppermute x20 -> x14, waiting for transfers between devices: 11.7 us -> 16.6 us  [shift(): return lax.ppermute(value, ('exp', 'unit'), pairs)]
    pallas_call x9 -> x11, Pallas kernels: 43.6 us -> 40.6 us  [call(): pl.pallas_call(kernel, out_shape=[jax.ShapeDtypeStruct(shape, kind) for s...]
    ppermute x10 -> x8, starting transfers between devices: 2.31 us -> 1.73 us  [swap(): return lax.ppermute(value, 'unit', [(u, u ^ 1) for u in range(unit_count)])]
  transfers between devices with their start and end apart: 30 -> 22, of which waited for: 6 -> 5; matrix products, arithmetic and copies ran while one was open for 0% -> 0% of each run, Pallas kernels for 28% -> 25%
where the time goes in v2:
time: 85.3 us; the launch traced here: 85 us
  Pallas kernels  40.6 us (48%)
  starting transfers between devices  23.6 us (28%)
  waiting for transfers between devices  16.6 us (19%)
  local copies, waits for them, and re-layouts  3.99 us (5%)
    pallas_call x11, Pallas kernels, call(): pl.pallas_call(kernel, out_shape=[jax.ShapeDtypeStruct(shape, kind) for s...  40.6 us
    ppermute x14, starting transfers between devices, shift(): return lax.ppermute(value, ('exp', 'unit'), pairs)  21.9 us
    ppermute x14, waiting for transfers between devices, shift(): return lax.ppermute(value, ('exp', 'unit'), pairs)  16.6 us
    unnamed x10, local copies, waits for them, and re-layouts  3.99 us
    ppermute x8, starting transfers between devices, swap(): return lax.ppermute(value, 'unit', [(u, u ^ 1) for u in range(unit_count)])  1.73 us
  transfers between devices with their start and end apart: 22, of which 5 were waited for; matrix products, arithmetic and copies ran while one was open for 0% of the time, Pallas kernels for 25%

profile of v2, /device:TPU:0, one launch (start us, length us, event | category | flops | bytes accessed | tf_op | source)
XLA Modules:
  0.0 85.0 jit_solution(15994465065555406044)
XLA Ops:
  0.0 1.2 %copy-done = bf16[128,4096]{1,0:T(8,128)(2,1)S(1)} copy-done((bf16[128,4096]{1,0:T(8,128)(2,1)S(1)}, bf16[128,4096]{1,0:T(8,128)(2,1)}, u32[]{:S(2)}) %copy-start) | copy-done | bytes 1048600
  1.2 0.7 copy-done.1
  1.9 0.7 copy-done.3
  2.6 0.8 shard_map.82
  3.4 0.0 copy-start.2
  3.4 0.7 copy-done.2
  4.1 0.7 copy-done.4
  4.8 3.1 %shard_map.83 = (bf16[40,4096]{1,0:T(8,128)(2,1)S(1)}, bf16[128,256]{1,0:T(8,128)(2,1)S(1)}, bf16[128,256]{1,0:T(8,128)(2,1)S(1)}, f32[8,3584]{1,0:T(8,128)S(1)}...) custom-call(bf16[128,4096]{1,0:T(8,128)(2,1)S(1)} %get-tuple-element.31.normed, ...), custom_call_target="tpu_custom_call" | custom-call | flops 167772160 | bytes 1048576 | tf_op jit(solution)/shard_map/pallas_call | solution.py:383
  7.9 3.1 %collective-permute-start = (bf16[40,1024]{1,0:T(8,128)(2,1)S(1)}, bf16[40,1024]{1,0:T(8,128)(2,1)S(1)}, u32[]{:S(2)}, u32[]{:S(2)}) collective-permute-start(bf16[40,1024]{1,0:T(8,128)(2,1)S(1)} %get-tuple-element.36), channel_id=1, source_target_pairs={{0,4},{1,5},{2,6},{3,7},{4,8},{5,9},{6,10},{7,11},{8,12},{9,13},{1... | collective-permute-start | bytes 245768 | tf_op jit(solution)/shard_map/ppermute | solution.py:415
  11.0 1.6 %collective-permute-start.6 = (bf16[40,1024]{1,0:T(8,128)(2,1)S(1)}, bf16[40,1024]{1,0:T(8,128)(2,1)S(1)}, u32[]{:S(2)}, u32[]{:S(2)}) collective-permute-start(bf16[40,1024]{1,0:T(8,128)(2,1)S(1)} %get-tuple-element.39), channel_id=1, source_target_pairs={{0,4},{1,5},{2,6},{3,7},{4,8},{5,9},{6,10},{7,11},{8,12},{9,13},{1... | collective-permute-start | bytes 245768 | tf_op jit(solution)/shard_map/ppermute | solution.py:415
  12.5 1.1 %collective-permute-start.7 = (bf16[40,1024]{1,0:T(8,128)(2,1)S(1)}, bf16[40,1024]{1,0:T(8,128)(2,1)S(1)}, u32[]{:S(2)}, u32[]{:S(2)}) collective-permute-start(bf16[40,1024]{1,0:T(8,128)(2,1)S(1)} %get-tuple-element.40), channel_id=1, source_target_pairs={{0,8},{1,9},{2,10},{3,11},{4,12},{5,13},{6,14},{7,15},{8,0},{9,1},... | collective-permute-start | bytes 245768 | tf_op jit(solution)/shard_map/ppermute | solution.py:415
  13.6 2.9 %collective-permute-start.8 = (bf16[40,1024]{1,0:T(8,128)(2,1)S(1)}, bf16[40,1024]{1,0:T(8,128)(2,1)S(1)}, u32[]{:S(2)}, u32[]{:S(2)}) collective-permute-start(bf16[40,1024]{1,0:T(8,128)(2,1)S(1)} %get-tuple-element.41), channel_id=1, source_target_pairs={{0,12},{1,13},{2,14},{3,15},{4,0},{5,1},{6,2},{7,3},{8,4},{9,5},{1... | collective-permute-start | bytes 245768 | tf_op jit(solution)/shard_map/ppermute | solution.py:415
  16.5 0.3 collective-permute-start.1
  16.8 0.0 collective-permute-done.refs_1_
  16.8 1.2 %collective-permute-start.2 = (bf16[40,1024]{1,0:T(8,128)(2,1)S(1)}, bf16[40,1024]{1,0:T(8,128)(2,1)S(1)}, u32[]{:S(2)}, u32[]{:S(2)}) collective-permute-start(bf16[40,1024]{1,0:T(8,128)(2,1)S(1)} %get-tuple-element.38), channel_id=1, source_target_pairs={{0,12},{1,13},{2,14},{3,15},{4,0},{5,1},{6,2},{7,3},{8,4},{9,5},{1... | collective-permute-start | bytes 245768 | tf_op jit(solution)/shard_map/ppermute | solution.py:415
  18.0 0.1 collective-permute-done.6.refs_1_
  18.2 0.0 collective-permute-start.9
  18.2 3.5 %collective-permute-done.7.refs_2_ = bf16[40,1024]{1,0:T(8,128)(2,1)S(1)} collective-permute-done((bf16[40,1024]{1,0:T(8,128)(2,1)S(1)}, bf16[40,1024]{1,0:T(8,128)(2,1)S(1)}, u32[]{:S(2)}, u32[]{:S(2)}) %collective-permute-start.7) | collective-permute-done | bytes 81952 | tf_op jit(solution)/shard_map/ppermute | solution.py:415
  21.7 0.0 collective-permute-start.10
  21.7 0.0 collective-permute-done.8.refs_3_
  21.7 0.5 collective-permute-start.11
  22.2 3.8 %collective-permute-done.1.refs_2_ = bf16[40,1024]{1,0:T(8,128)(2,1)S(1)} collective-permute-done((bf16[40,1024]{1,0:T(8,128)(2,1)S(1)}, bf16[40,1024]{1,0:T(8,128)(2,1)S(1)}, u32[]{:S(2)}, u32[]{:S(2)}) %collective-permute-start.1) | collective-permute-done | bytes 81952 | tf_op jit(solution)/shard_map/ppermute | solution.py:415
  26.1 0.5 collective-permute-start.4
  26.6 0.1 collective-permute-start.5
  26.6 10.5 %shard_map.84 = (f32[160,3584]{1,0:T(8,128)S(1)}, f32[160,3584]{1,0:T(8,128)S(1)}) custom-call(bf16[40,4096]{1,0:T(8,128)(2,1)S(1)} %get-tuple-element.35.refs_0_, bf16[40,1024]{1,0:T(8,128)(2,1)S(1)} %collective-permute-done.6.refs_1_, bf16[40,1024]{1,0:T(8,128)(2,1)S(1)} %collective-permute-done.7.refs_2_, ...), custom_call_target="tpu_custom_call" | custom-call | flops 4697620480 | bytes 29360128 | tf_op jit(solution)/shard_map/pallas_call | solution.py:383
  37.2 0.0 collective-permute-done.5.refs_6_
  37.2 10.9 %shard_map.85.refs_0_ = bf16[160,3584]{1,0:T(8,128)(2,1)S(1)} custom-call(bf16[40,4096]{1,0:T(8,128)(2,1)S(1)} %get-tuple-element.35.refs_0_, bf16[40,1024]{1,0:T(8,128)(2,1)S(1)} %collective-permute-done.refs_1_, bf16[40,1024]{1,0:T(8,128)(2,1)S(1)} %collective-permute-done.1.refs_2_, bf16[40,1024]{1,0:T(8,128)(2,1)S(1)} %collective-permute-done.2.refs_3_, ...), custom_call_target="tpu_custom_call" | custom-call | flops 4697620480 | bytes 29360128 | tf_op jit(solution)/shard_map/pallas_call | solution.py:383
  48.1 3.5 %shard_map.86 = bf16[160,1024]{1,0:T(8,128)(2,1)S(1)} custom-call(bf16[160,3584]{1,0:T(8,128)(2,1)S(1)} %shard_map.85.refs_0_, bf16[3584,4096]{1,0:T(8,128)(2,1)} %refs_1_.7), custom_call_target="tpu_custom_call" | custom-call | flops 1174405120 | bytes 7340032 | tf_op jit(solution)/shard_map/pallas_call | solution.py:383
  51.7 0.5 collective-permute-start.12
  52.2 3.5 %shard_map.89 = bf16[160,1024]{1,0:T(8,128)(2,1)S(1)} custom-call(bf16[160,3584]{1,0:T(8,128)(2,1)S(1)} %shard_map.85.refs_0_, bf16[3584,4096]{1,0:T(8,128)(2,1)} %refs_1_.7), custom_call_target="tpu_custom_call" | custom-call | flops 1174405120 | bytes 7340032 | tf_op jit(solution)/shard_map/pallas_call | solution.py:383
  55.7 0.1 collective-permute-start.17
  55.8 0.0 collective-permute-done.12.refs_2_
  55.8 3.5 %shard_map.87 = (bf16[40,1024]{1,0:T(8,128)(2,1)S(1)}, bf16[40,1024]{1,0:T(8,128)(2,1)S(1)}, bf16[40,1024]{1,0:T(8,128)(2,1)S(1)}, bf16[40,1024]{1,0:T(8,128)(2,1)S(1)}) custom-call(bf16[160,3584]{1,0:T(8,128)(2,1)S(1)} %shard_map.85.refs_0_, bf16[3584,4096]{1,0:T(8,128)(2,1)} %refs_1_.7, bf16[160,1024]{1,0:T(8,128)(2,1)S(1)} %collective-permute-done.12.refs_2_), custom_call_target="tpu_custom_call" | custom-call | flops 1174405120 | bytes 7340032 | tf_op jit(solution)/shard_map/pallas_call | solution.py:383
  59.3 3.6 %collective-permute-start.13 = (bf16[40,1024]{1,0:T(8,128)(2,1)S(1)}, bf16[40,1024]{1,0:T(8,128)(2,1)S(1)}, u32[]{:S(2)}, u32[]{:S(2)}) collective-permute-start(bf16[40,1024]{1,0:T(8,128)(2,1)S(1)} %get-tuple-element.46), channel_id=1, source_target_pairs={{0,12},{1,13},{2,14},{3,15},{4,0},{5,1},{6,2},{7,3},{8,4},{9,5},{1... | collective-permute-start | bytes 245768 | tf_op jit(solution)/shard_map/ppermute | solution.py:415
  62.9 0.1 collective-permute-start.14
  63.0 0.6 collective-permute-start.15
  63.6 0.0 collective-permute-done.17.refs_2_
  63.6 3.5 %shard_map.90 = (bf16[40,1024]{1,0:T(8,128)(2,1)S(1)}, bf16[40,1024]{1,0:T(8,128)(2,1)S(1)}, bf16[40,1024]{1,0:T(8,128)(2,1)S(1)}, bf16[40,1024]{1,0:T(8,128)(2,1)S(1)}) custom-call(bf16[160,3584]{1,0:T(8,128)(2,1)S(1)} %shard_map.85.refs_0_, bf16[3584,4096]{1,0:T(8,128)(2,1)} %refs_1_.7, bf16[160,1024]{1,0:T(8,128)(2,1)S(1)} %collective-permute-done.17.refs_2_), custom_call_target="tpu_custom_call" | custom-call | flops 1174405120 | bytes 7340032 | tf_op jit(solution)/shard_map/pallas_call | solution.py:383
  67.1 3.3 %collective-permute-start.18 = (bf16[40,1024]{1,0:T(8,128)(2,1)S(1)}, bf16[40,1024]{1,0:T(8,128)(2,1)S(1)}, u32[]{:S(2)}, u32[]{:S(2)}) collective-permute-start(bf16[40,1024]{1,0:T(8,128)(2,1)S(1)} %get-tuple-element.52), channel_id=1, source_target_pairs={{0,12},{1,13},{2,14},{3,15},{4,0},{5,1},{6,2},{7,3},{8,4},{9,5},{1... | collective-permute-start | bytes 245768 | tf_op jit(solution)/shard_map/ppermute | solution.py:415
  70.4 1.1 %collective-permute-start.19 = (bf16[40,1024]{1,0:T(8,128)(2,1)S(1)}, bf16[40,1024]{1,0:T(8,128)(2,1)S(1)}, u32[]{:S(2)}, u32[]{:S(2)}) collective-permute-start(bf16[40,1024]{1,0:T(8,128)(2,1)S(1)} %get-tuple-element.53), channel_id=1, source_target_pairs={{0,8},{1,9},{2,10},{3,11},{4,12},{5,13},{6,14},{7,15},{8,0},{9,1},... | collective-permute-start | bytes 245768 | tf_op jit(solution)/shard_map/ppermute | solution.py:415
  71.4 0.0 collective-permute-start.20
  71.4 0.3 shard_map.88
  71.7 1.6 %collective-permute-start.16 = (bf16[128,512]{1,0:T(8,128)(2,1)S(1)}, bf16[128,512]{1,0:T(8,128)(2,1)S(1)}, u32[]{:S(2)}, u32[]{:S(2)}) collective-permute-start(bf16[128,512]{1,0:T(8,128)(2,1)S(1)} %get-tuple-element.50), channel_id=1, source_target_pairs={{0,2},{1,3},{2,0},{3,1},{4,6},{5,7},{6,4},{7,5},{8,10},{9,11},{10,... | collective-permute-start | bytes 393224 | tf_op jit(solution)/shard_map/ppermute | solution.py:415
  73.3 5.6 %collective-permute-done.19.refs_2_ = bf16[40,1024]{1,0:T(8,128)(2,1)S(1)} collective-permute-done((bf16[40,1024]{1,0:T(8,128)(2,1)S(1)}, bf16[40,1024]{1,0:T(8,128)(2,1)S(1)}, u32[]{:S(2)}, u32[]{:S(2)}) %collective-permute-start.19) | collective-permute-done | bytes 81952 | tf_op jit(solution)/shard_map/ppermute | solution.py:415
  78.9 0.3 shard_map.91
  79.2 1.6 %collective-permute-start.21 = (bf16[128,512]{1,0:T(8,128)(2,1)S(1)}, bf16[128,512]{1,0:T(8,128)(2,1)S(1)}, u32[]{:S(2)}, u32[]{:S(2)}) collective-permute-start(bf16[128,512]{1,0:T(8,128)(2,1)S(1)} %get-tuple-element.56), channel_id=1, source_target_pairs={{0,2},{1,3},{2,0},{3,1},{4,6},{5,7},{6,4},{7,5},{8,10},{9,11},{10,... | collective-permute-start | bytes 393224 | tf_op jit(solution)/shard_map/ppermute | solution.py:415
  80.8 3.5 %collective-permute-done.21.refs_3_ = bf16[128,512]{1,0:T(8,128)(2,1)S(1)} collective-permute-done((bf16[128,512]{1,0:T(8,128)(2,1)S(1)}, bf16[128,512]{1,0:T(8,128)(2,1)S(1)}, u32[]{:S(2)}, u32[]{:S(2)}) %collective-permute-start.21) | collective-permute-done | bytes 131104 | tf_op jit(solution)/shard_map/ppermute | solution.py:415
  84.2 0.7 shard_map.92
  (17 shorter events, 0.0 us)
Async XLA Ops:
  0.0 1.2 %copy-start = (bf16[128,4096]{1,0:T(8,128)(2,1)S(1)}, bf16[128,4096]{1,0:T(8,128)(2,1)}, u32[]{:S(2)}) copy-start(bf16[128,4096]{1,0:T(8,128)(2,1)} %tokens_hbm.1) | copy-start | bytes 3145732
  1.2 0.7 copy-start.1
  1.9 0.7 copy-start.3
  3.4 0.7 copy-start.2
  4.1 0.7 copy-start.4
  7.9 8.9 %collective-permute-start = (bf16[40,1024]{1,0:T(8,128)(2,1)S(1)}, bf16[40,1024]{1,0:T(8,128)(2,1)S(1)}, u32[]{:S(2)}, u32[]{:S(2)}) collective-permute-start(bf16[40,1024]{1,0:T(8,128)(2,1)S(1)} %get-tuple-element.36), channel_id=1, source_target_pairs={{0,4},{1,5},{2,6},{3,7},{4,8},{5,9},{6,10},{7,11},{8,12},{9,13},{1... | collective-permute-start | bytes 245768 | tf_op jit(solution)/shard_map/ppermute | solution.py:415
  11.0 7.2 %collective-permute-start.6 = (bf16[40,1024]{1,0:T(8,128)(2,1)S(1)}, bf16[40,1024]{1,0:T(8,128)(2,1)S(1)}, u32[]{:S(2)}, u32[]{:S(2)}) collective-permute-start(bf16[40,1024]{1,0:T(8,128)(2,1)S(1)} %get-tuple-element.39), channel_id=1, source_target_pairs={{0,4},{1,5},{2,6},{3,7},{4,8},{5,9},{6,10},{7,11},{8,12},{9,13},{1... | collective-permute-start | bytes 245768 | tf_op jit(solution)/shard_map/ppermute | solution.py:415
  12.5 9.2 %collective-permute-start.7 = (bf16[40,1024]{1,0:T(8,128)(2,1)S(1)}, bf16[40,1024]{1,0:T(8,128)(2,1)S(1)}, u32[]{:S(2)}, u32[]{:S(2)}) collective-permute-start(bf16[40,1024]{1,0:T(8,128)(2,1)S(1)} %get-tuple-element.40), channel_id=1, source_target_pairs={{0,8},{1,9},{2,10},{3,11},{4,12},{5,13},{6,14},{7,15},{8,0},{9,1},... | collective-permute-start | bytes 245768 | tf_op jit(solution)/shard_map/ppermute | solution.py:415
  13.6 8.1 %collective-permute-start.8 = (bf16[40,1024]{1,0:T(8,128)(2,1)S(1)}, bf16[40,1024]{1,0:T(8,128)(2,1)S(1)}, u32[]{:S(2)}, u32[]{:S(2)}) collective-permute-start(bf16[40,1024]{1,0:T(8,128)(2,1)S(1)} %get-tuple-element.41), channel_id=1, source_target_pairs={{0,12},{1,13},{2,14},{3,15},{4,0},{5,1},{6,2},{7,3},{8,4},{9,5},{1... | collective-permute-start | bytes 245768 | tf_op jit(solution)/shard_map/ppermute | solution.py:415
  16.5 9.6 %collective-permute-start.1 = (bf16[40,1024]{1,0:T(8,128)(2,1)S(1)}, bf16[40,1024]{1,0:T(8,128)(2,1)S(1)}, u32[]{:S(2)}, u32[]{:S(2)}) collective-permute-start(bf16[40,1024]{1,0:T(8,128)(2,1)S(1)} %get-tuple-element.37), channel_id=1, source_target_pairs={{0,8},{1,9},{2,10},{3,11},{4,12},{5,13},{6,14},{7,15},{8,0},{9,1},... | collective-permute-start | bytes 245768 | tf_op jit(solution)/shard_map/ppermute | solution.py:415
  16.8 9.2 %collective-permute-start.2 = (bf16[40,1024]{1,0:T(8,128)(2,1)S(1)}, bf16[40,1024]{1,0:T(8,128)(2,1)S(1)}, u32[]{:S(2)}, u32[]{:S(2)}) collective-permute-start(bf16[40,1024]{1,0:T(8,128)(2,1)S(1)} %get-tuple-element.38), channel_id=1, source_target_pairs={{0,12},{1,13},{2,14},{3,15},{4,0},{5,1},{6,2},{7,3},{8,4},{9,5},{1... | collective-permute-start | bytes 245768 | tf_op jit(solution)/shard_map/ppermute | solution.py:415
  18.2 8.4 %collective-permute-start.9 = (bf16[40,1024]{1,0:T(8,128)(2,1)S(1)}, bf16[40,1024]{1,0:T(8,128)(2,1)S(1)}, u32[]{:S(2)}, u32[]{:S(2)}) collective-permute-start(bf16[40,1024]{1,0:T(8,128)(2,1)S(1)} %collective-permute-done.6.refs_1_), channel_id=1, source_target_pairs={{0,1},{1,0},{2,3},{3,2},{4,5},{5,4},{6,7},{7,6},{8,9},{9,8},{10,11... | collective-permute-start | bytes 245768 | tf_op jit(solution)/shard_map/ppermute | solution.py:418
  21.7 4.9 %collective-permute-start.10 = (bf16[40,1024]{1,0:T(8,128)(2,1)S(1)}, bf16[40,1024]{1,0:T(8,128)(2,1)S(1)}, u32[]{:S(2)}, u32[]{:S(2)}) collective-permute-start(bf16[40,1024]{1,0:T(8,128)(2,1)S(1)} %collective-permute-done.7.refs_2_), channel_id=1, source_target_pairs={{0,1},{1,0},{2,3},{3,2},{4,5},{5,4},{6,7},{7,6},{8,9},{9,8},{10,11... | collective-permute-start | bytes 245768 | tf_op jit(solution)/shard_map/ppermute | solution.py:418
  21.7 4.9 %collective-permute-start.11 = (bf16[40,1024]{1,0:T(8,128)(2,1)S(1)}, bf16[40,1024]{1,0:T(8,128)(2,1)S(1)}, u32[]{:S(2)}, u32[]{:S(2)}) collective-permute-start(bf16[40,1024]{1,0:T(8,128)(2,1)S(1)} %collective-permute-done.8.refs_3_), channel_id=1, source_target_pairs={{0,1},{1,0},{2,3},{3,2},{4,5},{5,4},{6,7},{7,6},{8,9},{9,8},{10,11... | collective-permute-start | bytes 245768 | tf_op jit(solution)/shard_map/ppermute | solution.py:418
  26.1 11.1 %collective-permute-start.3 = (bf16[40,1024]{1,0:T(8,128)(2,1)S(1)}, bf16[40,1024]{1,0:T(8,128)(2,1)S(1)}, u32[]{:S(2)}, u32[]{:S(2)}) collective-permute-start(bf16[40,1024]{1,0:T(8,128)(2,1)S(1)} %collective-permute-done.refs_1_), channel_id=1, source_target_pairs={{0,1},{1,0},{2,3},{3,2},{4,5},{5,4},{6,7},{7,6},{8,9},{9,8},{10,11... | collective-permute-start | bytes 245768 | tf_op jit(solution)/shard_map/ppermute | solution.py:418
  26.1 11.1 %collective-permute-start.4 = (bf16[40,1024]{1,0:T(8,128)(2,1)S(1)}, bf16[40,1024]{1,0:T(8,128)(2,1)S(1)}, u32[]{:S(2)}, u32[]{:S(2)}) collective-permute-start(bf16[40,1024]{1,0:T(8,128)(2,1)S(1)} %collective-permute-done.1.refs_2_), channel_id=1, source_target_pairs={{0,1},{1,0},{2,3},{3,2},{4,5},{5,4},{6,7},{7,6},{8,9},{9,8},{10,11... | collective-permute-start | bytes 245768 | tf_op jit(solution)/shard_map/ppermute | solution.py:418
  26.6 10.6 %collective-permute-start.5 = (bf16[40,1024]{1,0:T(8,128)(2,1)S(1)}, bf16[40,1024]{1,0:T(8,128)(2,1)S(1)}, u32[]{:S(2)}, u32[]{:S(2)}) collective-permute-start(bf16[40,1024]{1,0:T(8,128)(2,1)S(1)} %collective-permute-done.2.refs_3_), channel_id=1, source_target_pairs={{0,1},{1,0},{2,3},{3,2},{4,5},{5,4},{6,7},{7,6},{8,9},{9,8},{10,11... | collective-permute-start | bytes 245768 | tf_op jit(solution)/shard_map/ppermute | solution.py:418
  51.7 4.2 %collective-permute-start.12 = (bf16[160,1024]{1,0:T(8,128)(2,1)S(1)}, bf16[160,1024]{1,0:T(8,128)(2,1)S(1)}, u32[]{:S(2)}, u32[]{:S(2)}) collective-permute-start(bf16[160,1024]{1,0:T(8,128)(2,1)S(1)} %shard_map.86), channel_id=1, source_target_pairs={{0,1},{1,0},{2,3},{3,2},{4,5},{5,4},{6,7},{7,6},{8,9},{9,8},{10,11... | collective-permute-start | bytes 983048 | tf_op jit(solution)/shard_map/ppermute | solution.py:418
  55.7 7.9 %collective-permute-start.17 = (bf16[160,1024]{1,0:T(8,128)(2,1)S(1)}, bf16[160,1024]{1,0:T(8,128)(2,1)S(1)}, u32[]{:S(2)}, u32[]{:S(2)}) collective-permute-start(bf16[160,1024]{1,0:T(8,128)(2,1)S(1)} %shard_map.89), channel_id=1, source_target_pairs={{0,1},{1,0},{2,3},{3,2},{4,5},{5,4},{6,7},{7,6},{8,9},{9,8},{10,11... | collective-permute-start | bytes 983048 | tf_op jit(solution)/shard_map/ppermute | solution.py:418
  59.3 12.1 %collective-permute-start.13 = (bf16[40,1024]{1,0:T(8,128)(2,1)S(1)}, bf16[40,1024]{1,0:T(8,128)(2,1)S(1)}, u32[]{:S(2)}, u32[]{:S(2)}) collective-permute-start(bf16[40,1024]{1,0:T(8,128)(2,1)S(1)} %get-tuple-element.46), channel_id=1, source_target_pairs={{0,12},{1,13},{2,14},{3,15},{4,0},{5,1},{6,2},{7,3},{8,4},{9,5},{1... | collective-permute-start | bytes 245768 | tf_op jit(solution)/shard_map/ppermute | solution.py:415
  62.9 8.5 %collective-permute-start.14 = (bf16[40,1024]{1,0:T(8,128)(2,1)S(1)}, bf16[40,1024]{1,0:T(8,128)(2,1)S(1)}, u32[]{:S(2)}, u32[]{:S(2)}) collective-permute-start(bf16[40,1024]{1,0:T(8,128)(2,1)S(1)} %get-tuple-element.47), channel_id=1, source_target_pairs={{0,8},{1,9},{2,10},{3,11},{4,12},{5,13},{6,14},{7,15},{8,0},{9,1},... | collective-permute-start | bytes 245768 | tf_op jit(solution)/shard_map/ppermute | solution.py:415
  63.0 8.5 %collective-permute-start.15 = (bf16[40,1024]{1,0:T(8,128)(2,1)S(1)}, bf16[40,1024]{1,0:T(8,128)(2,1)S(1)}, u32[]{:S(2)}, u32[]{:S(2)}) collective-permute-start(bf16[40,1024]{1,0:T(8,128)(2,1)S(1)} %get-tuple-element.48), channel_id=1, source_target_pairs={{0,4},{1,5},{2,6},{3,7},{4,8},{5,9},{6,10},{7,11},{8,12},{9,13},{1... | collective-permute-start | bytes 245768 | tf_op jit(solution)/shard_map/ppermute | solution.py:415
  67.1 6.2 %collective-permute-start.18 = (bf16[40,1024]{1,0:T(8,128)(2,1)S(1)}, bf16[40,1024]{1,0:T(8,128)(2,1)S(1)}, u32[]{:S(2)}, u32[]{:S(2)}) collective-permute-start(bf16[40,1024]{1,0:T(8,128)(2,1)S(1)} %get-tuple-element.52), channel_id=1, source_target_pairs={{0,12},{1,13},{2,14},{3,15},{4,0},{5,1},{6,2},{7,3},{8,4},{9,5},{1... | collective-permute-start | bytes 245768 | tf_op jit(solution)/shard_map/ppermute | solution.py:415
  70.4 8.6 %collective-permute-start.19 = (bf16[40,1024]{1,0:T(8,128)(2,1)S(1)}, bf16[40,1024]{1,0:T(8,128)(2,1)S(1)}, u32[]{:S(2)}, u32[]{:S(2)}) collective-permute-start(bf16[40,1024]{1,0:T(8,128)(2,1)S(1)} %get-tuple-element.53), channel_id=1, source_target_pairs={{0,8},{1,9},{2,10},{3,11},{4,12},{5,13},{6,14},{7,15},{8,0},{9,1},... | collective-permute-start | bytes 245768 | tf_op jit(solution)/shard_map/ppermute | solution.py:415
  71.4 7.5 %collective-permute-start.20 = (bf16[40,1024]{1,0:T(8,128)(2,1)S(1)}, bf16[40,1024]{1,0:T(8,128)(2,1)S(1)}, u32[]{:S(2)}, u32[]{:S(2)}) collective-permute-start(bf16[40,1024]{1,0:T(8,128)(2,1)S(1)} %get-tuple-element.54), channel_id=1, source_target_pairs={{0,4},{1,5},{2,6},{3,7},{4,8},{5,9},{6,10},{7,11},{8,12},{9,13},{1... | collective-permute-start | bytes 245768 | tf_op jit(solution)/shard_map/ppermute | solution.py:415
  71.7 9.0 %collective-permute-start.16 = (bf16[128,512]{1,0:T(8,128)(2,1)S(1)}, bf16[128,512]{1,0:T(8,128)(2,1)S(1)}, u32[]{:S(2)}, u32[]{:S(2)}) collective-permute-start(bf16[128,512]{1,0:T(8,128)(2,1)S(1)} %get-tuple-element.50), channel_id=1, source_target_pairs={{0,2},{1,3},{2,0},{3,1},{4,6},{5,7},{6,4},{7,5},{8,10},{9,11},{10,... | collective-permute-start | bytes 393224 | tf_op jit(solution)/shard_map/ppermute | solution.py:415
  79.2 5.0 %collective-permute-start.21 = (bf16[128,512]{1,0:T(8,128)(2,1)S(1)}, bf16[128,512]{1,0:T(8,128)(2,1)S(1)}, u32[]{:S(2)}, u32[]{:S(2)}) collective-permute-start(bf16[128,512]{1,0:T(8,128)(2,1)S(1)} %get-tuple-element.56), channel_id=1, source_target_pairs={{0,2},{1,3},{2,0},{3,1},{4,6},{5,7},{6,4},{7,5},{8,10},{9,11},{10,... | collective-permute-start | bytes 393224 | tf_op jit(solution)/shard_map/ppermute | solution.py:415

commit v3 on v2

--- a/solution.py
+++ b/solution.py
@@ -16,12 +16,14 @@
 
 EPSILON = 1e-05
 
-IN_CHUNKS = 2
 OUT_CHUNKS = 2
 K_SLAB = 512
-K_DEPTH = 6
+K_DEPTH = 2
+N_TILE = 512
+NEAR_ROWS = 1024
+GATE_NEAR = 4
+UP_NEAR = 1
 N_ROWS = 512
-VMEM_LIMIT = 40 * 1024 * 1024
 
 F32 = jnp.float32
 BF16 = jnp.bfloat16
@@ -157,13 +159,7 @@
     return lax.rem(z + distance, exp_count) * groups + g
 
 
-def send_rows(normed, others, start, width, sends):
-    found = jnp.dot(others, normed[:, pl.ds(start, width)], preferred_element_type=F32)
-    for d, send in enumerate(sends):
-        send[...] = found[d * CAP : (d + 1) * CAP, :].astype(BF16)
-
-
-def route_kernel(sizes, width, tokens_hbm, gain_hbm, ids_hbm, normed, others, *rest):
+def route_kernel(sizes, width, tokens_hbm, gain_hbm, ids_hbm, normed, *rest):
     exp_count, groups = sizes
     sends, (tokens, gain, ids, sems) = rest[:-4], rest[-4:]
     pairs = ((tokens_hbm, tokens), (gain_hbm, gain), (ids_hbm, ids))
@@ -182,21 +178,27 @@
         normed[first : first + step, :] = (values * inv_rms * gain[...]).astype(BF16)
     named, before = count_earlier(ids, group_experts(exp_count, groups, z, g, rows))
     picks = [pick_rows(named, before, d) for d in range(1, exp_count)]
-    others[...] = jnp.concatenate(picks, axis=0).astype(BF16)
+    others = jnp.concatenate(picks, axis=0).astype(BF16)
     start = pl.multiple_of(s * (features // 2), 128)
-    send_rows(normed, others[...], start, width, sends)
-
-
-def prepare_kernel(sizes, width, normed, others, ids, weights, active, *rest):
+    found = jnp.dot(others, normed[:, pl.ds(start, width)], preferred_element_type=F32)
+    for d, send in enumerate(sends):
+        send[...] = found[d * CAP : (d + 1) * CAP, :].astype(BF16)
+
+
+def prepare_kernel(
+    sizes, normed, ids, weights, active, gate, up, own, combine_high, combine_low, mask, *rest
+):
     exp_count, groups = sizes
-    own, combine_high, combine_low, mask = rest[:4]
-    sends = rest[4:]
     rows, features = normed.shape
     z, g, s = place(sizes)
-    for n in range(len(sends) // (exp_count - 1)):
-        start = pl.multiple_of(s * (features // 2) + (n + 1) * width, 128)
-        batch = sends[n * (exp_count - 1) : (n + 1) * (exp_count - 1)]
-        send_rows(normed, others[...], start, width, batch)
+    copies = []
+    *nears, sems = rest
+    for n, near in enumerate(nears):
+        source, piece = (gate, n) if n < GATE_NEAR else (up, n - GATE_NEAR)
+        lines = pl.ds(piece * NEAR_ROWS, NEAR_ROWS)
+        copies.append(pltpu.make_async_copy(source.at[lines, :], near, sems.at[n]))
+    for copy in copies:
+        copy.start()
     named, before = count_earlier(ids, group_experts(exp_count, groups, z, g, rows))
     own[...] = jnp.dot(
         pick_rows(named, before, 0).astype(BF16), normed[...], preferred_element_type=F32
@@ -229,84 +231,82 @@
         return jnp.where(blocks == entry, 1.0, found)
 
     mask[...] = lax.fori_loop(0, active.shape[2], add_entry, jnp.zeros(mask.shape, F32))
-
-
-def hidden_kernel(sizes, chunk, width, first, last, *refs):
+    for copy in copies:
+        copy.wait()
+
+
+def hidden_kernel(sizes, own, *refs):
     exp_count, groups = sizes
     z, g, s = place(sizes)
     refs = list(refs)
-    own = refs.pop(0)
     mine = [refs.pop(0) for _ in range(exp_count - 1)]
     other = [refs.pop(0) for _ in range(exp_count - 1)]
-    gate, up = refs.pop(0), refs.pop(0)
-    gate_in, up_in = (None, None) if first else (refs.pop(0), refs.pop(0))
-    mask = refs.pop(0) if last else None
-    if last:
-        hidden = refs.pop(0)
-        gate_sum, up_sum = refs.pop(0), refs.pop(0)
-    else:
-        gate_sum, up_sum = refs.pop(0), refs.pop(0)
-    rows, slabs, sems = refs
+    gate_near = [refs.pop(0) for _ in range(GATE_NEAR)]
+    up_near = [refs.pop(0) for _ in range(UP_NEAR)]
+    up, mask, hidden, gate_sum, up_sum, rows, slabs, sems = refs
     half = own.shape[1] // 2
-    slab_count = width // K_SLAB
-    total = 2 * slab_count
-    depth = min(K_DEPTH, 2 * total)
-
-    def copy(index, ref, which):
-        side = jnp.where(index < slab_count, s, 1 - s)
-        row = side * half + chunk * width + lax.rem(index, slab_count) * K_SLAB
-        slot = lax.rem(index * 2 + which, depth)
+    near, features = UP_NEAR * NEAR_ROWS, up.shape[0]
+    unit_width = up.shape[1]
+    far_count = (features - near) // K_SLAB
+
+    def copy(index):
+        slot = index % K_DEPTH
         return pltpu.make_async_copy(
-            ref.at[pl.ds(pl.multiple_of(row, K_SLAB), K_SLAB), :], slabs.at[slot], sems.at[slot]
+            up.at[pl.ds(near + index * K_SLAB, K_SLAB), :], slabs.at[slot], sems.at[slot]
         )
 
-    for n in range(depth):
-        copy(n // 2, (gate, up)[n % 2], n % 2).start()
+    for n in range(min(K_DEPTH, far_count)):
+        copy(n).start()
     for side_of in range(2):
         source = (mine, other)[side_of]
         side = s if side_of == 0 else 1 - s
-        start = pl.multiple_of(side * half + chunk * width, 128)
-        pieces = [own[:, pl.ds(start, width)].astype(F32)] + [r[...].astype(F32) for r in source]
-        whole = jnp.concatenate(pieces, axis=0).astype(BF16)
-        for n in range(slab_count):
-            rows[side_of * slab_count + n] = whole[:, n * K_SLAB : (n + 1) * K_SLAB]
-    unit_width = gate.shape[1]
-    n_tile = 512
-    if first:
-        gate_sum[...] = jnp.zeros_like(gate_sum)
-        up_sum[...] = jnp.zeros_like(up_sum)
-    else:
-        gate_sum[...] = gate_in[...]
-        up_sum[...] = up_in[...]
-
-    def body(index, carry):
-        left = rows[index]
-        for which, (ref, acc) in enumerate(((gate, gate_sum), (up, up_sum))):
-            copy(index, ref, which).wait()
-            slot = lax.rem(index * 2 + which, depth)
-            for col in range(0, unit_width, n_tile):
-                end = min(col + n_tile, unit_width)
-                acc[:, col:end] += jnp.dot(
-                    left, slabs[slot, :, col:end], preferred_element_type=F32
-                )
-
-            @pl.when(index * 2 + which + depth < 2 * total)
-            def _():
-                copy(index + depth // 2, ref, which).start()
-
-        return carry
-
-    lax.fori_loop(0, total, body, 0)
-    if last:
-        for d in range(exp_count):
-            lines = slice(d * CAP, (d + 1) * CAP)
-            for col in range(0, unit_width, n_tile):
-                cols = slice(col, min(col + n_tile, unit_width))
-                product = jnp.maximum(gate_sum[lines, cols], 0.0) * jnp.maximum(
-                    up_sum[lines, cols], 0.0
-                )
-                gate_sum[lines, cols] = product * mask[d : d + 1, cols]
-        hidden[...] = gate_sum[...].astype(BF16)
+        start = pl.multiple_of(side * half, 128)
+        pieces = [own[:, pl.ds(start, half)].astype(F32)] + [r[...].astype(F32) for r in source]
+        rows[:, pl.ds(start, half)] = jnp.concatenate(pieces, axis=0).astype(BF16)
+
+    def each_tile(body):
+        def step(n, carry):
+            body(pl.ds(pl.multiple_of(n * N_TILE, N_TILE), N_TILE))
+            return carry
+
+        lax.fori_loop(0, unit_width // N_TILE, step, 0)
+
+    def product(nears, cols):
+        value = None
+        for n, near in enumerate(nears):
+            lines = slice(n * NEAR_ROWS, (n + 1) * NEAR_ROWS)
+            term = jnp.dot(rows[:, lines], near[:, cols], preferred_element_type=F32)
+            value = term if value is None else value + term
+        return value
+
+    def gate_tile(cols):
+        gate_sum[:, cols] = jnp.maximum(product(gate_near, cols), 0.0)
+
+    def near_tile(cols):
+        up_sum[:, cols] = product(up_near, cols)
+
+    each_tile(gate_tile)
+    each_tile(near_tile)
+    for n in range(far_count):
+        copy(n).wait()
+        left = slice(near + n * K_SLAB, near + (n + 1) * K_SLAB)
+
+        def far_tile(cols):
+            value = up_sum[:, cols] + jnp.dot(
+                rows[:, left], slabs[n % K_DEPTH, :, cols], preferred_element_type=F32
+            )
+            if n < far_count - 1:
+                up_sum[:, cols] = value
+                return
+            value = gate_sum[:, cols] * jnp.maximum(value, 0.0)
+            parts = []
+            for d in range(exp_count):
+                parts.append(value[d * CAP : (d + 1) * CAP, :] * mask[d : d + 1, cols])
+            hidden[:, cols] = jnp.concatenate(parts, axis=0).astype(BF16)
+
+        each_tile(far_tile)
+        if n + K_DEPTH < far_count:
+            copy(n + K_DEPTH).start()
 
 
 def output_kernel(sizes, chunk, width, keep, *refs):
@@ -376,17 +376,24 @@
         out[:, chunk * width : (chunk + 1) * width] = value.astype(BF16)
 
 
-def call(kernel, outs, ins, scratch=(), flops=0, moved=0, aliases=None):
+def call(kernel, outs, ins, scratch=(), flops=0, moved=0, limit=16):
     vmem = pl.BlockSpec(memory_space=pltpu.VMEM)
-    arrays = [a for a, _ in ins]
-    specs = [vmem if space is None else pl.BlockSpec(memory_space=space) for _, space in ins]
+    arrays, specs = [], []
+    for array, space in ins:
+        if space in (pltpu.HBM, pltpu.VMEM):
+            array = pltpu.with_memory_space_constraint(array, space)
+        arrays.append(array)
+        specs.append(vmem if space is None else pl.BlockSpec(memory_space=space))
+    shapes = []
+    for shape, kind, *space in outs:
+        shapes.append(space[0](shape, kind) if space else jax.ShapeDtypeStruct(shape, kind))
     return pl.pallas_call(
         kernel,
-        out_shape=[jax.ShapeDtypeStruct(shape, kind) for shape, kind in outs],
+        out_shape=shapes,
         in_specs=specs,
         out_specs=[vmem] * len(outs),
         scratch_shapes=list(scratch),
-        compiler_params=pltpu.CompilerParams(vmem_limit_bytes=VMEM_LIMIT),
+        compiler_params=pltpu.CompilerParams(vmem_limit_bytes=limit << 20),
         cost_estimate=pl.CostEstimate(flops=flops, bytes_accessed=moved, transcendentals=0),
     )(*arrays)
 
@@ -401,7 +408,7 @@
     unit_width = gate_weight.shape[1]
     slots = exp_count * CAP
     half = features // 2
-    width = half // IN_CHUNKS
+    width = half
     ids = route_ids.T
     weights = route_weight.T
 
@@ -418,10 +425,9 @@
         return lax.ppermute(value, "unit", [(u, u ^ 1) for u in range(unit_count)])
 
     batch = exp_count - 1
-    normed, others, *sends = call(
+    normed, *sends = call(
         functools.partial(route_kernel, sizes, width),
-        [((tok_count, features), BF16), ((batch * CAP, tok_count), BF16)]
-        + [((CAP, width), BF16)] * batch,
+        [((tok_count, features), BF16)] + [((CAP, width), BF16)] * batch,
         [
             (tokens, pltpu.HBM),
             (norm_gain.reshape(1, -1), pltpu.HBM),
@@ -437,52 +443,48 @@
         moved=4 * tok_count * features,
     )
     padded = -(-slots // 128) * 128
-    own, combine_high, combine_low, mask, *more = call(
-        functools.partial(prepare_kernel, sizes, width),
+    own, combine_high, combine_low, mask, *nears = call(
+        functools.partial(prepare_kernel, sizes),
         [
             ((CAP, features), BF16),
             ((tok_count, padded), BF16),
             ((tok_count, padded), BF16),
             ((max(8, exp_count), unit_width), F32),
         ]
-        + [((CAP, width), BF16)] * (batch * (IN_CHUNKS - 1)),
-        [(normed, None), (others, None), (ids, None), (weights, None), (active_blocks, pltpu.SMEM)],
+        + [((NEAR_ROWS, unit_width), BF16, pltpu.VMEM)] * (GATE_NEAR + UP_NEAR),
+        [
+            (normed, None),
+            (ids, None),
+            (weights, None),
+            (active_blocks, pltpu.SMEM),
+            (gate_weight, pltpu.HBM),
+            (up_weight, pltpu.HBM),
+        ],
+        [pltpu.SemaphoreType.DMA((GATE_NEAR + UP_NEAR,))],
         flops=2 * tok_count * slots * features,
-        moved=1 << 20,
-    )
-    sends = sends + more
-    mine, other = [], []
-    for chunk in range(IN_CHUNKS):
-        ready = sends[chunk * batch : (chunk + 1) * batch]
-        arrived = [shift(value, d + 1) for d, value in enumerate(ready)]
-        mine.append(arrived)
-        other.append([swap(value) for value in arrived])
-    sums = None
-    for chunk in range(IN_CHUNKS):
-        first, last = chunk == 0, chunk == IN_CHUNKS - 1
-        ins = [(own, None)] + [(v, None) for v in mine[chunk] + other[chunk]]
-        ins += [(gate_weight, pltpu.HBM), (up_weight, pltpu.HBM)]
-        if not first:
-            ins += [(v, None) for v in sums]
-        if last:
-            ins += [(mask, None)]
-        acc = ((slots, unit_width), F32)
-        scratch = [
-            pltpu.VMEM((2 * width // K_SLAB, slots, K_SLAB), BF16),
+        moved=2 * (GATE_NEAR + UP_NEAR) * NEAR_ROWS * unit_width,
+        limit=16,
+    )
+    mine = [shift(value, d + 1) for d, value in enumerate(sends)]
+    other = [swap(value) for value in mine]
+    acc = ((slots, unit_width), F32)
+    hidden = call(
+        functools.partial(hidden_kernel, sizes),
+        [((slots, unit_width), BF16)],
+        [(v, None) for v in [own] + mine + other]
+        + [(v, pltpu.VMEM) for v in nears]
+        + [(up_weight, pltpu.HBM), (mask, None)],
+        [
+            pltpu.VMEM(*acc),
+            pltpu.VMEM(*acc),
+            pltpu.VMEM((slots, features), BF16),
             pltpu.VMEM((K_DEPTH, K_SLAB, unit_width), BF16),
             pltpu.SemaphoreType.DMA((K_DEPTH,)),
-        ]
-        if last:
-            scratch = [pltpu.VMEM(*acc), pltpu.VMEM(*acc)] + scratch
-        sums = call(
-            functools.partial(hidden_kernel, sizes, chunk, width, first, last),
-            [((slots, unit_width), BF16)] if last else [acc, acc],
-            ins,
-            scratch,
-            flops=2 * 2 * slots * 2 * width * unit_width,
-            moved=2 * 2 * width * unit_width * 2,
-        )
-    hidden = sums[0]
+        ],
+        flops=2 * 2 * slots * features * unit_width,
+        moved=2 * features * unit_width * 2,
+        limit=16,
+    )[0]
     part = features // unit_count
     out_width = part // OUT_CHUNKS
 

time: 85.3 us -> 91.3 us (1.070)
  Pallas kernels: 40.6 us -> 49.3 us
  starting transfers between devices: 23.6 us -> 21.4 us
  local copies, waits for them, and re-layouts: 3.99 us -> 2.05 us
  waiting for transfers between devices: 16.6 us -> 18.2 us
    pallas_call x11 -> x10, Pallas kernels: 40.6 us -> 49.3 us  [call(): pl.pallas_call(kernel, out_shape=shapes, in_specs=specs, out_specs=[vmem]...]
    unnamed x10 -> x6, local copies, waits for them, and re-layouts: 3.99 us -> 2.05 us
    ppermute x14 -> x11, starting transfers between devices: 21.9 us -> 20.2 us  [shift(): return lax.ppermute(value, ('exp', 'unit'), pairs)]
    ppermute x14 -> x11, waiting for transfers between devices: 16.6 us -> 18.2 us  [shift(): return lax.ppermute(value, ('exp', 'unit'), pairs)]
  transfers between devices with their start and end apart: 22 -> 16, of which waited for: 5 -> 4; matrix products, arithmetic and copies ran while one was open for 0% -> 0% of each run, Pallas kernels for 25% -> 26%
where the time goes in v3:
time: 91.3 us; the launch traced here: 91 us
  Pallas kernels  49.3 us (54%)
  starting transfers between devices  21.4 us (23%)
  waiting for transfers between devices  18.2 us (20%)
  local copies, waits for them, and re-layouts  2.05 us (2%)
    pallas_call x10, Pallas kernels, call(): pl.pallas_call(kernel, out_shape=shapes, in_specs=specs, out_specs=[vmem]...  49.3 us
    ppermute x11, starting transfers between devices, shift(): return lax.ppermute(value, ('exp', 'unit'), pairs)  20.2 us
    ppermute x11, waiting for transfers between devices, shift(): return lax.ppermute(value, ('exp', 'unit'), pairs)  18.2 us
    unnamed x6, local copies, waits for them, and re-layouts  2.05 us
  transfers between devices with their start and end apart: 16, of which 4 were waited for; matrix products, arithmetic and copies ran while one was open for 0% of the time, Pallas kernels for 26%

profile of v3, /device:TPU:0, one launch (start us, length us, event | category | flops | bytes accessed | tf_op | source)
XLA Modules:
  0.0 91.0 jit_solution(11266124642082399281)
XLA Ops:
  0.0 2.0 %shard_map.82 = (bf16[128,4096]{1,0:T(8,128)(2,1)S(1)}, bf16[40,2048]{1,0:T(8,128)(2,1)S(1)}, bf16[40,2048]{1,0:T(8,128)(2,1)S(1)}, bf16[40,2048]{1,0:T(8,128)(2,1)S(1)}) custom-call(bf16[128,4096]{1,0:T(8,128)(2,1)} %tokens_hbm.1, f32[1,4096]{1,0:T(1,128)} %bitcast.6, s32[2,128]{1,0:T(2,128)} %bitcast.3), custom_call_target="tpu_custom_call" | custom-call | flops 83886080 | bytes 2097152 | tf_op jit(solution)/shard_map/pallas_call | solution.py:390
  2.0 3.1 %collective-permute-start = (bf16[40,2048]{1,0:T(8,128)(2,1)S(1)}, bf16[40,2048]{1,0:T(8,128)(2,1)S(1)}, u32[]{:S(2)}, u32[]{:S(2)}) collective-permute-start(bf16[40,2048]{1,0:T(8,128)(2,1)S(1)} %get-tuple-element.34), channel_id=1, source_target_pairs={{0,4},{1,5},{2,6},{3,7},{4,8},{5,9},{6,10},{7,11},{8,12},{9,13},{1... | collective-permute-start | bytes 491528 | tf_op jit(solution)/shard_map/ppermute | solution.py:422
  5.1 2.6 %collective-permute-start.1 = (bf16[40,2048]{1,0:T(8,128)(2,1)S(1)}, bf16[40,2048]{1,0:T(8,128)(2,1)S(1)}, u32[]{:S(2)}, u32[]{:S(2)}) collective-permute-start(bf16[40,2048]{1,0:T(8,128)(2,1)S(1)} %get-tuple-element.35), channel_id=1, source_target_pairs={{0,8},{1,9},{2,10},{3,11},{4,12},{5,13},{6,14},{7,15},{8,0},{9,1},... | collective-permute-start | bytes 491528 | tf_op jit(solution)/shard_map/ppermute | solution.py:422
  7.7 1.3 %collective-permute-start.2 = (bf16[40,2048]{1,0:T(8,128)(2,1)S(1)}, bf16[40,2048]{1,0:T(8,128)(2,1)S(1)}, u32[]{:S(2)}, u32[]{:S(2)}) collective-permute-start(bf16[40,2048]{1,0:T(8,128)(2,1)S(1)} %get-tuple-element.36), channel_id=1, source_target_pairs={{0,12},{1,13},{2,14},{3,15},{4,0},{5,1},{6,2},{7,3},{8,4},{9,5},{1... | collective-permute-start | bytes 491528 | tf_op jit(solution)/shard_map/ppermute | solution.py:422
  9.0 3.2 %collective-permute-done.refs_0_ = bf16[40,2048]{1,0:T(8,128)(2,1)S(1)} collective-permute-done((bf16[40,2048]{1,0:T(8,128)(2,1)S(1)}, bf16[40,2048]{1,0:T(8,128)(2,1)S(1)}, u32[]{:S(2)}, u32[]{:S(2)}) %collective-permute-start) | collective-permute-done | bytes 163872 | tf_op jit(solution)/shard_map/ppermute | solution.py:422
  12.2 0.0 collective-permute-start.3
  12.3 6.2 %collective-permute-done.1.refs_1_ = bf16[40,2048]{1,0:T(8,128)(2,1)S(1)} collective-permute-done((bf16[40,2048]{1,0:T(8,128)(2,1)S(1)}, bf16[40,2048]{1,0:T(8,128)(2,1)S(1)}, u32[]{:S(2)}, u32[]{:S(2)}) %collective-permute-start.1) | collective-permute-done | bytes 163872 | tf_op jit(solution)/shard_map/ppermute | solution.py:422
  18.4 0.0 collective-permute-start.4
  18.4 0.0 collective-permute-done.2.refs_2_
  18.4 0.5 collective-permute-start.5
  18.9 0.0 copy-start
  18.9 0.7 copy-done
  19.6 0.0 copy-start.1
  19.6 0.7 copy-done.1
  20.3 0.0 copy-start.2
  20.3 0.7 copy-done.2
  21.0 12.4 %shard_map.83 = (bf16[40,4096]{1,0:T(8,128)(2,1)S(1)}, bf16[128,256]{1,0:T(8,128)(2,1)S(1)}, bf16[128,256]{1,0:T(8,128)(2,1)S(1)}, f32[8,3584]{1,0:T(8,128)S(1)}...) custom-call(bf16[128,4096]{1,0:T(8,128)(2,1)S(1)} %get-tuple-element, ...), custom_call_target="tpu_custom_call" | custom-call | flops 167772160 | bytes 36700160 | tf_op jit(solution)/shard_map/pallas_call | solution.py:390
  33.4 0.0 collective-permute-done.3.refs_3_
  33.4 0.0 collective-permute-done.4.refs_4_
  33.4 0.0 collective-permute-done.5.refs_5_
  33.5 19.5 %shard_map.84.refs_0_ = bf16[160,3584]{1,0:T(8,128)(2,1)S(1)} custom-call(bf16[40,4096]{1,0:T(8,128)(2,1)S(1)} %get-tuple-element.33.own, bf16[40,2048]{1,0:T(8,128)(2,1)S(1)} %collective-permute-done.refs_0_, bf16[40,2048]{1,0:T(8,128)(2,1)S(1)} %collective-permute-done.1.refs_1_, bf16[40,2048]{1,0:T(8,128)(2,1)S(1)} %collective-permute-done.2.refs_2_, ...), custom_call_target="tpu_custom_call" | custom-call | flops 9395240960 | bytes 58720256 | tf_op jit(solution)/shard_map/pallas_call | solution.py:390
  52.9 3.5 %shard_map.85 = bf16[160,1024]{1,0:T(8,128)(2,1)S(1)} custom-call(bf16[160,3584]{1,0:T(8,128)(2,1)S(1)} %shard_map.84.refs_0_, bf16[3584,4096]{1,0:T(8,128)(2,1)} %refs_1_.7), custom_call_target="tpu_custom_call" | custom-call | flops 1174405120 | bytes 7340032 | tf_op jit(solution)/shard_map/pallas_call | solution.py:390
  56.5 0.1 collective-permute-start.6
  56.5 3.5 %shard_map.88 = bf16[160,1024]{1,0:T(8,128)(2,1)S(1)} custom-call(bf16[160,3584]{1,0:T(8,128)(2,1)S(1)} %shard_map.84.refs_0_, bf16[3584,4096]{1,0:T(8,128)(2,1)} %refs_1_.7), custom_call_target="tpu_custom_call" | custom-call | flops 1174405120 | bytes 7340032 | tf_op jit(solution)/shard_map/pallas_call | solution.py:390
  60.1 0.5 collective-permute-start.11
  60.6 0.0 collective-permute-done.6.refs_2_
  60.6 3.5 %shard_map.86 = (bf16[40,1024]{1,0:T(8,128)(2,1)S(1)}, bf16[40,1024]{1,0:T(8,128)(2,1)S(1)}, bf16[40,1024]{1,0:T(8,128)(2,1)S(1)}, bf16[40,1024]{1,0:T(8,128)(2,1)S(1)}) custom-call(bf16[160,3584]{1,0:T(8,128)(2,1)S(1)} %shard_map.84.refs_0_, bf16[3584,4096]{1,0:T(8,128)(2,1)} %refs_1_.7, bf16[160,1024]{1,0:T(8,128)(2,1)S(1)} %collective-permute-done.6.refs_2_), custom_call_target="tpu_custom_call" | custom-call | flops 1174405120 | bytes 7340032 | tf_op jit(solution)/shard_map/pallas_call | solution.py:390
  64.1 5.1 %collective-permute-start.7 = (bf16[40,1024]{1,0:T(8,128)(2,1)S(1)}, bf16[40,1024]{1,0:T(8,128)(2,1)S(1)}, u32[]{:S(2)}, u32[]{:S(2)}) collective-permute-start(bf16[40,1024]{1,0:T(8,128)(2,1)S(1)} %get-tuple-element.44), channel_id=1, source_target_pairs={{0,12},{1,13},{2,14},{3,15},{4,0},{5,1},{6,2},{7,3},{8,4},{9,5},{1... | collective-permute-start | bytes 245768 | tf_op jit(solution)/shard_map/ppermute | solution.py:422
  69.2 0.0 collective-permute-start.8
  69.2 0.6 collective-permute-start.9
  69.9 0.0 collective-permute-done.11.refs_2_
  69.9 3.5 %shard_map.89 = (bf16[40,1024]{1,0:T(8,128)(2,1)S(1)}, bf16[40,1024]{1,0:T(8,128)(2,1)S(1)}, bf16[40,1024]{1,0:T(8,128)(2,1)S(1)}, bf16[40,1024]{1,0:T(8,128)(2,1)S(1)}) custom-call(bf16[160,3584]{1,0:T(8,128)(2,1)S(1)} %shard_map.84.refs_0_, bf16[3584,4096]{1,0:T(8,128)(2,1)} %refs_1_.7, bf16[160,1024]{1,0:T(8,128)(2,1)S(1)} %collective-permute-done.11.refs_2_), custom_call_target="tpu_custom_call" | custom-call | flops 1174405120 | bytes 7340032 | tf_op jit(solution)/shard_map/pallas_call | solution.py:390
  73.4 3.2 %collective-permute-start.12 = (bf16[40,1024]{1,0:T(8,128)(2,1)S(1)}, bf16[40,1024]{1,0:T(8,128)(2,1)S(1)}, u32[]{:S(2)}, u32[]{:S(2)}) collective-permute-start(bf16[40,1024]{1,0:T(8,128)(2,1)S(1)} %get-tuple-element.50), channel_id=1, source_target_pairs={{0,12},{1,13},{2,14},{3,15},{4,0},{5,1},{6,2},{7,3},{8,4},{9,5},{1... | collective-permute-start | bytes 245768 | tf_op jit(solution)/shard_map/ppermute | solution.py:422
  76.6 1.1 %collective-permute-start.13 = (bf16[40,1024]{1,0:T(8,128)(2,1)S(1)}, bf16[40,1024]{1,0:T(8,128)(2,1)S(1)}, u32[]{:S(2)}, u32[]{:S(2)}) collective-permute-start(bf16[40,1024]{1,0:T(8,128)(2,1)S(1)} %get-tuple-element.51), channel_id=1, source_target_pairs={{0,8},{1,9},{2,10},{3,11},{4,12},{5,13},{6,14},{7,15},{8,0},{9,1},... | collective-permute-start | bytes 245768 | tf_op jit(solution)/shard_map/ppermute | solution.py:422
  77.7 0.0 collective-permute-done.7.refs_1_
  77.7 0.0 collective-permute-start.14
  77.7 0.0 collective-permute-done.8.refs_2_
  77.7 0.0 collective-permute-done.9.refs_3_
  77.8 0.3 shard_map.87
  78.1 1.6 %collective-permute-start.10 = (bf16[128,512]{1,0:T(8,128)(2,1)S(1)}, bf16[128,512]{1,0:T(8,128)(2,1)S(1)}, u32[]{:S(2)}, u32[]{:S(2)}) collective-permute-start(bf16[128,512]{1,0:T(8,128)(2,1)S(1)} %get-tuple-element.48), channel_id=1, source_target_pairs={{0,2},{1,3},{2,0},{3,1},{4,6},{5,7},{6,4},{7,5},{8,10},{9,11},{10,... | collective-permute-start | bytes 393224 | tf_op jit(solution)/shard_map/ppermute | solution.py:422
  79.6 0.0 collective-permute-done.12.refs_1_
  79.6 5.3 %collective-permute-done.13.refs_2_ = bf16[40,1024]{1,0:T(8,128)(2,1)S(1)} collective-permute-done((bf16[40,1024]{1,0:T(8,128)(2,1)S(1)}, bf16[40,1024]{1,0:T(8,128)(2,1)S(1)}, u32[]{:S(2)}, u32[]{:S(2)}) %collective-permute-start.13) | collective-permute-done | bytes 81952 | tf_op jit(solution)/shard_map/ppermute | solution.py:422
  84.9 0.0 collective-permute-done.14.refs_3_
  84.9 0.3 shard_map.90
  85.2 1.6 %collective-permute-start.15 = (bf16[128,512]{1,0:T(8,128)(2,1)S(1)}, bf16[128,512]{1,0:T(8,128)(2,1)S(1)}, u32[]{:S(2)}, u32[]{:S(2)}) collective-permute-start(bf16[128,512]{1,0:T(8,128)(2,1)S(1)} %get-tuple-element.54), channel_id=1, source_target_pairs={{0,2},{1,3},{2,0},{3,1},{4,6},{5,7},{6,4},{7,5},{8,10},{9,11},{10,... | collective-permute-start | bytes 393224 | tf_op jit(solution)/shard_map/ppermute | solution.py:422
  86.8 0.0 collective-permute-done.10.refs_1_
  86.8 3.5 %collective-permute-done.15.refs_3_ = bf16[128,512]{1,0:T(8,128)(2,1)S(1)} collective-permute-done((bf16[128,512]{1,0:T(8,128)(2,1)S(1)}, bf16[128,512]{1,0:T(8,128)(2,1)S(1)}, u32[]{:S(2)}, u32[]{:S(2)}) %collective-permute-start.15) | collective-permute-done | bytes 131104 | tf_op jit(solution)/shard_map/ppermute | solution.py:422
  90.2 0.7 shard_map.91
Async XLA Ops:
  2.0 10.2 %collective-permute-start = (bf16[40,2048]{1,0:T(8,128)(2,1)S(1)}, bf16[40,2048]{1,0:T(8,128)(2,1)S(1)}, u32[]{:S(2)}, u32[]{:S(2)}) collective-permute-start(bf16[40,2048]{1,0:T(8,128)(2,1)S(1)} %get-tuple-element.34), channel_id=1, source_target_pairs={{0,4},{1,5},{2,6},{3,7},{4,8},{5,9},{6,10},{7,11},{8,12},{9,13},{1... | collective-permute-start | bytes 491528 | tf_op jit(solution)/shard_map/ppermute | solution.py:422
  5.1 13.3 %collective-permute-start.1 = (bf16[40,2048]{1,0:T(8,128)(2,1)S(1)}, bf16[40,2048]{1,0:T(8,128)(2,1)S(1)}, u32[]{:S(2)}, u32[]{:S(2)}) collective-permute-start(bf16[40,2048]{1,0:T(8,128)(2,1)S(1)} %get-tuple-element.35), channel_id=1, source_target_pairs={{0,8},{1,9},{2,10},{3,11},{4,12},{5,13},{6,14},{7,15},{8,0},{9,1},... | collective-permute-start | bytes 491528 | tf_op jit(solution)/shard_map/ppermute | solution.py:422
  7.7 10.8 %collective-permute-start.2 = (bf16[40,2048]{1,0:T(8,128)(2,1)S(1)}, bf16[40,2048]{1,0:T(8,128)(2,1)S(1)}, u32[]{:S(2)}, u32[]{:S(2)}) collective-permute-start(bf16[40,2048]{1,0:T(8,128)(2,1)S(1)} %get-tuple-element.36), channel_id=1, source_target_pairs={{0,12},{1,13},{2,14},{3,15},{4,0},{5,1},{6,2},{7,3},{8,4},{9,5},{1... | collective-permute-start | bytes 491528 | tf_op jit(solution)/shard_map/ppermute | solution.py:422
  12.2 21.2 %collective-permute-start.3 = (bf16[40,2048]{1,0:T(8,128)(2,1)S(1)}, bf16[40,2048]{1,0:T(8,128)(2,1)S(1)}, u32[]{:S(2)}, u32[]{:S(2)}) collective-permute-start(bf16[40,2048]{1,0:T(8,128)(2,1)S(1)} %collective-permute-done.refs_0_), channel_id=1, source_target_pairs={{0,1},{1,0},{2,3},{3,2},{4,5},{5,4},{6,7},{7,6},{8,9},{9,8},{10,11... | collective-permute-start | bytes 491528 | tf_op jit(solution)/shard_map/ppermute | solution.py:425
  18.4 15.0 %collective-permute-start.4 = (bf16[40,2048]{1,0:T(8,128)(2,1)S(1)}, bf16[40,2048]{1,0:T(8,128)(2,1)S(1)}, u32[]{:S(2)}, u32[]{:S(2)}) collective-permute-start(bf16[40,2048]{1,0:T(8,128)(2,1)S(1)} %collective-permute-done.1.refs_1_), channel_id=1, source_target_pairs={{0,1},{1,0},{2,3},{3,2},{4,5},{5,4},{6,7},{7,6},{8,9},{9,8},{10,11... | collective-permute-start | bytes 491528 | tf_op jit(solution)/shard_map/ppermute | solution.py:425
  18.4 15.0 %collective-permute-start.5 = (bf16[40,2048]{1,0:T(8,128)(2,1)S(1)}, bf16[40,2048]{1,0:T(8,128)(2,1)S(1)}, u32[]{:S(2)}, u32[]{:S(2)}) collective-permute-start(bf16[40,2048]{1,0:T(8,128)(2,1)S(1)} %collective-permute-done.2.refs_2_), channel_id=1, source_target_pairs={{0,1},{1,0},{2,3},{3,2},{4,5},{5,4},{6,7},{7,6},{8,9},{9,8},{10,11... | collective-permute-start | bytes 491528 | tf_op jit(solution)/shard_map/ppermute | solution.py:425
  18.9 0.7 copy-start
  19.6 0.7 copy-start.1
  20.3 0.7 copy-start.2
  56.5 4.2 %collective-permute-start.6 = (bf16[160,1024]{1,0:T(8,128)(2,1)S(1)}, bf16[160,1024]{1,0:T(8,128)(2,1)S(1)}, u32[]{:S(2)}, u32[]{:S(2)}) collective-permute-start(bf16[160,1024]{1,0:T(8,128)(2,1)S(1)} %shard_map.85), channel_id=1, source_target_pairs={{0,1},{1,0},{2,3},{3,2},{4,5},{5,4},{6,7},{7,6},{8,9},{9,8},{10,11... | collective-permute-start | bytes 983048 | tf_op jit(solution)/shard_map/ppermute | solution.py:425
  60.1 9.8 %collective-permute-start.11 = (bf16[160,1024]{1,0:T(8,128)(2,1)S(1)}, bf16[160,1024]{1,0:T(8,128)(2,1)S(1)}, u32[]{:S(2)}, u32[]{:S(2)}) collective-permute-start(bf16[160,1024]{1,0:T(8,128)(2,1)S(1)} %shard_map.88), channel_id=1, source_target_pairs={{0,1},{1,0},{2,3},{3,2},{4,5},{5,4},{6,7},{7,6},{8,9},{9,8},{10,11... | collective-permute-start | bytes 983048 | tf_op jit(solution)/shard_map/ppermute | solution.py:425
  64.1 13.6 %collective-permute-start.7 = (bf16[40,1024]{1,0:T(8,128)(2,1)S(1)}, bf16[40,1024]{1,0:T(8,128)(2,1)S(1)}, u32[]{:S(2)}, u32[]{:S(2)}) collective-permute-start(bf16[40,1024]{1,0:T(8,128)(2,1)S(1)} %get-tuple-element.44), channel_id=1, source_target_pairs={{0,12},{1,13},{2,14},{3,15},{4,0},{5,1},{6,2},{7,3},{8,4},{9,5},{1... | collective-permute-start | bytes 245768 | tf_op jit(solution)/shard_map/ppermute | solution.py:422
  69.2 8.5 %collective-permute-start.8 = (bf16[40,1024]{1,0:T(8,128)(2,1)S(1)}, bf16[40,1024]{1,0:T(8,128)(2,1)S(1)}, u32[]{:S(2)}, u32[]{:S(2)}) collective-permute-start(bf16[40,1024]{1,0:T(8,128)(2,1)S(1)} %get-tuple-element.45), channel_id=1, source_target_pairs={{0,8},{1,9},{2,10},{3,11},{4,12},{5,13},{6,14},{7,15},{8,0},{9,1},... | collective-permute-start | bytes 245768 | tf_op jit(solution)/shard_map/ppermute | solution.py:422
  69.2 8.5 %collective-permute-start.9 = (bf16[40,1024]{1,0:T(8,128)(2,1)S(1)}, bf16[40,1024]{1,0:T(8,128)(2,1)S(1)}, u32[]{:S(2)}, u32[]{:S(2)}) collective-permute-start(bf16[40,1024]{1,0:T(8,128)(2,1)S(1)} %get-tuple-element.46), channel_id=1, source_target_pairs={{0,4},{1,5},{2,6},{3,7},{4,8},{5,9},{6,10},{7,11},{8,12},{9,13},{1... | collective-permute-start | bytes 245768 | tf_op jit(solution)/shard_map/ppermute | solution.py:422
  73.4 6.2 %collective-permute-start.12 = (bf16[40,1024]{1,0:T(8,128)(2,1)S(1)}, bf16[40,1024]{1,0:T(8,128)(2,1)S(1)}, u32[]{:S(2)}, u32[]{:S(2)}) collective-permute-start(bf16[40,1024]{1,0:T(8,128)(2,1)S(1)} %get-tuple-element.50), channel_id=1, source_target_pairs={{0,12},{1,13},{2,14},{3,15},{4,0},{5,1},{6,2},{7,3},{8,4},{9,5},{1... | collective-permute-start | bytes 245768 | tf_op jit(solution)/shard_map/ppermute | solution.py:422
  76.6 8.3 %collective-permute-start.13 = (bf16[40,1024]{1,0:T(8,128)(2,1)S(1)}, bf16[40,1024]{1,0:T(8,128)(2,1)S(1)}, u32[]{:S(2)}, u32[]{:S(2)}) collective-permute-start(bf16[40,1024]{1,0:T(8,128)(2,1)S(1)} %get-tuple-element.51), channel_id=1, source_target_pairs={{0,8},{1,9},{2,10},{3,11},{4,12},{5,13},{6,14},{7,15},{8,0},{9,1},... | collective-permute-start | bytes 245768 | tf_op jit(solution)/shard_map/ppermute | solution.py:422
  77.7 7.2 %collective-permute-start.14 = (bf16[40,1024]{1,0:T(8,128)(2,1)S(1)}, bf16[40,1024]{1,0:T(8,128)(2,1)S(1)}, u32[]{:S(2)}, u32[]{:S(2)}) collective-permute-start(bf16[40,1024]{1,0:T(8,128)(2,1)S(1)} %get-tuple-element.52), channel_id=1, source_target_pairs={{0,4},{1,5},{2,6},{3,7},{4,8},{5,9},{6,10},{7,11},{8,12},{9,13},{1... | collective-permute-start | bytes 245768 | tf_op jit(solution)/shard_map/ppermute | solution.py:422
  78.1 8.7 %collective-permute-start.10 = (bf16[128,512]{1,0:T(8,128)(2,1)S(1)}, bf16[128,512]{1,0:T(8,128)(2,1)S(1)}, u32[]{:S(2)}, u32[]{:S(2)}) collective-permute-start(bf16[128,512]{1,0:T(8,128)(2,1)S(1)} %get-tuple-element.48), channel_id=1, source_target_pairs={{0,2},{1,3},{2,0},{3,1},{4,6},{5,7},{6,4},{7,5},{8,10},{9,11},{10,... | collective-permute-start | bytes 393224 | tf_op jit(solution)/shard_map/ppermute | solution.py:422
  85.2 5.0 %collective-permute-start.15 = (bf16[128,512]{1,0:T(8,128)(2,1)S(1)}, bf16[128,512]{1,0:T(8,128)(2,1)S(1)}, u32[]{:S(2)}, u32[]{:S(2)}) collective-permute-start(bf16[128,512]{1,0:T(8,128)(2,1)S(1)} %get-tuple-element.54), channel_id=1, source_target_pairs={{0,2},{1,3},{2,0},{3,1},{4,6},{5,7},{6,4},{7,5},{8,10},{9,11},{10,... | collective-permute-start | bytes 393224 | tf_op jit(solution)/shard_map/ppermute | solution.py:422

commit v4 on v3

--- a/solution.py
+++ b/solution.py
@@ -235,12 +235,15 @@
         copy.wait()
 
 
-def hidden_kernel(sizes, own, *refs):
+def join_kernel(after, *refs):
+    pieces = [r[...].astype(F32) for r in refs[:-1]]
+    refs[-1][...] = jnp.concatenate(pieces, axis=0).astype(BF16)
+
+
+def hidden_kernel(sizes, own, mine, other, *refs):
     exp_count, groups = sizes
     z, g, s = place(sizes)
     refs = list(refs)
-    mine = [refs.pop(0) for _ in range(exp_count - 1)]
-    other = [refs.pop(0) for _ in range(exp_count - 1)]
     gate_near = [refs.pop(0) for _ in range(GATE_NEAR)]
     up_near = [refs.pop(0) for _ in range(UP_NEAR)]
     up, mask, hidden, gate_sum, up_sum, rows, slabs, sems = refs
@@ -257,12 +260,10 @@
 
     for n in range(min(K_DEPTH, far_count)):
         copy(n).start()
-    for side_of in range(2):
-        source = (mine, other)[side_of]
-        side = s if side_of == 0 else 1 - s
-        start = pl.multiple_of(side * half, 128)
-        pieces = [own[:, pl.ds(start, half)].astype(F32)] + [r[...].astype(F32) for r in source]
-        rows[:, pl.ds(start, half)] = jnp.concatenate(pieces, axis=0).astype(BF16)
+    for source, side in ((mine, s), (other, 1 - s)):
+        cols = pl.ds(pl.multiple_of(side * half, 128), half)
+        pieces = [own[:, cols].astype(F32), source[...].astype(F32)]
+        rows[:, cols] = jnp.concatenate(pieces, axis=0).astype(BF16)
 
     def each_tile(body):
         def step(n, carry):
@@ -465,13 +466,19 @@
         moved=2 * (GATE_NEAR + UP_NEAR) * NEAR_ROWS * unit_width,
         limit=16,
     )
-    mine = [shift(value, d + 1) for d, value in enumerate(sends)]
-    other = [swap(value) for value in mine]
+    arrived = [shift(value, d + 1) for d, value in enumerate(sends)]
+    mine = call(
+        join_kernel,
+        [((batch * CAP, width), BF16)],
+        [(mask, pl.ANY)] + [(v, None) for v in arrived],
+        moved=1 << 20,
+    )[0]
+    other = swap(mine)
     acc = ((slots, unit_width), F32)
     hidden = call(
         functools.partial(hidden_kernel, sizes),
         [((slots, unit_width), BF16)],
-        [(v, None) for v in [own] + mine + other]
+        [(own, None), (mine, None), (other, None)]
         + [(v, pltpu.VMEM) for v in nears]
         + [(up_weight, pltpu.HBM), (mask, None)],
         [

time: 91.3 us -> 79.7 us (0.87)
  waiting for transfers between devices: 18.2 us -> 9.98 us
  starting transfers between devices: 21.4 us -> 17.9 us
    ppermute x11, waiting for transfers between devices: 18.2 us -> 8.12 us  [shift(): return lax.ppermute(value, ('exp', 'unit'), pairs)]
    ppermute x11, starting transfers between devices: 20.2 us -> 17.2 us  [shift(): return lax.ppermute(value, ('exp', 'unit'), pairs)]
    ppermute x5 -> x3, waiting for transfers between devices: 0.01 us -> 1.86 us  [swap(): return lax.ppermute(value, 'unit', [(u, u ^ 1) for u in range(unit_count)])]
    pallas_call x10 -> x11, Pallas kernels: 49.3 us -> 49.2 us  [call(): pl.pallas_call(kernel, out_shape=shapes, in_specs=specs, out_specs=[vmem]...]
  transfers between devices with their start and end apart: 16 -> 14, of which waited for: 4 -> 4; matrix products, arithmetic and copies ran while one was open for 0% -> 0% of each run, Pallas kernels for 26% -> 30%
where the time goes in v4:
time: 79.7 us; the launch traced here: 79.3 us
  Pallas kernels  49.2 us (62%)
  starting transfers between devices  17.9 us (22%)
  waiting for transfers between devices  9.98 us (13%)
  local copies, waits for them, and re-layouts  2.05 us (3%)
    pallas_call x11, Pallas kernels, call(): pl.pallas_call(kernel, out_shape=shapes, in_specs=specs, out_specs=[vmem]...  49.2 us
    ppermute x11, starting transfers between devices, shift(): return lax.ppermute(value, ('exp', 'unit'), pairs)  17.2 us
    ppermute x11, waiting for transfers between devices, shift(): return lax.ppermute(value, ('exp', 'unit'), pairs)  8.12 us
    unnamed x6, local copies, waits for them, and re-layouts  2.05 us
    ppermute x3, waiting for transfers between devices, swap(): return lax.ppermute(value, 'unit', [(u, u ^ 1) for u in range(unit_count)])  1.86 us
  transfers between devices with their start and end apart: 14, of which 4 were waited for; matrix products, arithmetic and copies ran while one was open for 0% of the time, Pallas kernels for 30%

profile of v4, /device:TPU:0, one launch (start us, length us, event | category | flops | bytes accessed | tf_op | source)
XLA Modules:
  0.0 79.3 jit_solution(13280168844607394319)
XLA Ops:
  0.0 2.0 %shard_map.82 = (bf16[128,4096]{1,0:T(8,128)(2,1)S(1)}, bf16[40,2048]{1,0:T(8,128)(2,1)S(1)}, bf16[40,2048]{1,0:T(8,128)(2,1)S(1)}, bf16[40,2048]{1,0:T(8,128)(2,1)S(1)}) custom-call(bf16[128,4096]{1,0:T(8,128)(2,1)} %tokens_hbm.1, f32[1,4096]{1,0:T(1,128)} %bitcast.6, s32[2,128]{1,0:T(2,128)} %bitcast.3), custom_call_target="tpu_custom_call" | custom-call | flops 83886080 | bytes 2097152 | tf_op jit(solution)/shard_map/pallas_call | solution.py:391
  2.0 3.1 %collective-permute-start = (bf16[40,2048]{1,0:T(8,128)(2,1)S(1)}, bf16[40,2048]{1,0:T(8,128)(2,1)S(1)}, u32[]{:S(2)}, u32[]{:S(2)}) collective-permute-start(bf16[40,2048]{1,0:T(8,128)(2,1)S(1)} %get-tuple-element.35), channel_id=1, source_target_pairs={{0,4},{1,5},{2,6},{3,7},{4,8},{5,9},{6,10},{7,11},{8,12},{9,13},{1... | collective-permute-start | bytes 491528 | tf_op jit(solution)/shard_map/ppermute | solution.py:423
  5.1 2.6 %collective-permute-start.1 = (bf16[40,2048]{1,0:T(8,128)(2,1)S(1)}, bf16[40,2048]{1,0:T(8,128)(2,1)S(1)}, u32[]{:S(2)}, u32[]{:S(2)}) collective-permute-start(bf16[40,2048]{1,0:T(8,128)(2,1)S(1)} %get-tuple-element.36), channel_id=1, source_target_pairs={{0,8},{1,9},{2,10},{3,11},{4,12},{5,13},{6,14},{7,15},{8,0},{9,1},... | collective-permute-start | bytes 491528 | tf_op jit(solution)/shard_map/ppermute | solution.py:423
  7.7 1.3 %collective-permute-start.2 = (bf16[40,2048]{1,0:T(8,128)(2,1)S(1)}, bf16[40,2048]{1,0:T(8,128)(2,1)S(1)}, u32[]{:S(2)}, u32[]{:S(2)}) collective-permute-start(bf16[40,2048]{1,0:T(8,128)(2,1)S(1)} %get-tuple-element.37), channel_id=1, source_target_pairs={{0,12},{1,13},{2,14},{3,15},{4,0},{5,1},{6,2},{7,3},{8,4},{9,5},{1... | collective-permute-start | bytes 491528 | tf_op jit(solution)/shard_map/ppermute | solution.py:423
  9.0 0.0 copy-start
  9.0 0.7 copy-done
  9.7 0.0 copy-start.1
  9.7 0.7 copy-done.1
  10.4 0.0 copy-start.2
  10.4 0.7 copy-done.2
  11.1 12.4 %shard_map.83 = (bf16[40,4096]{1,0:T(8,128)(2,1)S(1)}, bf16[128,256]{1,0:T(8,128)(2,1)S(1)}, bf16[128,256]{1,0:T(8,128)(2,1)S(1)}, f32[8,3584]{1,0:T(8,128)S(1)}...) custom-call(bf16[128,4096]{1,0:T(8,128)(2,1)S(1)} %get-tuple-element, ...), custom_call_target="tpu_custom_call" | custom-call | flops 167772160 | bytes 36700160 | tf_op jit(solution)/shard_map/pallas_call | solution.py:391
  23.5 0.0 collective-permute-done.refs_0_
  23.5 0.0 collective-permute-done.1.refs_1_
  23.5 0.0 collective-permute-done.2.refs_2_
  23.6 0.1 collective-permute-start.3
  23.7 1.9 %collective-permute-done.3.other = bf16[120,2048]{1,0:T(8,128)(2,1)S(1)} collective-permute-done((bf16[120,2048]{1,0:T(8,128)(2,1)S(1)}, bf16[120,2048]{1,0:T(8,128)(2,1)S(1)}, u32[]{:S(2)}, u32[]{:S(2)}) %collective-permute-start.3) | collective-permute-done | bytes 491552 | tf_op jit(solution)/shard_map/ppermute | solution.py:426
  25.5 19.4 %shard_map.85.refs_0_ = bf16[160,3584]{1,0:T(8,128)(2,1)S(1)} custom-call(bf16[40,4096]{1,0:T(8,128)(2,1)S(1)} %get-tuple-element.33.own, bf16[120,2048]{1,0:T(8,128)(2,1)S(1)} %shard_map.84.mine, bf16[120,2048]{1,0:T(8,128)(2,1)S(1)} %collective-permute-done.3.other, bf16[1024,3584]{1,0:T(8,128)(2,1)S(1)} %get-tuple-element.38.refs_0_, ...), custom_call_target="tpu_custom_call" | custom-call | flops 9395240960 | bytes 58720256 | tf_op jit(solution)/shard_map/pallas_call | solution.py:391
  45.0 3.5 %shard_map.86 = bf16[160,1024]{1,0:T(8,128)(2,1)S(1)} custom-call(bf16[160,3584]{1,0:T(8,128)(2,1)S(1)} %shard_map.85.refs_0_, bf16[3584,4096]{1,0:T(8,128)(2,1)} %refs_1_.7), custom_call_target="tpu_custom_call" | custom-call | flops 1174405120 | bytes 7340032 | tf_op jit(solution)/shard_map/pallas_call | solution.py:391
  48.5 0.2 collective-permute-start.4
  48.7 3.5 %shard_map.89 = bf16[160,1024]{1,0:T(8,128)(2,1)S(1)} custom-call(bf16[160,3584]{1,0:T(8,128)(2,1)S(1)} %shard_map.85.refs_0_, bf16[3584,4096]{1,0:T(8,128)(2,1)} %refs_1_.7), custom_call_target="tpu_custom_call" | custom-call | flops 1174405120 | bytes 7340032 | tf_op jit(solution)/shard_map/pallas_call | solution.py:391
  52.2 0.4 collective-permute-start.9
  52.7 0.0 collective-permute-done.4.refs_2_
  52.7 3.5 %shard_map.87 = (bf16[40,1024]{1,0:T(8,128)(2,1)S(1)}, bf16[40,1024]{1,0:T(8,128)(2,1)S(1)}, bf16[40,1024]{1,0:T(8,128)(2,1)S(1)}, bf16[40,1024]{1,0:T(8,128)(2,1)S(1)}) custom-call(bf16[160,3584]{1,0:T(8,128)(2,1)S(1)} %shard_map.85.refs_0_, bf16[3584,4096]{1,0:T(8,128)(2,1)} %refs_1_.7, bf16[160,1024]{1,0:T(8,128)(2,1)S(1)} %collective-permute-done.4.refs_2_), custom_call_target="tpu_custom_call" | custom-call | flops 1174405120 | bytes 7340032 | tf_op jit(solution)/shard_map/pallas_call | solution.py:391
  56.2 0.5 collective-permute-start.5
  56.7 1.7 %collective-permute-start.6 = (bf16[40,1024]{1,0:T(8,128)(2,1)S(1)}, bf16[40,1024]{1,0:T(8,128)(2,1)S(1)}, u32[]{:S(2)}, u32[]{:S(2)}) collective-permute-start(bf16[40,1024]{1,0:T(8,128)(2,1)S(1)} %get-tuple-element.45), channel_id=1, source_target_pairs={{0,8},{1,9},{2,10},{3,11},{4,12},{5,13},{6,14},{7,15},{8,0},{9,1},... | collective-permute-start | bytes 245768 | tf_op jit(solution)/shard_map/ppermute | solution.py:423
  58.4 0.1 collective-permute-start.7
  58.4 0.0 collective-permute-done.9.refs_2_
  58.4 3.5 %shard_map.90 = (bf16[40,1024]{1,0:T(8,128)(2,1)S(1)}, bf16[40,1024]{1,0:T(8,128)(2,1)S(1)}, bf16[40,1024]{1,0:T(8,128)(2,1)S(1)}, bf16[40,1024]{1,0:T(8,128)(2,1)S(1)}) custom-call(bf16[160,3584]{1,0:T(8,128)(2,1)S(1)} %shard_map.85.refs_0_, bf16[3584,4096]{1,0:T(8,128)(2,1)} %refs_1_.7, bf16[160,1024]{1,0:T(8,128)(2,1)S(1)} %collective-permute-done.9.refs_2_), custom_call_target="tpu_custom_call" | custom-call | flops 1174405120 | bytes 7340032 | tf_op jit(solution)/shard_map/pallas_call | solution.py:391
  61.9 3.8 %collective-permute-start.10 = (bf16[40,1024]{1,0:T(8,128)(2,1)S(1)}, bf16[40,1024]{1,0:T(8,128)(2,1)S(1)}, u32[]{:S(2)}, u32[]{:S(2)}) collective-permute-start(bf16[40,1024]{1,0:T(8,128)(2,1)S(1)} %get-tuple-element.50), channel_id=1, source_target_pairs={{0,12},{1,13},{2,14},{3,15},{4,0},{5,1},{6,2},{7,3},{8,4},{9,5},{1... | collective-permute-start | bytes 245768 | tf_op jit(solution)/shard_map/ppermute | solution.py:423
  65.7 0.0 collective-permute-start.11
  65.7 0.0 collective-permute-done.5.refs_1_
  65.7 1.0 %collective-permute-start.12 = (bf16[40,1024]{1,0:T(8,128)(2,1)S(1)}, bf16[40,1024]{1,0:T(8,128)(2,1)S(1)}, u32[]{:S(2)}, u32[]{:S(2)}) collective-permute-start(bf16[40,1024]{1,0:T(8,128)(2,1)S(1)} %get-tuple-element.52), channel_id=1, source_target_pairs={{0,4},{1,5},{2,6},{3,7},{4,8},{5,9},{6,10},{7,11},{8,12},{9,13},{1... | collective-permute-start | bytes 245768 | tf_op jit(solution)/shard_map/ppermute | solution.py:423
  66.8 0.1 collective-permute-done.6.refs_2_
  66.9 0.0 collective-permute-done.7.refs_3_
  66.9 0.3 shard_map.88
  67.2 1.6 %collective-permute-start.8 = (bf16[128,512]{1,0:T(8,128)(2,1)S(1)}, bf16[128,512]{1,0:T(8,128)(2,1)S(1)}, u32[]{:S(2)}, u32[]{:S(2)}) collective-permute-start(bf16[128,512]{1,0:T(8,128)(2,1)S(1)} %get-tuple-element.48), channel_id=1, source_target_pairs={{0,2},{1,3},{2,0},{3,1},{4,6},{5,7},{6,4},{7,5},{8,10},{9,11},{10,... | collective-permute-start | bytes 393224 | tf_op jit(solution)/shard_map/ppermute | solution.py:423
  68.7 0.0 collective-permute-done.10.refs_1_
  68.7 4.4 %collective-permute-done.11.refs_2_ = bf16[40,1024]{1,0:T(8,128)(2,1)S(1)} collective-permute-done((bf16[40,1024]{1,0:T(8,128)(2,1)S(1)}, bf16[40,1024]{1,0:T(8,128)(2,1)S(1)}, u32[]{:S(2)}, u32[]{:S(2)}) %collective-permute-start.11) | collective-permute-done | bytes 81952 | tf_op jit(solution)/shard_map/ppermute | solution.py:423
  73.1 0.0 collective-permute-done.12.refs_3_
  73.1 0.3 shard_map.91
  73.4 1.6 %collective-permute-start.13 = (bf16[128,512]{1,0:T(8,128)(2,1)S(1)}, bf16[128,512]{1,0:T(8,128)(2,1)S(1)}, u32[]{:S(2)}, u32[]{:S(2)}) collective-permute-start(bf16[128,512]{1,0:T(8,128)(2,1)S(1)} %get-tuple-element.54), channel_id=1, source_target_pairs={{0,2},{1,3},{2,0},{3,1},{4,6},{5,7},{6,4},{7,5},{8,10},{9,11},{10,... | collective-permute-start | bytes 393224 | tf_op jit(solution)/shard_map/ppermute | solution.py:423
  75.0 0.0 collective-permute-done.8.refs_1_
  75.0 3.6 %collective-permute-done.13.refs_3_ = bf16[128,512]{1,0:T(8,128)(2,1)S(1)} collective-permute-done((bf16[128,512]{1,0:T(8,128)(2,1)S(1)}, bf16[128,512]{1,0:T(8,128)(2,1)S(1)}, u32[]{:S(2)}, u32[]{:S(2)}) %collective-permute-start.13) | collective-permute-done | bytes 131104 | tf_op jit(solution)/shard_map/ppermute | solution.py:423
  78.6 0.7 shard_map.92
  (1 shorter events, 0.0 us)
Async XLA Ops:
  2.0 21.5 %collective-permute-start = (bf16[40,2048]{1,0:T(8,128)(2,1)S(1)}, bf16[40,2048]{1,0:T(8,128)(2,1)S(1)}, u32[]{:S(2)}, u32[]{:S(2)}) collective-permute-start(bf16[40,2048]{1,0:T(8,128)(2,1)S(1)} %get-tuple-element.35), channel_id=1, source_target_pairs={{0,4},{1,5},{2,6},{3,7},{4,8},{5,9},{6,10},{7,11},{8,12},{9,13},{1... | collective-permute-start | bytes 491528 | tf_op jit(solution)/shard_map/ppermute | solution.py:423
  5.1 18.4 %collective-permute-start.1 = (bf16[40,2048]{1,0:T(8,128)(2,1)S(1)}, bf16[40,2048]{1,0:T(8,128)(2,1)S(1)}, u32[]{:S(2)}, u32[]{:S(2)}) collective-permute-start(bf16[40,2048]{1,0:T(8,128)(2,1)S(1)} %get-tuple-element.36), channel_id=1, source_target_pairs={{0,8},{1,9},{2,10},{3,11},{4,12},{5,13},{6,14},{7,15},{8,0},{9,1},... | collective-permute-start | bytes 491528 | tf_op jit(solution)/shard_map/ppermute | solution.py:423
  7.7 15.9 %collective-permute-start.2 = (bf16[40,2048]{1,0:T(8,128)(2,1)S(1)}, bf16[40,2048]{1,0:T(8,128)(2,1)S(1)}, u32[]{:S(2)}, u32[]{:S(2)}) collective-permute-start(bf16[40,2048]{1,0:T(8,128)(2,1)S(1)} %get-tuple-element.37), channel_id=1, source_target_pairs={{0,12},{1,13},{2,14},{3,15},{4,0},{5,1},{6,2},{7,3},{8,4},{9,5},{1... | collective-permute-start | bytes 491528 | tf_op jit(solution)/shard_map/ppermute | solution.py:423
  9.0 0.7 copy-start
  9.7 0.7 copy-start.1
  10.4 0.7 copy-start.2
  23.6 1.9 %collective-permute-start.3 = (bf16[120,2048]{1,0:T(8,128)(2,1)S(1)}, bf16[120,2048]{1,0:T(8,128)(2,1)S(1)}, u32[]{:S(2)}, u32[]{:S(2)}) collective-permute-start(bf16[120,2048]{1,0:T(8,128)(2,1)S(1)} %shard_map.84.mine), channel_id=1, source_target_pairs={{0,1},{1,0},{2,3},{3,2},{4,5},{5,4},{6,7},{7,6},{8,9},{9,8},{10,11... | collective-permute-start | bytes 1474568 | tf_op jit(solution)/shard_map/ppermute | solution.py:426
  48.5 4.2 %collective-permute-start.4 = (bf16[160,1024]{1,0:T(8,128)(2,1)S(1)}, bf16[160,1024]{1,0:T(8,128)(2,1)S(1)}, u32[]{:S(2)}, u32[]{:S(2)}) collective-permute-start(bf16[160,1024]{1,0:T(8,128)(2,1)S(1)} %shard_map.86), channel_id=1, source_target_pairs={{0,1},{1,0},{2,3},{3,2},{4,5},{5,4},{6,7},{7,6},{8,9},{9,8},{10,11... | collective-permute-start | bytes 983048 | tf_op jit(solution)/shard_map/ppermute | solution.py:426
  52.2 6.2 %collective-permute-start.9 = (bf16[160,1024]{1,0:T(8,128)(2,1)S(1)}, bf16[160,1024]{1,0:T(8,128)(2,1)S(1)}, u32[]{:S(2)}, u32[]{:S(2)}) collective-permute-start(bf16[160,1024]{1,0:T(8,128)(2,1)S(1)} %shard_map.89), channel_id=1, source_target_pairs={{0,1},{1,0},{2,3},{3,2},{4,5},{5,4},{6,7},{7,6},{8,9},{9,8},{10,11... | collective-permute-start | bytes 983048 | tf_op jit(solution)/shard_map/ppermute | solution.py:426
  56.2 9.6 %collective-permute-start.5 = (bf16[40,1024]{1,0:T(8,128)(2,1)S(1)}, bf16[40,1024]{1,0:T(8,128)(2,1)S(1)}, u32[]{:S(2)}, u32[]{:S(2)}) collective-permute-start(bf16[40,1024]{1,0:T(8,128)(2,1)S(1)} %get-tuple-element.44), channel_id=1, source_target_pairs={{0,12},{1,13},{2,14},{3,15},{4,0},{5,1},{6,2},{7,3},{8,4},{9,5},{1... | collective-permute-start | bytes 245768 | tf_op jit(solution)/shard_map/ppermute | solution.py:423
  56.7 10.2 %collective-permute-start.6 = (bf16[40,1024]{1,0:T(8,128)(2,1)S(1)}, bf16[40,1024]{1,0:T(8,128)(2,1)S(1)}, u32[]{:S(2)}, u32[]{:S(2)}) collective-permute-start(bf16[40,1024]{1,0:T(8,128)(2,1)S(1)} %get-tuple-element.45), channel_id=1, source_target_pairs={{0,8},{1,9},{2,10},{3,11},{4,12},{5,13},{6,14},{7,15},{8,0},{9,1},... | collective-permute-start | bytes 245768 | tf_op jit(solution)/shard_map/ppermute | solution.py:423
  58.4 8.5 %collective-permute-start.7 = (bf16[40,1024]{1,0:T(8,128)(2,1)S(1)}, bf16[40,1024]{1,0:T(8,128)(2,1)S(1)}, u32[]{:S(2)}, u32[]{:S(2)}) collective-permute-start(bf16[40,1024]{1,0:T(8,128)(2,1)S(1)} %get-tuple-element.46), channel_id=1, source_target_pairs={{0,4},{1,5},{2,6},{3,7},{4,8},{5,9},{6,10},{7,11},{8,12},{9,13},{1... | collective-permute-start | bytes 245768 | tf_op jit(solution)/shard_map/ppermute | solution.py:423
  61.9 6.8 %collective-permute-start.10 = (bf16[40,1024]{1,0:T(8,128)(2,1)S(1)}, bf16[40,1024]{1,0:T(8,128)(2,1)S(1)}, u32[]{:S(2)}, u32[]{:S(2)}) collective-permute-start(bf16[40,1024]{1,0:T(8,128)(2,1)S(1)} %get-tuple-element.50), channel_id=1, source_target_pairs={{0,12},{1,13},{2,14},{3,15},{4,0},{5,1},{6,2},{7,3},{8,4},{9,5},{1... | collective-permute-start | bytes 245768 | tf_op jit(solution)/shard_map/ppermute | solution.py:423
  65.7 7.4 %collective-permute-start.11 = (bf16[40,1024]{1,0:T(8,128)(2,1)S(1)}, bf16[40,1024]{1,0:T(8,128)(2,1)S(1)}, u32[]{:S(2)}, u32[]{:S(2)}) collective-permute-start(bf16[40,1024]{1,0:T(8,128)(2,1)S(1)} %get-tuple-element.51), channel_id=1, source_target_pairs={{0,8},{1,9},{2,10},{3,11},{4,12},{5,13},{6,14},{7,15},{8,0},{9,1},... | collective-permute-start | bytes 245768 | tf_op jit(solution)/shard_map/ppermute | solution.py:423
  65.7 7.4 %collective-permute-start.12 = (bf16[40,1024]{1,0:T(8,128)(2,1)S(1)}, bf16[40,1024]{1,0:T(8,128)(2,1)S(1)}, u32[]{:S(2)}, u32[]{:S(2)}) collective-permute-start(bf16[40,1024]{1,0:T(8,128)(2,1)S(1)} %get-tuple-element.52), channel_id=1, source_target_pairs={{0,4},{1,5},{2,6},{3,7},{4,8},{5,9},{6,10},{7,11},{8,12},{9,13},{1... | collective-permute-start | bytes 245768 | tf_op jit(solution)/shard_map/ppermute | solution.py:423
  67.2 7.8 %collective-permute-start.8 = (bf16[128,512]{1,0:T(8,128)(2,1)S(1)}, bf16[128,512]{1,0:T(8,128)(2,1)S(1)}, u32[]{:S(2)}, u32[]{:S(2)}) collective-permute-start(bf16[128,512]{1,0:T(8,128)(2,1)S(1)} %get-tuple-element.48), channel_id=1, source_target_pairs={{0,2},{1,3},{2,0},{3,1},{4,6},{5,7},{6,4},{7,5},{8,10},{9,11},{10,... | collective-permute-start | bytes 393224 | tf_op jit(solution)/shard_map/ppermute | solution.py:423
  73.4 5.2 %collective-permute-start.13 = (bf16[128,512]{1,0:T(8,128)(2,1)S(1)}, bf16[128,512]{1,0:T(8,128)(2,1)S(1)}, u32[]{:S(2)}, u32[]{:S(2)}) collective-permute-start(bf16[128,512]{1,0:T(8,128)(2,1)S(1)} %get-tuple-element.54), channel_id=1, source_target_pairs={{0,2},{1,3},{2,0},{3,1},{4,6},{5,7},{6,4},{7,5},{8,10},{9,11},{10,... | collective-permute-start | bytes 393224 | tf_op jit(solution)/shard_map/ppermute | solution.py:423

commit v5 on v4

--- a/solution.py
+++ b/solution.py
@@ -17,13 +17,11 @@
 EPSILON = 1e-05
 
 OUT_CHUNKS = 2
-K_SLAB = 512
-K_DEPTH = 2
-N_TILE = 512
-NEAR_ROWS = 1024
-GATE_NEAR = 4
-UP_NEAR = 1
-N_ROWS = 512
+BLOCK = 512
+K_BLOCKS = 2
+READY = 4
+BUFFERS = 5
+LIMIT = 8
 
 F32 = jnp.float32
 BF16 = jnp.bfloat16
@@ -159,9 +157,9 @@
     return lax.rem(z + distance, exp_count) * groups + g
 
 
-def route_kernel(sizes, width, tokens_hbm, gain_hbm, ids_hbm, normed, *rest):
-    exp_count, groups = sizes
-    sends, (tokens, gain, ids, sems) = rest[:-4], rest[-4:]
+def route_kernel(sizes, width, tokens_hbm, gain_hbm, ids_hbm, own, *rest):
+    exp_count, groups = sizes
+    sends, (tokens, normed, gain, ids, sems) = rest[:-5], rest[-5:]
     pairs = ((tokens_hbm, tokens), (gain_hbm, gain), (ids_hbm, ids))
     copies = [pltpu.make_async_copy(a, b, sems.at[n]) for n, (a, b) in enumerate(pairs)]
     for copy in copies:
@@ -177,32 +175,77 @@
         inv_rms = lax.rsqrt(mean + EPSILON)
         normed[first : first + step, :] = (values * inv_rms * gain[...]).astype(BF16)
     named, before = count_earlier(ids, group_experts(exp_count, groups, z, g, rows))
-    picks = [pick_rows(named, before, d) for d in range(1, exp_count)]
-    others = jnp.concatenate(picks, axis=0).astype(BF16)
+    picks = [pick_rows(named, before, d) for d in range(exp_count)]
+    others = jnp.concatenate(picks[1:], axis=0).astype(BF16)
     start = pl.multiple_of(s * (features // 2), 128)
     found = jnp.dot(others, normed[:, pl.ds(start, width)], preferred_element_type=F32)
     for d, send in enumerate(sends):
         send[...] = found[d * CAP : (d + 1) * CAP, :].astype(BF16)
-
-
-def prepare_kernel(
-    sizes, normed, ids, weights, active, gate, up, own, combine_high, combine_low, mask, *rest
-):
-    exp_count, groups = sizes
-    rows, features = normed.shape
+    own[...] = jnp.dot(
+        picks[0].astype(BF16), normed[...], preferred_element_type=F32
+    ).astype(BF16)
+
+
+def fetch_rows(weight, piece, buffer, sem):
+    def start(index, carry):
+        line = piece * K_BLOCKS + lax.rem(index, K_BLOCKS)
+        column = index // K_BLOCKS
+        pltpu.make_async_copy(
+            weight.at[
+                pl.ds(pl.multiple_of(line * BLOCK, BLOCK), BLOCK),
+                pl.ds(pl.multiple_of(column * BLOCK, BLOCK), BLOCK),
+            ],
+            buffer.at[index],
+            sem,
+        ).start()
+        return carry
+
+    lax.fori_loop(0, buffer.shape[0], start, 0)
+
+
+def fetch_columns(sizes, down, chunk, keep, buffer, sem):
+    exp_count, groups = sizes
     z, g, s = place(sizes)
-    copies = []
-    *nears, sems = rest
-    for n, near in enumerate(nears):
-        source, piece = (gate, n) if n < GATE_NEAR else (up, n - GATE_NEAR)
-        lines = pl.ds(piece * NEAR_ROWS, NEAR_ROWS)
-        copies.append(pltpu.make_async_copy(source.at[lines, :], near, sems.at[n]))
+    side = s if keep else 1 - s
+    part = down.shape[1] // (2 * groups)
+    lines = down.shape[0] // BLOCK
+
+    def start(index, carry):
+        group = lax.rem(g + index // lines, groups)
+        column = (group * 2 + side) * part + chunk * BLOCK
+        pltpu.make_async_copy(
+            down.at[
+                pl.ds(pl.multiple_of(lax.rem(index, lines) * BLOCK, BLOCK), BLOCK),
+                pl.ds(pl.multiple_of(column, BLOCK), BLOCK),
+            ],
+            buffer.at[index],
+            sem,
+        ).start()
+        return carry
+
+    lax.fori_loop(0, buffer.shape[0], start, 0)
+
+
+def await_all(buffer, sem):
+    pltpu.make_async_copy(buffer, buffer, sem).wait()
+
+
+def stacked(buffer, column, count):
+    blocks = buffer[column * count : (column + 1) * count]
+    return blocks.reshape(count * BLOCK, BLOCK)
+
+
+def table_kernel(sizes, ids_hbm, weights_hbm, after, combine_high, combine_low, ids, weights, sems):
+    exp_count, groups = sizes
+    pairs = ((ids_hbm, ids), (weights_hbm, weights))
+    copies = [pltpu.make_async_copy(a, b, sems.at[n]) for n, (a, b) in enumerate(pairs)]
     for copy in copies:
         copy.start()
+    for copy in copies:
+        copy.wait()
+    rows = ids.shape[1]
+    z, g, s = place(sizes)
     named, before = count_earlier(ids, group_experts(exp_count, groups, z, g, rows))
-    own[...] = jnp.dot(
-        pick_rows(named, before, 0).astype(BF16), normed[...], preferred_element_type=F32
-    ).astype(BF16)
     zero = jnp.zeros((CAP, rows), F32)
     parts = []
     for d in range(exp_count):
@@ -218,6 +261,17 @@
     high = table.astype(BF16)
     combine_high[...] = high
     combine_low[...] = (table - high.astype(F32)).astype(BF16)
+
+
+def prepare_kernel(sizes, rows, active_hbm, gate, after, mask, *rest):
+    exp_count, groups = sizes
+    *buffers, active, small_sem, sems = rest
+    z, g, s = place(sizes)
+    small = pltpu.make_async_copy(active_hbm, active, small_sem)
+    small.start()
+    for n, buffer in enumerate(buffers[:READY]):
+        fetch_rows(gate, n, buffer, sems.at[n])
+    small.wait()
     unit_width = mask.shape[1]
     blocks = lax.broadcasted_iota(jnp.int32, mask.shape, 1) // BLK + s * (unit_width // BLK)
     source = lax.broadcasted_iota(jnp.int32, (mask.shape[0], 1), 0)
@@ -231,8 +285,8 @@
         return jnp.where(blocks == entry, 1.0, found)
 
     mask[...] = lax.fori_loop(0, active.shape[2], add_entry, jnp.zeros(mask.shape, F32))
-    for copy in copies:
-        copy.wait()
+    for n, buffer in enumerate(buffers[:READY]):
+        await_all(buffer, sems.at[n])
 
 
 def join_kernel(after, *refs):
@@ -244,112 +298,77 @@
     exp_count, groups = sizes
     z, g, s = place(sizes)
     refs = list(refs)
-    gate_near = [refs.pop(0) for _ in range(GATE_NEAR)]
-    up_near = [refs.pop(0) for _ in range(UP_NEAR)]
-    up, mask, hidden, gate_sum, up_sum, rows, slabs, sems = refs
+    refs = refs[BUFFERS:]
+    up, down, mask, hidden = [refs.pop(0) for _ in range(4)]
+    buffers = [refs.pop(0) for _ in range(BUFFERS)]
+    gate_sum, up_sum, rows, sems = refs
     half = own.shape[1] // 2
-    near, features = UP_NEAR * NEAR_ROWS, up.shape[0]
-    unit_width = up.shape[1]
-    far_count = (features - near) // K_SLAB
-
-    def copy(index):
-        slot = index % K_DEPTH
-        return pltpu.make_async_copy(
-            up.at[pl.ds(near + index * K_SLAB, K_SLAB), :], slabs.at[slot], sems.at[slot]
-        )
-
-    for n in range(min(K_DEPTH, far_count)):
-        copy(n).start()
+    features, unit_width = up.shape
+    columns = unit_width // BLOCK
+    pieces = features // (K_BLOCKS * BLOCK)
+    count = len(buffers)
+
+    def fetch(piece):
+        buffer, sem = buffers[piece % count], sems.at[piece % count]
+        if piece < 2 * pieces:
+            fetch_rows(up, piece - pieces, buffer, sem)
+        elif piece < 2 * pieces + OUT_CHUNKS:
+            fetch_columns(sizes, down, piece - 2 * pieces, False, buffer, sem)
+
+    for piece in range(READY, count):
+        fetch(piece)
     for source, side in ((mine, s), (other, 1 - s)):
         cols = pl.ds(pl.multiple_of(side * half, 128), half)
-        pieces = [own[:, cols].astype(F32), source[...].astype(F32)]
-        rows[:, cols] = jnp.concatenate(pieces, axis=0).astype(BF16)
-
-    def each_tile(body):
-        def step(n, carry):
-            body(pl.ds(pl.multiple_of(n * N_TILE, N_TILE), N_TILE))
-            return carry
-
-        lax.fori_loop(0, unit_width // N_TILE, step, 0)
-
-    def product(nears, cols):
-        value = None
-        for n, near in enumerate(nears):
-            lines = slice(n * NEAR_ROWS, (n + 1) * NEAR_ROWS)
-            term = jnp.dot(rows[:, lines], near[:, cols], preferred_element_type=F32)
-            value = term if value is None else value + term
-        return value
-
-    def gate_tile(cols):
-        gate_sum[:, cols] = jnp.maximum(product(gate_near, cols), 0.0)
-
-    def near_tile(cols):
-        up_sum[:, cols] = product(up_near, cols)
-
-    each_tile(gate_tile)
-    each_tile(near_tile)
-    for n in range(far_count):
-        copy(n).wait()
-        left = slice(near + n * K_SLAB, near + (n + 1) * K_SLAB)
-
-        def far_tile(cols):
-            value = up_sum[:, cols] + jnp.dot(
-                rows[:, left], slabs[n % K_DEPTH, :, cols], preferred_element_type=F32
-            )
-            if n < far_count - 1:
-                up_sum[:, cols] = value
-                return
-            value = gate_sum[:, cols] * jnp.maximum(value, 0.0)
+        joined = [own[:, cols].astype(F32), source[...].astype(F32)]
+        rows[:, cols] = jnp.concatenate(joined, axis=0).astype(BF16)
+    for piece in range(2 * pieces):
+        buffer = buffers[piece % count]
+        if piece >= READY:
+            await_all(buffer, sems.at[piece % count])
+        step = piece % pieces
+        total = gate_sum if piece < pieces else up_sum
+        left = rows[:, step * K_BLOCKS * BLOCK : (step + 1) * K_BLOCKS * BLOCK]
+        for column in range(columns):
+            cols = slice(column * BLOCK, (column + 1) * BLOCK)
+            value = jnp.dot(left, stacked(buffer, column, K_BLOCKS), preferred_element_type=F32)
+            if step > 0:
+                value = total[:, cols] + value
+            if piece < 2 * pieces - 1:
+                total[:, cols] = value
+                continue
+            value = jnp.maximum(gate_sum[:, cols], 0.0) * jnp.maximum(value, 0.0)
             parts = []
             for d in range(exp_count):
                 parts.append(value[d * CAP : (d + 1) * CAP, :] * mask[d : d + 1, cols])
             hidden[:, cols] = jnp.concatenate(parts, axis=0).astype(BF16)
-
-        each_tile(far_tile)
-        if n + K_DEPTH < far_count:
-            copy(n + K_DEPTH).start()
-
-
-def output_kernel(sizes, chunk, width, keep, *refs):
-    exp_count, groups = sizes
-    z, g, s = place(sizes)
-    refs = list(refs)
-    hidden, down = refs.pop(0), refs.pop(0)
-    received = refs.pop(0) if keep else None
-    total_sum, slabs, sems = refs[-3:]
-    outs = refs[:-3]
-    side = s if keep else 1 - s
-    part = down.shape[1] // (2 * groups)
-    pieces = down.shape[0] // N_ROWS
-
-    def copy(index):
-        group = lax.rem(g + index // pieces, groups)
-        column = pl.multiple_of((group * 2 + side) * part + chunk * width, 128)
-        lines = pl.ds(index % pieces * N_ROWS, N_ROWS)
-        return pltpu.make_async_copy(
-            down.at[lines, pl.ds(column, width)], slabs.at[index], sems.at[index]
+        fetch(piece + count)
+    for piece in range(2 * pieces, 2 * pieces + OUT_CHUNKS):
+        await_all(buffers[piece % count], sems.at[piece % count])
+
+
+def give_kernel(sizes, chunk, hidden, weights, down, given, kept_weights, sem):
+    exp_count, groups = sizes
+    fetch_columns(sizes, down, chunk, True, kept_weights, sem)
+    lines = down.shape[0] // BLOCK
+    for offset in range(groups):
+        value = jnp.dot(
+            hidden[...], stacked(weights, offset, lines), preferred_element_type=F32
         )
-
-    for index in range(groups * pieces):
-        copy(index).start()
+        given[:, offset * BLOCK : (offset + 1) * BLOCK] = value.astype(BF16)
+    await_all(kept_weights, sem)
+
+
+def keep_kernel(sizes, hidden, weights, received, *outs):
+    exp_count, groups = sizes
+    lines = hidden.shape[1] // BLOCK
     for offset in range(groups):
-        for piece in range(pieces):
-            index = offset * pieces + piece
-            copy(index).wait()
-            value = jnp.dot(
-                hidden[:, piece * N_ROWS : (piece + 1) * N_ROWS],
-                slabs[index],
-                preferred_element_type=F32,
-            )
-            total_sum[...] = value if piece == 0 else total_sum[...] + value
-        cols = slice(offset * width, (offset + 1) * width)
-        if keep:
-            for d in range(exp_count):
-                lines = slice(d * CAP, (d + 1) * CAP)
-                value = total_sum[lines, :] + received[:, cols].astype(F32)[lines, :]
-                outs[d][:, cols] = value.astype(BF16)
-        else:
-            outs[0][:, cols] = total_sum[...].astype(BF16)
+        cols = slice(offset * BLOCK, (offset + 1) * BLOCK)
+        value = jnp.dot(
+            hidden[...], stacked(weights, offset, lines), preferred_element_type=F32
+        )
+        value = value + received[:, cols].astype(F32)
+        for d in range(exp_count):
+            outs[d][:, cols] = value[d * CAP : (d + 1) * CAP, :].astype(BF16)
 
 
 def combine_kernel(exp_count, high, low, *refs):
@@ -377,7 +396,7 @@
         out[:, chunk * width : (chunk + 1) * width] = value.astype(BF16)
 
 
-def call(kernel, outs, ins, scratch=(), flops=0, moved=0, limit=16):
+def call(kernel, outs, ins, scratch=(), flops=0, moved=0, aliases=None):
     vmem = pl.BlockSpec(memory_space=pltpu.VMEM)
     arrays, specs = [], []
     for array, space in ins:
@@ -394,7 +413,8 @@
         in_specs=specs,
         out_specs=[vmem] * len(outs),
         scratch_shapes=list(scratch),
-        compiler_params=pltpu.CompilerParams(vmem_limit_bytes=limit << 20),
+        input_output_aliases=aliases or {},
+        compiler_params=pltpu.CompilerParams(vmem_limit_bytes=LIMIT << 20),
         cost_estimate=pl.CostEstimate(flops=flops, bytes_accessed=moved, transcendentals=0),
     )(*arrays)
 
@@ -426,9 +446,9 @@
         return lax.ppermute(value, "unit", [(u, u ^ 1) for u in range(unit_count)])
 
     batch = exp_count - 1
-    normed, *sends = call(
+    own, *sends = call(
         functools.partial(route_kernel, sizes, width),
-        [((tok_count, features), BF16)] + [((CAP, width), BF16)] * batch,
+        [((CAP, features), BF16)] + [((CAP, width), BF16)] * batch,
         [
             (tokens, pltpu.HBM),
             (norm_gain.reshape(1, -1), pltpu.HBM),
@@ -436,6 +456,7 @@
         ],
         [
             pltpu.VMEM((tok_count, features), BF16),
+            pltpu.VMEM((tok_count, features), BF16),
             pltpu.VMEM((1, features), F32),
             pltpu.VMEM(ids.shape, jnp.int32),
             pltpu.SemaphoreType.DMA((3,)),
@@ -443,28 +464,20 @@
         flops=2 * tok_count * slots * width,
         moved=4 * tok_count * features,
     )
-    padded = -(-slots // 128) * 128
-    own, combine_high, combine_low, mask, *nears = call(
-        functools.partial(prepare_kernel, sizes),
+    blocks = K_BLOCKS * unit_width // BLOCK
+    buffer = ((blocks, BLOCK, BLOCK), BF16, pltpu.VMEM)
+    piece_bytes = 2 * blocks * BLOCK * BLOCK
+    mask, *ready = call(
+        functools.partial(prepare_kernel, sizes, tok_count),
+        [((max(8, exp_count), unit_width), F32)] + [buffer] * BUFFERS,
+        [(active_blocks, pltpu.HBM), (gate_weight, pltpu.HBM), (own, pl.ANY)],
         [
-            ((CAP, features), BF16),
-            ((tok_count, padded), BF16),
-            ((tok_count, padded), BF16),
-            ((max(8, exp_count), unit_width), F32),
-        ]
-        + [((NEAR_ROWS, unit_width), BF16, pltpu.VMEM)] * (GATE_NEAR + UP_NEAR),
-        [
-            (normed, None),
-            (ids, None),
-            (weights, None),
-            (active_blocks, pltpu.SMEM),
-            (gate_weight, pltpu.HBM),
-            (up_weight, pltpu.HBM),
+            pltpu.SMEM(active_blocks.shape, jnp.int32),
+            pltpu.SemaphoreType.DMA,
+            pltpu.SemaphoreType.DMA((READY,)),
         ],
-        [pltpu.SemaphoreType.DMA((GATE_NEAR + UP_NEAR,))],
         flops=2 * tok_count * slots * features,
-        moved=2 * (GATE_NEAR + UP_NEAR) * NEAR_ROWS * unit_width,
-        limit=16,
+        moved=READY * piece_bytes,
     )
     arrived = [shift(value, d + 1) for d, value in enumerate(sends)]
     mine = call(
@@ -474,49 +487,64 @@
         moved=1 << 20,
     )[0]
     other = swap(mine)
-    acc = ((slots, unit_width), F32)
-    hidden = call(
+    padded = -(-slots // 128) * 128
+    combine_high, combine_low = call(
+        functools.partial(table_kernel, sizes),
+        [((tok_count, padded), BF16)] * 2,
+        [(ids, pltpu.HBM), (weights, pltpu.HBM), (mine, pl.ANY)],
+        [
+            pltpu.VMEM(ids.shape, jnp.int32),
+            pltpu.VMEM(weights.shape, F32),
+            pltpu.SemaphoreType.DMA((2,)),
+        ],
+        moved=1 << 21,
+    )
+    acc = pltpu.VMEM((slots, unit_width), F32)
+    hidden, *buffers = call(
         functools.partial(hidden_kernel, sizes),
-        [((slots, unit_width), BF16)],
+        [((slots, unit_width), BF16)] + [buffer] * BUFFERS,
         [(own, None), (mine, None), (other, None)]
-        + [(v, pltpu.VMEM) for v in nears]
-        + [(up_weight, pltpu.HBM), (mask, None)],
+        + [(v, pltpu.VMEM) for v in ready]
+        + [(up_weight, pltpu.HBM), (down_weight, pltpu.HBM), (mask, None)],
         [
-            pltpu.VMEM(*acc),
-            pltpu.VMEM(*acc),
+            acc,
+            acc,
             pltpu.VMEM((slots, features), BF16),
-            pltpu.VMEM((K_DEPTH, K_SLAB, unit_width), BF16),
-            pltpu.SemaphoreType.DMA((K_DEPTH,)),
+            pltpu.SemaphoreType.DMA((BUFFERS,)),
         ],
         flops=2 * 2 * slots * features * unit_width,
-        moved=2 * features * unit_width * 2,
-        limit=16,
-    )[0]
+        moved=6 * piece_bytes,
+        aliases={3 + n: 1 + n for n in range(BUFFERS)},
+    )
+    first = 2 * features // (K_BLOCKS * BLOCK)
     part = features // unit_count
-    out_width = part // OUT_CHUNKS
-
-    def output(chunk, keep, received):
-        pieces = groups * (unit_width // N_ROWS)
-        return call(
-            functools.partial(output_kernel, sizes, chunk, out_width, keep),
-            [((CAP, groups * out_width), BF16)] * exp_count
-            if keep
-            else [((slots, groups * out_width), BF16)],
-            [(hidden, None), (down_weight, pltpu.HBM)] + [(v, None) for v in received],
+    out_width = BLOCK
+    given, kept_weights = [], []
+    for chunk in range(OUT_CHUNKS):
+        value, kept = call(
+            functools.partial(give_kernel, sizes, chunk),
+            [((slots, groups * BLOCK), BF16), buffer],
             [
-                pltpu.VMEM((slots, out_width), F32),
-                pltpu.VMEM((pieces, N_ROWS, out_width), BF16),
-                pltpu.SemaphoreType.DMA((pieces,)),
+                (hidden, None),
+                (buffers[(first + chunk) % BUFFERS], pltpu.VMEM),
+                (down_weight, pltpu.HBM),
             ],
-            flops=2 * slots * unit_width * groups * out_width,
-            moved=2 * unit_width * groups * out_width,
+            [pltpu.SemaphoreType.DMA],
+            flops=2 * slots * unit_width * groups * BLOCK,
+            moved=piece_bytes,
         )
-
-    given = [output(chunk, False, ())[0] for chunk in range(OUT_CHUNKS)]
+        given.append(value)
+        kept_weights.append(kept)
     taken = [swap(value) for value in given]
     last = []
     for chunk in range(OUT_CHUNKS):
-        kept = output(chunk, True, [taken[chunk]])
+        kept = call(
+            functools.partial(keep_kernel, sizes),
+            [((CAP, groups * BLOCK), BF16)] * exp_count,
+            [(hidden, None), (kept_weights[chunk], pltpu.VMEM), (taken[chunk], None)],
+            flops=2 * slots * unit_width * groups * BLOCK,
+            moved=piece_bytes,
+        )
         home = [kept[0]] + [shift(kept[d], -d) for d in range(1, exp_count)]
         stay, *gives = call(
             functools.partial(combine_kernel, exp_count),
@@ -543,6 +571,9 @@
         and unit_count % 2 == 0
         and exp_count * unit_count // 2 == EXPERTS
         and TILE % tokens.shape[0] == 0
+        and unit_width % BLOCK == 0
+        and tokens.shape[1] == unit_count * OUT_CHUNKS * BLOCK == READY * K_BLOCKS * BLOCK
+        and unit_count // 2 == K_BLOCKS
     )
     return (paired_experts if paired else spread_experts)(*operands)
 

time: 79.7 us -> 70.1 us (0.88)
  Pallas kernels: 49.2 us -> 37.4 us
  starting transfers between devices: 17.9 us -> 20.5 us
  local copies, waits for them, and re-layouts: 2.05 us -> 0 us
  waiting for transfers between devices: 9.98 us -> 11.9 us
    pallas_call x11 -> x12, Pallas kernels: 49.2 us -> 37.4 us  [call(): pl.pallas_call(kernel, out_shape=shapes, in_specs=specs, out_specs=[vmem]...]
    ppermute x11, starting transfers between devices: 17.2 us -> 19.8 us  [shift(): return lax.ppermute(value, ('exp', 'unit'), pairs)]
    unnamed x6 -> x0, local copies, waits for them, and re-layouts: 2.05 us -> none
    ppermute x11, waiting for transfers between devices: 8.12 us -> 10 us  [shift(): return lax.ppermute(value, ('exp', 'unit'), pairs)]
  transfers between devices with their start and end apart: 14 -> 14, of which waited for: 4 -> 4; matrix products, arithmetic and copies ran while one was open for 0% -> 0% of each run, Pallas kernels for 30% -> 25%
where the time goes in v5:
time: 70.1 us; the launch traced here: 69.9 us
  Pallas kernels  37.4 us (53%)
  starting transfers between devices  20.5 us (29%)
  waiting for transfers between devices  11.9 us (17%)
    pallas_call x12, Pallas kernels, call(): pl.pallas_call(kernel, out_shape=shapes, in_specs=specs, out_specs=[vmem]...  37.4 us
    ppermute x11, starting transfers between devices, shift(): return lax.ppermute(value, ('exp', 'unit'), pairs)  19.8 us
    ppermute x11, waiting for transfers between devices, shift(): return lax.ppermute(value, ('exp', 'unit'), pairs)  10 us
    ppermute x3, waiting for transfers between devices, swap(): return lax.ppermute(value, 'unit', [(u, u ^ 1) for u in range(unit_count)])  1.86 us
  transfers between devices with their start and end apart: 14, of which 4 were waited for; matrix products, arithmetic and copies ran while one was open for 0% of the time, Pallas kernels for 25%

profile of v5, /device:TPU:0, one launch (start us, length us, event | category | flops | bytes accessed | tf_op | source)
XLA Modules:
  0.0 69.9 jit_solution(7604073818240414536)
XLA Ops:
  0.0 2.2 %shard_map.82 = (bf16[40,4096]{1,0:T(8,128)(2,1)S(1)}, bf16[40,2048]{1,0:T(8,128)(2,1)S(1)}, bf16[40,2048]{1,0:T(8,128)(2,1)S(1)}, bf16[40,2048]{1,0:T(8,128)(2,1)S(1)}) custom-call(bf16[128,4096]{1,0:T(8,128)(2,1)} %tokens_hbm.1, f32[1,4096]{1,0:T(1,128)} %bitcast.3, s32[2,128]{1,0:T(2,128)} %bitcast.4), custom_call_target="tpu_custom_call" | custom-call | flops 83886080 | bytes 2097152 | tf_op jit(solution)/shard_map/pallas_call | solution.py:410
  2.2 3.1 %collective-permute-start = (bf16[40,2048]{1,0:T(8,128)(2,1)S(1)}, bf16[40,2048]{1,0:T(8,128)(2,1)S(1)}, u32[]{:S(2)}, u32[]{:S(2)}) collective-permute-start(bf16[40,2048]{1,0:T(8,128)(2,1)S(1)} %get-tuple-element.38), channel_id=1, source_target_pairs={{0,4},{1,5},{2,6},{3,7},{4,8},{5,9},{6,10},{7,11},{8,12},{9,13},{1... | collective-permute-start | bytes 491528 | tf_op jit(solution)/shard_map/ppermute | solution.py:443
  5.2 2.6 %collective-permute-start.1 = (bf16[40,2048]{1,0:T(8,128)(2,1)S(1)}, bf16[40,2048]{1,0:T(8,128)(2,1)S(1)}, u32[]{:S(2)}, u32[]{:S(2)}) collective-permute-start(bf16[40,2048]{1,0:T(8,128)(2,1)S(1)} %get-tuple-element.39), channel_id=1, source_target_pairs={{0,8},{1,9},{2,10},{3,11},{4,12},{5,13},{6,14},{7,15},{8,0},{9,1},... | collective-permute-start | bytes 491528 | tf_op jit(solution)/shard_map/ppermute | solution.py:443
  7.8 1.3 %collective-permute-start.2 = (bf16[40,2048]{1,0:T(8,128)(2,1)S(1)}, bf16[40,2048]{1,0:T(8,128)(2,1)S(1)}, u32[]{:S(2)}, u32[]{:S(2)}) collective-permute-start(bf16[40,2048]{1,0:T(8,128)(2,1)S(1)} %get-tuple-element.40), channel_id=1, source_target_pairs={{0,12},{1,13},{2,14},{3,15},{4,0},{5,1},{6,2},{7,3},{8,4},{9,5},{1... | collective-permute-start | bytes 491528 | tf_op jit(solution)/shard_map/ppermute | solution.py:443
  9.2 9.7 %shard_map.83 = (f32[8,3584]{1,0:T(8,128)S(1)}, bf16[14,512,512]{2,1,0:T(8,128)(2,1)S(1)}, bf16[14,512,512]{2,1,0:T(8,128)(2,1)S(1)}, bf16[14,512,512]{2,1,0:T(8...) custom-call(s32[2,8,48]{2,1,0:T(8,128)} %active_hbm.1, bf16[4096,3584]{1,0:T(8,128)(2,1)} %gate.1, ...), custom_call_target="tpu_custom_call" | custom-call | flops 167772160 | bytes 29360128 | tf_op jit(solution)/shard_map/pallas_call | solution.py:410
  18.9 0.0 collective-permute-done.refs_0_
  18.9 0.0 collective-permute-done.1.refs_1_
  18.9 0.0 collective-permute-done.2.refs_2_
  19.0 0.1 collective-permute-start.3
  19.1 1.9 %collective-permute-done.3.other = bf16[120,2048]{1,0:T(8,128)(2,1)S(1)} collective-permute-done((bf16[120,2048]{1,0:T(8,128)(2,1)S(1)}, bf16[120,2048]{1,0:T(8,128)(2,1)S(1)}, u32[]{:S(2)}, u32[]{:S(2)}) %collective-permute-start.3) | collective-permute-done | bytes 491552 | tf_op jit(solution)/shard_map/ppermute | solution.py:446
  20.9 14.1 %shard_map.86 = (bf16[160,3584]{1,0:T(8,128)(2,1)S(1)}, bf16[14,512,512]{2,1,0:T(8,128)(2,1)S(1)}, bf16[14,512,512]{2,1,0:T(8,128)(2,1)S(1)}, bf16[14,512,512]{2...) custom-call(bf16[40,4096]{1,0:T(8,128)(2,1)S(1)} %get-tuple-element., ...), custom_call_target="tpu_custom_call", output_to_operand_aliasing={{1}: (3, {}), {2}: (4, {}), {3}: (5, {}), {4}: (6, {}), {5}... | custom-call | flops 9395240960 | bytes 44040192 | tf_op jit(solution)/shard_map/pallas_call | solution.py:410
  35.0 3.2 %shard_map.90 = (bf16[160,1024]{1,0:T(8,128)(2,1)S(1)}, bf16[14,512,512]{2,1,0:T(8,128)(2,1)S(1)}) custom-call(bf16[160,3584]{1,0:T(8,128)(2,1)S(1)} %get-tuple-element.48.hidden, bf16[14,512,512]{2,1,0:T(8,128)(2,1)S(1)} %get-tuple-element.58.weights, bf16[3584,4096]{1,0:T(8,128)(2,1)} %down.3), custom_call_target="tpu_custom_call" | custom-call | flops 1174405120 | bytes 7340032 | tf_op jit(solution)/shard_map/pallas_call | solution.py:410
  38.2 0.2 collective-permute-start.9
  38.5 3.2 %shard_map.87 = (bf16[160,1024]{1,0:T(8,128)(2,1)S(1)}, bf16[14,512,512]{2,1,0:T(8,128)(2,1)S(1)}) custom-call(bf16[160,3584]{1,0:T(8,128)(2,1)S(1)} %get-tuple-element.48.hidden, bf16[14,512,512]{2,1,0:T(8,128)(2,1)S(1)} %get-tuple-element.49.weights, bf16[3584,4096]{1,0:T(8,128)(2,1)} %down.3), custom_call_target="tpu_custom_call" | custom-call | flops 1174405120 | bytes 7340032 | tf_op jit(solution)/shard_map/pallas_call | solution.py:410
  41.6 0.4 collective-permute-start.4
  42.0 0.0 collective-permute-done.9.received
  42.0 1.4 %shard_map.91 = (bf16[40,1024]{1,0:T(8,128)(2,1)S(1)}, bf16[40,1024]{1,0:T(8,128)(2,1)S(1)}, bf16[40,1024]{1,0:T(8,128)(2,1)S(1)}, bf16[40,1024]{1,0:T(8,128)(2,1)S(1)}) custom-call(bf16[160,3584]{1,0:T(8,128)(2,1)S(1)} %get-tuple-element.48.hidden, bf16[14,512,512]{2,1,0:T(8,128)(2,1)S(1)} %get-tuple-element.59.weights, ...), custom_call_target="tpu_custom_call" | custom-call | flops 1174405120 | bytes 7340032 | tf_op jit(solution)/shard_map/pallas_call | solution.py:410
  43.4 4.7 %collective-permute-start.10 = (bf16[40,1024]{1,0:T(8,128)(2,1)S(1)}, bf16[40,1024]{1,0:T(8,128)(2,1)S(1)}, u32[]{:S(2)}, u32[]{:S(2)}) collective-permute-start(bf16[40,1024]{1,0:T(8,128)(2,1)S(1)} %get-tuple-element.62), channel_id=1, source_target_pairs={{0,12},{1,13},{2,14},{3,15},{4,0},{5,1},{6,2},{7,3},{8,4},{9,5},{1... | collective-permute-start | bytes 245768 | tf_op jit(solution)/shard_map/ppermute | solution.py:443
  48.1 0.4 collective-permute-start.11
  48.5 0.2 collective-permute-start.12
  48.8 0.0 collective-permute-done.4.received
  48.8 1.4 %shard_map.88 = (bf16[40,1024]{1,0:T(8,128)(2,1)S(1)}, bf16[40,1024]{1,0:T(8,128)(2,1)S(1)}, bf16[40,1024]{1,0:T(8,128)(2,1)S(1)}, bf16[40,1024]{1,0:T(8,128)(2,1)S(1)}) custom-call(bf16[160,3584]{1,0:T(8,128)(2,1)S(1)} %get-tuple-element.48.hidden, bf16[14,512,512]{2,1,0:T(8,128)(2,1)S(1)} %get-tuple-element.50.weights, ...), custom_call_target="tpu_custom_call" | custom-call | flops 1174405120 | bytes 7340032 | tf_op jit(solution)/shard_map/pallas_call | solution.py:410
  50.1 3.6 %collective-permute-start.5 = (bf16[40,1024]{1,0:T(8,128)(2,1)S(1)}, bf16[40,1024]{1,0:T(8,128)(2,1)S(1)}, u32[]{:S(2)}, u32[]{:S(2)}) collective-permute-start(bf16[40,1024]{1,0:T(8,128)(2,1)S(1)} %get-tuple-element.53), channel_id=1, source_target_pairs={{0,12},{1,13},{2,14},{3,15},{4,0},{5,1},{6,2},{7,3},{8,4},{9,5},{1... | collective-permute-start | bytes 245768 | tf_op jit(solution)/shard_map/ppermute | solution.py:443
  53.8 0.7 %collective-permute-start.6 = (bf16[40,1024]{1,0:T(8,128)(2,1)S(1)}, bf16[40,1024]{1,0:T(8,128)(2,1)S(1)}, u32[]{:S(2)}, u32[]{:S(2)}) collective-permute-start(bf16[40,1024]{1,0:T(8,128)(2,1)S(1)} %get-tuple-element.54), channel_id=1, source_target_pairs={{0,8},{1,9},{2,10},{3,11},{4,12},{5,13},{6,14},{7,15},{8,0},{9,1},... | collective-permute-start | bytes 245768 | tf_op jit(solution)/shard_map/ppermute | solution.py:443
  54.5 0.0 collective-permute-done.10.refs_1_
  54.5 0.0 collective-permute-start.7
  54.5 1.0 %shard_map.85 = (bf16[128,256]{1,0:T(8,128)(2,1)S(1)}, bf16[128,256]{1,0:T(8,128)(2,1)S(1)}) custom-call(s32[2,128]{1,0:T(2,128)} %bitcast.5, f32[2,128]{1,0:T(2,128)} %bitcast.6, bf16[120,2048]{1,0:T(8,128)(2,1)S(1)} %shard_map.84.after.mine), custom_call_target="tpu_custom_call" | custom-call | bytes 2097152 | tf_op jit(solution)/shard_map/pallas_call | solution.py:410
  55.5 1.3 %collective-permute-done.11.refs_2_ = bf16[40,1024]{1,0:T(8,128)(2,1)S(1)} collective-permute-done((bf16[40,1024]{1,0:T(8,128)(2,1)S(1)}, bf16[40,1024]{1,0:T(8,128)(2,1)S(1)}, u32[]{:S(2)}, u32[]{:S(2)}) %collective-permute-start.11) | collective-permute-done | bytes 81952 | tf_op jit(solution)/shard_map/ppermute | solution.py:443
  56.7 0.0 collective-permute-done.12.refs_3_
  56.7 0.3 shard_map.92
  57.1 1.5 %collective-permute-start.13 = (bf16[128,512]{1,0:T(8,128)(2,1)S(1)}, bf16[128,512]{1,0:T(8,128)(2,1)S(1)}, u32[]{:S(2)}, u32[]{:S(2)}) collective-permute-start(bf16[128,512]{1,0:T(8,128)(2,1)S(1)} %get-tuple-element.66), channel_id=1, source_target_pairs={{0,2},{1,3},{2,0},{3,1},{4,6},{5,7},{6,4},{7,5},{8,10},{9,11},{10,... | collective-permute-start | bytes 393224 | tf_op jit(solution)/shard_map/ppermute | solution.py:443
  58.6 0.0 collective-permute-done.5.refs_1_
  58.6 4.7 %collective-permute-done.6.refs_2_ = bf16[40,1024]{1,0:T(8,128)(2,1)S(1)} collective-permute-done((bf16[40,1024]{1,0:T(8,128)(2,1)S(1)}, bf16[40,1024]{1,0:T(8,128)(2,1)S(1)}, u32[]{:S(2)}, u32[]{:S(2)}) %collective-permute-start.6) | collective-permute-done | bytes 81952 | tf_op jit(solution)/shard_map/ppermute | solution.py:443
  63.3 0.0 collective-permute-done.7.refs_3_
  63.3 0.3 shard_map.89
  63.6 1.6 %collective-permute-start.8 = (bf16[128,512]{1,0:T(8,128)(2,1)S(1)}, bf16[128,512]{1,0:T(8,128)(2,1)S(1)}, u32[]{:S(2)}, u32[]{:S(2)}) collective-permute-start(bf16[128,512]{1,0:T(8,128)(2,1)S(1)} %get-tuple-element.57), channel_id=1, source_target_pairs={{0,2},{1,3},{2,0},{3,1},{4,6},{5,7},{6,4},{7,5},{8,10},{9,11},{10,... | collective-permute-start | bytes 393224 | tf_op jit(solution)/shard_map/ppermute | solution.py:443
  65.1 0.0 collective-permute-done.13.refs_3_
  65.1 4.0 %collective-permute-done.8.refs_1_ = bf16[128,512]{1,0:T(8,128)(2,1)S(1)} collective-permute-done((bf16[128,512]{1,0:T(8,128)(2,1)S(1)}, bf16[128,512]{1,0:T(8,128)(2,1)S(1)}, u32[]{:S(2)}, u32[]{:S(2)}) %collective-permute-start.8) | collective-permute-done | bytes 131104 | tf_op jit(solution)/shard_map/ppermute | solution.py:443
  69.2 0.7 %shard_map.93 = bf16[128,1024]{1,0:T(8,128)(2,1)} custom-call(f32[128,512]{1,0:T(8,128)S(1)} %get-tuple-element.56.refs_0_, bf16[128,512]{1,0:T(8,128)(2,1)S(1)} %collective-permute-done.8.refs_1_, f32[128,512]{1,0:T(8,128)S(1)} %get-tuple-element.65.refs_2_, bf16[128,512]{1,0:T(8,128)(2,1)S(1)} %collective-permute-done.13.refs_3_), custom_call_target="tpu_custom_call" | custom-call | bytes 1048576 | tf_op jit(solution)/shard_map/pallas_call | solution.py:410
  (1 shorter events, 0.0 us)
Async XLA Ops:
  2.2 16.8 %collective-permute-start = (bf16[40,2048]{1,0:T(8,128)(2,1)S(1)}, bf16[40,2048]{1,0:T(8,128)(2,1)S(1)}, u32[]{:S(2)}, u32[]{:S(2)}) collective-permute-start(bf16[40,2048]{1,0:T(8,128)(2,1)S(1)} %get-tuple-element.38), channel_id=1, source_target_pairs={{0,4},{1,5},{2,6},{3,7},{4,8},{5,9},{6,10},{7,11},{8,12},{9,13},{1... | collective-permute-start | bytes 491528 | tf_op jit(solution)/shard_map/ppermute | solution.py:443
  5.2 13.7 %collective-permute-start.1 = (bf16[40,2048]{1,0:T(8,128)(2,1)S(1)}, bf16[40,2048]{1,0:T(8,128)(2,1)S(1)}, u32[]{:S(2)}, u32[]{:S(2)}) collective-permute-start(bf16[40,2048]{1,0:T(8,128)(2,1)S(1)} %get-tuple-element.39), channel_id=1, source_target_pairs={{0,8},{1,9},{2,10},{3,11},{4,12},{5,13},{6,14},{7,15},{8,0},{9,1},... | collective-permute-start | bytes 491528 | tf_op jit(solution)/shard_map/ppermute | solution.py:443
  7.8 11.1 %collective-permute-start.2 = (bf16[40,2048]{1,0:T(8,128)(2,1)S(1)}, bf16[40,2048]{1,0:T(8,128)(2,1)S(1)}, u32[]{:S(2)}, u32[]{:S(2)}) collective-permute-start(bf16[40,2048]{1,0:T(8,128)(2,1)S(1)} %get-tuple-element.40), channel_id=1, source_target_pairs={{0,12},{1,13},{2,14},{3,15},{4,0},{5,1},{6,2},{7,3},{8,4},{9,5},{1... | collective-permute-start | bytes 491528 | tf_op jit(solution)/shard_map/ppermute | solution.py:443
  19.0 1.9 %collective-permute-start.3 = (bf16[120,2048]{1,0:T(8,128)(2,1)S(1)}, bf16[120,2048]{1,0:T(8,128)(2,1)S(1)}, u32[]{:S(2)}, u32[]{:S(2)}) collective-permute-start(bf16[120,2048]{1,0:T(8,128)(2,1)S(1)} %shard_map.84.after.mine), channel_id=1, source_target_pairs={{0,1},{1,0},{2,3},{3,2},{4,5},{5,4},{6,7},{7,6},{8,9},{9,8},{10,11... | collective-permute-start | bytes 1474568 | tf_op jit(solution)/shard_map/ppermute | solution.py:446
  38.2 3.8 %collective-permute-start.9 = (bf16[160,1024]{1,0:T(8,128)(2,1)S(1)}, bf16[160,1024]{1,0:T(8,128)(2,1)S(1)}, u32[]{:S(2)}, u32[]{:S(2)}) collective-permute-start(bf16[160,1024]{1,0:T(8,128)(2,1)S(1)} %get-tuple-element.60), channel_id=1, source_target_pairs={{0,1},{1,0},{2,3},{3,2},{4,5},{5,4},{6,7},{7,6},{8,9},{9,8},{10,11... | collective-permute-start | bytes 983048 | tf_op jit(solution)/shard_map/ppermute | solution.py:446
  41.6 7.1 %collective-permute-start.4 = (bf16[160,1024]{1,0:T(8,128)(2,1)S(1)}, bf16[160,1024]{1,0:T(8,128)(2,1)S(1)}, u32[]{:S(2)}, u32[]{:S(2)}) collective-permute-start(bf16[160,1024]{1,0:T(8,128)(2,1)S(1)} %get-tuple-element.51), channel_id=1, source_target_pairs={{0,1},{1,0},{2,3},{3,2},{4,5},{5,4},{6,7},{7,6},{8,9},{9,8},{10,11... | collective-permute-start | bytes 983048 | tf_op jit(solution)/shard_map/ppermute | solution.py:446
  43.4 11.1 %collective-permute-start.10 = (bf16[40,1024]{1,0:T(8,128)(2,1)S(1)}, bf16[40,1024]{1,0:T(8,128)(2,1)S(1)}, u32[]{:S(2)}, u32[]{:S(2)}) collective-permute-start(bf16[40,1024]{1,0:T(8,128)(2,1)S(1)} %get-tuple-element.62), channel_id=1, source_target_pairs={{0,12},{1,13},{2,14},{3,15},{4,0},{5,1},{6,2},{7,3},{8,4},{9,5},{1... | collective-permute-start | bytes 245768 | tf_op jit(solution)/shard_map/ppermute | solution.py:443
  48.1 8.6 %collective-permute-start.11 = (bf16[40,1024]{1,0:T(8,128)(2,1)S(1)}, bf16[40,1024]{1,0:T(8,128)(2,1)S(1)}, u32[]{:S(2)}, u32[]{:S(2)}) collective-permute-start(bf16[40,1024]{1,0:T(8,128)(2,1)S(1)} %get-tuple-element.63), channel_id=1, source_target_pairs={{0,8},{1,9},{2,10},{3,11},{4,12},{5,13},{6,14},{7,15},{8,0},{9,1},... | collective-permute-start | bytes 245768 | tf_op jit(solution)/shard_map/ppermute | solution.py:443
  48.5 8.2 %collective-permute-start.12 = (bf16[40,1024]{1,0:T(8,128)(2,1)S(1)}, bf16[40,1024]{1,0:T(8,128)(2,1)S(1)}, u32[]{:S(2)}, u32[]{:S(2)}) collective-permute-start(bf16[40,1024]{1,0:T(8,128)(2,1)S(1)} %get-tuple-element.64), channel_id=1, source_target_pairs={{0,4},{1,5},{2,6},{3,7},{4,8},{5,9},{6,10},{7,11},{8,12},{9,13},{1... | collective-permute-start | bytes 245768 | tf_op jit(solution)/shard_map/ppermute | solution.py:443
  50.1 8.5 %collective-permute-start.5 = (bf16[40,1024]{1,0:T(8,128)(2,1)S(1)}, bf16[40,1024]{1,0:T(8,128)(2,1)S(1)}, u32[]{:S(2)}, u32[]{:S(2)}) collective-permute-start(bf16[40,1024]{1,0:T(8,128)(2,1)S(1)} %get-tuple-element.53), channel_id=1, source_target_pairs={{0,12},{1,13},{2,14},{3,15},{4,0},{5,1},{6,2},{7,3},{8,4},{9,5},{1... | collective-permute-start | bytes 245768 | tf_op jit(solution)/shard_map/ppermute | solution.py:443
  53.8 9.5 %collective-permute-start.6 = (bf16[40,1024]{1,0:T(8,128)(2,1)S(1)}, bf16[40,1024]{1,0:T(8,128)(2,1)S(1)}, u32[]{:S(2)}, u32[]{:S(2)}) collective-permute-start(bf16[40,1024]{1,0:T(8,128)(2,1)S(1)} %get-tuple-element.54), channel_id=1, source_target_pairs={{0,8},{1,9},{2,10},{3,11},{4,12},{5,13},{6,14},{7,15},{8,0},{9,1},... | collective-permute-start | bytes 245768 | tf_op jit(solution)/shard_map/ppermute | solution.py:443
  54.5 8.8 %collective-permute-start.7 = (bf16[40,1024]{1,0:T(8,128)(2,1)S(1)}, bf16[40,1024]{1,0:T(8,128)(2,1)S(1)}, u32[]{:S(2)}, u32[]{:S(2)}) collective-permute-start(bf16[40,1024]{1,0:T(8,128)(2,1)S(1)} %get-tuple-element.55), channel_id=1, source_target_pairs={{0,4},{1,5},{2,6},{3,7},{4,8},{5,9},{6,10},{7,11},{8,12},{9,13},{1... | collective-permute-start | bytes 245768 | tf_op jit(solution)/shard_map/ppermute | solution.py:443
  57.1 8.1 %collective-permute-start.13 = (bf16[128,512]{1,0:T(8,128)(2,1)S(1)}, bf16[128,512]{1,0:T(8,128)(2,1)S(1)}, u32[]{:S(2)}, u32[]{:S(2)}) collective-permute-start(bf16[128,512]{1,0:T(8,128)(2,1)S(1)} %get-tuple-element.66), channel_id=1, source_target_pairs={{0,2},{1,3},{2,0},{3,1},{4,6},{5,7},{6,4},{7,5},{8,10},{9,11},{10,... | collective-permute-start | bytes 393224 | tf_op jit(solution)/shard_map/ppermute | solution.py:443
  63.6 5.6 %collective-permute-start.8 = (bf16[128,512]{1,0:T(8,128)(2,1)S(1)}, bf16[128,512]{1,0:T(8,128)(2,1)S(1)}, u32[]{:S(2)}, u32[]{:S(2)}) collective-permute-start(bf16[128,512]{1,0:T(8,128)(2,1)S(1)} %get-tuple-element.57), channel_id=1, source_target_pairs={{0,2},{1,3},{2,0},{3,1},{4,6},{5,7},{6,4},{7,5},{8,10},{9,11},{10,... | collective-permute-start | bytes 393224 | tf_op jit(solution)/shard_map/ppermute | solution.py:443

commit v6 on v5

--- a/solution.py
+++ b/solution.py
@@ -16,7 +16,6 @@
 
 EPSILON = 1e-05
 
-OUT_CHUNKS = 2
 BLOCK = 512
 K_BLOCKS = 2
 READY = 4
@@ -203,16 +202,16 @@
     lax.fori_loop(0, buffer.shape[0], start, 0)
 
 
-def fetch_columns(sizes, down, chunk, keep, buffer, sem):
+def fetch_columns(sizes, down, offset, keep, buffer, sem):
     exp_count, groups = sizes
     z, g, s = place(sizes)
     side = s if keep else 1 - s
     part = down.shape[1] // (2 * groups)
     lines = down.shape[0] // BLOCK
+    first = (lax.rem(g + offset, groups) * 2 + side) * part
 
     def start(index, carry):
-        group = lax.rem(g + index // lines, groups)
-        column = (group * 2 + side) * part + chunk * BLOCK
+        column = first + index // lines * BLOCK
         pltpu.make_async_copy(
             down.at[
                 pl.ds(pl.multiple_of(lax.rem(index, lines) * BLOCK, BLOCK), BLOCK),
@@ -245,22 +244,24 @@
         copy.wait()
     rows = ids.shape[1]
     z, g, s = place(sizes)
-    named, before = count_earlier(ids, group_experts(exp_count, groups, z, g, rows))
     zero = jnp.zeros((CAP, rows), F32)
-    parts = []
-    for d in range(exp_count):
-        here = pick_rows(named, before, d) > 0
-        expert = lax.rem(z + d, exp_count) * groups + g
-        first = jnp.where(here & (ids[0:1, :] == expert), weights[0:1, :], zero)
-        second = jnp.where(here & (ids[1:2, :] == expert), weights[1:2, :], zero)
-        parts.append(first + second)
-    padded = combine_high.shape[1]
-    if padded > exp_count * CAP:
-        parts.append(jnp.zeros((padded - exp_count * CAP, rows), F32))
-    table = jnp.concatenate(parts, axis=0).T
-    high = table.astype(BF16)
-    combine_high[...] = high
-    combine_low[...] = (table - high.astype(F32)).astype(BF16)
+    padded = combine_high.shape[2]
+    for order in range(groups):
+        group = lax.rem(g - (order + 1) % groups + groups, groups)
+        named, before = count_earlier(ids, group_experts(exp_count, groups, z, group, rows))
+        parts = []
+        for d in range(exp_count):
+            here = pick_rows(named, before, d) > 0
+            expert = lax.rem(z + d, exp_count) * groups + group
+            first = jnp.where(here & (ids[0:1, :] == expert), weights[0:1, :], zero)
+            second = jnp.where(here & (ids[1:2, :] == expert), weights[1:2, :], zero)
+            parts.append(first + second)
+        if padded > exp_count * CAP:
+            parts.append(jnp.zeros((padded - exp_count * CAP, rows), F32))
+        table = jnp.concatenate(parts, axis=0).T
+        high = table.astype(BF16)
+        combine_high[order] = high
+        combine_low[order] = (table - high.astype(F32)).astype(BF16)
 
 
 def prepare_kernel(sizes, rows, active_hbm, gate, after, mask, *rest):
@@ -312,8 +313,8 @@
         buffer, sem = buffers[piece % count], sems.at[piece % count]
         if piece < 2 * pieces:
             fetch_rows(up, piece - pieces, buffer, sem)
-        elif piece < 2 * pieces + OUT_CHUNKS:
-            fetch_columns(sizes, down, piece - 2 * pieces, False, buffer, sem)
+        elif piece < 2 * pieces + groups:
+            fetch_columns(sizes, down, piece - 2 * pieces + 1, False, buffer, sem)
 
     for piece in range(READY, count):
         fetch(piece)
@@ -342,58 +343,41 @@
                 parts.append(value[d * CAP : (d + 1) * CAP, :] * mask[d : d + 1, cols])
             hidden[:, cols] = jnp.concatenate(parts, axis=0).astype(BF16)
         fetch(piece + count)
-    for piece in range(2 * pieces, 2 * pieces + OUT_CHUNKS):
+    for piece in range(2 * pieces, 2 * pieces + groups):
         await_all(buffers[piece % count], sems.at[piece % count])
 
 
-def give_kernel(sizes, chunk, hidden, weights, down, given, kept_weights, sem):
-    exp_count, groups = sizes
-    fetch_columns(sizes, down, chunk, True, kept_weights, sem)
+def give_kernel(sizes, offset, hidden, weights, down, given, kept_weights, sem):
+    fetch_columns(sizes, down, offset, True, kept_weights, sem)
     lines = down.shape[0] // BLOCK
-    for offset in range(groups):
-        value = jnp.dot(
-            hidden[...], stacked(weights, offset, lines), preferred_element_type=F32
-        )
-        given[:, offset * BLOCK : (offset + 1) * BLOCK] = value.astype(BF16)
+    for column in range(given.shape[1] // BLOCK):
+        value = jnp.dot(hidden[...], stacked(weights, column, lines), preferred_element_type=F32)
+        given[:, column * BLOCK : (column + 1) * BLOCK] = value.astype(BF16)
     await_all(kept_weights, sem)
 
 
 def keep_kernel(sizes, hidden, weights, received, *outs):
     exp_count, groups = sizes
     lines = hidden.shape[1] // BLOCK
-    for offset in range(groups):
-        cols = slice(offset * BLOCK, (offset + 1) * BLOCK)
-        value = jnp.dot(
-            hidden[...], stacked(weights, offset, lines), preferred_element_type=F32
-        )
+    for column in range(received.shape[1] // BLOCK):
+        cols = slice(column * BLOCK, (column + 1) * BLOCK)
+        value = jnp.dot(hidden[...], stacked(weights, column, lines), preferred_element_type=F32)
         value = value + received[:, cols].astype(F32)
         for d in range(exp_count):
             outs[d][:, cols] = value[d * CAP : (d + 1) * CAP, :].astype(BF16)
 
 
-def combine_kernel(exp_count, high, low, *refs):
-    pieces = [r[...].astype(F32) for r in refs[:exp_count]]
-    kept, gives = refs[exp_count], refs[exp_count + 1 :]
-    total = exp_count * CAP
-    width = kept.shape[1]
-    found = jnp.concatenate(pieces, axis=0).astype(BF16)
-    value = jnp.dot(high[:, :total], found, preferred_element_type=F32)
-    value = value + jnp.dot(low[:, :total], found, preferred_element_type=F32)
-    kept[...] = value[:, :width]
-    for n, give in enumerate(gives):
-        give[...] = value[:, (n + 1) * width : (n + 2) * width].astype(BF16)
-
-
-def finish_kernel(chunks, *refs):
-    out = refs[-1]
-    per_chunk = (len(refs) - 1) // chunks
-    width = refs[0].shape[1]
-    for chunk in range(chunks):
-        kept, *others = refs[chunk * per_chunk : (chunk + 1) * per_chunk]
-        value = kept[...]
-        for other in others:
-            value = value + other[...].astype(F32)
-        out[:, chunk * width : (chunk + 1) * width] = value.astype(BF16)
+def combine_kernel(order, high, low, *refs):
+    refs = list(refs)
+    out = refs.pop()
+    before = refs.pop(0) if order > 0 else None
+    found = jnp.concatenate([r[...].astype(F32) for r in refs], axis=0).astype(BF16)
+    count = found.shape[0]
+    value = jnp.dot(high[order, :, :count], found, preferred_element_type=F32)
+    value = value + jnp.dot(low[order, :, :count], found, preferred_element_type=F32)
+    if before is not None:
+        value = before[...] + value
+    out[...] = value.astype(out.dtype)
 
 
 def call(kernel, outs, ins, scratch=(), flops=0, moved=0, aliases=None):
@@ -490,7 +474,7 @@
     padded = -(-slots // 128) * 128
     combine_high, combine_low = call(
         functools.partial(table_kernel, sizes),
-        [((tok_count, padded), BF16)] * 2,
+        [((groups, tok_count, padded), BF16)] * 2,
         [(ids, pltpu.HBM), (weights, pltpu.HBM), (mine, pl.ANY)],
         [
             pltpu.VMEM(ids.shape, jnp.int32),
@@ -518,48 +502,49 @@
     )
     first = 2 * features // (K_BLOCKS * BLOCK)
     part = features // unit_count
-    out_width = BLOCK
+    offsets = [(order + 1) % groups for order in range(groups)]
     given, kept_weights = [], []
-    for chunk in range(OUT_CHUNKS):
+    for order, offset in enumerate(offsets):
         value, kept = call(
-            functools.partial(give_kernel, sizes, chunk),
-            [((slots, groups * BLOCK), BF16), buffer],
+            functools.partial(give_kernel, sizes, offset),
+            [((slots, part), BF16), buffer],
             [
                 (hidden, None),
-                (buffers[(first + chunk) % BUFFERS], pltpu.VMEM),
+                (buffers[(first + order) % BUFFERS], pltpu.VMEM),
                 (down_weight, pltpu.HBM),
             ],
             [pltpu.SemaphoreType.DMA],
-            flops=2 * slots * unit_width * groups * BLOCK,
+            flops=2 * slots * unit_width * part,
             moved=piece_bytes,
         )
         given.append(value)
         kept_weights.append(kept)
     taken = [swap(value) for value in given]
-    last = []
-    for chunk in range(OUT_CHUNKS):
+    homes = []
+    for order, offset in enumerate(offsets):
         kept = call(
             functools.partial(keep_kernel, sizes),
-            [((CAP, groups * BLOCK), BF16)] * exp_count,
-            [(hidden, None), (kept_weights[chunk], pltpu.VMEM), (taken[chunk], None)],
-            flops=2 * slots * unit_width * groups * BLOCK,
+            [((CAP, part), BF16)] * exp_count,
+            [(hidden, None), (kept_weights[order], pltpu.VMEM), (taken[order], None)],
+            flops=2 * slots * unit_width * part,
             moved=piece_bytes,
         )
-        home = [kept[0]] + [shift(kept[d], -d) for d in range(1, exp_count)]
-        stay, *gives = call(
-            functools.partial(combine_kernel, exp_count),
-            [((tok_count, out_width), F32)] + [((tok_count, out_width), BF16)] * (groups - 1),
-            [(combine_high, None), (combine_low, None)] + [(v, None) for v in home],
-            flops=4 * tok_count * slots * groups * out_width,
+        homes.append(
+            [shift(v, -d, offset) if d or offset else v for d, v in enumerate(kept)]
+        )
+    mixed = None
+    for order, home in enumerate(homes):
+        last = order == groups - 1
+        mixed = call(
+            functools.partial(combine_kernel, order),
+            [((tok_count, part), BF16 if last else F32)],
+            [(combine_high, None), (combine_low, None)]
+            + ([(mixed, None)] if order else [])
+            + [(v, None) for v in home],
+            flops=4 * tok_count * slots * part,
             moved=1 << 20,
-        )
-        last += [stay] + [shift(value, 0, n + 1) for n, value in enumerate(gives)]
-    return call(
-        functools.partial(finish_kernel, OUT_CHUNKS),
-        [((tok_count, part), BF16)],
-        [(v, None) for v in last],
-        moved=1 << 20,
-    )[0]
+        )[0]
+    return mixed
 
 
 def per_device(*operands):
@@ -572,8 +557,7 @@
         and exp_count * unit_count // 2 == EXPERTS
         and TILE % tokens.shape[0] == 0
         and unit_width % BLOCK == 0
-        and tokens.shape[1] == unit_count * OUT_CHUNKS * BLOCK == READY * K_BLOCKS * BLOCK
-        and unit_count // 2 == K_BLOCKS
+        and tokens.shape[1] == READY * K_BLOCKS * BLOCK == unit_count * K_BLOCKS * BLOCK
     )
     return (paired_experts if paired else spread_experts)(*operands)
 

time: 70.1 us -> 65.8 us (0.939)
  waiting for transfers between devices: 11.9 us -> 8.07 us
    ppermute x11 -> x10, waiting for transfers between devices: 10 us -> 6.22 us  [shift(): return lax.ppermute(value, ('exp', 'unit'), pairs)]
    ppermute x11 -> x10, starting transfers between devices: 19.8 us -> 19.3 us  [shift(): return lax.ppermute(value, ('exp', 'unit'), pairs)]
    pallas_call x12 -> x11, Pallas kernels: 37.4 us -> 37.3 us  [call(): pl.pallas_call(kernel, out_shape=shapes, in_specs=specs, out_specs=[vmem]...]
  transfers between devices with their start and end apart: 14 -> 13, of which waited for: 4 -> 4; matrix products, arithmetic and copies ran while one was open for 0% -> 0% of each run, Pallas kernels for 25% -> 26%
where the time goes in v6:
time: 65.8 us; the launch traced here: 65.6 us
  Pallas kernels  37.3 us (57%)
  starting transfers between devices  20 us (30%)
  waiting for transfers between devices  8.07 us (12%)
    pallas_call x11, Pallas kernels, call(): pl.pallas_call(kernel, out_shape=shapes, in_specs=specs, out_specs=[vmem]...  37.3 us
    ppermute x10, starting transfers between devices, shift(): return lax.ppermute(value, ('exp', 'unit'), pairs)  19.3 us
    ppermute x10, waiting for transfers between devices, shift(): return lax.ppermute(value, ('exp', 'unit'), pairs)  6.22 us
    ppermute x3, waiting for transfers between devices, swap(): return lax.ppermute(value, 'unit', [(u, u ^ 1) for u in range(unit_count)])  1.86 us
  transfers between devices with their start and end apart: 13, of which 4 were waited for; matrix products, arithmetic and copies ran while one was open for 0% of the time, Pallas kernels for 26%

profile of v6, /device:TPU:0, one launch (start us, length us, event | category | flops | bytes accessed | tf_op | source)
XLA Modules:
  0.0 65.6 jit_solution(11290263208921876674)
XLA Ops:
  0.0 2.2 %shard_map.82 = (bf16[40,4096]{1,0:T(8,128)(2,1)S(1)}, bf16[40,2048]{1,0:T(8,128)(2,1)S(1)}, bf16[40,2048]{1,0:T(8,128)(2,1)S(1)}, bf16[40,2048]{1,0:T(8,128)(2,1)S(1)}) custom-call(bf16[128,4096]{1,0:T(8,128)(2,1)} %tokens_hbm.1, f32[1,4096]{1,0:T(1,128)} %bitcast.3, s32[2,128]{1,0:T(2,128)} %bitcast.4), custom_call_target="tpu_custom_call" | custom-call | flops 83886080 | bytes 2097152 | tf_op jit(solution)/shard_map/pallas_call | solution.py:394
  2.2 3.1 %collective-permute-start = (bf16[40,2048]{1,0:T(8,128)(2,1)S(1)}, bf16[40,2048]{1,0:T(8,128)(2,1)S(1)}, u32[]{:S(2)}, u32[]{:S(2)}) collective-permute-start(bf16[40,2048]{1,0:T(8,128)(2,1)S(1)} %get-tuple-element.34), channel_id=1, source_target_pairs={{0,4},{1,5},{2,6},{3,7},{4,8},{5,9},{6,10},{7,11},{8,12},{9,13},{1... | collective-permute-start | bytes 491528 | tf_op jit(solution)/shard_map/ppermute | solution.py:427
  5.2 2.6 %collective-permute-start.1 = (bf16[40,2048]{1,0:T(8,128)(2,1)S(1)}, bf16[40,2048]{1,0:T(8,128)(2,1)S(1)}, u32[]{:S(2)}, u32[]{:S(2)}) collective-permute-start(bf16[40,2048]{1,0:T(8,128)(2,1)S(1)} %get-tuple-element.35), channel_id=1, source_target_pairs={{0,8},{1,9},{2,10},{3,11},{4,12},{5,13},{6,14},{7,15},{8,0},{9,1},... | collective-permute-start | bytes 491528 | tf_op jit(solution)/shard_map/ppermute | solution.py:427
  7.8 1.3 %collective-permute-start.2 = (bf16[40,2048]{1,0:T(8,128)(2,1)S(1)}, bf16[40,2048]{1,0:T(8,128)(2,1)S(1)}, u32[]{:S(2)}, u32[]{:S(2)}) collective-permute-start(bf16[40,2048]{1,0:T(8,128)(2,1)S(1)} %get-tuple-element.36), channel_id=1, source_target_pairs={{0,12},{1,13},{2,14},{3,15},{4,0},{5,1},{6,2},{7,3},{8,4},{9,5},{1... | collective-permute-start | bytes 491528 | tf_op jit(solution)/shard_map/ppermute | solution.py:427
  9.2 9.7 %shard_map.83 = (f32[8,3584]{1,0:T(8,128)S(1)}, bf16[14,512,512]{2,1,0:T(8,128)(2,1)S(1)}, bf16[14,512,512]{2,1,0:T(8,128)(2,1)S(1)}, bf16[14,512,512]{2,1,0:T(8...) custom-call(s32[2,8,48]{2,1,0:T(8,128)} %active_hbm.1, bf16[4096,3584]{1,0:T(8,128)(2,1)} %gate.1, ...), custom_call_target="tpu_custom_call" | custom-call | flops 167772160 | bytes 29360128 | tf_op jit(solution)/shard_map/pallas_call | solution.py:394
  18.9 0.0 collective-permute-done.refs_0_
  18.9 0.0 collective-permute-done.1.refs_1_
  18.9 0.0 collective-permute-done.2.refs_2_
  19.0 0.1 collective-permute-start.3
  19.1 1.9 %collective-permute-done.3.other = bf16[120,2048]{1,0:T(8,128)(2,1)S(1)} collective-permute-done((bf16[120,2048]{1,0:T(8,128)(2,1)S(1)}, bf16[120,2048]{1,0:T(8,128)(2,1)S(1)}, u32[]{:S(2)}, u32[]{:S(2)}) %collective-permute-start.3) | collective-permute-done | bytes 491552 | tf_op jit(solution)/shard_map/ppermute | solution.py:430
  20.9 14.1 %shard_map.86 = (bf16[160,3584]{1,0:T(8,128)(2,1)S(1)}, bf16[14,512,512]{2,1,0:T(8,128)(2,1)S(1)}, bf16[14,512,512]{2,1,0:T(8,128)(2,1)S(1)}, bf16[14,512,512]{2...) custom-call(bf16[40,4096]{1,0:T(8,128)(2,1)S(1)} %get-tuple-element., ...), custom_call_target="tpu_custom_call", output_to_operand_aliasing={{1}: (3, {}), {2}: (4, {}), {3}: (5, {}), {4}: (6, {}), {5}... | custom-call | flops 9395240960 | bytes 44040192 | tf_op jit(solution)/shard_map/pallas_call | solution.py:394
  35.0 3.2 %shard_map.87 = (bf16[160,1024]{1,0:T(8,128)(2,1)S(1)}, bf16[14,512,512]{2,1,0:T(8,128)(2,1)S(1)}) custom-call(bf16[160,3584]{1,0:T(8,128)(2,1)S(1)} %get-tuple-element.44.hidden, bf16[14,512,512]{2,1,0:T(8,128)(2,1)S(1)} %get-tuple-element.45.weights, bf16[3584,4096]{1,0:T(8,128)(2,1)} %down.3), custom_call_target="tpu_custom_call" | custom-call | flops 1174405120 | bytes 7340032 | tf_op jit(solution)/shard_map/pallas_call | solution.py:394
  38.2 0.2 collective-permute-start.4
  38.4 3.2 %shard_map.90 = (bf16[160,1024]{1,0:T(8,128)(2,1)S(1)}, bf16[14,512,512]{2,1,0:T(8,128)(2,1)S(1)}) custom-call(bf16[160,3584]{1,0:T(8,128)(2,1)S(1)} %get-tuple-element.44.hidden, bf16[14,512,512]{2,1,0:T(8,128)(2,1)S(1)} %get-tuple-element.52.weights, bf16[3584,4096]{1,0:T(8,128)(2,1)} %down.3), custom_call_target="tpu_custom_call" | custom-call | flops 1174405120 | bytes 7340032 | tf_op jit(solution)/shard_map/pallas_call | solution.py:394
  41.6 0.4 collective-permute-start.9
  42.0 0.0 collective-permute-done.4.received
  42.0 1.4 %shard_map.88 = (bf16[40,1024]{1,0:T(8,128)(2,1)S(1)}, bf16[40,1024]{1,0:T(8,128)(2,1)S(1)}, bf16[40,1024]{1,0:T(8,128)(2,1)S(1)}, bf16[40,1024]{1,0:T(8,128)(2,1)S(1)}) custom-call(bf16[160,3584]{1,0:T(8,128)(2,1)S(1)} %get-tuple-element.44.hidden, bf16[14,512,512]{2,1,0:T(8,128)(2,1)S(1)} %get-tuple-element.46.weights, ...), custom_call_target="tpu_custom_call" | custom-call | flops 1174405120 | bytes 7340032 | tf_op jit(solution)/shard_map/pallas_call | solution.py:394
  43.4 1.6 %collective-permute-start.5 = (bf16[40,1024]{1,0:T(8,128)(2,1)S(1)}, bf16[40,1024]{1,0:T(8,128)(2,1)S(1)}, u32[]{:S(2)}, u32[]{:S(2)}) collective-permute-start(bf16[40,1024]{1,0:T(8,128)(2,1)S(1)} %get-tuple-element.48), channel_id=1, source_target_pairs={{0,2},{1,3},{2,0},{3,1},{4,6},{5,7},{6,4},{7,5},{8,10},{9,11},{10,... | collective-permute-start | bytes 245768 | tf_op jit(solution)/shard_map/ppermute | solution.py:427
  44.9 4.6 %collective-permute-start.6 = (bf16[40,1024]{1,0:T(8,128)(2,1)S(1)}, bf16[40,1024]{1,0:T(8,128)(2,1)S(1)}, u32[]{:S(2)}, u32[]{:S(2)}) collective-permute-start(bf16[40,1024]{1,0:T(8,128)(2,1)S(1)} %get-tuple-element.49), channel_id=1, source_target_pairs={{0,14},{1,15},{2,12},{3,13},{4,2},{5,3},{6,0},{7,1},{8,6},{9,7},{1... | collective-permute-start | bytes 245768 | tf_op jit(solution)/shard_map/ppermute | solution.py:427
  49.6 1.3 %collective-permute-start.7 = (bf16[40,1024]{1,0:T(8,128)(2,1)S(1)}, bf16[40,1024]{1,0:T(8,128)(2,1)S(1)}, u32[]{:S(2)}, u32[]{:S(2)}) collective-permute-start(bf16[40,1024]{1,0:T(8,128)(2,1)S(1)} %get-tuple-element.50), channel_id=1, source_target_pairs={{0,10},{1,11},{2,8},{3,9},{4,14},{5,15},{6,12},{7,13},{8,2},{9,3},... | collective-permute-start | bytes 245768 | tf_op jit(solution)/shard_map/ppermute | solution.py:427
  50.9 0.2 collective-permute-start.8
  51.1 0.0 collective-permute-done.9.received
  51.1 1.4 %shard_map.91 = (bf16[40,1024]{1,0:T(8,128)(2,1)S(1)}, bf16[40,1024]{1,0:T(8,128)(2,1)S(1)}, bf16[40,1024]{1,0:T(8,128)(2,1)S(1)}, bf16[40,1024]{1,0:T(8,128)(2,1)S(1)}) custom-call(bf16[160,3584]{1,0:T(8,128)(2,1)S(1)} %get-tuple-element.44.hidden, bf16[14,512,512]{2,1,0:T(8,128)(2,1)S(1)} %get-tuple-element.53.weights, ...), custom_call_target="tpu_custom_call" | custom-call | flops 1174405120 | bytes 7340032 | tf_op jit(solution)/shard_map/pallas_call | solution.py:394
  52.4 3.7 %collective-permute-start.10 = (bf16[40,1024]{1,0:T(8,128)(2,1)S(1)}, bf16[40,1024]{1,0:T(8,128)(2,1)S(1)}, u32[]{:S(2)}, u32[]{:S(2)}) collective-permute-start(bf16[40,1024]{1,0:T(8,128)(2,1)S(1)} %get-tuple-element.56), channel_id=1, source_target_pairs={{0,12},{1,13},{2,14},{3,15},{4,0},{5,1},{6,2},{7,3},{8,4},{9,5},{1... | collective-permute-start | bytes 245768 | tf_op jit(solution)/shard_map/ppermute | solution.py:427
  56.1 0.0 collective-permute-done.5.refs_0_
  56.1 0.7 %collective-permute-start.11 = (bf16[40,1024]{1,0:T(8,128)(2,1)S(1)}, bf16[40,1024]{1,0:T(8,128)(2,1)S(1)}, u32[]{:S(2)}, u32[]{:S(2)}) collective-permute-start(bf16[40,1024]{1,0:T(8,128)(2,1)S(1)} %get-tuple-element.57), channel_id=1, source_target_pairs={{0,8},{1,9},{2,10},{3,11},{4,12},{5,13},{6,14},{7,15},{8,0},{9,1},... | collective-permute-start | bytes 245768 | tf_op jit(solution)/shard_map/ppermute | solution.py:427
  56.8 0.0 collective-permute-done.6.refs_1_
  56.9 0.2 collective-permute-start.12
  57.1 1.0 %shard_map.85 = (bf16[2,128,256]{2,1,0:T(8,128)(2,1)S(1)}, bf16[2,128,256]{2,1,0:T(8,128)(2,1)S(1)}) custom-call(s32[2,128]{1,0:T(2,128)} %bitcast.5, f32[2,128]{1,0:T(2,128)} %bitcast.6, bf16[120,2048]{1,0:T(8,128)(2,1)S(1)} %shard_map.84.after.mine), custom_call_target="tpu_custom_call" | custom-call | bytes 2097152 | tf_op jit(solution)/shard_map/pallas_call | solution.py:394
  58.1 0.3 collective-permute-done.7.refs_2_
  58.4 0.6 collective-permute-done.8.refs_3_
  59.0 0.3 shard_map.89.refs_0_
  59.3 0.0 collective-permute-done.10.refs_2_
  59.3 5.3 %collective-permute-done.11.refs_3_ = bf16[40,1024]{1,0:T(8,128)(2,1)S(1)} collective-permute-done((bf16[40,1024]{1,0:T(8,128)(2,1)S(1)}, bf16[40,1024]{1,0:T(8,128)(2,1)S(1)}, u32[]{:S(2)}, u32[]{:S(2)}) %collective-permute-start.11) | collective-permute-done | bytes 81952 | tf_op jit(solution)/shard_map/ppermute | solution.py:427
  64.6 0.0 collective-permute-done.12.refs_4_
  64.6 1.0 %shard_map.92 = bf16[128,1024]{1,0:T(8,128)(2,1)} custom-call(bf16[2,128,256]{2,1,0:T(8,128)(2,1)S(1)} %get-tuple-element.37.high, bf16[2,128,256]{2,1,0:T(8,128)(2,1)S(1)} %get-tuple-element.38.low, f32[128,1024]{1,0:T(8,128)S(1)} %shard_map.89.refs_0_, bf16[40,1024]{1,0:T(8,128)(2,1)S(1)} %get-tuple-element.55.refs_1_, ...), custom_call_target="tpu_custom_call" | custom-call | flops 83886080 | bytes 1048576 | tf_op jit(solution)/shard_map/pallas_call | solution.py:394
  (1 shorter events, 0.0 us)
Async XLA Ops:
  2.2 16.8 %collective-permute-start = (bf16[40,2048]{1,0:T(8,128)(2,1)S(1)}, bf16[40,2048]{1,0:T(8,128)(2,1)S(1)}, u32[]{:S(2)}, u32[]{:S(2)}) collective-permute-start(bf16[40,2048]{1,0:T(8,128)(2,1)S(1)} %get-tuple-element.34), channel_id=1, source_target_pairs={{0,4},{1,5},{2,6},{3,7},{4,8},{5,9},{6,10},{7,11},{8,12},{9,13},{1... | collective-permute-start | bytes 491528 | tf_op jit(solution)/shard_map/ppermute | solution.py:427
  5.2 13.7 %collective-permute-start.1 = (bf16[40,2048]{1,0:T(8,128)(2,1)S(1)}, bf16[40,2048]{1,0:T(8,128)(2,1)S(1)}, u32[]{:S(2)}, u32[]{:S(2)}) collective-permute-start(bf16[40,2048]{1,0:T(8,128)(2,1)S(1)} %get-tuple-element.35), channel_id=1, source_target_pairs={{0,8},{1,9},{2,10},{3,11},{4,12},{5,13},{6,14},{7,15},{8,0},{9,1},... | collective-permute-start | bytes 491528 | tf_op jit(solution)/shard_map/ppermute | solution.py:427
  7.8 11.1 %collective-permute-start.2 = (bf16[40,2048]{1,0:T(8,128)(2,1)S(1)}, bf16[40,2048]{1,0:T(8,128)(2,1)S(1)}, u32[]{:S(2)}, u32[]{:S(2)}) collective-permute-start(bf16[40,2048]{1,0:T(8,128)(2,1)S(1)} %get-tuple-element.36), channel_id=1, source_target_pairs={{0,12},{1,13},{2,14},{3,15},{4,0},{5,1},{6,2},{7,3},{8,4},{9,5},{1... | collective-permute-start | bytes 491528 | tf_op jit(solution)/shard_map/ppermute | solution.py:427
  19.0 1.9 %collective-permute-start.3 = (bf16[120,2048]{1,0:T(8,128)(2,1)S(1)}, bf16[120,2048]{1,0:T(8,128)(2,1)S(1)}, u32[]{:S(2)}, u32[]{:S(2)}) collective-permute-start(bf16[120,2048]{1,0:T(8,128)(2,1)S(1)} %shard_map.84.after.mine), channel_id=1, source_target_pairs={{0,1},{1,0},{2,3},{3,2},{4,5},{5,4},{6,7},{7,6},{8,9},{9,8},{10,11... | collective-permute-start | bytes 1474568 | tf_op jit(solution)/shard_map/ppermute | solution.py:430
  38.2 3.8 %collective-permute-start.4 = (bf16[160,1024]{1,0:T(8,128)(2,1)S(1)}, bf16[160,1024]{1,0:T(8,128)(2,1)S(1)}, u32[]{:S(2)}, u32[]{:S(2)}) collective-permute-start(bf16[160,1024]{1,0:T(8,128)(2,1)S(1)} %get-tuple-element.47), channel_id=1, source_target_pairs={{0,1},{1,0},{2,3},{3,2},{4,5},{5,4},{6,7},{7,6},{8,9},{9,8},{10,11... | collective-permute-start | bytes 983048 | tf_op jit(solution)/shard_map/ppermute | solution.py:430
  41.6 9.5 %collective-permute-start.9 = (bf16[160,1024]{1,0:T(8,128)(2,1)S(1)}, bf16[160,1024]{1,0:T(8,128)(2,1)S(1)}, u32[]{:S(2)}, u32[]{:S(2)}) collective-permute-start(bf16[160,1024]{1,0:T(8,128)(2,1)S(1)} %get-tuple-element.54), channel_id=1, source_target_pairs={{0,1},{1,0},{2,3},{3,2},{4,5},{5,4},{6,7},{7,6},{8,9},{9,8},{10,11... | collective-permute-start | bytes 983048 | tf_op jit(solution)/shard_map/ppermute | solution.py:430
  43.4 12.7 %collective-permute-start.5 = (bf16[40,1024]{1,0:T(8,128)(2,1)S(1)}, bf16[40,1024]{1,0:T(8,128)(2,1)S(1)}, u32[]{:S(2)}, u32[]{:S(2)}) collective-permute-start(bf16[40,1024]{1,0:T(8,128)(2,1)S(1)} %get-tuple-element.48), channel_id=1, source_target_pairs={{0,2},{1,3},{2,0},{3,1},{4,6},{5,7},{6,4},{7,5},{8,10},{9,11},{10,... | collective-permute-start | bytes 245768 | tf_op jit(solution)/shard_map/ppermute | solution.py:427
  44.9 11.9 %collective-permute-start.6 = (bf16[40,1024]{1,0:T(8,128)(2,1)S(1)}, bf16[40,1024]{1,0:T(8,128)(2,1)S(1)}, u32[]{:S(2)}, u32[]{:S(2)}) collective-permute-start(bf16[40,1024]{1,0:T(8,128)(2,1)S(1)} %get-tuple-element.49), channel_id=1, source_target_pairs={{0,14},{1,15},{2,12},{3,13},{4,2},{5,3},{6,0},{7,1},{8,6},{9,7},{1... | collective-permute-start | bytes 245768 | tf_op jit(solution)/shard_map/ppermute | solution.py:427
  49.6 8.8 %collective-permute-start.7 = (bf16[40,1024]{1,0:T(8,128)(2,1)S(1)}, bf16[40,1024]{1,0:T(8,128)(2,1)S(1)}, u32[]{:S(2)}, u32[]{:S(2)}) collective-permute-start(bf16[40,1024]{1,0:T(8,128)(2,1)S(1)} %get-tuple-element.50), channel_id=1, source_target_pairs={{0,10},{1,11},{2,8},{3,9},{4,14},{5,15},{6,12},{7,13},{8,2},{9,3},... | collective-permute-start | bytes 245768 | tf_op jit(solution)/shard_map/ppermute | solution.py:427
  50.9 8.1 %collective-permute-start.8 = (bf16[40,1024]{1,0:T(8,128)(2,1)S(1)}, bf16[40,1024]{1,0:T(8,128)(2,1)S(1)}, u32[]{:S(2)}, u32[]{:S(2)}) collective-permute-start(bf16[40,1024]{1,0:T(8,128)(2,1)S(1)} %get-tuple-element.51), channel_id=1, source_target_pairs={{0,6},{1,7},{2,4},{3,5},{4,10},{5,11},{6,8},{7,9},{8,14},{9,15},{1... | collective-permute-start | bytes 245768 | tf_op jit(solution)/shard_map/ppermute | solution.py:427
  52.4 6.9 %collective-permute-start.10 = (bf16[40,1024]{1,0:T(8,128)(2,1)S(1)}, bf16[40,1024]{1,0:T(8,128)(2,1)S(1)}, u32[]{:S(2)}, u32[]{:S(2)}) collective-permute-start(bf16[40,1024]{1,0:T(8,128)(2,1)S(1)} %get-tuple-element.56), channel_id=1, source_target_pairs={{0,12},{1,13},{2,14},{3,15},{4,0},{5,1},{6,2},{7,3},{8,4},{9,5},{1... | collective-permute-start | bytes 245768 | tf_op jit(solution)/shard_map/ppermute | solution.py:427
  56.1 8.5 %collective-permute-start.11 = (bf16[40,1024]{1,0:T(8,128)(2,1)S(1)}, bf16[40,1024]{1,0:T(8,128)(2,1)S(1)}, u32[]{:S(2)}, u32[]{:S(2)}) collective-permute-start(bf16[40,1024]{1,0:T(8,128)(2,1)S(1)} %get-tuple-element.57), channel_id=1, source_target_pairs={{0,8},{1,9},{2,10},{3,11},{4,12},{5,13},{6,14},{7,15},{8,0},{9,1},... | collective-permute-start | bytes 245768 | tf_op jit(solution)/shard_map/ppermute | solution.py:427
  56.9 7.7 %collective-permute-start.12 = (bf16[40,1024]{1,0:T(8,128)(2,1)S(1)}, bf16[40,1024]{1,0:T(8,128)(2,1)S(1)}, u32[]{:S(2)}, u32[]{:S(2)}) collective-permute-start(bf16[40,1024]{1,0:T(8,128)(2,1)S(1)} %get-tuple-element.58), channel_id=1, source_target_pairs={{0,4},{1,5},{2,6},{3,7},{4,8},{5,9},{6,10},{7,11},{8,12},{9,13},{1... | collective-permute-start | bytes 245768 | tf_op jit(solution)/shard_map/ppermute | solution.py:427

commit v7 on v6

--- a/solution.py
+++ b/solution.py
@@ -17,9 +17,8 @@
 EPSILON = 1e-05
 
 BLOCK = 512
-K_BLOCKS = 2
-READY = 4
-BUFFERS = 5
+READY = 10
+BUFFERS = 12
 LIMIT = 8
 
 F32 = jnp.float32
@@ -185,14 +184,11 @@
     ).astype(BF16)
 
 
-def fetch_rows(weight, piece, buffer, sem):
+def fetch_rows(weight, line, buffer, sem):
     def start(index, carry):
-        line = piece * K_BLOCKS + lax.rem(index, K_BLOCKS)
-        column = index // K_BLOCKS
         pltpu.make_async_copy(
             weight.at[
-                pl.ds(pl.multiple_of(line * BLOCK, BLOCK), BLOCK),
-                pl.ds(pl.multiple_of(column * BLOCK, BLOCK), BLOCK),
+                pl.ds(line * BLOCK, BLOCK), pl.ds(pl.multiple_of(index * BLOCK, BLOCK), BLOCK)
             ],
             buffer.at[index],
             sem,
@@ -202,19 +198,17 @@
     lax.fori_loop(0, buffer.shape[0], start, 0)
 
 
-def fetch_columns(sizes, down, offset, keep, buffer, sem):
+def fetch_columns(sizes, down, offset, keep, step, buffer, sem):
     exp_count, groups = sizes
     z, g, s = place(sizes)
     side = s if keep else 1 - s
     part = down.shape[1] // (2 * groups)
-    lines = down.shape[0] // BLOCK
-    first = (lax.rem(g + offset, groups) * 2 + side) * part
+    column = (lax.rem(g + offset, groups) * 2 + side) * part + step * BLOCK
 
     def start(index, carry):
-        column = first + index // lines * BLOCK
         pltpu.make_async_copy(
             down.at[
-                pl.ds(pl.multiple_of(lax.rem(index, lines) * BLOCK, BLOCK), BLOCK),
+                pl.ds(pl.multiple_of(index * BLOCK, BLOCK), BLOCK),
                 pl.ds(pl.multiple_of(column, BLOCK), BLOCK),
             ],
             buffer.at[index],
@@ -229,9 +223,8 @@
     pltpu.make_async_copy(buffer, buffer, sem).wait()
 
 
-def stacked(buffer, column, count):
-    blocks = buffer[column * count : (column + 1) * count]
-    return blocks.reshape(count * BLOCK, BLOCK)
+def stacked(buffer):
+    return buffer[...].reshape(buffer.shape[0] * BLOCK, BLOCK)
 
 
 def table_kernel(sizes, ids_hbm, weights_hbm, after, combine_high, combine_low, ids, weights, sems):
@@ -264,14 +257,15 @@
         combine_low[order] = (table - high.astype(F32)).astype(BF16)
 
 
-def prepare_kernel(sizes, rows, active_hbm, gate, after, mask, *rest):
+def prepare_kernel(sizes, rows, active_hbm, gate, up, after, mask, *rest):
     exp_count, groups = sizes
     *buffers, active, small_sem, sems = rest
     z, g, s = place(sizes)
     small = pltpu.make_async_copy(active_hbm, active, small_sem)
     small.start()
+    lines = gate.shape[0] // BLOCK
     for n, buffer in enumerate(buffers[:READY]):
-        fetch_rows(gate, n, buffer, sems.at[n])
+        fetch_rows(gate if n < lines else up, n % lines, buffer, sems.at[n])
     small.wait()
     unit_width = mask.shape[1]
     blocks = lax.broadcasted_iota(jnp.int32, mask.shape, 1) // BLK + s * (unit_width // BLK)
@@ -305,36 +299,39 @@
     gate_sum, up_sum, rows, sems = refs
     half = own.shape[1] // 2
     features, unit_width = up.shape
-    columns = unit_width // BLOCK
-    pieces = features // (K_BLOCKS * BLOCK)
+    columns, lines = unit_width // BLOCK, features // BLOCK
+    given = features // (2 * groups) // BLOCK
     count = len(buffers)
 
-    def fetch(piece):
-        buffer, sem = buffers[piece % count], sems.at[piece % count]
-        if piece < 2 * pieces:
-            fetch_rows(up, piece - pieces, buffer, sem)
-        elif piece < 2 * pieces + groups:
-            fetch_columns(sizes, down, piece - 2 * pieces + 1, False, buffer, sem)
-
-    for piece in range(READY, count):
-        fetch(piece)
+    def fetch(index):
+        buffer, sem = buffers[index % count], sems.at[index % count]
+        if index < 2 * lines:
+            fetch_rows(up, index - lines, buffer, sem)
+        elif index < 2 * lines + groups * given:
+            order, step = divmod(index - 2 * lines, given)
+            fetch_columns(sizes, down, order + 1, False, step, buffer, sem)
+
+    for index in range(READY, count):
+        fetch(index)
     for source, side in ((mine, s), (other, 1 - s)):
         cols = pl.ds(pl.multiple_of(side * half, 128), half)
         joined = [own[:, cols].astype(F32), source[...].astype(F32)]
         rows[:, cols] = jnp.concatenate(joined, axis=0).astype(BF16)
-    for piece in range(2 * pieces):
-        buffer = buffers[piece % count]
-        if piece >= READY:
-            await_all(buffer, sems.at[piece % count])
-        step = piece % pieces
-        total = gate_sum if piece < pieces else up_sum
-        left = rows[:, step * K_BLOCKS * BLOCK : (step + 1) * K_BLOCKS * BLOCK]
+    for index in range(0, 2 * lines, 2):
+        pair = [buffers[(index + n) % count] for n in range(2)]
+        for n in range(2):
+            if index + n >= READY:
+                await_all(pair[n], sems.at[(index + n) % count])
+        line = index % lines
+        total = gate_sum if index < lines else up_sum
+        left = [rows[:, (line + n) * BLOCK : (line + n + 1) * BLOCK] for n in range(2)]
         for column in range(columns):
             cols = slice(column * BLOCK, (column + 1) * BLOCK)
-            value = jnp.dot(left, stacked(buffer, column, K_BLOCKS), preferred_element_type=F32)
-            if step > 0:
+            value = jnp.dot(left[0], pair[0][column], preferred_element_type=F32)
+            value = value + jnp.dot(left[1], pair[1][column], preferred_element_type=F32)
+            if line > 0:
                 value = total[:, cols] + value
-            if piece < 2 * pieces - 1:
+            if index < 2 * lines - 2:
                 total[:, cols] = value
                 continue
             value = jnp.maximum(gate_sum[:, cols], 0.0) * jnp.maximum(value, 0.0)
@@ -342,26 +339,36 @@
             for d in range(exp_count):
                 parts.append(value[d * CAP : (d + 1) * CAP, :] * mask[d : d + 1, cols])
             hidden[:, cols] = jnp.concatenate(parts, axis=0).astype(BF16)
-        fetch(piece + count)
-    for piece in range(2 * pieces, 2 * pieces + groups):
-        await_all(buffers[piece % count], sems.at[piece % count])
-
-
-def give_kernel(sizes, offset, hidden, weights, down, given, kept_weights, sem):
-    fetch_columns(sizes, down, offset, True, kept_weights, sem)
-    lines = down.shape[0] // BLOCK
-    for column in range(given.shape[1] // BLOCK):
-        value = jnp.dot(hidden[...], stacked(weights, column, lines), preferred_element_type=F32)
-        given[:, column * BLOCK : (column + 1) * BLOCK] = value.astype(BF16)
-    await_all(kept_weights, sem)
-
-
-def keep_kernel(sizes, hidden, weights, received, *outs):
-    exp_count, groups = sizes
-    lines = hidden.shape[1] // BLOCK
-    for column in range(received.shape[1] // BLOCK):
-        cols = slice(column * BLOCK, (column + 1) * BLOCK)
-        value = jnp.dot(hidden[...], stacked(weights, column, lines), preferred_element_type=F32)
+        for n in range(2):
+            fetch(index + n + count)
+    for index in range(2 * lines, 2 * lines + groups * given):
+        await_all(buffers[index % count], sems.at[index % count])
+
+
+def give_kernel(sizes, offset, hidden, *refs):
+    exp_count, groups = sizes
+    steps = (len(refs) - 3) // 2
+    weights, (down, given), kept_weights, sems = (
+        refs[:steps],
+        refs[steps : steps + 2],
+        refs[steps + 2 : -1],
+        refs[-1],
+    )
+    for step, buffer in enumerate(kept_weights):
+        fetch_columns(sizes, down, offset, True, step, buffer, sems.at[step])
+    for step, buffer in enumerate(weights):
+        value = jnp.dot(hidden[...], stacked(buffer), preferred_element_type=F32)
+        given[:, step * BLOCK : (step + 1) * BLOCK] = value.astype(BF16)
+    for step, buffer in enumerate(kept_weights):
+        await_all(buffer, sems.at[step])
+
+
+def keep_kernel(sizes, hidden, received, *refs):
+    exp_count, groups = sizes
+    weights, outs = refs[:-exp_count], refs[-exp_count:]
+    for step, buffer in enumerate(weights):
+        cols = slice(step * BLOCK, (step + 1) * BLOCK)
+        value = jnp.dot(hidden[...], stacked(buffer), preferred_element_type=F32)
         value = value + received[:, cols].astype(F32)
         for d in range(exp_count):
             outs[d][:, cols] = value[d * CAP : (d + 1) * CAP, :].astype(BF16)
@@ -448,13 +455,18 @@
         flops=2 * tok_count * slots * width,
         moved=4 * tok_count * features,
     )
-    blocks = K_BLOCKS * unit_width // BLOCK
+    blocks = unit_width // BLOCK
     buffer = ((blocks, BLOCK, BLOCK), BF16, pltpu.VMEM)
     piece_bytes = 2 * blocks * BLOCK * BLOCK
     mask, *ready = call(
         functools.partial(prepare_kernel, sizes, tok_count),
         [((max(8, exp_count), unit_width), F32)] + [buffer] * BUFFERS,
-        [(active_blocks, pltpu.HBM), (gate_weight, pltpu.HBM), (own, pl.ANY)],
+        [
+            (active_blocks, pltpu.HBM),
+            (gate_weight, pltpu.HBM),
+            (up_weight, pltpu.HBM),
+            (own, pl.ANY),
+        ],
         [
             pltpu.SMEM(active_blocks.shape, jnp.int32),
             pltpu.SemaphoreType.DMA,
@@ -497,25 +509,24 @@
             pltpu.SemaphoreType.DMA((BUFFERS,)),
         ],
         flops=2 * 2 * slots * features * unit_width,
-        moved=6 * piece_bytes,
+        moved=10 * piece_bytes,
         aliases={3 + n: 1 + n for n in range(BUFFERS)},
     )
-    first = 2 * features // (K_BLOCKS * BLOCK)
     part = features // unit_count
+    steps = part // BLOCK
     offsets = [(order + 1) % groups for order in range(groups)]
     given, kept_weights = [], []
     for order, offset in enumerate(offsets):
-        value, kept = call(
+        first = 2 * features // BLOCK + order * steps
+        value, *kept = call(
             functools.partial(give_kernel, sizes, offset),
-            [((slots, part), BF16), buffer],
-            [
-                (hidden, None),
-                (buffers[(first + order) % BUFFERS], pltpu.VMEM),
-                (down_weight, pltpu.HBM),
-            ],
-            [pltpu.SemaphoreType.DMA],
+            [((slots, part), BF16)] + [buffer] * steps,
+            [(hidden, None)]
+            + [(buffers[(first + step) % BUFFERS], pltpu.VMEM) for step in range(steps)]
+            + [(down_weight, pltpu.HBM)],
+            [pltpu.SemaphoreType.DMA((steps,))],
             flops=2 * slots * unit_width * part,
-            moved=piece_bytes,
+            moved=steps * piece_bytes,
         )
         given.append(value)
         kept_weights.append(kept)
@@ -525,7 +536,8 @@
         kept = call(
             functools.partial(keep_kernel, sizes),
             [((CAP, part), BF16)] * exp_count,
-            [(hidden, None), (kept_weights[order], pltpu.VMEM), (taken[order], None)],
+            [(hidden, None), (taken[order], None)]
+            + [(v, pltpu.VMEM) for v in kept_weights[order]],
             flops=2 * slots * unit_width * part,
             moved=piece_bytes,
         )
@@ -557,7 +569,8 @@
         and exp_count * unit_count // 2 == EXPERTS
         and TILE % tokens.shape[0] == 0
         and unit_width % BLOCK == 0
-        and tokens.shape[1] == READY * K_BLOCKS * BLOCK == unit_count * K_BLOCKS * BLOCK
+        and tokens.shape[1] % (unit_count * BLOCK) == 0
+        and tokens.shape[1] <= READY * BLOCK <= 2 * tokens.shape[1]
     )
     return (paired_experts if paired else spread_experts)(*operands)
 

time: 65.8 us -> 64.1 us (0.974)
  starting transfers between devices: 20 us -> 17.9 us
    ppermute x10, starting transfers between devices: 19.3 us -> 17.2 us  [shift(): return lax.ppermute(value, ('exp', 'unit'), pairs)]
  transfers between devices with their start and end apart: 13 -> 13, of which waited for: 4 -> 3; matrix products, arithmetic and copies ran while one was open for 0% -> 0% of each run, Pallas kernels for 26% -> 30%
where the time goes in v7:
time: 64.1 us; the launch traced here: 63.9 us
  Pallas kernels  37.4 us (58%)
  starting transfers between devices  17.9 us (28%)
  waiting for transfers between devices  8.43 us (13%)
    pallas_call x11, Pallas kernels, call(): pl.pallas_call(kernel, out_shape=shapes, in_specs=specs, out_specs=[vmem]...  37.4 us
    ppermute x10, starting transfers between devices, shift(): return lax.ppermute(value, ('exp', 'unit'), pairs)  17.2 us
    ppermute x10, waiting for transfers between devices, shift(): return lax.ppermute(value, ('exp', 'unit'), pairs)  6.57 us
    ppermute x3, waiting for transfers between devices, swap(): return lax.ppermute(value, 'unit', [(u, u ^ 1) for u in range(unit_count)])  1.86 us
  transfers between devices with their start and end apart: 13, of which 3 were waited for; matrix products, arithmetic and copies ran while one was open for 0% of the time, Pallas kernels for 30%

profile of v7, /device:TPU:0, one launch (start us, length us, event | category | flops | bytes accessed | tf_op | source)
XLA Modules:
  0.0 63.9 jit_solution(6474741353460582519)
XLA Ops:
  0.0 2.2 %shard_map.82 = (bf16[40,4096]{1,0:T(8,128)(2,1)S(1)}, bf16[40,2048]{1,0:T(8,128)(2,1)S(1)}, bf16[40,2048]{1,0:T(8,128)(2,1)S(1)}, bf16[40,2048]{1,0:T(8,128)(2,1)S(1)}) custom-call(bf16[128,4096]{1,0:T(8,128)(2,1)} %tokens_hbm.1, f32[1,4096]{1,0:T(1,128)} %bitcast.3, s32[2,128]{1,0:T(2,128)} %bitcast.4), custom_call_target="tpu_custom_call" | custom-call | flops 83886080 | bytes 2097152 | tf_op jit(solution)/shard_map/pallas_call | solution.py:401
  2.2 3.1 %collective-permute-start = (bf16[40,2048]{1,0:T(8,128)(2,1)S(1)}, bf16[40,2048]{1,0:T(8,128)(2,1)S(1)}, u32[]{:S(2)}, u32[]{:S(2)}) collective-permute-start(bf16[40,2048]{1,0:T(8,128)(2,1)S(1)} %get-tuple-element.45), channel_id=1, source_target_pairs={{0,4},{1,5},{2,6},{3,7},{4,8},{5,9},{6,10},{7,11},{8,12},{9,13},{1... | collective-permute-start | bytes 491528 | tf_op jit(solution)/shard_map/ppermute | solution.py:434
  5.2 2.6 %collective-permute-start.1 = (bf16[40,2048]{1,0:T(8,128)(2,1)S(1)}, bf16[40,2048]{1,0:T(8,128)(2,1)S(1)}, u32[]{:S(2)}, u32[]{:S(2)}) collective-permute-start(bf16[40,2048]{1,0:T(8,128)(2,1)S(1)} %get-tuple-element.46), channel_id=1, source_target_pairs={{0,8},{1,9},{2,10},{3,11},{4,12},{5,13},{6,14},{7,15},{8,0},{9,1},... | collective-permute-start | bytes 491528 | tf_op jit(solution)/shard_map/ppermute | solution.py:434
  7.8 1.3 %collective-permute-start.2 = (bf16[40,2048]{1,0:T(8,128)(2,1)S(1)}, bf16[40,2048]{1,0:T(8,128)(2,1)S(1)}, u32[]{:S(2)}, u32[]{:S(2)}) collective-permute-start(bf16[40,2048]{1,0:T(8,128)(2,1)S(1)} %get-tuple-element.47), channel_id=1, source_target_pairs={{0,12},{1,13},{2,14},{3,15},{4,0},{5,1},{6,2},{7,3},{8,4},{9,5},{1... | collective-permute-start | bytes 491528 | tf_op jit(solution)/shard_map/ppermute | solution.py:434
  9.2 11.9 %shard_map.83 = (f32[8,3584]{1,0:T(8,128)S(1)}, bf16[7,512,512]{2,1,0:T(8,128)(2,1)S(1)}, bf16[7,512,512]{2,1,0:T(8,128)(2,1)S(1)}, bf16[7,512,512]{2,1,0:T(8,12...) custom-call(s32[2,8,48]{2,1,0:T(8,128)} %active_hbm.1, ...), custom_call_target="tpu_custom_call" | custom-call | flops 167772160 | bytes 36700160 | tf_op jit(solution)/shard_map/pallas_call | solution.py:401
  21.1 0.0 collective-permute-done.refs_0_
  21.1 0.0 collective-permute-done.1.refs_1_
  21.1 0.0 collective-permute-done.2.refs_2_
  21.2 0.1 collective-permute-start.3
  21.3 1.9 %collective-permute-done.3.other = bf16[120,2048]{1,0:T(8,128)(2,1)S(1)} collective-permute-done((bf16[120,2048]{1,0:T(8,128)(2,1)S(1)}, bf16[120,2048]{1,0:T(8,128)(2,1)S(1)}, u32[]{:S(2)}, u32[]{:S(2)}) %collective-permute-start.3) | collective-permute-done | bytes 491552 | tf_op jit(solution)/shard_map/ppermute | solution.py:437
  23.1 12.0 %shard_map.86 = (bf16[160,3584]{1,0:T(8,128)(2,1)S(1)}, bf16[7,512,512]{2,1,0:T(8,128)(2,1)S(1)}, bf16[7,512,512]{2,1,0:T(8,128)(2,1)S(1)}, bf16[7,512,512]{2,1,...) custom-call(bf16[40,4096]{1,0:T(8,128)(2,1)S(1)} %get-tuple-element., ...), custom_call_target="tpu_custom_call", output_to_operand_aliasing={{1}: (3, {}), {2}: (4, {}), {3}: (5, {}), {4}: (6, {}), {5}... | custom-call | flops 9395240960 | bytes 36700160 | tf_op jit(solution)/shard_map/pallas_call | solution.py:401
  35.1 3.2 %shard_map.87 = (bf16[160,1024]{1,0:T(8,128)(2,1)S(1)}, bf16[7,512,512]{2,1,0:T(8,128)(2,1)S(1)}, bf16[7,512,512]{2,1,0:T(8,128)(2,1)S(1)}) custom-call(bf16[160,3584]{1,0:T(8,128)(2,1)S(1)} %get-tuple-element.62.hidden, bf16[7,512,512]{2,1,0:T(8,128)(2,1)S(1)} %get-tuple-element.63.refs_0_, bf16[7,512,512]{2,1,0:T(8,128)(2,1)S(1)} %get-tuple-element.64.refs_1_, ...), custom_call_target="tpu_custom_call" | custom-call | flops 1174405120 | bytes 7340032 | tf_op jit(solution)/shard_map/pallas_call | solution.py:401
  38.3 0.2 collective-permute-start.4
  38.5 3.1 %shard_map.90 = (bf16[160,1024]{1,0:T(8,128)(2,1)S(1)}, bf16[7,512,512]{2,1,0:T(8,128)(2,1)S(1)}, bf16[7,512,512]{2,1,0:T(8,128)(2,1)S(1)}) custom-call(bf16[160,3584]{1,0:T(8,128)(2,1)S(1)} %get-tuple-element.62.hidden, bf16[7,512,512]{2,1,0:T(8,128)(2,1)S(1)} %get-tuple-element.72.refs_0_, bf16[7,512,512]{2,1,0:T(8,128)(2,1)S(1)} %get-tuple-element.73.refs_1_, ...), custom_call_target="tpu_custom_call" | custom-call | flops 1174405120 | bytes 7340032 | tf_op jit(solution)/shard_map/pallas_call | solution.py:401
  41.7 0.4 collective-permute-start.9
  42.1 0.0 collective-permute-done.4.received
  42.1 1.4 %shard_map.88 = (bf16[40,1024]{1,0:T(8,128)(2,1)S(1)}, bf16[40,1024]{1,0:T(8,128)(2,1)S(1)}, bf16[40,1024]{1,0:T(8,128)(2,1)S(1)}, bf16[40,1024]{1,0:T(8,128)(2,1)S(1)}) custom-call(bf16[160,3584]{1,0:T(8,128)(2,1)S(1)} %get-tuple-element.62.hidden, bf16[160,1024]{1,0:T(8,128)(2,1)S(1)} %collective-permute-done.4.received, ...), custom_call_target="tpu_custom_call" | custom-call | flops 1174405120 | bytes 3670016 | tf_op jit(solution)/shard_map/pallas_call | solution.py:401
  43.5 1.6 %collective-permute-start.5 = (bf16[40,1024]{1,0:T(8,128)(2,1)S(1)}, bf16[40,1024]{1,0:T(8,128)(2,1)S(1)}, u32[]{:S(2)}, u32[]{:S(2)}) collective-permute-start(bf16[40,1024]{1,0:T(8,128)(2,1)S(1)} %get-tuple-element.68), channel_id=1, source_target_pairs={{0,2},{1,3},{2,0},{3,1},{4,6},{5,7},{6,4},{7,5},{8,10},{9,11},{10,... | collective-permute-start | bytes 245768 | tf_op jit(solution)/shard_map/ppermute | solution.py:434
  45.0 2.5 %collective-permute-start.6 = (bf16[40,1024]{1,0:T(8,128)(2,1)S(1)}, bf16[40,1024]{1,0:T(8,128)(2,1)S(1)}, u32[]{:S(2)}, u32[]{:S(2)}) collective-permute-start(bf16[40,1024]{1,0:T(8,128)(2,1)S(1)} %get-tuple-element.69), channel_id=1, source_target_pairs={{0,14},{1,15},{2,12},{3,13},{4,2},{5,3},{6,0},{7,1},{8,6},{9,7},{1... | collective-permute-start | bytes 245768 | tf_op jit(solution)/shard_map/ppermute | solution.py:434
  47.5 1.3 %collective-permute-start.7 = (bf16[40,1024]{1,0:T(8,128)(2,1)S(1)}, bf16[40,1024]{1,0:T(8,128)(2,1)S(1)}, u32[]{:S(2)}, u32[]{:S(2)}) collective-permute-start(bf16[40,1024]{1,0:T(8,128)(2,1)S(1)} %get-tuple-element.70), channel_id=1, source_target_pairs={{0,10},{1,11},{2,8},{3,9},{4,14},{5,15},{6,12},{7,13},{8,2},{9,3},... | collective-permute-start | bytes 245768 | tf_op jit(solution)/shard_map/ppermute | solution.py:434
  48.8 0.2 collective-permute-start.8
  49.0 0.0 collective-permute-done.9.received
  49.0 1.4 %shard_map.91 = (bf16[40,1024]{1,0:T(8,128)(2,1)S(1)}, bf16[40,1024]{1,0:T(8,128)(2,1)S(1)}, bf16[40,1024]{1,0:T(8,128)(2,1)S(1)}, bf16[40,1024]{1,0:T(8,128)(2,1)S(1)}) custom-call(bf16[160,3584]{1,0:T(8,128)(2,1)S(1)} %get-tuple-element.62.hidden, bf16[160,1024]{1,0:T(8,128)(2,1)S(1)} %collective-permute-done.9.received, ...), custom_call_target="tpu_custom_call" | custom-call | flops 1174405120 | bytes 3670016 | tf_op jit(solution)/shard_map/pallas_call | solution.py:401
  50.4 3.7 %collective-permute-start.10 = (bf16[40,1024]{1,0:T(8,128)(2,1)S(1)}, bf16[40,1024]{1,0:T(8,128)(2,1)S(1)}, u32[]{:S(2)}, u32[]{:S(2)}) collective-permute-start(bf16[40,1024]{1,0:T(8,128)(2,1)S(1)} %get-tuple-element.78), channel_id=1, source_target_pairs={{0,12},{1,13},{2,14},{3,15},{4,0},{5,1},{6,2},{7,3},{8,4},{9,5},{1... | collective-permute-start | bytes 245768 | tf_op jit(solution)/shard_map/ppermute | solution.py:434
  54.0 0.0 collective-permute-done.5.refs_0_
  54.0 0.7 %collective-permute-start.11 = (bf16[40,1024]{1,0:T(8,128)(2,1)S(1)}, bf16[40,1024]{1,0:T(8,128)(2,1)S(1)}, u32[]{:S(2)}, u32[]{:S(2)}) collective-permute-start(bf16[40,1024]{1,0:T(8,128)(2,1)S(1)} %get-tuple-element.79), channel_id=1, source_target_pairs={{0,8},{1,9},{2,10},{3,11},{4,12},{5,13},{6,14},{7,15},{8,0},{9,1},... | collective-permute-start | bytes 245768 | tf_op jit(solution)/shard_map/ppermute | solution.py:434
  54.8 0.0 collective-permute-done.6.refs_1_
  54.8 0.3 collective-permute-start.12
  55.1 1.0 %shard_map.85 = (bf16[2,128,256]{2,1,0:T(8,128)(2,1)S(1)}, bf16[2,128,256]{2,1,0:T(8,128)(2,1)S(1)}) custom-call(s32[2,128]{1,0:T(2,128)} %bitcast.5, f32[2,128]{1,0:T(2,128)} %bitcast.6, bf16[120,2048]{1,0:T(8,128)(2,1)S(1)} %shard_map.84.after.mine), custom_call_target="tpu_custom_call" | custom-call | bytes 2097152 | tf_op jit(solution)/shard_map/pallas_call | solution.py:401
  56.1 1.3 %collective-permute-done.7.refs_2_ = bf16[40,1024]{1,0:T(8,128)(2,1)S(1)} collective-permute-done((bf16[40,1024]{1,0:T(8,128)(2,1)S(1)}, bf16[40,1024]{1,0:T(8,128)(2,1)S(1)}, u32[]{:S(2)}, u32[]{:S(2)}) %collective-permute-start.7) | collective-permute-done | bytes 81952 | tf_op jit(solution)/shard_map/ppermute | solution.py:434
  57.4 0.0 collective-permute-done.8.refs_3_
  57.4 0.3 shard_map.89.refs_0_
  57.7 0.0 collective-permute-done.10.refs_2_
  57.7 5.2 %collective-permute-done.11.refs_3_ = bf16[40,1024]{1,0:T(8,128)(2,1)S(1)} collective-permute-done((bf16[40,1024]{1,0:T(8,128)(2,1)S(1)}, bf16[40,1024]{1,0:T(8,128)(2,1)S(1)}, u32[]{:S(2)}, u32[]{:S(2)}) %collective-permute-start.11) | collective-permute-done | bytes 81952 | tf_op jit(solution)/shard_map/ppermute | solution.py:434
  62.9 0.0 collective-permute-done.12.refs_4_
  62.9 1.0 %shard_map.92 = bf16[128,1024]{1,0:T(8,128)(2,1)} custom-call(bf16[2,128,256]{2,1,0:T(8,128)(2,1)S(1)} %get-tuple-element.48.high, bf16[2,128,256]{2,1,0:T(8,128)(2,1)S(1)} %get-tuple-element.49.low, f32[128,1024]{1,0:T(8,128)S(1)} %shard_map.89.refs_0_, bf16[40,1024]{1,0:T(8,128)(2,1)S(1)} %get-tuple-element.77.refs_1_, ...), custom_call_target="tpu_custom_call" | custom-call | flops 83886080 | bytes 1048576 | tf_op jit(solution)/shard_map/pallas_call | solution.py:401
  (1 shorter events, 0.0 us)
Async XLA Ops:
  2.2 18.9 %collective-permute-start = (bf16[40,2048]{1,0:T(8,128)(2,1)S(1)}, bf16[40,2048]{1,0:T(8,128)(2,1)S(1)}, u32[]{:S(2)}, u32[]{:S(2)}) collective-permute-start(bf16[40,2048]{1,0:T(8,128)(2,1)S(1)} %get-tuple-element.45), channel_id=1, source_target_pairs={{0,4},{1,5},{2,6},{3,7},{4,8},{5,9},{6,10},{7,11},{8,12},{9,13},{1... | collective-permute-start | bytes 491528 | tf_op jit(solution)/shard_map/ppermute | solution.py:434
  5.2 15.9 %collective-permute-start.1 = (bf16[40,2048]{1,0:T(8,128)(2,1)S(1)}, bf16[40,2048]{1,0:T(8,128)(2,1)S(1)}, u32[]{:S(2)}, u32[]{:S(2)}) collective-permute-start(bf16[40,2048]{1,0:T(8,128)(2,1)S(1)} %get-tuple-element.46), channel_id=1, source_target_pairs={{0,8},{1,9},{2,10},{3,11},{4,12},{5,13},{6,14},{7,15},{8,0},{9,1},... | collective-permute-start | bytes 491528 | tf_op jit(solution)/shard_map/ppermute | solution.py:434
  7.8 13.3 %collective-permute-start.2 = (bf16[40,2048]{1,0:T(8,128)(2,1)S(1)}, bf16[40,2048]{1,0:T(8,128)(2,1)S(1)}, u32[]{:S(2)}, u32[]{:S(2)}) collective-permute-start(bf16[40,2048]{1,0:T(8,128)(2,1)S(1)} %get-tuple-element.47), channel_id=1, source_target_pairs={{0,12},{1,13},{2,14},{3,15},{4,0},{5,1},{6,2},{7,3},{8,4},{9,5},{1... | collective-permute-start | bytes 491528 | tf_op jit(solution)/shard_map/ppermute | solution.py:434
  21.2 1.9 %collective-permute-start.3 = (bf16[120,2048]{1,0:T(8,128)(2,1)S(1)}, bf16[120,2048]{1,0:T(8,128)(2,1)S(1)}, u32[]{:S(2)}, u32[]{:S(2)}) collective-permute-start(bf16[120,2048]{1,0:T(8,128)(2,1)S(1)} %shard_map.84.after.mine), channel_id=1, source_target_pairs={{0,1},{1,0},{2,3},{3,2},{4,5},{5,4},{6,7},{7,6},{8,9},{9,8},{10,11... | collective-permute-start | bytes 1474568 | tf_op jit(solution)/shard_map/ppermute | solution.py:437
  38.3 3.8 %collective-permute-start.4 = (bf16[160,1024]{1,0:T(8,128)(2,1)S(1)}, bf16[160,1024]{1,0:T(8,128)(2,1)S(1)}, u32[]{:S(2)}, u32[]{:S(2)}) collective-permute-start(bf16[160,1024]{1,0:T(8,128)(2,1)S(1)} %get-tuple-element.65), channel_id=1, source_target_pairs={{0,1},{1,0},{2,3},{3,2},{4,5},{5,4},{6,7},{7,6},{8,9},{9,8},{10,11... | collective-permute-start | bytes 983048 | tf_op jit(solution)/shard_map/ppermute | solution.py:437
  41.7 7.3 %collective-permute-start.9 = (bf16[160,1024]{1,0:T(8,128)(2,1)S(1)}, bf16[160,1024]{1,0:T(8,128)(2,1)S(1)}, u32[]{:S(2)}, u32[]{:S(2)}) collective-permute-start(bf16[160,1024]{1,0:T(8,128)(2,1)S(1)} %get-tuple-element.74), channel_id=1, source_target_pairs={{0,1},{1,0},{2,3},{3,2},{4,5},{5,4},{6,7},{7,6},{8,9},{9,8},{10,11... | collective-permute-start | bytes 983048 | tf_op jit(solution)/shard_map/ppermute | solution.py:437
  43.5 10.6 %collective-permute-start.5 = (bf16[40,1024]{1,0:T(8,128)(2,1)S(1)}, bf16[40,1024]{1,0:T(8,128)(2,1)S(1)}, u32[]{:S(2)}, u32[]{:S(2)}) collective-permute-start(bf16[40,1024]{1,0:T(8,128)(2,1)S(1)} %get-tuple-element.68), channel_id=1, source_target_pairs={{0,2},{1,3},{2,0},{3,1},{4,6},{5,7},{6,4},{7,5},{8,10},{9,11},{10,... | collective-permute-start | bytes 245768 | tf_op jit(solution)/shard_map/ppermute | solution.py:434
  45.0 9.7 %collective-permute-start.6 = (bf16[40,1024]{1,0:T(8,128)(2,1)S(1)}, bf16[40,1024]{1,0:T(8,128)(2,1)S(1)}, u32[]{:S(2)}, u32[]{:S(2)}) collective-permute-start(bf16[40,1024]{1,0:T(8,128)(2,1)S(1)} %get-tuple-element.69), channel_id=1, source_target_pairs={{0,14},{1,15},{2,12},{3,13},{4,2},{5,3},{6,0},{7,1},{8,6},{9,7},{1... | collective-permute-start | bytes 245768 | tf_op jit(solution)/shard_map/ppermute | solution.py:434
  47.5 9.9 %collective-permute-start.7 = (bf16[40,1024]{1,0:T(8,128)(2,1)S(1)}, bf16[40,1024]{1,0:T(8,128)(2,1)S(1)}, u32[]{:S(2)}, u32[]{:S(2)}) collective-permute-start(bf16[40,1024]{1,0:T(8,128)(2,1)S(1)} %get-tuple-element.70), channel_id=1, source_target_pairs={{0,10},{1,11},{2,8},{3,9},{4,14},{5,15},{6,12},{7,13},{8,2},{9,3},... | collective-permute-start | bytes 245768 | tf_op jit(solution)/shard_map/ppermute | solution.py:434
  48.8 8.6 %collective-permute-start.8 = (bf16[40,1024]{1,0:T(8,128)(2,1)S(1)}, bf16[40,1024]{1,0:T(8,128)(2,1)S(1)}, u32[]{:S(2)}, u32[]{:S(2)}) collective-permute-start(bf16[40,1024]{1,0:T(8,128)(2,1)S(1)} %get-tuple-element.71), channel_id=1, source_target_pairs={{0,6},{1,7},{2,4},{3,5},{4,10},{5,11},{6,8},{7,9},{8,14},{9,15},{1... | collective-permute-start | bytes 245768 | tf_op jit(solution)/shard_map/ppermute | solution.py:434
  50.4 7.4 %collective-permute-start.10 = (bf16[40,1024]{1,0:T(8,128)(2,1)S(1)}, bf16[40,1024]{1,0:T(8,128)(2,1)S(1)}, u32[]{:S(2)}, u32[]{:S(2)}) collective-permute-start(bf16[40,1024]{1,0:T(8,128)(2,1)S(1)} %get-tuple-element.78), channel_id=1, source_target_pairs={{0,12},{1,13},{2,14},{3,15},{4,0},{5,1},{6,2},{7,3},{8,4},{9,5},{1... | collective-permute-start | bytes 245768 | tf_op jit(solution)/shard_map/ppermute | solution.py:434
  54.0 8.9 %collective-permute-start.11 = (bf16[40,1024]{1,0:T(8,128)(2,1)S(1)}, bf16[40,1024]{1,0:T(8,128)(2,1)S(1)}, u32[]{:S(2)}, u32[]{:S(2)}) collective-permute-start(bf16[40,1024]{1,0:T(8,128)(2,1)S(1)} %get-tuple-element.79), channel_id=1, source_target_pairs={{0,8},{1,9},{2,10},{3,11},{4,12},{5,13},{6,14},{7,15},{8,0},{9,1},... | collective-permute-start | bytes 245768 | tf_op jit(solution)/shard_map/ppermute | solution.py:434
  54.8 8.2 %collective-permute-start.12 = (bf16[40,1024]{1,0:T(8,128)(2,1)S(1)}, bf16[40,1024]{1,0:T(8,128)(2,1)S(1)}, u32[]{:S(2)}, u32[]{:S(2)}) collective-permute-start(bf16[40,1024]{1,0:T(8,128)(2,1)S(1)} %get-tuple-element.80), channel_id=1, source_target_pairs={{0,4},{1,5},{2,6},{3,7},{4,8},{5,9},{6,10},{7,11},{8,12},{9,13},{1... | collective-permute-start | bytes 245768 | tf_op jit(solution)/shard_map/ppermute | solution.py:434

commit v8 on v7

--- a/solution.py
+++ b/solution.py
@@ -17,7 +17,7 @@
 EPSILON = 1e-05
 
 BLOCK = 512
-READY = 10
+READY = 11
 BUFFERS = 12
 LIMIT = 8
 
@@ -155,35 +155,6 @@
     return lax.rem(z + distance, exp_count) * groups + g
 
 
-def route_kernel(sizes, width, tokens_hbm, gain_hbm, ids_hbm, own, *rest):
-    exp_count, groups = sizes
-    sends, (tokens, normed, gain, ids, sems) = rest[:-5], rest[-5:]
-    pairs = ((tokens_hbm, tokens), (gain_hbm, gain), (ids_hbm, ids))
-    copies = [pltpu.make_async_copy(a, b, sems.at[n]) for n, (a, b) in enumerate(pairs)]
-    for copy in copies:
-        copy.start()
-    rows, features = tokens.shape
-    z, g, s = place(sizes)
-    for copy in copies:
-        copy.wait()
-    step = 16
-    for first in range(0, rows, step):
-        values = tokens[first : first + step, :].astype(F32)
-        mean = jnp.sum(values * values, axis=1, keepdims=True) * (1.0 / features)
-        inv_rms = lax.rsqrt(mean + EPSILON)
-        normed[first : first + step, :] = (values * inv_rms * gain[...]).astype(BF16)
-    named, before = count_earlier(ids, group_experts(exp_count, groups, z, g, rows))
-    picks = [pick_rows(named, before, d) for d in range(exp_count)]
-    others = jnp.concatenate(picks[1:], axis=0).astype(BF16)
-    start = pl.multiple_of(s * (features // 2), 128)
-    found = jnp.dot(others, normed[:, pl.ds(start, width)], preferred_element_type=F32)
-    for d, send in enumerate(sends):
-        send[...] = found[d * CAP : (d + 1) * CAP, :].astype(BF16)
-    own[...] = jnp.dot(
-        picks[0].astype(BF16), normed[...], preferred_element_type=F32
-    ).astype(BF16)
-
-
 def fetch_rows(weight, line, buffer, sem):
     def start(index, carry):
         pltpu.make_async_copy(
@@ -227,6 +198,49 @@
     return buffer[...].reshape(buffer.shape[0] * BLOCK, BLOCK)
 
 
+def route_kernel(sizes, width, tokens_hbm, gain_hbm, ids_hbm, gate, own, buffer, *rest):
+    exp_count, groups = sizes
+    sends, (tokens, normed, gain, ids, sems, gate_sem) = rest[:-6], rest[-6:]
+    rows, features = tokens.shape
+    count = 4
+    lines = [pl.ds(n * (rows // count), rows // count) for n in range(count)]
+    pairs = [(gain_hbm, gain), (ids_hbm, ids)]
+    pairs += [(tokens_hbm.at[part, :], tokens.at[part, :]) for part in lines]
+    copies = [pltpu.make_async_copy(a, b, sems.at[n]) for n, (a, b) in enumerate(pairs)]
+    for copy in copies:
+        copy.start()
+    fetch_rows(gate, 0, buffer, gate_sem)
+    z, g, s = place(sizes)
+    copies[0].wait()
+    copies[1].wait()
+    named, before = count_earlier(ids, group_experts(exp_count, groups, z, g, rows))
+    picks = [pick_rows(named, before, d) for d in range(exp_count)]
+    others = jnp.concatenate(picks[1:], axis=0).astype(BF16)
+    step = 16
+    for first in range(0, rows, step):
+        if first % (rows // count) == 0:
+            copies[2 + first // (rows // count)].wait()
+        values = tokens[first : first + step, :].astype(F32)
+        mean = jnp.sum(values * values, axis=1, keepdims=True) * (1.0 / features)
+        inv_rms = lax.rsqrt(mean + EPSILON)
+        normed[first : first + step, :] = (values * inv_rms * gain[...]).astype(BF16)
+    start = pl.multiple_of(s * (features // 2), 128)
+    found = jnp.dot(others, normed[:, pl.ds(start, width)], preferred_element_type=F32)
+    for d, send in enumerate(sends):
+        send[...] = found[d * CAP : (d + 1) * CAP, :].astype(BF16)
+    own[...] = jnp.dot(
+        picks[0].astype(BF16), normed[...], preferred_element_type=F32
+    ).astype(BF16)
+    await_all(buffer, gate_sem)
+
+
+def arrivals(sizes):
+    exp_count, groups = sizes
+    early = [(o, d) for o in range(1, groups) for d in range(1, exp_count)] + [(0, 0)]
+    late = [(0, d) for d in range(1, exp_count)] + [(o, 0) for o in range(1, groups)]
+    return early, late
+
+
 def table_kernel(sizes, ids_hbm, weights_hbm, after, combine_high, combine_low, ids, weights, sems):
     exp_count, groups = sizes
     pairs = ((ids_hbm, ids), (weights_hbm, weights))
@@ -239,32 +253,41 @@
     z, g, s = place(sizes)
     zero = jnp.zeros((CAP, rows), F32)
     padded = combine_high.shape[2]
-    for order in range(groups):
-        group = lax.rem(g - (order + 1) % groups + groups, groups)
-        named, before = count_earlier(ids, group_experts(exp_count, groups, z, group, rows))
+    batches = arrivals(sizes)
+    experts = [
+        lax.rem(z + d, exp_count) * groups + lax.rem(g - o + groups, groups)
+        for batch in batches
+        for o, d in batch
+    ]
+    line = lax.broadcasted_iota(jnp.int32, (max(8, len(experts)), rows), 0)
+    listed = jnp.full(line.shape, -1, jnp.int32)
+    for n, expert in enumerate(experts):
+        listed = jnp.where(line == n, expert, listed)
+    named, before = count_earlier(ids, listed)
+    for order, batch in enumerate(batches):
         parts = []
-        for d in range(exp_count):
-            here = pick_rows(named, before, d) > 0
-            expert = lax.rem(z + d, exp_count) * groups + group
-            first = jnp.where(here & (ids[0:1, :] == expert), weights[0:1, :], zero)
-            second = jnp.where(here & (ids[1:2, :] == expert), weights[1:2, :], zero)
+        for n in range(len(batch)):
+            entry = order * len(batch) + n
+            here = pick_rows(named, before, entry) > 0
+            first = jnp.where(here & (ids[0:1, :] == experts[entry]), weights[0:1, :], zero)
+            second = jnp.where(here & (ids[1:2, :] == experts[entry]), weights[1:2, :], zero)
             parts.append(first + second)
-        if padded > exp_count * CAP:
-            parts.append(jnp.zeros((padded - exp_count * CAP, rows), F32))
+        if padded > len(batch) * CAP:
+            parts.append(jnp.zeros((padded - len(batch) * CAP, rows), F32))
         table = jnp.concatenate(parts, axis=0).T
         high = table.astype(BF16)
         combine_high[order] = high
         combine_low[order] = (table - high.astype(F32)).astype(BF16)
 
 
-def prepare_kernel(sizes, rows, active_hbm, gate, up, after, mask, *rest):
+def prepare_kernel(sizes, rows, active_hbm, gate, up, after, _, mask, *rest):
     exp_count, groups = sizes
     *buffers, active, small_sem, sems = rest
     z, g, s = place(sizes)
     small = pltpu.make_async_copy(active_hbm, active, small_sem)
     small.start()
     lines = gate.shape[0] // BLOCK
-    for n, buffer in enumerate(buffers[:READY]):
+    for n, buffer in enumerate(buffers[1:READY], 1):
         fetch_rows(gate if n < lines else up, n % lines, buffer, sems.at[n])
     small.wait()
     unit_width = mask.shape[1]
@@ -280,7 +303,7 @@
         return jnp.where(blocks == entry, 1.0, found)
 
     mask[...] = lax.fori_loop(0, active.shape[2], add_entry, jnp.zeros(mask.shape, F32))
-    for n, buffer in enumerate(buffers[:READY]):
+    for n, buffer in enumerate(buffers[1:READY], 1):
         await_all(buffer, sems.at[n])
 
 
@@ -365,13 +388,18 @@
 
 def keep_kernel(sizes, hidden, received, *refs):
     exp_count, groups = sizes
-    weights, outs = refs[:-exp_count], refs[-exp_count:]
+    passed = (len(refs) - received.shape[1] // BLOCK - exp_count) // 2
+    weights = refs[: received.shape[1] // BLOCK]
+    handed = refs[len(weights) : len(weights) + passed]
+    outs = refs[len(weights) + passed :]
     for step, buffer in enumerate(weights):
         cols = slice(step * BLOCK, (step + 1) * BLOCK)
         value = jnp.dot(hidden[...], stacked(buffer), preferred_element_type=F32)
         value = value + received[:, cols].astype(F32)
         for d in range(exp_count):
             outs[d][:, cols] = value[d * CAP : (d + 1) * CAP, :].astype(BF16)
+    for given, out in zip(handed, outs[exp_count:]):
+        out[...] = given[...]
 
 
 def combine_kernel(order, high, low, *refs):
@@ -437,27 +465,28 @@
         return lax.ppermute(value, "unit", [(u, u ^ 1) for u in range(unit_count)])
 
     batch = exp_count - 1
-    own, *sends = call(
+    buffer = ((unit_width // BLOCK, BLOCK, BLOCK), BF16, pltpu.VMEM)
+    piece_bytes = 2 * unit_width * BLOCK
+    own, ready, *sends = call(
         functools.partial(route_kernel, sizes, width),
-        [((CAP, features), BF16)] + [((CAP, width), BF16)] * batch,
+        [((CAP, features), BF16), buffer] + [((CAP, width), BF16)] * batch,
         [
             (tokens, pltpu.HBM),
             (norm_gain.reshape(1, -1), pltpu.HBM),
             (ids, pltpu.HBM),
+            (gate_weight, pltpu.HBM),
         ],
         [
             pltpu.VMEM((tok_count, features), BF16),
             pltpu.VMEM((tok_count, features), BF16),
             pltpu.VMEM((1, features), F32),
             pltpu.VMEM(ids.shape, jnp.int32),
-            pltpu.SemaphoreType.DMA((3,)),
+            pltpu.SemaphoreType.DMA((6,)),
+            pltpu.SemaphoreType.DMA,
         ],
         flops=2 * tok_count * slots * width,
-        moved=4 * tok_count * features,
-    )
-    blocks = unit_width // BLOCK
-    buffer = ((blocks, BLOCK, BLOCK), BF16, pltpu.VMEM)
-    piece_bytes = 2 * blocks * BLOCK * BLOCK
+        moved=4 * tok_count * features + piece_bytes,
+    )
     mask, *ready = call(
         functools.partial(prepare_kernel, sizes, tok_count),
         [((max(8, exp_count), unit_width), F32)] + [buffer] * BUFFERS,
@@ -466,6 +495,7 @@
             (gate_weight, pltpu.HBM),
             (up_weight, pltpu.HBM),
             (own, pl.ANY),
+            (ready, pltpu.VMEM),
         ],
         [
             pltpu.SMEM(active_blocks.shape, jnp.int32),
@@ -473,7 +503,8 @@
             pltpu.SemaphoreType.DMA((READY,)),
         ],
         flops=2 * tok_count * slots * features,
-        moved=READY * piece_bytes,
+        moved=(READY - 1) * piece_bytes,
+        aliases={4: 1},
     )
     arrived = [shift(value, d + 1) for d, value in enumerate(sends)]
     mine = call(
@@ -486,7 +517,7 @@
     padded = -(-slots // 128) * 128
     combine_high, combine_low = call(
         functools.partial(table_kernel, sizes),
-        [((groups, tok_count, padded), BF16)] * 2,
+        [((2, tok_count, padded), BF16)] * 2,
         [(ids, pltpu.HBM), (weights, pltpu.HBM), (mine, pl.ANY)],
         [
             pltpu.VMEM(ids.shape, jnp.int32),
@@ -531,28 +562,35 @@
         given.append(value)
         kept_weights.append(kept)
     taken = [swap(value) for value in given]
-    homes = []
+    kept, stays = {}, []
     for order, offset in enumerate(offsets):
-        kept = call(
+        last = order == groups - 1
+        outs = call(
             functools.partial(keep_kernel, sizes),
-            [((CAP, part), BF16)] * exp_count,
+            [((CAP, part), BF16)] * (exp_count + (len(stays) if last else 0)),
             [(hidden, None), (taken[order], None)]
-            + [(v, pltpu.VMEM) for v in kept_weights[order]],
+            + [(v, pltpu.VMEM) for v in kept_weights[order]]
+            + [(v, None) for v in (stays if last else [])],
             flops=2 * slots * unit_width * part,
             moved=piece_bytes,
         )
-        homes.append(
-            [shift(v, -d, offset) if d or offset else v for d, v in enumerate(kept)]
-        )
+        for d in range(exp_count):
+            kept[offset, d] = outs[d]
+        if last:
+            for n, other_offset in enumerate(offsets[:-1]):
+                kept[other_offset, 0] = outs[exp_count + n]
+        else:
+            stays.append(outs[0])
+    home = {(o, d): shift(v, -d, o) if o or d else v for (o, d), v in kept.items()}
     mixed = None
-    for order, home in enumerate(homes):
-        last = order == groups - 1
+    for order, batch in enumerate(arrivals(sizes)):
+        last = order == 1
         mixed = call(
             functools.partial(combine_kernel, order),
             [((tok_count, part), BF16 if last else F32)],
             [(combine_high, None), (combine_low, None)]
             + ([(mixed, None)] if order else [])
-            + [(v, None) for v in home],
+            + [(home[key], None) for key in batch],
             flops=4 * tok_count * slots * part,
             moved=1 << 20,
         )[0]
@@ -569,6 +607,7 @@
         and exp_count * unit_count // 2 == EXPERTS
         and TILE % tokens.shape[0] == 0
         and unit_width % BLOCK == 0
+        and unit_count == 4
         and tokens.shape[1] % (unit_count * BLOCK) == 0
         and tokens.shape[1] <= READY * BLOCK <= 2 * tokens.shape[1]
     )

time: 64.1 us -> 64.4 us (level)
  waiting for transfers between devices: 8.43 us -> 9.65 us
    ppermute x10, waiting for transfers between devices: 6.57 us -> 7.79 us  [shift(): return lax.ppermute(value, ('exp', 'unit'), pairs)]
  transfers between devices with their start and end apart: 13 -> 13, of which waited for: 3 -> 4; matrix products, arithmetic and copies ran while one was open for 0% -> 0% of each run, Pallas kernels for 30% -> 30%
where the time goes in v8:
time: 64.4 us; the launch traced here: 64.1 us
  Pallas kernels  36.8 us (57%)
  starting transfers between devices  17.5 us (27%)
  waiting for transfers between devices  9.65 us (15%)
    pallas_call x11, Pallas kernels, call(): pl.pallas_call(kernel, out_shape=shapes, in_specs=specs, out_specs=[vmem]...  36.8 us
    ppermute x10, starting transfers between devices, shift(): return lax.ppermute(value, ('exp', 'unit'), pairs)  16.8 us
    ppermute x10, waiting for transfers between devices, shift(): return lax.ppermute(value, ('exp', 'unit'), pairs)  7.79 us
    ppermute x3, waiting for transfers between devices, swap(): return lax.ppermute(value, 'unit', [(u, u ^ 1) for u in range(unit_count)])  1.86 us
  transfers between devices with their start and end apart: 13, of which 4 were waited for; matrix products, arithmetic and copies ran while one was open for 0% of the time, Pallas kernels for 30%

profile of v8, /device:TPU:0, one launch (start us, length us, event | category | flops | bytes accessed | tf_op | source)
XLA Modules:
  0.0 64.1 jit_solution(3141502772464759817)
XLA Ops:
  0.0 2.4 %shard_map.82 = (bf16[40,4096]{1,0:T(8,128)(2,1)S(1)}, bf16[7,512,512]{2,1,0:T(8,128)(2,1)S(1)}, bf16[40,2048]{1,0:T(8,128)(2,1)S(1)}, bf16[40,2048]{1,0:T(8,128)(2,1)S(1)}, bf16[40,2048]{1,0:T(8,128)(2,1)S(1)}) custom-call(bf16[128,4096]{1,0:T(8,128)(2,1)} %tokens_hbm.1, f32[1,4096]{1,0:T(1,128)} %bitcast.3, s32[2,128]{1,0:T(2,128)} %bitcast.4, ...), custom_call_target="tpu_custom_call" | custom-call | flops 83886080 | bytes 5767168 | tf_op jit(solution)/shard_map/pallas_call | solution.py:429
  2.4 3.1 %collective-permute-start = (bf16[40,2048]{1,0:T(8,128)(2,1)S(1)}, bf16[40,2048]{1,0:T(8,128)(2,1)S(1)}, u32[]{:S(2)}, u32[]{:S(2)}) collective-permute-start(bf16[40,2048]{1,0:T(8,128)(2,1)S(1)} %get-tuple-element.48), channel_id=1, source_target_pairs={{0,4},{1,5},{2,6},{3,7},{4,8},{5,9},{6,10},{7,11},{8,12},{9,13},{1... | collective-permute-start | bytes 491528 | tf_op jit(solution)/shard_map/ppermute | solution.py:462
  5.5 2.6 %collective-permute-start.1 = (bf16[40,2048]{1,0:T(8,128)(2,1)S(1)}, bf16[40,2048]{1,0:T(8,128)(2,1)S(1)}, u32[]{:S(2)}, u32[]{:S(2)}) collective-permute-start(bf16[40,2048]{1,0:T(8,128)(2,1)S(1)} %get-tuple-element.49), channel_id=1, source_target_pairs={{0,8},{1,9},{2,10},{3,11},{4,12},{5,13},{6,14},{7,15},{8,0},{9,1},... | collective-permute-start | bytes 491528 | tf_op jit(solution)/shard_map/ppermute | solution.py:462
  8.1 1.3 %collective-permute-start.2 = (bf16[40,2048]{1,0:T(8,128)(2,1)S(1)}, bf16[40,2048]{1,0:T(8,128)(2,1)S(1)}, u32[]{:S(2)}, u32[]{:S(2)}) collective-permute-start(bf16[40,2048]{1,0:T(8,128)(2,1)S(1)} %get-tuple-element.50), channel_id=1, source_target_pairs={{0,12},{1,13},{2,14},{3,15},{4,0},{5,1},{6,2},{7,3},{8,4},{9,5},{1... | collective-permute-start | bytes 491528 | tf_op jit(solution)/shard_map/ppermute | solution.py:462
  9.4 11.9 %shard_map.83 = (f32[8,3584]{1,0:T(8,128)S(1)}, bf16[7,512,512]{2,1,0:T(8,128)(2,1)S(1)}, bf16[7,512,512]{2,1,0:T(8,128)(2,1)S(1)}, bf16[7,512,512]{2,1,0:T(8,12...) custom-call(s32[2,8,48]{2,1,0:T(8,128)} %active_hbm.1, ...), custom_call_target="tpu_custom_call", output_to_operand_aliasing={{1}: (4, {})} | custom-call | flops 167772160 | bytes 36700160 | tf_op jit(solution)/shard_map/pallas_call | solution.py:429
  21.4 0.0 collective-permute-done.refs_0_
  21.4 0.0 collective-permute-done.1.refs_1_
  21.4 0.0 collective-permute-done.2.refs_2_
  21.4 0.1 collective-permute-start.3
  21.5 1.9 %collective-permute-done.3.other = bf16[120,2048]{1,0:T(8,128)(2,1)S(1)} collective-permute-done((bf16[120,2048]{1,0:T(8,128)(2,1)S(1)}, bf16[120,2048]{1,0:T(8,128)(2,1)S(1)}, u32[]{:S(2)}, u32[]{:S(2)}) %collective-permute-start.3) | collective-permute-done | bytes 491552 | tf_op jit(solution)/shard_map/ppermute | solution.py:465
  23.4 11.2 %shard_map.86 = (bf16[160,3584]{1,0:T(8,128)(2,1)S(1)}, bf16[7,512,512]{2,1,0:T(8,128)(2,1)S(1)}, bf16[7,512,512]{2,1,0:T(8,128)(2,1)S(1)}, bf16[7,512,512]{2,1,...) custom-call(bf16[40,4096]{1,0:T(8,128)(2,1)S(1)} %get-tuple-element., ...), custom_call_target="tpu_custom_call", output_to_operand_aliasing={{1}: (3, {}), {2}: (4, {}), {3}: (5, {}), {4}: (6, {}), {5}... | custom-call | flops 9395240960 | bytes 36700160 | tf_op jit(solution)/shard_map/pallas_call | solution.py:429
  34.5 3.2 %shard_map.87 = (bf16[160,1024]{1,0:T(8,128)(2,1)S(1)}, bf16[7,512,512]{2,1,0:T(8,128)(2,1)S(1)}, bf16[7,512,512]{2,1,0:T(8,128)(2,1)S(1)}) custom-call(bf16[160,3584]{1,0:T(8,128)(2,1)S(1)} %get-tuple-element.65.hidden, bf16[7,512,512]{2,1,0:T(8,128)(2,1)S(1)} %get-tuple-element.66.refs_0_, bf16[7,512,512]{2,1,0:T(8,128)(2,1)S(1)} %get-tuple-element.67.refs_1_, ...), custom_call_target="tpu_custom_call" | custom-call | flops 1174405120 | bytes 7340032 | tf_op jit(solution)/shard_map/pallas_call | solution.py:429
  37.7 0.2 collective-permute-start.4
  37.9 3.1 %shard_map.89 = (bf16[160,1024]{1,0:T(8,128)(2,1)S(1)}, bf16[7,512,512]{2,1,0:T(8,128)(2,1)S(1)}, bf16[7,512,512]{2,1,0:T(8,128)(2,1)S(1)}) custom-call(bf16[160,3584]{1,0:T(8,128)(2,1)S(1)} %get-tuple-element.65.hidden, bf16[7,512,512]{2,1,0:T(8,128)(2,1)S(1)} %get-tuple-element.74.refs_0_, bf16[7,512,512]{2,1,0:T(8,128)(2,1)S(1)} %get-tuple-element.75.refs_1_, ...), custom_call_target="tpu_custom_call" | custom-call | flops 1174405120 | bytes 7340032 | tf_op jit(solution)/shard_map/pallas_call | solution.py:429
  41.1 0.4 collective-permute-start.8
  41.5 0.0 collective-permute-done.4.received
  41.5 1.4 %shard_map.88 = (bf16[40,1024]{1,0:T(8,128)(2,1)S(1)}, bf16[40,1024]{1,0:T(8,128)(2,1)S(1)}, bf16[40,1024]{1,0:T(8,128)(2,1)S(1)}, bf16[40,1024]{1,0:T(8,128)(2,1)S(1)}) custom-call(bf16[160,3584]{1,0:T(8,128)(2,1)S(1)} %get-tuple-element.65.hidden, bf16[160,1024]{1,0:T(8,128)(2,1)S(1)} %collective-permute-done.4.received, ...), custom_call_target="tpu_custom_call" | custom-call | flops 1174405120 | bytes 3670016 | tf_op jit(solution)/shard_map/pallas_call | solution.py:429
  42.9 3.5 %collective-permute-start.5 = (bf16[40,1024]{1,0:T(8,128)(2,1)S(1)}, bf16[40,1024]{1,0:T(8,128)(2,1)S(1)}, u32[]{:S(2)}, u32[]{:S(2)}) collective-permute-start(bf16[40,1024]{1,0:T(8,128)(2,1)S(1)} %get-tuple-element.71), channel_id=1, source_target_pairs={{0,14},{1,15},{2,12},{3,13},{4,2},{5,3},{6,0},{7,1},{8,6},{9,7},{1... | collective-permute-start | bytes 245768 | tf_op jit(solution)/shard_map/ppermute | solution.py:462
  46.3 0.4 collective-permute-start.6
  46.7 0.5 collective-permute-start.7
  47.2 0.0 collective-permute-done.8.received
  47.2 1.4 %shard_map.90 = (bf16[40,1024]{1,0:T(8,128)(2,1)S(1)}, bf16[40,1024]{1,0:T(8,128)(2,1)S(1)}, bf16[40,1024]{1,0:T(8,128)(2,1)S(1)}, bf16[40,1024]{1,0:T(8,128)(2,1)S(1)}, bf16[40,1024]{1,0:T(8,128)(2,1)S(1)}) custom-call(bf16[160,3584]{1,0:T(8,128)(2,1)S(1)} %get-tuple-element.65.hidden, bf16[160,1024]{1,0:T(8,128)(2,1)S(1)} %collective-permute-done.8.received, ...), custom_call_target="tpu_custom_call" | custom-call | flops 1174405120 | bytes 3670016 | tf_op jit(solution)/shard_map/pallas_call | solution.py:429
  48.5 2.6 %collective-permute-start.10 = (bf16[40,1024]{1,0:T(8,128)(2,1)S(1)}, bf16[40,1024]{1,0:T(8,128)(2,1)S(1)}, u32[]{:S(2)}, u32[]{:S(2)}) collective-permute-start(bf16[40,1024]{1,0:T(8,128)(2,1)S(1)} %get-tuple-element.82), channel_id=1, source_target_pairs={{0,8},{1,9},{2,10},{3,11},{4,12},{5,13},{6,14},{7,15},{8,0},{9,1},... | collective-permute-start | bytes 245768 | tf_op jit(solution)/shard_map/ppermute | solution.py:462
  51.1 2.3 %collective-permute-start.11 = (bf16[40,1024]{1,0:T(8,128)(2,1)S(1)}, bf16[40,1024]{1,0:T(8,128)(2,1)S(1)}, u32[]{:S(2)}, u32[]{:S(2)}) collective-permute-start(bf16[40,1024]{1,0:T(8,128)(2,1)S(1)} %get-tuple-element.83), channel_id=1, source_target_pairs={{0,4},{1,5},{2,6},{3,7},{4,8},{5,9},{6,10},{7,11},{8,12},{9,13},{1... | collective-permute-start | bytes 245768 | tf_op jit(solution)/shard_map/ppermute | solution.py:462
  53.5 0.0 collective-permute-done.5.refs_0_
  53.5 0.5 collective-permute-start.12
  54.0 4.6 %collective-permute-done.6.refs_1_ = bf16[40,1024]{1,0:T(8,128)(2,1)S(1)} collective-permute-done((bf16[40,1024]{1,0:T(8,128)(2,1)S(1)}, bf16[40,1024]{1,0:T(8,128)(2,1)S(1)}, u32[]{:S(2)}, u32[]{:S(2)}) %collective-permute-start.6) | collective-permute-done | bytes 81952 | tf_op jit(solution)/shard_map/ppermute | solution.py:462
  58.7 0.0 collective-permute-start.9
  58.7 1.0 %shard_map.85 = (bf16[2,128,256]{2,1,0:T(8,128)(2,1)S(1)}, bf16[2,128,256]{2,1,0:T(8,128)(2,1)S(1)}) custom-call(s32[2,128]{1,0:T(2,128)} %bitcast.5, f32[2,128]{1,0:T(2,128)} %bitcast.6, bf16[120,2048]{1,0:T(8,128)(2,1)S(1)} %shard_map.84.after.mine), custom_call_target="tpu_custom_call" | custom-call | bytes 2097152 | tf_op jit(solution)/shard_map/pallas_call | solution.py:429
  59.7 0.0 collective-permute-done.7.refs_2_
  59.7 0.3 shard_map.91.refs_0_
  60.0 0.1 collective-permute-done.10.refs_2_
  60.1 0.0 collective-permute-done.11.refs_3_
  60.1 0.0 collective-permute-done.12.refs_4_
  60.1 3.0 %collective-permute-done.9.refs_1_ = bf16[40,1024]{1,0:T(8,128)(2,1)S(1)} collective-permute-done((bf16[40,1024]{1,0:T(8,128)(2,1)S(1)}, bf16[40,1024]{1,0:T(8,128)(2,1)S(1)}, u32[]{:S(2)}, u32[]{:S(2)}) %collective-permute-start.9) | collective-permute-done | bytes 81952 | tf_op jit(solution)/shard_map/ppermute | solution.py:462
  63.1 1.0 %shard_map.92 = bf16[128,1024]{1,0:T(8,128)(2,1)} custom-call(bf16[2,128,256]{2,1,0:T(8,128)(2,1)S(1)} %get-tuple-element.51.high, bf16[2,128,256]{2,1,0:T(8,128)(2,1)S(1)} %get-tuple-element.52.low, f32[128,1024]{1,0:T(8,128)S(1)} %shard_map.91.refs_0_, bf16[40,1024]{1,0:T(8,128)(2,1)S(1)} %collective-permute-done.9.refs_1_, ...), custom_call_target="tpu_custom_call" | custom-call | flops 83886080 | bytes 1048576 | tf_op jit(solution)/shard_map/pallas_call | solution.py:429
  (1 shorter events, 0.0 us)
Async XLA Ops:
  2.4 18.9 %collective-permute-start = (bf16[40,2048]{1,0:T(8,128)(2,1)S(1)}, bf16[40,2048]{1,0:T(8,128)(2,1)S(1)}, u32[]{:S(2)}, u32[]{:S(2)}) collective-permute-start(bf16[40,2048]{1,0:T(8,128)(2,1)S(1)} %get-tuple-element.48), channel_id=1, source_target_pairs={{0,4},{1,5},{2,6},{3,7},{4,8},{5,9},{6,10},{7,11},{8,12},{9,13},{1... | collective-permute-start | bytes 491528 | tf_op jit(solution)/shard_map/ppermute | solution.py:462
  5.5 15.9 %collective-permute-start.1 = (bf16[40,2048]{1,0:T(8,128)(2,1)S(1)}, bf16[40,2048]{1,0:T(8,128)(2,1)S(1)}, u32[]{:S(2)}, u32[]{:S(2)}) collective-permute-start(bf16[40,2048]{1,0:T(8,128)(2,1)S(1)} %get-tuple-element.49), channel_id=1, source_target_pairs={{0,8},{1,9},{2,10},{3,11},{4,12},{5,13},{6,14},{7,15},{8,0},{9,1},... | collective-permute-start | bytes 491528 | tf_op jit(solution)/shard_map/ppermute | solution.py:462
  8.1 13.3 %collective-permute-start.2 = (bf16[40,2048]{1,0:T(8,128)(2,1)S(1)}, bf16[40,2048]{1,0:T(8,128)(2,1)S(1)}, u32[]{:S(2)}, u32[]{:S(2)}) collective-permute-start(bf16[40,2048]{1,0:T(8,128)(2,1)S(1)} %get-tuple-element.50), channel_id=1, source_target_pairs={{0,12},{1,13},{2,14},{3,15},{4,0},{5,1},{6,2},{7,3},{8,4},{9,5},{1... | collective-permute-start | bytes 491528 | tf_op jit(solution)/shard_map/ppermute | solution.py:462
  21.4 1.9 %collective-permute-start.3 = (bf16[120,2048]{1,0:T(8,128)(2,1)S(1)}, bf16[120,2048]{1,0:T(8,128)(2,1)S(1)}, u32[]{:S(2)}, u32[]{:S(2)}) collective-permute-start(bf16[120,2048]{1,0:T(8,128)(2,1)S(1)} %shard_map.84.after.mine), channel_id=1, source_target_pairs={{0,1},{1,0},{2,3},{3,2},{4,5},{5,4},{6,7},{7,6},{8,9},{9,8},{10,11... | collective-permute-start | bytes 1474568 | tf_op jit(solution)/shard_map/ppermute | solution.py:465
  37.7 3.8 %collective-permute-start.4 = (bf16[160,1024]{1,0:T(8,128)(2,1)S(1)}, bf16[160,1024]{1,0:T(8,128)(2,1)S(1)}, u32[]{:S(2)}, u32[]{:S(2)}) collective-permute-start(bf16[160,1024]{1,0:T(8,128)(2,1)S(1)} %get-tuple-element.68), channel_id=1, source_target_pairs={{0,1},{1,0},{2,3},{3,2},{4,5},{5,4},{6,7},{7,6},{8,9},{9,8},{10,11... | collective-permute-start | bytes 983048 | tf_op jit(solution)/shard_map/ppermute | solution.py:465
  41.1 6.1 %collective-permute-start.8 = (bf16[160,1024]{1,0:T(8,128)(2,1)S(1)}, bf16[160,1024]{1,0:T(8,128)(2,1)S(1)}, u32[]{:S(2)}, u32[]{:S(2)}) collective-permute-start(bf16[160,1024]{1,0:T(8,128)(2,1)S(1)} %get-tuple-element.76), channel_id=1, source_target_pairs={{0,1},{1,0},{2,3},{3,2},{4,5},{5,4},{6,7},{7,6},{8,9},{9,8},{10,11... | collective-permute-start | bytes 983048 | tf_op jit(solution)/shard_map/ppermute | solution.py:465
  42.9 10.6 %collective-permute-start.5 = (bf16[40,1024]{1,0:T(8,128)(2,1)S(1)}, bf16[40,1024]{1,0:T(8,128)(2,1)S(1)}, u32[]{:S(2)}, u32[]{:S(2)}) collective-permute-start(bf16[40,1024]{1,0:T(8,128)(2,1)S(1)} %get-tuple-element.71), channel_id=1, source_target_pairs={{0,14},{1,15},{2,12},{3,13},{4,2},{5,3},{6,0},{7,1},{8,6},{9,7},{1... | collective-permute-start | bytes 245768 | tf_op jit(solution)/shard_map/ppermute | solution.py:462
  46.3 12.3 %collective-permute-start.6 = (bf16[40,1024]{1,0:T(8,128)(2,1)S(1)}, bf16[40,1024]{1,0:T(8,128)(2,1)S(1)}, u32[]{:S(2)}, u32[]{:S(2)}) collective-permute-start(bf16[40,1024]{1,0:T(8,128)(2,1)S(1)} %get-tuple-element.72), channel_id=1, source_target_pairs={{0,10},{1,11},{2,8},{3,9},{4,14},{5,15},{6,12},{7,13},{8,2},{9,3},... | collective-permute-start | bytes 245768 | tf_op jit(solution)/shard_map/ppermute | solution.py:462
  46.7 12.9 %collective-permute-start.7 = (bf16[40,1024]{1,0:T(8,128)(2,1)S(1)}, bf16[40,1024]{1,0:T(8,128)(2,1)S(1)}, u32[]{:S(2)}, u32[]{:S(2)}) collective-permute-start(bf16[40,1024]{1,0:T(8,128)(2,1)S(1)} %get-tuple-element.73), channel_id=1, source_target_pairs={{0,6},{1,7},{2,4},{3,5},{4,10},{5,11},{6,8},{7,9},{8,14},{9,15},{1... | collective-permute-start | bytes 245768 | tf_op jit(solution)/shard_map/ppermute | solution.py:462
  48.5 11.5 %collective-permute-start.10 = (bf16[40,1024]{1,0:T(8,128)(2,1)S(1)}, bf16[40,1024]{1,0:T(8,128)(2,1)S(1)}, u32[]{:S(2)}, u32[]{:S(2)}) collective-permute-start(bf16[40,1024]{1,0:T(8,128)(2,1)S(1)} %get-tuple-element.82), channel_id=1, source_target_pairs={{0,8},{1,9},{2,10},{3,11},{4,12},{5,13},{6,14},{7,15},{8,0},{9,1},... | collective-permute-start | bytes 245768 | tf_op jit(solution)/shard_map/ppermute | solution.py:462
  51.1 9.0 %collective-permute-start.11 = (bf16[40,1024]{1,0:T(8,128)(2,1)S(1)}, bf16[40,1024]{1,0:T(8,128)(2,1)S(1)}, u32[]{:S(2)}, u32[]{:S(2)}) collective-permute-start(bf16[40,1024]{1,0:T(8,128)(2,1)S(1)} %get-tuple-element.83), channel_id=1, source_target_pairs={{0,4},{1,5},{2,6},{3,7},{4,8},{5,9},{6,10},{7,11},{8,12},{9,13},{1... | collective-permute-start | bytes 245768 | tf_op jit(solution)/shard_map/ppermute | solution.py:462
  53.5 6.6 %collective-permute-start.12 = (bf16[40,1024]{1,0:T(8,128)(2,1)S(1)}, bf16[40,1024]{1,0:T(8,128)(2,1)S(1)}, u32[]{:S(2)}, u32[]{:S(2)}) collective-permute-start(bf16[40,1024]{1,0:T(8,128)(2,1)S(1)} %get-tuple-element.84), channel_id=1, source_target_pairs={{0,2},{1,3},{2,0},{3,1},{4,6},{5,7},{6,4},{7,5},{8,10},{9,11},{10,... | collective-permute-start | bytes 245768 | tf_op jit(solution)/shard_map/ppermute | solution.py:462
  58.7 4.4 %collective-permute-start.9 = (bf16[40,1024]{1,0:T(8,128)(2,1)S(1)}, bf16[40,1024]{1,0:T(8,128)(2,1)S(1)}, u32[]{:S(2)}, u32[]{:S(2)}) collective-permute-start(bf16[40,1024]{1,0:T(8,128)(2,1)S(1)} %get-tuple-element.81), channel_id=1, source_target_pairs={{0,12},{1,13},{2,14},{3,15},{4,0},{5,1},{6,2},{7,3},{8,4},{9,5},{1... | collective-permute-start | bytes 245768 | tf_op jit(solution)/shard_map/ppermute | solution.py:462

commit v9 on v8

--- a/solution.py
+++ b/solution.py
@@ -236,8 +236,9 @@
 
 def arrivals(sizes):
     exp_count, groups = sizes
-    early = [(o, d) for o in range(1, groups) for d in range(1, exp_count)] + [(0, 0)]
-    late = [(0, d) for d in range(1, exp_count)] + [(o, 0) for o in range(1, groups)]
+    order = list(range(1, exp_count)) + [0]
+    early = [(o, d) for o in range(1, groups) for d in order]
+    late = [(0, d) for d in order]
     return early, late
 
 
@@ -317,7 +318,7 @@
     z, g, s = place(sizes)
     refs = list(refs)
     refs = refs[BUFFERS:]
-    up, down, mask, hidden = [refs.pop(0) for _ in range(4)]
+    up, down, mask, _, hidden = [refs.pop(0) for _ in range(5)]
     buffers = [refs.pop(0) for _ in range(BUFFERS)]
     gate_sum, up_sum, rows, sems = refs
     half = own.shape[1] // 2
@@ -388,18 +389,13 @@
 
 def keep_kernel(sizes, hidden, received, *refs):
     exp_count, groups = sizes
-    passed = (len(refs) - received.shape[1] // BLOCK - exp_count) // 2
-    weights = refs[: received.shape[1] // BLOCK]
-    handed = refs[len(weights) : len(weights) + passed]
-    outs = refs[len(weights) + passed :]
+    weights, outs = refs[:-exp_count], refs[-exp_count:]
     for step, buffer in enumerate(weights):
         cols = slice(step * BLOCK, (step + 1) * BLOCK)
         value = jnp.dot(hidden[...], stacked(buffer), preferred_element_type=F32)
         value = value + received[:, cols].astype(F32)
         for d in range(exp_count):
             outs[d][:, cols] = value[d * CAP : (d + 1) * CAP, :].astype(BF16)
-    for given, out in zip(handed, outs[exp_count:]):
-        out[...] = given[...]
 
 
 def combine_kernel(order, high, low, *refs):
@@ -532,7 +528,8 @@
         [((slots, unit_width), BF16)] + [buffer] * BUFFERS,
         [(own, None), (mine, None), (other, None)]
         + [(v, pltpu.VMEM) for v in ready]
-        + [(up_weight, pltpu.HBM), (down_weight, pltpu.HBM), (mask, None)],
+        + [(up_weight, pltpu.HBM), (down_weight, pltpu.HBM), (mask, None)]
+        + [(combine_low, pl.ANY)],
         [
             acc,
             acc,
@@ -562,26 +559,18 @@
         given.append(value)
         kept_weights.append(kept)
     taken = [swap(value) for value in given]
-    kept, stays = {}, []
+    home = {}
     for order, offset in enumerate(offsets):
-        last = order == groups - 1
-        outs = call(
+        kept = call(
             functools.partial(keep_kernel, sizes),
-            [((CAP, part), BF16)] * (exp_count + (len(stays) if last else 0)),
+            [((CAP, part), BF16)] * exp_count,
             [(hidden, None), (taken[order], None)]
-            + [(v, pltpu.VMEM) for v in kept_weights[order]]
-            + [(v, None) for v in (stays if last else [])],
+            + [(v, pltpu.VMEM) for v in kept_weights[order]],
             flops=2 * slots * unit_width * part,
             moved=piece_bytes,
         )
-        for d in range(exp_count):
-            kept[offset, d] = outs[d]
-        if last:
-            for n, other_offset in enumerate(offsets[:-1]):
-                kept[other_offset, 0] = outs[exp_count + n]
-        else:
-            stays.append(outs[0])
-    home = {(o, d): shift(v, -d, o) if o or d else v for (o, d), v in kept.items()}
+        for d in list(range(1, exp_count)) + [0]:
+            home[offset, d] = shift(kept[d], -d, offset) if d or offset else kept[d]
     mixed = None
     for order, batch in enumerate(arrivals(sizes)):
         last = order == 1

time: 64.4 us -> 62.9 us (0.977)
  waiting for transfers between devices: 9.65 us -> 7.93 us
    ppermute x3, waiting for transfers between devices: 1.86 us -> 0.84 us  [swap(): return lax.ppermute(value, 'unit', [(u, u ^ 1) for u in range(unit_count)])]
    ppermute x10, waiting for transfers between devices: 7.79 us -> 7.09 us  [shift(): return lax.ppermute(value, ('exp', 'unit'), pairs)]
where the time goes in v9:
time: 62.9 us; the launch traced here: 62.5 us
  Pallas kernels  36.8 us (59%)
  starting transfers between devices  17.6 us (28%)
  waiting for transfers between devices  7.93 us (13%)
    pallas_call x11, Pallas kernels, call(): pl.pallas_call(kernel, out_shape=shapes, in_specs=specs, out_specs=[vmem]...  36.8 us
    ppermute x10, starting transfers between devices, shift(): return lax.ppermute(value, ('exp', 'unit'), pairs)  16.9 us
    ppermute x10, waiting for transfers between devices, shift(): return lax.ppermute(value, ('exp', 'unit'), pairs)  7.09 us
  transfers between devices with their start and end apart: 13, of which 4 were waited for; matrix products, arithmetic and copies ran while one was open for 0% of the time, Pallas kernels for 30%

profile of v9, /device:TPU:0, one launch (start us, length us, event | category | flops | bytes accessed | tf_op | source)
XLA Modules:
  0.0 62.5 jit_solution(17812514416459684470)
XLA Ops:
  0.0 2.4 %shard_map.82 = (bf16[40,4096]{1,0:T(8,128)(2,1)S(1)}, bf16[7,512,512]{2,1,0:T(8,128)(2,1)S(1)}, bf16[40,2048]{1,0:T(8,128)(2,1)S(1)}, bf16[40,2048]{1,0:T(8,128)(2,1)S(1)}, bf16[40,2048]{1,0:T(8,128)(2,1)S(1)}) custom-call(bf16[128,4096]{1,0:T(8,128)(2,1)} %tokens_hbm.1, f32[1,4096]{1,0:T(1,128)} %bitcast.3, s32[2,128]{1,0:T(2,128)} %bitcast.4, ...), custom_call_target="tpu_custom_call" | custom-call | flops 83886080 | bytes 5767168 | tf_op jit(solution)/shard_map/pallas_call | solution.py:425
  2.4 3.1 %collective-permute-start = (bf16[40,2048]{1,0:T(8,128)(2,1)S(1)}, bf16[40,2048]{1,0:T(8,128)(2,1)S(1)}, u32[]{:S(2)}, u32[]{:S(2)}) collective-permute-start(bf16[40,2048]{1,0:T(8,128)(2,1)S(1)} %get-tuple-element.47), channel_id=1, source_target_pairs={{0,4},{1,5},{2,6},{3,7},{4,8},{5,9},{6,10},{7,11},{8,12},{9,13},{1... | collective-permute-start | bytes 491528 | tf_op jit(solution)/shard_map/ppermute | solution.py:458
  5.5 2.6 %collective-permute-start.1 = (bf16[40,2048]{1,0:T(8,128)(2,1)S(1)}, bf16[40,2048]{1,0:T(8,128)(2,1)S(1)}, u32[]{:S(2)}, u32[]{:S(2)}) collective-permute-start(bf16[40,2048]{1,0:T(8,128)(2,1)S(1)} %get-tuple-element.48), channel_id=1, source_target_pairs={{0,8},{1,9},{2,10},{3,11},{4,12},{5,13},{6,14},{7,15},{8,0},{9,1},... | collective-permute-start | bytes 491528 | tf_op jit(solution)/shard_map/ppermute | solution.py:458
  8.1 1.3 %collective-permute-start.2 = (bf16[40,2048]{1,0:T(8,128)(2,1)S(1)}, bf16[40,2048]{1,0:T(8,128)(2,1)S(1)}, u32[]{:S(2)}, u32[]{:S(2)}) collective-permute-start(bf16[40,2048]{1,0:T(8,128)(2,1)S(1)} %get-tuple-element.49), channel_id=1, source_target_pairs={{0,12},{1,13},{2,14},{3,15},{4,0},{5,1},{6,2},{7,3},{8,4},{9,5},{1... | collective-permute-start | bytes 491528 | tf_op jit(solution)/shard_map/ppermute | solution.py:458
  9.4 11.9 %shard_map.83 = (f32[8,3584]{1,0:T(8,128)S(1)}, bf16[7,512,512]{2,1,0:T(8,128)(2,1)S(1)}, bf16[7,512,512]{2,1,0:T(8,128)(2,1)S(1)}, bf16[7,512,512]{2,1,0:T(8,12...) custom-call(s32[2,8,48]{2,1,0:T(8,128)} %active_hbm.1, ...), custom_call_target="tpu_custom_call", output_to_operand_aliasing={{1}: (4, {})} | custom-call | flops 167772160 | bytes 36700160 | tf_op jit(solution)/shard_map/pallas_call | solution.py:425
  21.4 0.0 collective-permute-done.refs_0_
  21.4 0.0 collective-permute-done.1.refs_1_
  21.4 0.0 collective-permute-done.2.refs_2_
  21.4 0.1 collective-permute-start.3
  21.5 1.0 %shard_map.85 = (bf16[2,128,256]{2,1,0:T(8,128)(2,1)S(1)}, bf16[2,128,256]{2,1,0:T(8,128)(2,1)S(1)}) custom-call(s32[2,128]{1,0:T(2,128)} %bitcast.5, f32[2,128]{1,0:T(2,128)} %bitcast.6, bf16[120,2048]{1,0:T(8,128)(2,1)S(1)} %shard_map.84.after.mine), custom_call_target="tpu_custom_call" | custom-call | bytes 2097152 | tf_op jit(solution)/shard_map/pallas_call | solution.py:425
  22.5 0.8 %collective-permute-done.3.other = bf16[120,2048]{1,0:T(8,128)(2,1)S(1)} collective-permute-done((bf16[120,2048]{1,0:T(8,128)(2,1)S(1)}, bf16[120,2048]{1,0:T(8,128)(2,1)S(1)}, u32[]{:S(2)}, u32[]{:S(2)}) %collective-permute-start.3) | collective-permute-done | bytes 491552 | tf_op jit(solution)/shard_map/ppermute | solution.py:461
  23.4 11.2 %shard_map.86 = (bf16[160,3584]{1,0:T(8,128)(2,1)S(1)}, bf16[7,512,512]{2,1,0:T(8,128)(2,1)S(1)}, bf16[7,512,512]{2,1,0:T(8,128)(2,1)S(1)}, bf16[7,512,512]{2,1,...) custom-call(bf16[40,4096]{1,0:T(8,128)(2,1)S(1)} %get-tuple-element., ...), custom_call_target="tpu_custom_call", output_to_operand_aliasing={{1}: (3, {}), {2}: (4, {}), {3}: (5, {}), {4}: (6, {}), {5}... | custom-call | flops 9395240960 | bytes 36700160 | tf_op jit(solution)/shard_map/pallas_call | solution.py:425
  34.5 3.2 %shard_map.87 = (bf16[160,1024]{1,0:T(8,128)(2,1)S(1)}, bf16[7,512,512]{2,1,0:T(8,128)(2,1)S(1)}, bf16[7,512,512]{2,1,0:T(8,128)(2,1)S(1)}) custom-call(bf16[160,3584]{1,0:T(8,128)(2,1)S(1)} %get-tuple-element.64.hidden, bf16[7,512,512]{2,1,0:T(8,128)(2,1)S(1)} %get-tuple-element.65.refs_0_, bf16[7,512,512]{2,1,0:T(8,128)(2,1)S(1)} %get-tuple-element.66.refs_1_, ...), custom_call_target="tpu_custom_call" | custom-call | flops 1174405120 | bytes 7340032 | tf_op jit(solution)/shard_map/pallas_call | solution.py:425
  37.7 0.2 collective-permute-start.4
  37.9 3.1 %shard_map.90 = (bf16[160,1024]{1,0:T(8,128)(2,1)S(1)}, bf16[7,512,512]{2,1,0:T(8,128)(2,1)S(1)}, bf16[7,512,512]{2,1,0:T(8,128)(2,1)S(1)}) custom-call(bf16[160,3584]{1,0:T(8,128)(2,1)S(1)} %get-tuple-element.64.hidden, bf16[7,512,512]{2,1,0:T(8,128)(2,1)S(1)} %get-tuple-element.74.refs_0_, bf16[7,512,512]{2,1,0:T(8,128)(2,1)S(1)} %get-tuple-element.75.refs_1_, ...), custom_call_target="tpu_custom_call" | custom-call | flops 1174405120 | bytes 7340032 | tf_op jit(solution)/shard_map/pallas_call | solution.py:425
  41.1 0.4 collective-permute-start.9
  41.5 0.0 collective-permute-done.4.received
  41.5 1.4 %shard_map.88 = (bf16[40,1024]{1,0:T(8,128)(2,1)S(1)}, bf16[40,1024]{1,0:T(8,128)(2,1)S(1)}, bf16[40,1024]{1,0:T(8,128)(2,1)S(1)}, bf16[40,1024]{1,0:T(8,128)(2,1)S(1)}) custom-call(bf16[160,3584]{1,0:T(8,128)(2,1)S(1)} %get-tuple-element.64.hidden, bf16[160,1024]{1,0:T(8,128)(2,1)S(1)} %collective-permute-done.4.received, ...), custom_call_target="tpu_custom_call" | custom-call | flops 1174405120 | bytes 3670016 | tf_op jit(solution)/shard_map/pallas_call | solution.py:425
  42.9 3.5 %collective-permute-start.5 = (bf16[40,1024]{1,0:T(8,128)(2,1)S(1)}, bf16[40,1024]{1,0:T(8,128)(2,1)S(1)}, u32[]{:S(2)}, u32[]{:S(2)}) collective-permute-start(bf16[40,1024]{1,0:T(8,128)(2,1)S(1)} %get-tuple-element.70), channel_id=1, source_target_pairs={{0,14},{1,15},{2,12},{3,13},{4,2},{5,3},{6,0},{7,1},{8,6},{9,7},{1... | collective-permute-start | bytes 245768 | tf_op jit(solution)/shard_map/ppermute | solution.py:458
  46.3 0.4 collective-permute-start.6
  46.7 0.5 collective-permute-start.7
  47.2 1.3 %collective-permute-start.8 = (bf16[40,1024]{1,0:T(8,128)(2,1)S(1)}, bf16[40,1024]{1,0:T(8,128)(2,1)S(1)}, u32[]{:S(2)}, u32[]{:S(2)}) collective-permute-start(bf16[40,1024]{1,0:T(8,128)(2,1)S(1)} %get-tuple-element.73), channel_id=1, source_target_pairs={{0,2},{1,3},{2,0},{3,1},{4,6},{5,7},{6,4},{7,5},{8,10},{9,11},{10,... | collective-permute-start | bytes 245768 | tf_op jit(solution)/shard_map/ppermute | solution.py:458
  48.5 0.0 collective-permute-done.9.received
  48.5 1.4 %shard_map.91 = (bf16[40,1024]{1,0:T(8,128)(2,1)S(1)}, bf16[40,1024]{1,0:T(8,128)(2,1)S(1)}, bf16[40,1024]{1,0:T(8,128)(2,1)S(1)}, bf16[40,1024]{1,0:T(8,128)(2,1)S(1)}) custom-call(bf16[160,3584]{1,0:T(8,128)(2,1)S(1)} %get-tuple-element.64.hidden, bf16[160,1024]{1,0:T(8,128)(2,1)S(1)} %collective-permute-done.9.received, ...), custom_call_target="tpu_custom_call" | custom-call | flops 1174405120 | bytes 3670016 | tf_op jit(solution)/shard_map/pallas_call | solution.py:425
  49.8 3.6 %collective-permute-start.10 = (bf16[40,1024]{1,0:T(8,128)(2,1)S(1)}, bf16[40,1024]{1,0:T(8,128)(2,1)S(1)}, u32[]{:S(2)}, u32[]{:S(2)}) collective-permute-start(bf16[40,1024]{1,0:T(8,128)(2,1)S(1)} %get-tuple-element.79), channel_id=1, source_target_pairs={{0,12},{1,13},{2,14},{3,15},{4,0},{5,1},{6,2},{7,3},{8,4},{9,5},{1... | collective-permute-start | bytes 245768 | tf_op jit(solution)/shard_map/ppermute | solution.py:458
  53.4 0.0 collective-permute-done.5.refs_0_
  53.4 0.7 %collective-permute-start.11 = (bf16[40,1024]{1,0:T(8,128)(2,1)S(1)}, bf16[40,1024]{1,0:T(8,128)(2,1)S(1)}, u32[]{:S(2)}, u32[]{:S(2)}) collective-permute-start(bf16[40,1024]{1,0:T(8,128)(2,1)S(1)} %get-tuple-element.80), channel_id=1, source_target_pairs={{0,8},{1,9},{2,10},{3,11},{4,12},{5,13},{6,14},{7,15},{8,0},{9,1},... | collective-permute-start | bytes 245768 | tf_op jit(solution)/shard_map/ppermute | solution.py:458
  54.2 1.0 %collective-permute-done.6.refs_1_ = bf16[40,1024]{1,0:T(8,128)(2,1)S(1)} collective-permute-done((bf16[40,1024]{1,0:T(8,128)(2,1)S(1)}, bf16[40,1024]{1,0:T(8,128)(2,1)S(1)}, u32[]{:S(2)}, u32[]{:S(2)}) %collective-permute-start.6) | collective-permute-done | bytes 81952 | tf_op jit(solution)/shard_map/ppermute | solution.py:458
  55.2 0.0 collective-permute-start.12
  55.2 0.0 collective-permute-done.7.refs_2_
  55.2 0.0 collective-permute-done.8.refs_3_
  55.2 0.3 shard_map.89.refs_0_
  55.5 0.8 %collective-permute-done.10.refs_1_ = bf16[40,1024]{1,0:T(8,128)(2,1)S(1)} collective-permute-done((bf16[40,1024]{1,0:T(8,128)(2,1)S(1)}, bf16[40,1024]{1,0:T(8,128)(2,1)S(1)}, u32[]{:S(2)}, u32[]{:S(2)}) %collective-permute-start.10) | collective-permute-done | bytes 81952 | tf_op jit(solution)/shard_map/ppermute | solution.py:458
  56.3 5.3 %collective-permute-done.11.refs_2_ = bf16[40,1024]{1,0:T(8,128)(2,1)S(1)} collective-permute-done((bf16[40,1024]{1,0:T(8,128)(2,1)S(1)}, bf16[40,1024]{1,0:T(8,128)(2,1)S(1)}, u32[]{:S(2)}, u32[]{:S(2)}) %collective-permute-start.11) | collective-permute-done | bytes 81952 | tf_op jit(solution)/shard_map/ppermute | solution.py:458
  61.5 0.0 collective-permute-done.12.refs_3_
  61.5 1.0 %shard_map.92 = bf16[128,1024]{1,0:T(8,128)(2,1)} custom-call(bf16[2,128,256]{2,1,0:T(8,128)(2,1)S(1)} %get-tuple-element.50.high, bf16[2,128,256]{2,1,0:T(8,128)(2,1)S(1)} %get-tuple-element.51.refs_15_.low, f32[128,1024]{1,0:T(8,128)S(1)} %shard_map.89.refs_0_, bf16[40,1024]{1,0:T(8,128)(2,1)S(1)} %collective-permute-done.10.refs_1_, ...), custom_call_target="tpu_custom_call" | custom-call | flops 83886080 | bytes 1048576 | tf_op jit(solution)/shard_map/pallas_call | solution.py:425
  (1 shorter events, 0.0 us)
Async XLA Ops:
  2.4 18.9 %collective-permute-start = (bf16[40,2048]{1,0:T(8,128)(2,1)S(1)}, bf16[40,2048]{1,0:T(8,128)(2,1)S(1)}, u32[]{:S(2)}, u32[]{:S(2)}) collective-permute-start(bf16[40,2048]{1,0:T(8,128)(2,1)S(1)} %get-tuple-element.47), channel_id=1, source_target_pairs={{0,4},{1,5},{2,6},{3,7},{4,8},{5,9},{6,10},{7,11},{8,12},{9,13},{1... | collective-permute-start | bytes 491528 | tf_op jit(solution)/shard_map/ppermute | solution.py:458
  5.5 15.9 %collective-permute-start.1 = (bf16[40,2048]{1,0:T(8,128)(2,1)S(1)}, bf16[40,2048]{1,0:T(8,128)(2,1)S(1)}, u32[]{:S(2)}, u32[]{:S(2)}) collective-permute-start(bf16[40,2048]{1,0:T(8,128)(2,1)S(1)} %get-tuple-element.48), channel_id=1, source_target_pairs={{0,8},{1,9},{2,10},{3,11},{4,12},{5,13},{6,14},{7,15},{8,0},{9,1},... | collective-permute-start | bytes 491528 | tf_op jit(solution)/shard_map/ppermute | solution.py:458
  8.1 13.3 %collective-permute-start.2 = (bf16[40,2048]{1,0:T(8,128)(2,1)S(1)}, bf16[40,2048]{1,0:T(8,128)(2,1)S(1)}, u32[]{:S(2)}, u32[]{:S(2)}) collective-permute-start(bf16[40,2048]{1,0:T(8,128)(2,1)S(1)} %get-tuple-element.49), channel_id=1, source_target_pairs={{0,12},{1,13},{2,14},{3,15},{4,0},{5,1},{6,2},{7,3},{8,4},{9,5},{1... | collective-permute-start | bytes 491528 | tf_op jit(solution)/shard_map/ppermute | solution.py:458
  21.4 1.9 %collective-permute-start.3 = (bf16[120,2048]{1,0:T(8,128)(2,1)S(1)}, bf16[120,2048]{1,0:T(8,128)(2,1)S(1)}, u32[]{:S(2)}, u32[]{:S(2)}) collective-permute-start(bf16[120,2048]{1,0:T(8,128)(2,1)S(1)} %shard_map.84.after.mine), channel_id=1, source_target_pairs={{0,1},{1,0},{2,3},{3,2},{4,5},{5,4},{6,7},{7,6},{8,9},{9,8},{10,11... | collective-permute-start | bytes 1474568 | tf_op jit(solution)/shard_map/ppermute | solution.py:461
  37.7 3.8 %collective-permute-start.4 = (bf16[160,1024]{1,0:T(8,128)(2,1)S(1)}, bf16[160,1024]{1,0:T(8,128)(2,1)S(1)}, u32[]{:S(2)}, u32[]{:S(2)}) collective-permute-start(bf16[160,1024]{1,0:T(8,128)(2,1)S(1)} %get-tuple-element.67), channel_id=1, source_target_pairs={{0,1},{1,0},{2,3},{3,2},{4,5},{5,4},{6,7},{7,6},{8,9},{9,8},{10,11... | collective-permute-start | bytes 983048 | tf_op jit(solution)/shard_map/ppermute | solution.py:461
  41.1 7.4 %collective-permute-start.9 = (bf16[160,1024]{1,0:T(8,128)(2,1)S(1)}, bf16[160,1024]{1,0:T(8,128)(2,1)S(1)}, u32[]{:S(2)}, u32[]{:S(2)}) collective-permute-start(bf16[160,1024]{1,0:T(8,128)(2,1)S(1)} %get-tuple-element.76), channel_id=1, source_target_pairs={{0,1},{1,0},{2,3},{3,2},{4,5},{5,4},{6,7},{7,6},{8,9},{9,8},{10,11... | collective-permute-start | bytes 983048 | tf_op jit(solution)/shard_map/ppermute | solution.py:461
  42.9 10.5 %collective-permute-start.5 = (bf16[40,1024]{1,0:T(8,128)(2,1)S(1)}, bf16[40,1024]{1,0:T(8,128)(2,1)S(1)}, u32[]{:S(2)}, u32[]{:S(2)}) collective-permute-start(bf16[40,1024]{1,0:T(8,128)(2,1)S(1)} %get-tuple-element.70), channel_id=1, source_target_pairs={{0,14},{1,15},{2,12},{3,13},{4,2},{5,3},{6,0},{7,1},{8,6},{9,7},{1... | collective-permute-start | bytes 245768 | tf_op jit(solution)/shard_map/ppermute | solution.py:458
  46.3 8.8 %collective-permute-start.6 = (bf16[40,1024]{1,0:T(8,128)(2,1)S(1)}, bf16[40,1024]{1,0:T(8,128)(2,1)S(1)}, u32[]{:S(2)}, u32[]{:S(2)}) collective-permute-start(bf16[40,1024]{1,0:T(8,128)(2,1)S(1)} %get-tuple-element.71), channel_id=1, source_target_pairs={{0,10},{1,11},{2,8},{3,9},{4,14},{5,15},{6,12},{7,13},{8,2},{9,3},... | collective-permute-start | bytes 245768 | tf_op jit(solution)/shard_map/ppermute | solution.py:458
  46.7 8.5 %collective-permute-start.7 = (bf16[40,1024]{1,0:T(8,128)(2,1)S(1)}, bf16[40,1024]{1,0:T(8,128)(2,1)S(1)}, u32[]{:S(2)}, u32[]{:S(2)}) collective-permute-start(bf16[40,1024]{1,0:T(8,128)(2,1)S(1)} %get-tuple-element.72), channel_id=1, source_target_pairs={{0,6},{1,7},{2,4},{3,5},{4,10},{5,11},{6,8},{7,9},{8,14},{9,15},{1... | collective-permute-start | bytes 245768 | tf_op jit(solution)/shard_map/ppermute | solution.py:458
  47.2 8.0 %collective-permute-start.8 = (bf16[40,1024]{1,0:T(8,128)(2,1)S(1)}, bf16[40,1024]{1,0:T(8,128)(2,1)S(1)}, u32[]{:S(2)}, u32[]{:S(2)}) collective-permute-start(bf16[40,1024]{1,0:T(8,128)(2,1)S(1)} %get-tuple-element.73), channel_id=1, source_target_pairs={{0,2},{1,3},{2,0},{3,1},{4,6},{5,7},{6,4},{7,5},{8,10},{9,11},{10,... | collective-permute-start | bytes 245768 | tf_op jit(solution)/shard_map/ppermute | solution.py:458
  49.8 6.5 %collective-permute-start.10 = (bf16[40,1024]{1,0:T(8,128)(2,1)S(1)}, bf16[40,1024]{1,0:T(8,128)(2,1)S(1)}, u32[]{:S(2)}, u32[]{:S(2)}) collective-permute-start(bf16[40,1024]{1,0:T(8,128)(2,1)S(1)} %get-tuple-element.79), channel_id=1, source_target_pairs={{0,12},{1,13},{2,14},{3,15},{4,0},{5,1},{6,2},{7,3},{8,4},{9,5},{1... | collective-permute-start | bytes 245768 | tf_op jit(solution)/shard_map/ppermute | solution.py:458
  53.4 8.1 %collective-permute-start.11 = (bf16[40,1024]{1,0:T(8,128)(2,1)S(1)}, bf16[40,1024]{1,0:T(8,128)(2,1)S(1)}, u32[]{:S(2)}, u32[]{:S(2)}) collective-permute-start(bf16[40,1024]{1,0:T(8,128)(2,1)S(1)} %get-tuple-element.80), channel_id=1, source_target_pairs={{0,8},{1,9},{2,10},{3,11},{4,12},{5,13},{6,14},{7,15},{8,0},{9,1},... | collective-permute-start | bytes 245768 | tf_op jit(solution)/shard_map/ppermute | solution.py:458
  55.2 6.4 %collective-permute-start.12 = (bf16[40,1024]{1,0:T(8,128)(2,1)S(1)}, bf16[40,1024]{1,0:T(8,128)(2,1)S(1)}, u32[]{:S(2)}, u32[]{:S(2)}) collective-permute-start(bf16[40,1024]{1,0:T(8,128)(2,1)S(1)} %get-tuple-element.81), channel_id=1, source_target_pairs={{0,4},{1,5},{2,6},{3,7},{4,8},{5,9},{6,10},{7,11},{8,12},{9,13},{1... | collective-permute-start | bytes 245768 | tf_op jit(solution)/shard_map/ppermute | solution.py:458

commit v10 on v9

--- a/solution.py
+++ b/solution.py
@@ -318,7 +318,7 @@
     z, g, s = place(sizes)
     refs = list(refs)
     refs = refs[BUFFERS:]
-    up, down, mask, _, hidden = [refs.pop(0) for _ in range(5)]
+    up, down, mask, _, hidden, gives = [refs.pop(0) for _ in range(6)]
     buffers = [refs.pop(0) for _ in range(BUFFERS)]
     gate_sum, up_sum, rows, sems = refs
     half = own.shape[1] // 2
@@ -334,6 +334,9 @@
         elif index < 2 * lines + groups * given:
             order, step = divmod(index - 2 * lines, given)
             fetch_columns(sizes, down, order + 1, False, step, buffer, sem)
+        elif index < 2 * lines + (groups + 1) * given:
+            step = index - 2 * lines - groups * given
+            fetch_columns(sizes, down, 1, True, step, buffer, sem)
 
     for index in range(READY, count):
         fetch(index)
@@ -365,8 +368,13 @@
             hidden[:, cols] = jnp.concatenate(parts, axis=0).astype(BF16)
         for n in range(2):
             fetch(index + n + count)
-    for index in range(2 * lines, 2 * lines + groups * given):
-        await_all(buffers[index % count], sems.at[index % count])
+    for index in range(2 * lines, 2 * lines + (groups + 1) * given):
+        buffer = buffers[index % count]
+        await_all(buffer, sems.at[index % count])
+        step = index - 2 * lines
+        if step < given:
+            value = jnp.dot(hidden[...], stacked(buffer), preferred_element_type=F32)
+            gives[:, step * BLOCK : (step + 1) * BLOCK] = value.astype(BF16)
 
 
 def give_kernel(sizes, offset, hidden, *refs):
@@ -523,9 +531,10 @@
         moved=1 << 21,
     )
     acc = pltpu.VMEM((slots, unit_width), F32)
-    hidden, *buffers = call(
+    part = features // unit_count
+    hidden, first_given, *buffers = call(
         functools.partial(hidden_kernel, sizes),
-        [((slots, unit_width), BF16)] + [buffer] * BUFFERS,
+        [((slots, unit_width), BF16), ((slots, part), BF16)] + [buffer] * BUFFERS,
         [(own, None), (mine, None), (other, None)]
         + [(v, pltpu.VMEM) for v in ready]
         + [(up_weight, pltpu.HBM), (down_weight, pltpu.HBM), (mask, None)]
@@ -538,13 +547,14 @@
         ],
         flops=2 * 2 * slots * features * unit_width,
         moved=10 * piece_bytes,
-        aliases={3 + n: 1 + n for n in range(BUFFERS)},
-    )
-    part = features // unit_count
+        aliases={3 + n: 2 + n for n in range(BUFFERS)},
+    )
     steps = part // BLOCK
     offsets = [(order + 1) % groups for order in range(groups)]
-    given, kept_weights = [], []
-    for order, offset in enumerate(offsets):
+    first = 2 * features // BLOCK + groups * steps
+    given = [first_given]
+    kept_weights = [[buffers[(first + step) % BUFFERS] for step in range(steps)]]
+    for order, offset in list(enumerate(offsets))[1:]:
         first = 2 * features // BLOCK + order * steps
         value, *kept = call(
             functools.partial(give_kernel, sizes, offset),

time: 62.9 us -> 61.8 us (0.983)
  Pallas kernels: 36.8 us -> 35.8 us
    pallas_call x11 -> x10, Pallas kernels: 36.8 us -> 35.8 us  [call(): pl.pallas_call(kernel, out_shape=shapes, in_specs=specs, out_specs=[vmem]...]
  transfers between devices with their start and end apart: 13 -> 13, of which waited for: 4 -> 4; matrix products, arithmetic and copies ran while one was open for 0% -> 0% of each run, Pallas kernels for 30% -> 31%
where the time goes in v10:
time: 61.8 us; the launch traced here: 61.5 us
  Pallas kernels  35.8 us (58%)
  starting transfers between devices  17.6 us (28%)
  waiting for transfers between devices  7.94 us (13%)
    pallas_call x10, Pallas kernels, call(): pl.pallas_call(kernel, out_shape=shapes, in_specs=specs, out_specs=[vmem]...  35.8 us
    ppermute x10, starting transfers between devices, shift(): return lax.ppermute(value, ('exp', 'unit'), pairs)  16.9 us
    ppermute x10, waiting for transfers between devices, shift(): return lax.ppermute(value, ('exp', 'unit'), pairs)  7.1 us
  transfers between devices with their start and end apart: 13, of which 4 were waited for; matrix products, arithmetic and copies ran while one was open for 0% of the time, Pallas kernels for 31%

profile of v10, /device:TPU:0, one launch (start us, length us, event | category | flops | bytes accessed | tf_op | source)
XLA Modules:
  0.0 61.5 jit_solution(10614125713955093689)
XLA Ops:
  0.0 2.4 %shard_map.82 = (bf16[40,4096]{1,0:T(8,128)(2,1)S(1)}, bf16[7,512,512]{2,1,0:T(8,128)(2,1)S(1)}, bf16[40,2048]{1,0:T(8,128)(2,1)S(1)}, bf16[40,2048]{1,0:T(8,128)(2,1)S(1)}, bf16[40,2048]{1,0:T(8,128)(2,1)S(1)}) custom-call(bf16[128,4096]{1,0:T(8,128)(2,1)} %tokens_hbm.1, f32[1,4096]{1,0:T(1,128)} %bitcast.3, s32[2,128]{1,0:T(2,128)} %bitcast.4, ...), custom_call_target="tpu_custom_call" | custom-call | flops 83886080 | bytes 5767168 | tf_op jit(solution)/shard_map/pallas_call | solution.py:433
  2.4 3.1 %collective-permute-start = (bf16[40,2048]{1,0:T(8,128)(2,1)S(1)}, bf16[40,2048]{1,0:T(8,128)(2,1)S(1)}, u32[]{:S(2)}, u32[]{:S(2)}) collective-permute-start(bf16[40,2048]{1,0:T(8,128)(2,1)S(1)} %get-tuple-element.45), channel_id=1, source_target_pairs={{0,4},{1,5},{2,6},{3,7},{4,8},{5,9},{6,10},{7,11},{8,12},{9,13},{1... | collective-permute-start | bytes 491528 | tf_op jit(solution)/shard_map/ppermute | solution.py:466
  5.5 2.6 %collective-permute-start.1 = (bf16[40,2048]{1,0:T(8,128)(2,1)S(1)}, bf16[40,2048]{1,0:T(8,128)(2,1)S(1)}, u32[]{:S(2)}, u32[]{:S(2)}) collective-permute-start(bf16[40,2048]{1,0:T(8,128)(2,1)S(1)} %get-tuple-element.46), channel_id=1, source_target_pairs={{0,8},{1,9},{2,10},{3,11},{4,12},{5,13},{6,14},{7,15},{8,0},{9,1},... | collective-permute-start | bytes 491528 | tf_op jit(solution)/shard_map/ppermute | solution.py:466
  8.1 1.3 %collective-permute-start.2 = (bf16[40,2048]{1,0:T(8,128)(2,1)S(1)}, bf16[40,2048]{1,0:T(8,128)(2,1)S(1)}, u32[]{:S(2)}, u32[]{:S(2)}) collective-permute-start(bf16[40,2048]{1,0:T(8,128)(2,1)S(1)} %get-tuple-element.47), channel_id=1, source_target_pairs={{0,12},{1,13},{2,14},{3,15},{4,0},{5,1},{6,2},{7,3},{8,4},{9,5},{1... | collective-permute-start | bytes 491528 | tf_op jit(solution)/shard_map/ppermute | solution.py:466
  9.4 11.9 %shard_map.83 = (f32[8,3584]{1,0:T(8,128)S(1)}, bf16[7,512,512]{2,1,0:T(8,128)(2,1)S(1)}, bf16[7,512,512]{2,1,0:T(8,128)(2,1)S(1)}, bf16[7,512,512]{2,1,0:T(8,12...) custom-call(s32[2,8,48]{2,1,0:T(8,128)} %active_hbm.1, ...), custom_call_target="tpu_custom_call", output_to_operand_aliasing={{1}: (4, {})} | custom-call | flops 167772160 | bytes 36700160 | tf_op jit(solution)/shard_map/pallas_call | solution.py:433
  21.4 0.0 collective-permute-done.refs_0_
  21.4 0.0 collective-permute-done.1.refs_1_
  21.4 0.0 collective-permute-done.2.refs_2_
  21.4 0.1 collective-permute-start.3
  21.5 1.0 %shard_map.85 = (bf16[2,128,256]{2,1,0:T(8,128)(2,1)S(1)}, bf16[2,128,256]{2,1,0:T(8,128)(2,1)S(1)}) custom-call(s32[2,128]{1,0:T(2,128)} %bitcast.5, f32[2,128]{1,0:T(2,128)} %bitcast.6, bf16[120,2048]{1,0:T(8,128)(2,1)S(1)} %shard_map.84.after.mine), custom_call_target="tpu_custom_call" | custom-call | bytes 2097152 | tf_op jit(solution)/shard_map/pallas_call | solution.py:433
  22.5 0.8 %collective-permute-done.3.other = bf16[120,2048]{1,0:T(8,128)(2,1)S(1)} collective-permute-done((bf16[120,2048]{1,0:T(8,128)(2,1)S(1)}, bf16[120,2048]{1,0:T(8,128)(2,1)S(1)}, u32[]{:S(2)}, u32[]{:S(2)}) %collective-permute-start.3) | collective-permute-done | bytes 491552 | tf_op jit(solution)/shard_map/ppermute | solution.py:469
  23.4 13.3 %shard_map.86 = (bf16[160,3584]{1,0:T(8,128)(2,1)S(1)}, bf16[160,1024]{1,0:T(8,128)(2,1)S(1)}, bf16[7,512,512]{2,1,0:T(8,128)(2,1)S(1)}, bf16[7,512,512]{2,1,0:T...) custom-call(bf16[40,4096]{1,0:T(8,128)(2,1)S(1)} %get-tuple-element., ...), custom_call_target="tpu_custom_call", output_to_operand_aliasing={{2}: (3, {}), {3}: (4, {}), {4}: (5, {}), {5}: (6, {}), {6}... | custom-call | flops 9395240960 | bytes 36700160 | tf_op jit(solution)/shard_map/pallas_call | solution.py:433
  36.7 0.2 collective-permute-start.4
  36.9 3.1 %shard_map.89 = (bf16[160,1024]{1,0:T(8,128)(2,1)S(1)}, bf16[7,512,512]{2,1,0:T(8,128)(2,1)S(1)}, bf16[7,512,512]{2,1,0:T(8,128)(2,1)S(1)}) custom-call(bf16[160,3584]{1,0:T(8,128)(2,1)S(1)} %get-tuple-element.62.hidden, bf16[7,512,512]{2,1,0:T(8,128)(2,1)S(1)} %get-tuple-element.70.refs_0_, bf16[7,512,512]{2,1,0:T(8,128)(2,1)S(1)} %get-tuple-element.71.refs_1_, ...), custom_call_target="tpu_custom_call" | custom-call | flops 1174405120 | bytes 7340032 | tf_op jit(solution)/shard_map/pallas_call | solution.py:433
  40.0 0.4 collective-permute-start.9
  40.5 0.0 collective-permute-done.4.received
  40.5 1.4 %shard_map.87 = (bf16[40,1024]{1,0:T(8,128)(2,1)S(1)}, bf16[40,1024]{1,0:T(8,128)(2,1)S(1)}, bf16[40,1024]{1,0:T(8,128)(2,1)S(1)}, bf16[40,1024]{1,0:T(8,128)(2,1)S(1)}) custom-call(bf16[160,3584]{1,0:T(8,128)(2,1)S(1)} %get-tuple-element.62.hidden, bf16[160,1024]{1,0:T(8,128)(2,1)S(1)} %collective-permute-done.4.received, ...), custom_call_target="tpu_custom_call" | custom-call | flops 1174405120 | bytes 3670016 | tf_op jit(solution)/shard_map/pallas_call | solution.py:433
  41.8 3.5 %collective-permute-start.5 = (bf16[40,1024]{1,0:T(8,128)(2,1)S(1)}, bf16[40,1024]{1,0:T(8,128)(2,1)S(1)}, u32[]{:S(2)}, u32[]{:S(2)}) collective-permute-start(bf16[40,1024]{1,0:T(8,128)(2,1)S(1)} %get-tuple-element.66), channel_id=1, source_target_pairs={{0,14},{1,15},{2,12},{3,13},{4,2},{5,3},{6,0},{7,1},{8,6},{9,7},{1... | collective-permute-start | bytes 245768 | tf_op jit(solution)/shard_map/ppermute | solution.py:466
  45.3 0.4 collective-permute-start.6
  45.7 0.5 collective-permute-start.7
  46.1 1.3 %collective-permute-start.8 = (bf16[40,1024]{1,0:T(8,128)(2,1)S(1)}, bf16[40,1024]{1,0:T(8,128)(2,1)S(1)}, u32[]{:S(2)}, u32[]{:S(2)}) collective-permute-start(bf16[40,1024]{1,0:T(8,128)(2,1)S(1)} %get-tuple-element.69), channel_id=1, source_target_pairs={{0,2},{1,3},{2,0},{3,1},{4,6},{5,7},{6,4},{7,5},{8,10},{9,11},{10,... | collective-permute-start | bytes 245768 | tf_op jit(solution)/shard_map/ppermute | solution.py:466
  47.4 0.0 collective-permute-done.9.received
  47.4 1.4 %shard_map.90 = (bf16[40,1024]{1,0:T(8,128)(2,1)S(1)}, bf16[40,1024]{1,0:T(8,128)(2,1)S(1)}, bf16[40,1024]{1,0:T(8,128)(2,1)S(1)}, bf16[40,1024]{1,0:T(8,128)(2,1)S(1)}) custom-call(bf16[160,3584]{1,0:T(8,128)(2,1)S(1)} %get-tuple-element.62.hidden, bf16[160,1024]{1,0:T(8,128)(2,1)S(1)} %collective-permute-done.9.received, ...), custom_call_target="tpu_custom_call" | custom-call | flops 1174405120 | bytes 3670016 | tf_op jit(solution)/shard_map/pallas_call | solution.py:433
  48.8 3.6 %collective-permute-start.10 = (bf16[40,1024]{1,0:T(8,128)(2,1)S(1)}, bf16[40,1024]{1,0:T(8,128)(2,1)S(1)}, u32[]{:S(2)}, u32[]{:S(2)}) collective-permute-start(bf16[40,1024]{1,0:T(8,128)(2,1)S(1)} %get-tuple-element.75), channel_id=1, source_target_pairs={{0,12},{1,13},{2,14},{3,15},{4,0},{5,1},{6,2},{7,3},{8,4},{9,5},{1... | collective-permute-start | bytes 245768 | tf_op jit(solution)/shard_map/ppermute | solution.py:466
  52.4 0.0 collective-permute-done.5.refs_0_
  52.4 0.7 %collective-permute-start.11 = (bf16[40,1024]{1,0:T(8,128)(2,1)S(1)}, bf16[40,1024]{1,0:T(8,128)(2,1)S(1)}, u32[]{:S(2)}, u32[]{:S(2)}) collective-permute-start(bf16[40,1024]{1,0:T(8,128)(2,1)S(1)} %get-tuple-element.76), channel_id=1, source_target_pairs={{0,8},{1,9},{2,10},{3,11},{4,12},{5,13},{6,14},{7,15},{8,0},{9,1},... | collective-permute-start | bytes 245768 | tf_op jit(solution)/shard_map/ppermute | solution.py:466
  53.1 1.0 %collective-permute-done.6.refs_1_ = bf16[40,1024]{1,0:T(8,128)(2,1)S(1)} collective-permute-done((bf16[40,1024]{1,0:T(8,128)(2,1)S(1)}, bf16[40,1024]{1,0:T(8,128)(2,1)S(1)}, u32[]{:S(2)}, u32[]{:S(2)}) %collective-permute-start.6) | collective-permute-done | bytes 81952 | tf_op jit(solution)/shard_map/ppermute | solution.py:466
  54.1 0.0 collective-permute-start.12
  54.1 0.0 collective-permute-done.7.refs_2_
  54.1 0.0 collective-permute-done.8.refs_3_
  54.1 0.3 shard_map.88.refs_0_
  54.4 0.8 %collective-permute-done.10.refs_1_ = bf16[40,1024]{1,0:T(8,128)(2,1)S(1)} collective-permute-done((bf16[40,1024]{1,0:T(8,128)(2,1)S(1)}, bf16[40,1024]{1,0:T(8,128)(2,1)S(1)}, u32[]{:S(2)}, u32[]{:S(2)}) %collective-permute-start.10) | collective-permute-done | bytes 81952 | tf_op jit(solution)/shard_map/ppermute | solution.py:466
  55.2 5.3 %collective-permute-done.11.refs_2_ = bf16[40,1024]{1,0:T(8,128)(2,1)S(1)} collective-permute-done((bf16[40,1024]{1,0:T(8,128)(2,1)S(1)}, bf16[40,1024]{1,0:T(8,128)(2,1)S(1)}, u32[]{:S(2)}, u32[]{:S(2)}) %collective-permute-start.11) | collective-permute-done | bytes 81952 | tf_op jit(solution)/shard_map/ppermute | solution.py:466
  60.5 0.0 collective-permute-done.12.refs_3_
  60.5 1.0 %shard_map.91 = bf16[128,1024]{1,0:T(8,128)(2,1)} custom-call(bf16[2,128,256]{2,1,0:T(8,128)(2,1)S(1)} %get-tuple-element.48.high, bf16[2,128,256]{2,1,0:T(8,128)(2,1)S(1)} %get-tuple-element.49.refs_15_.low, f32[128,1024]{1,0:T(8,128)S(1)} %shard_map.88.refs_0_, bf16[40,1024]{1,0:T(8,128)(2,1)S(1)} %collective-permute-done.10.refs_1_, ...), custom_call_target="tpu_custom_call" | custom-call | flops 83886080 | bytes 1048576 | tf_op jit(solution)/shard_map/pallas_call | solution.py:433
  (1 shorter events, 0.0 us)
Async XLA Ops:
  2.4 18.9 %collective-permute-start = (bf16[40,2048]{1,0:T(8,128)(2,1)S(1)}, bf16[40,2048]{1,0:T(8,128)(2,1)S(1)}, u32[]{:S(2)}, u32[]{:S(2)}) collective-permute-start(bf16[40,2048]{1,0:T(8,128)(2,1)S(1)} %get-tuple-element.45), channel_id=1, source_target_pairs={{0,4},{1,5},{2,6},{3,7},{4,8},{5,9},{6,10},{7,11},{8,12},{9,13},{1... | collective-permute-start | bytes 491528 | tf_op jit(solution)/shard_map/ppermute | solution.py:466
  5.5 15.9 %collective-permute-start.1 = (bf16[40,2048]{1,0:T(8,128)(2,1)S(1)}, bf16[40,2048]{1,0:T(8,128)(2,1)S(1)}, u32[]{:S(2)}, u32[]{:S(2)}) collective-permute-start(bf16[40,2048]{1,0:T(8,128)(2,1)S(1)} %get-tuple-element.46), channel_id=1, source_target_pairs={{0,8},{1,9},{2,10},{3,11},{4,12},{5,13},{6,14},{7,15},{8,0},{9,1},... | collective-permute-start | bytes 491528 | tf_op jit(solution)/shard_map/ppermute | solution.py:466
  8.1 13.3 %collective-permute-start.2 = (bf16[40,2048]{1,0:T(8,128)(2,1)S(1)}, bf16[40,2048]{1,0:T(8,128)(2,1)S(1)}, u32[]{:S(2)}, u32[]{:S(2)}) collective-permute-start(bf16[40,2048]{1,0:T(8,128)(2,1)S(1)} %get-tuple-element.47), channel_id=1, source_target_pairs={{0,12},{1,13},{2,14},{3,15},{4,0},{5,1},{6,2},{7,3},{8,4},{9,5},{1... | collective-permute-start | bytes 491528 | tf_op jit(solution)/shard_map/ppermute | solution.py:466
  21.4 1.9 %collective-permute-start.3 = (bf16[120,2048]{1,0:T(8,128)(2,1)S(1)}, bf16[120,2048]{1,0:T(8,128)(2,1)S(1)}, u32[]{:S(2)}, u32[]{:S(2)}) collective-permute-start(bf16[120,2048]{1,0:T(8,128)(2,1)S(1)} %shard_map.84.after.mine), channel_id=1, source_target_pairs={{0,1},{1,0},{2,3},{3,2},{4,5},{5,4},{6,7},{7,6},{8,9},{9,8},{10,11... | collective-permute-start | bytes 1474568 | tf_op jit(solution)/shard_map/ppermute | solution.py:469
  36.7 3.8 %collective-permute-start.4 = (bf16[160,1024]{1,0:T(8,128)(2,1)S(1)}, bf16[160,1024]{1,0:T(8,128)(2,1)S(1)}, u32[]{:S(2)}, u32[]{:S(2)}) collective-permute-start(bf16[160,1024]{1,0:T(8,128)(2,1)S(1)} %get-tuple-element.63), channel_id=1, source_target_pairs={{0,1},{1,0},{2,3},{3,2},{4,5},{5,4},{6,7},{7,6},{8,9},{9,8},{10,11... | collective-permute-start | bytes 983048 | tf_op jit(solution)/shard_map/ppermute | solution.py:469
  40.0 7.4 %collective-permute-start.9 = (bf16[160,1024]{1,0:T(8,128)(2,1)S(1)}, bf16[160,1024]{1,0:T(8,128)(2,1)S(1)}, u32[]{:S(2)}, u32[]{:S(2)}) collective-permute-start(bf16[160,1024]{1,0:T(8,128)(2,1)S(1)} %get-tuple-element.72), channel_id=1, source_target_pairs={{0,1},{1,0},{2,3},{3,2},{4,5},{5,4},{6,7},{7,6},{8,9},{9,8},{10,11... | collective-permute-start | bytes 983048 | tf_op jit(solution)/shard_map/ppermute | solution.py:469
  41.8 10.5 %collective-permute-start.5 = (bf16[40,1024]{1,0:T(8,128)(2,1)S(1)}, bf16[40,1024]{1,0:T(8,128)(2,1)S(1)}, u32[]{:S(2)}, u32[]{:S(2)}) collective-permute-start(bf16[40,1024]{1,0:T(8,128)(2,1)S(1)} %get-tuple-element.66), channel_id=1, source_target_pairs={{0,14},{1,15},{2,12},{3,13},{4,2},{5,3},{6,0},{7,1},{8,6},{9,7},{1... | collective-permute-start | bytes 245768 | tf_op jit(solution)/shard_map/ppermute | solution.py:466
  45.3 8.8 %collective-permute-start.6 = (bf16[40,1024]{1,0:T(8,128)(2,1)S(1)}, bf16[40,1024]{1,0:T(8,128)(2,1)S(1)}, u32[]{:S(2)}, u32[]{:S(2)}) collective-permute-start(bf16[40,1024]{1,0:T(8,128)(2,1)S(1)} %get-tuple-element.67), channel_id=1, source_target_pairs={{0,10},{1,11},{2,8},{3,9},{4,14},{5,15},{6,12},{7,13},{8,2},{9,3},... | collective-permute-start | bytes 245768 | tf_op jit(solution)/shard_map/ppermute | solution.py:466
  45.7 8.5 %collective-permute-start.7 = (bf16[40,1024]{1,0:T(8,128)(2,1)S(1)}, bf16[40,1024]{1,0:T(8,128)(2,1)S(1)}, u32[]{:S(2)}, u32[]{:S(2)}) collective-permute-start(bf16[40,1024]{1,0:T(8,128)(2,1)S(1)} %get-tuple-element.68), channel_id=1, source_target_pairs={{0,6},{1,7},{2,4},{3,5},{4,10},{5,11},{6,8},{7,9},{8,14},{9,15},{1... | collective-permute-start | bytes 245768 | tf_op jit(solution)/shard_map/ppermute | solution.py:466
  46.1 8.0 %collective-permute-start.8 = (bf16[40,1024]{1,0:T(8,128)(2,1)S(1)}, bf16[40,1024]{1,0:T(8,128)(2,1)S(1)}, u32[]{:S(2)}, u32[]{:S(2)}) collective-permute-start(bf16[40,1024]{1,0:T(8,128)(2,1)S(1)} %get-tuple-element.69), channel_id=1, source_target_pairs={{0,2},{1,3},{2,0},{3,1},{4,6},{5,7},{6,4},{7,5},{8,10},{9,11},{10,... | collective-permute-start | bytes 245768 | tf_op jit(solution)/shard_map/ppermute | solution.py:466
  48.8 6.5 %collective-permute-start.10 = (bf16[40,1024]{1,0:T(8,128)(2,1)S(1)}, bf16[40,1024]{1,0:T(8,128)(2,1)S(1)}, u32[]{:S(2)}, u32[]{:S(2)}) collective-permute-start(bf16[40,1024]{1,0:T(8,128)(2,1)S(1)} %get-tuple-element.75), channel_id=1, source_target_pairs={{0,12},{1,13},{2,14},{3,15},{4,0},{5,1},{6,2},{7,3},{8,4},{9,5},{1... | collective-permute-start | bytes 245768 | tf_op jit(solution)/shard_map/ppermute | solution.py:466
  52.4 8.1 %collective-permute-start.11 = (bf16[40,1024]{1,0:T(8,128)(2,1)S(1)}, bf16[40,1024]{1,0:T(8,128)(2,1)S(1)}, u32[]{:S(2)}, u32[]{:S(2)}) collective-permute-start(bf16[40,1024]{1,0:T(8,128)(2,1)S(1)} %get-tuple-element.76), channel_id=1, source_target_pairs={{0,8},{1,9},{2,10},{3,11},{4,12},{5,13},{6,14},{7,15},{8,0},{9,1},... | collective-permute-start | bytes 245768 | tf_op jit(solution)/shard_map/ppermute | solution.py:466
  54.1 6.4 %collective-permute-start.12 = (bf16[40,1024]{1,0:T(8,128)(2,1)S(1)}, bf16[40,1024]{1,0:T(8,128)(2,1)S(1)}, u32[]{:S(2)}, u32[]{:S(2)}) collective-permute-start(bf16[40,1024]{1,0:T(8,128)(2,1)S(1)} %get-tuple-element.77), channel_id=1, source_target_pairs={{0,4},{1,5},{2,6},{3,7},{4,8},{5,9},{6,10},{7,11},{8,12},{9,13},{1... | collective-permute-start | bytes 245768 | tf_op jit(solution)/shard_map/ppermute | solution.py:466

commit v11 on v10

--- a/solution.py
+++ b/solution.py
@@ -234,9 +234,14 @@
     await_all(buffer, gate_sem)
 
 
+def distances(exp_count):
+    middle = exp_count // 2
+    return [middle] + [d for d in range(1, exp_count) if d != middle]
+
+
 def arrivals(sizes):
     exp_count, groups = sizes
-    order = list(range(1, exp_count)) + [0]
+    order = distances(exp_count) + [0]
     early = [(o, d) for o in range(1, groups) for d in order]
     late = [(0, d) for d in order]
     return early, late
@@ -308,8 +313,8 @@
         await_all(buffer, sems.at[n])
 
 
-def join_kernel(after, *refs):
-    pieces = [r[...].astype(F32) for r in refs[:-1]]
+def join_kernel(order, after, *refs):
+    pieces = [refs[order.index(d + 1)][...].astype(F32) for d in range(len(order))]
     refs[-1][...] = jnp.concatenate(pieces, axis=0).astype(BF16)
 
 
@@ -379,31 +384,33 @@
 
 def give_kernel(sizes, offset, hidden, *refs):
     exp_count, groups = sizes
-    steps = (len(refs) - 3) // 2
-    weights, (down, given), kept_weights, sems = (
-        refs[:steps],
-        refs[steps : steps + 2],
-        refs[steps + 2 : -1],
-        refs[-1],
-    )
-    for step, buffer in enumerate(kept_weights):
-        fetch_columns(sizes, down, offset, True, step, buffer, sems.at[step])
+    *weights, down, given, kept_weights, sem = refs
+    fetch_columns(sizes, down, offset, True, 0, kept_weights, sem)
     for step, buffer in enumerate(weights):
         value = jnp.dot(hidden[...], stacked(buffer), preferred_element_type=F32)
         given[:, step * BLOCK : (step + 1) * BLOCK] = value.astype(BF16)
-    for step, buffer in enumerate(kept_weights):
-        await_all(buffer, sems.at[step])
-
-
-def keep_kernel(sizes, hidden, received, *refs):
-    exp_count, groups = sizes
-    weights, outs = refs[:-exp_count], refs[-exp_count:]
+    await_all(kept_weights, sem)
+
+
+def keep_kernel(sizes, ahead, hidden, received, *refs):
+    exp_count, groups = sizes
+    refs = list(refs)
+    if ahead is not None:
+        sem, down = refs.pop(), refs.pop(0)
+        next_weights = refs[received.shape[1] // BLOCK + exp_count :]
+        for step, buffer in enumerate(next_weights, 1):
+            fetch_columns(sizes, down, ahead, True, step, buffer, sem.at[step - 1])
+    weights = refs[: received.shape[1] // BLOCK]
+    outs = refs[len(weights) : len(weights) + exp_count]
     for step, buffer in enumerate(weights):
         cols = slice(step * BLOCK, (step + 1) * BLOCK)
         value = jnp.dot(hidden[...], stacked(buffer), preferred_element_type=F32)
         value = value + received[:, cols].astype(F32)
         for d in range(exp_count):
             outs[d][:, cols] = value[d * CAP : (d + 1) * CAP, :].astype(BF16)
+    if ahead is not None:
+        for step, buffer in enumerate(next_weights, 1):
+            await_all(buffer, sem.at[step - 1])
 
 
 def combine_kernel(order, high, low, *refs):
@@ -510,9 +517,9 @@
         moved=(READY - 1) * piece_bytes,
         aliases={4: 1},
     )
-    arrived = [shift(value, d + 1) for d, value in enumerate(sends)]
+    arrived = [shift(sends[d - 1], d) for d in distances(exp_count)]
     mine = call(
-        join_kernel,
+        functools.partial(join_kernel, distances(exp_count)),
         [((batch * CAP, width), BF16)],
         [(mask, pl.ANY)] + [(v, None) for v in arrived],
         moved=1 << 20,
@@ -558,28 +565,34 @@
         first = 2 * features // BLOCK + order * steps
         value, *kept = call(
             functools.partial(give_kernel, sizes, offset),
-            [((slots, part), BF16)] + [buffer] * steps,
+            [((slots, part), BF16), buffer],
             [(hidden, None)]
             + [(buffers[(first + step) % BUFFERS], pltpu.VMEM) for step in range(steps)]
             + [(down_weight, pltpu.HBM)],
-            [pltpu.SemaphoreType.DMA((steps,))],
+            [pltpu.SemaphoreType.DMA],
             flops=2 * slots * unit_width * part,
-            moved=steps * piece_bytes,
+            moved=piece_bytes,
         )
         given.append(value)
         kept_weights.append(kept)
     taken = [swap(value) for value in given]
     home = {}
     for order, offset in enumerate(offsets):
-        kept = call(
-            functools.partial(keep_kernel, sizes),
-            [((CAP, part), BF16)] * exp_count,
+        more = order < groups - 1
+        outs = call(
+            functools.partial(keep_kernel, sizes, offsets[order + 1] if more else None),
+            [((CAP, part), BF16)] * exp_count + [buffer] * (steps - 1 if more else 0),
             [(hidden, None), (taken[order], None)]
+            + ([(down_weight, pltpu.HBM)] if more else [])
             + [(v, pltpu.VMEM) for v in kept_weights[order]],
+            [pltpu.SemaphoreType.DMA((steps - 1,))] if more else [],
             flops=2 * slots * unit_width * part,
             moved=piece_bytes,
         )
-        for d in list(range(1, exp_count)) + [0]:
+        kept = outs[:exp_count]
+        if more:
+            kept_weights[order + 1] = list(kept_weights[order + 1]) + list(outs[exp_count:])
+        for d in distances(exp_count) + [0]:
             home[offset, d] = shift(kept[d], -d, offset) if d or offset else kept[d]
     mixed = None
     for order, batch in enumerate(arrivals(sizes)):

time: 61.8 us -> 60.9 us (0.985)
  waiting for transfers between devices: 7.94 us -> 6.49 us
  starting transfers between devices: 17.6 us -> 18.6 us
    ppermute x10, waiting for transfers between devices: 7.1 us -> 5.64 us  [shift(): return lax.ppermute(value, ('exp', 'unit'), pairs)]
    ppermute x10, starting transfers between devices: 16.9 us -> 17.9 us  [shift(): return lax.ppermute(value, ('exp', 'unit'), pairs)]
  transfers between devices with their start and end apart: 13 -> 13, of which waited for: 4 -> 6; matrix products, arithmetic and copies ran while one was open for 0% -> 0% of each run, Pallas kernels for 31% -> 31%
where the time goes in v11:
time: 60.9 us; the launch traced here: 60.5 us
  Pallas kernels  35.3 us (58%)
  starting transfers between devices  18.6 us (31%)
  waiting for transfers between devices  6.49 us (11%)
    pallas_call x10, Pallas kernels, call(): pl.pallas_call(kernel, out_shape=shapes, in_specs=specs, out_specs=[vmem]...  35.3 us
    ppermute x10, starting transfers between devices, shift(): return lax.ppermute(value, ('exp', 'unit'), pairs)  17.9 us
    ppermute x10, waiting for transfers between devices, shift(): return lax.ppermute(value, ('exp', 'unit'), pairs)  5.64 us
  transfers between devices with their start and end apart: 13, of which 6 were waited for; matrix products, arithmetic and copies ran while one was open for 0% of the time, Pallas kernels for 31%

profile of v11, /device:TPU:0, one launch (start us, length us, event | category | flops | bytes accessed | tf_op | source)
XLA Modules:
  0.0 60.5 jit_solution(3357721241507437521)
XLA Ops:
  0.0 2.4 %shard_map.82 = (bf16[40,4096]{1,0:T(8,128)(2,1)S(1)}, bf16[7,512,512]{2,1,0:T(8,128)(2,1)S(1)}, bf16[40,2048]{1,0:T(8,128)(2,1)S(1)}, bf16[40,2048]{1,0:T(8,128)(2,1)S(1)}, bf16[40,2048]{1,0:T(8,128)(2,1)S(1)}) custom-call(bf16[128,4096]{1,0:T(8,128)(2,1)} %tokens_hbm.1, f32[1,4096]{1,0:T(1,128)} %bitcast.3, s32[2,128]{1,0:T(2,128)} %bitcast.4, ...), custom_call_target="tpu_custom_call" | custom-call | flops 83886080 | bytes 5767168 | tf_op jit(solution)/shard_map/pallas_call | solution.py:440
  2.4 4.1 %collective-permute-start = (bf16[40,2048]{1,0:T(8,128)(2,1)S(1)}, bf16[40,2048]{1,0:T(8,128)(2,1)S(1)}, u32[]{:S(2)}, u32[]{:S(2)}) collective-permute-start(bf16[40,2048]{1,0:T(8,128)(2,1)S(1)} %get-tuple-element.45), channel_id=1, source_target_pairs={{0,8},{1,9},{2,10},{3,11},{4,12},{5,13},{6,14},{7,15},{8,0},{9,1},... | collective-permute-start | bytes 491528 | tf_op jit(solution)/shard_map/ppermute | solution.py:473
  6.5 1.6 %collective-permute-start.1 = (bf16[40,2048]{1,0:T(8,128)(2,1)S(1)}, bf16[40,2048]{1,0:T(8,128)(2,1)S(1)}, u32[]{:S(2)}, u32[]{:S(2)}) collective-permute-start(bf16[40,2048]{1,0:T(8,128)(2,1)S(1)} %get-tuple-element.46), channel_id=1, source_target_pairs={{0,4},{1,5},{2,6},{3,7},{4,8},{5,9},{6,10},{7,11},{8,12},{9,13},{1... | collective-permute-start | bytes 491528 | tf_op jit(solution)/shard_map/ppermute | solution.py:473
  8.1 2.2 %collective-permute-start.2 = (bf16[40,2048]{1,0:T(8,128)(2,1)S(1)}, bf16[40,2048]{1,0:T(8,128)(2,1)S(1)}, u32[]{:S(2)}, u32[]{:S(2)}) collective-permute-start(bf16[40,2048]{1,0:T(8,128)(2,1)S(1)} %get-tuple-element.47), channel_id=1, source_target_pairs={{0,12},{1,13},{2,14},{3,15},{4,0},{5,1},{6,2},{7,3},{8,4},{9,5},{1... | collective-permute-start | bytes 491528 | tf_op jit(solution)/shard_map/ppermute | solution.py:473
  10.4 11.9 %shard_map.83 = (f32[8,3584]{1,0:T(8,128)S(1)}, bf16[7,512,512]{2,1,0:T(8,128)(2,1)S(1)}, bf16[7,512,512]{2,1,0:T(8,128)(2,1)S(1)}, bf16[7,512,512]{2,1,0:T(8,12...) custom-call(s32[2,8,48]{2,1,0:T(8,128)} %active_hbm.1, ...), custom_call_target="tpu_custom_call", output_to_operand_aliasing={{1}: (4, {})} | custom-call | flops 167772160 | bytes 36700160 | tf_op jit(solution)/shard_map/pallas_call | solution.py:440
  22.3 0.0 collective-permute-done.refs_0_
  22.3 0.0 collective-permute-done.1.refs_1_
  22.3 0.0 collective-permute-done.2.refs_2_
  22.4 0.1 collective-permute-start.3
  22.4 1.0 %shard_map.85 = (bf16[2,128,256]{2,1,0:T(8,128)(2,1)S(1)}, bf16[2,128,256]{2,1,0:T(8,128)(2,1)S(1)}) custom-call(s32[2,128]{1,0:T(2,128)} %bitcast.5, f32[2,128]{1,0:T(2,128)} %bitcast.6, bf16[120,2048]{1,0:T(8,128)(2,1)S(1)} %shard_map.84.after.mine), custom_call_target="tpu_custom_call" | custom-call | bytes 2097152 | tf_op jit(solution)/shard_map/pallas_call | solution.py:440
  23.4 0.8 %collective-permute-done.3.other = bf16[120,2048]{1,0:T(8,128)(2,1)S(1)} collective-permute-done((bf16[120,2048]{1,0:T(8,128)(2,1)S(1)}, bf16[120,2048]{1,0:T(8,128)(2,1)S(1)}, u32[]{:S(2)}, u32[]{:S(2)}) %collective-permute-start.3) | collective-permute-done | bytes 491552 | tf_op jit(solution)/shard_map/ppermute | solution.py:476
  24.3 13.3 %shard_map.86 = (bf16[160,3584]{1,0:T(8,128)(2,1)S(1)}, bf16[160,1024]{1,0:T(8,128)(2,1)S(1)}, bf16[7,512,512]{2,1,0:T(8,128)(2,1)S(1)}, bf16[7,512,512]{2,1,0:T...) custom-call(bf16[40,4096]{1,0:T(8,128)(2,1)S(1)} %get-tuple-element., ...), custom_call_target="tpu_custom_call", output_to_operand_aliasing={{2}: (3, {}), {3}: (4, {}), {4}: (5, {}), {5}: (6, {}), {6}... | custom-call | flops 9395240960 | bytes 36700160 | tf_op jit(solution)/shard_map/pallas_call | solution.py:440
  37.6 0.2 collective-permute-start.4
  37.8 2.0 %shard_map.89 = (bf16[160,1024]{1,0:T(8,128)(2,1)S(1)}, bf16[7,512,512]{2,1,0:T(8,128)(2,1)S(1)}) custom-call(bf16[160,3584]{1,0:T(8,128)(2,1)S(1)} %get-tuple-element.62.hidden, bf16[7,512,512]{2,1,0:T(8,128)(2,1)S(1)} %get-tuple-element.70.refs_0_, bf16[7,512,512]{2,1,0:T(8,128)(2,1)S(1)} %get-tuple-element.71.refs_1_, bf16[3584,4096]{1,0:T(8,128)(2,1)} %refs_2_.1), custom_call_target="tpu_custom_call" | custom-call | flops 1174405120 | bytes 3670016 | tf_op jit(solution)/shard_map/pallas_call | solution.py:440
  39.8 0.4 collective-permute-start.9
  40.3 0.0 collective-permute-done.4.received
  40.3 2.0 %shard_map.87 = (bf16[40,1024]{1,0:T(8,128)(2,1)S(1)}, bf16[40,1024]{1,0:T(8,128)(2,1)S(1)}, bf16[40,1024]{1,0:T(8,128)(2,1)S(1)}, bf16[40,1024]{1,0:T(8,128)(2,1)S(1)}, bf16[7,512,512]{2,1,0:T(8,128)(2,1)S(1)}) custom-call(bf16[160,3584]{1,0:T(8,128)(2,1)S(1)} %get-tuple-element.62.hidden, bf16[160,1024]{1,0:T(8,128)(2,1)S(1)} %collective-permute-done.4.received, ...), custom_call_target="tpu_custom_call" | custom-call | flops 1174405120 | bytes 3670016 | tf_op jit(solution)/shard_map/pallas_call | solution.py:440
  42.3 2.6 %collective-permute-start.5 = (bf16[40,1024]{1,0:T(8,128)(2,1)S(1)}, bf16[40,1024]{1,0:T(8,128)(2,1)S(1)}, u32[]{:S(2)}, u32[]{:S(2)}) collective-permute-start(bf16[40,1024]{1,0:T(8,128)(2,1)S(1)} %get-tuple-element.66), channel_id=1, source_target_pairs={{0,10},{1,11},{2,8},{3,9},{4,14},{5,15},{6,12},{7,13},{8,2},{9,3},... | collective-permute-start | bytes 245768 | tf_op jit(solution)/shard_map/ppermute | solution.py:473
  44.9 0.5 collective-permute-start.6
  45.4 2.4 %collective-permute-start.7 = (bf16[40,1024]{1,0:T(8,128)(2,1)S(1)}, bf16[40,1024]{1,0:T(8,128)(2,1)S(1)}, u32[]{:S(2)}, u32[]{:S(2)}) collective-permute-start(bf16[40,1024]{1,0:T(8,128)(2,1)S(1)} %get-tuple-element.68), channel_id=1, source_target_pairs={{0,6},{1,7},{2,4},{3,5},{4,10},{5,11},{6,8},{7,9},{8,14},{9,15},{1... | collective-permute-start | bytes 245768 | tf_op jit(solution)/shard_map/ppermute | solution.py:473
  47.8 0.5 collective-permute-start.8
  48.3 0.0 collective-permute-done.9.received
  48.3 1.4 %shard_map.90 = (bf16[40,1024]{1,0:T(8,128)(2,1)S(1)}, bf16[40,1024]{1,0:T(8,128)(2,1)S(1)}, bf16[40,1024]{1,0:T(8,128)(2,1)S(1)}, bf16[40,1024]{1,0:T(8,128)(2,1)S(1)}) custom-call(bf16[160,3584]{1,0:T(8,128)(2,1)S(1)} %get-tuple-element.62.hidden, bf16[160,1024]{1,0:T(8,128)(2,1)S(1)} %collective-permute-done.9.received, ...), custom_call_target="tpu_custom_call" | custom-call | flops 1174405120 | bytes 3670016 | tf_op jit(solution)/shard_map/pallas_call | solution.py:440
  49.7 1.4 %collective-permute-start.10 = (bf16[40,1024]{1,0:T(8,128)(2,1)S(1)}, bf16[40,1024]{1,0:T(8,128)(2,1)S(1)}, u32[]{:S(2)}, u32[]{:S(2)}) collective-permute-start(bf16[40,1024]{1,0:T(8,128)(2,1)S(1)} %get-tuple-element.75), channel_id=1, source_target_pairs={{0,8},{1,9},{2,10},{3,11},{4,12},{5,13},{6,14},{7,15},{8,0},{9,1},... | collective-permute-start | bytes 245768 | tf_op jit(solution)/shard_map/ppermute | solution.py:473
  51.1 0.0 collective-permute-done.5.refs_0_
  51.1 1.1 %collective-permute-start.11 = (bf16[40,1024]{1,0:T(8,128)(2,1)S(1)}, bf16[40,1024]{1,0:T(8,128)(2,1)S(1)}, u32[]{:S(2)}, u32[]{:S(2)}) collective-permute-start(bf16[40,1024]{1,0:T(8,128)(2,1)S(1)} %get-tuple-element.76), channel_id=1, source_target_pairs={{0,12},{1,13},{2,14},{3,15},{4,0},{5,1},{6,2},{7,3},{8,4},{9,5},{1... | collective-permute-start | bytes 245768 | tf_op jit(solution)/shard_map/ppermute | solution.py:473
  52.2 1.0 %collective-permute-done.6.refs_1_ = bf16[40,1024]{1,0:T(8,128)(2,1)S(1)} collective-permute-done((bf16[40,1024]{1,0:T(8,128)(2,1)S(1)}, bf16[40,1024]{1,0:T(8,128)(2,1)S(1)}, u32[]{:S(2)}, u32[]{:S(2)}) %collective-permute-start.6) | collective-permute-done | bytes 81952 | tf_op jit(solution)/shard_map/ppermute | solution.py:473
  53.2 1.4 %collective-permute-start.12 = (bf16[40,1024]{1,0:T(8,128)(2,1)S(1)}, bf16[40,1024]{1,0:T(8,128)(2,1)S(1)}, u32[]{:S(2)}, u32[]{:S(2)}) collective-permute-start(bf16[40,1024]{1,0:T(8,128)(2,1)S(1)} %get-tuple-element.77), channel_id=1, source_target_pairs={{0,4},{1,5},{2,6},{3,7},{4,8},{5,9},{6,10},{7,11},{8,12},{9,13},{1... | collective-permute-start | bytes 245768 | tf_op jit(solution)/shard_map/ppermute | solution.py:473
  54.6 0.0 collective-permute-done.7.refs_2_
  54.6 0.2 collective-permute-done.8.refs_3_
  54.9 0.3 shard_map.88.refs_0_
  55.2 1.7 %collective-permute-done.10.refs_1_ = bf16[40,1024]{1,0:T(8,128)(2,1)S(1)} collective-permute-done((bf16[40,1024]{1,0:T(8,128)(2,1)S(1)}, bf16[40,1024]{1,0:T(8,128)(2,1)S(1)}, u32[]{:S(2)}, u32[]{:S(2)}) %collective-permute-start.10) | collective-permute-done | bytes 81952 | tf_op jit(solution)/shard_map/ppermute | solution.py:473
  56.8 0.4 collective-permute-done.11.refs_2_
  57.2 2.3 %collective-permute-done.12.refs_3_ = bf16[40,1024]{1,0:T(8,128)(2,1)S(1)} collective-permute-done((bf16[40,1024]{1,0:T(8,128)(2,1)S(1)}, bf16[40,1024]{1,0:T(8,128)(2,1)S(1)}, u32[]{:S(2)}, u32[]{:S(2)}) %collective-permute-start.12) | collective-permute-done | bytes 81952 | tf_op jit(solution)/shard_map/ppermute | solution.py:473
  59.5 1.0 %shard_map.91 = bf16[128,1024]{1,0:T(8,128)(2,1)} custom-call(bf16[2,128,256]{2,1,0:T(8,128)(2,1)S(1)} %get-tuple-element.48.high, bf16[2,128,256]{2,1,0:T(8,128)(2,1)S(1)} %get-tuple-element.49.refs_15_.low, f32[128,1024]{1,0:T(8,128)S(1)} %shard_map.88.refs_0_, bf16[40,1024]{1,0:T(8,128)(2,1)S(1)} %collective-permute-done.10.refs_1_, ...), custom_call_target="tpu_custom_call" | custom-call | flops 83886080 | bytes 1048576 | tf_op jit(solution)/shard_map/pallas_call | solution.py:440
  (1 shorter events, 0.0 us)
Async XLA Ops:
  2.4 19.9 %collective-permute-start = (bf16[40,2048]{1,0:T(8,128)(2,1)S(1)}, bf16[40,2048]{1,0:T(8,128)(2,1)S(1)}, u32[]{:S(2)}, u32[]{:S(2)}) collective-permute-start(bf16[40,2048]{1,0:T(8,128)(2,1)S(1)} %get-tuple-element.45), channel_id=1, source_target_pairs={{0,8},{1,9},{2,10},{3,11},{4,12},{5,13},{6,14},{7,15},{8,0},{9,1},... | collective-permute-start | bytes 491528 | tf_op jit(solution)/shard_map/ppermute | solution.py:473
  6.5 15.8 %collective-permute-start.1 = (bf16[40,2048]{1,0:T(8,128)(2,1)S(1)}, bf16[40,2048]{1,0:T(8,128)(2,1)S(1)}, u32[]{:S(2)}, u32[]{:S(2)}) collective-permute-start(bf16[40,2048]{1,0:T(8,128)(2,1)S(1)} %get-tuple-element.46), channel_id=1, source_target_pairs={{0,4},{1,5},{2,6},{3,7},{4,8},{5,9},{6,10},{7,11},{8,12},{9,13},{1... | collective-permute-start | bytes 491528 | tf_op jit(solution)/shard_map/ppermute | solution.py:473
  8.1 14.2 %collective-permute-start.2 = (bf16[40,2048]{1,0:T(8,128)(2,1)S(1)}, bf16[40,2048]{1,0:T(8,128)(2,1)S(1)}, u32[]{:S(2)}, u32[]{:S(2)}) collective-permute-start(bf16[40,2048]{1,0:T(8,128)(2,1)S(1)} %get-tuple-element.47), channel_id=1, source_target_pairs={{0,12},{1,13},{2,14},{3,15},{4,0},{5,1},{6,2},{7,3},{8,4},{9,5},{1... | collective-permute-start | bytes 491528 | tf_op jit(solution)/shard_map/ppermute | solution.py:473
  22.4 1.9 %collective-permute-start.3 = (bf16[120,2048]{1,0:T(8,128)(2,1)S(1)}, bf16[120,2048]{1,0:T(8,128)(2,1)S(1)}, u32[]{:S(2)}, u32[]{:S(2)}) collective-permute-start(bf16[120,2048]{1,0:T(8,128)(2,1)S(1)} %shard_map.84.after.mine), channel_id=1, source_target_pairs={{0,1},{1,0},{2,3},{3,2},{4,5},{5,4},{6,7},{7,6},{8,9},{9,8},{10,11... | collective-permute-start | bytes 1474568 | tf_op jit(solution)/shard_map/ppermute | solution.py:476
  37.6 2.7 %collective-permute-start.4 = (bf16[160,1024]{1,0:T(8,128)(2,1)S(1)}, bf16[160,1024]{1,0:T(8,128)(2,1)S(1)}, u32[]{:S(2)}, u32[]{:S(2)}) collective-permute-start(bf16[160,1024]{1,0:T(8,128)(2,1)S(1)} %get-tuple-element.63), channel_id=1, source_target_pairs={{0,1},{1,0},{2,3},{3,2},{4,5},{5,4},{6,7},{7,6},{8,9},{9,8},{10,11... | collective-permute-start | bytes 983048 | tf_op jit(solution)/shard_map/ppermute | solution.py:476
  39.8 8.5 %collective-permute-start.9 = (bf16[160,1024]{1,0:T(8,128)(2,1)S(1)}, bf16[160,1024]{1,0:T(8,128)(2,1)S(1)}, u32[]{:S(2)}, u32[]{:S(2)}) collective-permute-start(bf16[160,1024]{1,0:T(8,128)(2,1)S(1)} %get-tuple-element.72), channel_id=1, source_target_pairs={{0,1},{1,0},{2,3},{3,2},{4,5},{5,4},{6,7},{7,6},{8,9},{9,8},{10,11... | collective-permute-start | bytes 983048 | tf_op jit(solution)/shard_map/ppermute | solution.py:476
  42.3 8.8 %collective-permute-start.5 = (bf16[40,1024]{1,0:T(8,128)(2,1)S(1)}, bf16[40,1024]{1,0:T(8,128)(2,1)S(1)}, u32[]{:S(2)}, u32[]{:S(2)}) collective-permute-start(bf16[40,1024]{1,0:T(8,128)(2,1)S(1)} %get-tuple-element.66), channel_id=1, source_target_pairs={{0,10},{1,11},{2,8},{3,9},{4,14},{5,15},{6,12},{7,13},{8,2},{9,3},... | collective-permute-start | bytes 245768 | tf_op jit(solution)/shard_map/ppermute | solution.py:473
  44.9 8.4 %collective-permute-start.6 = (bf16[40,1024]{1,0:T(8,128)(2,1)S(1)}, bf16[40,1024]{1,0:T(8,128)(2,1)S(1)}, u32[]{:S(2)}, u32[]{:S(2)}) collective-permute-start(bf16[40,1024]{1,0:T(8,128)(2,1)S(1)} %get-tuple-element.67), channel_id=1, source_target_pairs={{0,14},{1,15},{2,12},{3,13},{4,2},{5,3},{6,0},{7,1},{8,6},{9,7},{1... | collective-permute-start | bytes 245768 | tf_op jit(solution)/shard_map/ppermute | solution.py:473
  45.4 9.3 %collective-permute-start.7 = (bf16[40,1024]{1,0:T(8,128)(2,1)S(1)}, bf16[40,1024]{1,0:T(8,128)(2,1)S(1)}, u32[]{:S(2)}, u32[]{:S(2)}) collective-permute-start(bf16[40,1024]{1,0:T(8,128)(2,1)S(1)} %get-tuple-element.68), channel_id=1, source_target_pairs={{0,6},{1,7},{2,4},{3,5},{4,10},{5,11},{6,8},{7,9},{8,14},{9,15},{1... | collective-permute-start | bytes 245768 | tf_op jit(solution)/shard_map/ppermute | solution.py:473
  47.8 7.1 %collective-permute-start.8 = (bf16[40,1024]{1,0:T(8,128)(2,1)S(1)}, bf16[40,1024]{1,0:T(8,128)(2,1)S(1)}, u32[]{:S(2)}, u32[]{:S(2)}) collective-permute-start(bf16[40,1024]{1,0:T(8,128)(2,1)S(1)} %get-tuple-element.69), channel_id=1, source_target_pairs={{0,2},{1,3},{2,0},{3,1},{4,6},{5,7},{6,4},{7,5},{8,10},{9,11},{10,... | collective-permute-start | bytes 245768 | tf_op jit(solution)/shard_map/ppermute | solution.py:473
  49.7 7.1 %collective-permute-start.10 = (bf16[40,1024]{1,0:T(8,128)(2,1)S(1)}, bf16[40,1024]{1,0:T(8,128)(2,1)S(1)}, u32[]{:S(2)}, u32[]{:S(2)}) collective-permute-start(bf16[40,1024]{1,0:T(8,128)(2,1)S(1)} %get-tuple-element.75), channel_id=1, source_target_pairs={{0,8},{1,9},{2,10},{3,11},{4,12},{5,13},{6,14},{7,15},{8,0},{9,1},... | collective-permute-start | bytes 245768 | tf_op jit(solution)/shard_map/ppermute | solution.py:473
  51.1 6.1 %collective-permute-start.11 = (bf16[40,1024]{1,0:T(8,128)(2,1)S(1)}, bf16[40,1024]{1,0:T(8,128)(2,1)S(1)}, u32[]{:S(2)}, u32[]{:S(2)}) collective-permute-start(bf16[40,1024]{1,0:T(8,128)(2,1)S(1)} %get-tuple-element.76), channel_id=1, source_target_pairs={{0,12},{1,13},{2,14},{3,15},{4,0},{5,1},{6,2},{7,3},{8,4},{9,5},{1... | collective-permute-start | bytes 245768 | tf_op jit(solution)/shard_map/ppermute | solution.py:473
  53.2 6.3 %collective-permute-start.12 = (bf16[40,1024]{1,0:T(8,128)(2,1)S(1)}, bf16[40,1024]{1,0:T(8,128)(2,1)S(1)}, u32[]{:S(2)}, u32[]{:S(2)}) collective-permute-start(bf16[40,1024]{1,0:T(8,128)(2,1)S(1)} %get-tuple-element.77), channel_id=1, source_target_pairs={{0,4},{1,5},{2,6},{3,7},{4,8},{5,9},{6,10},{7,11},{8,12},{9,13},{1... | collective-permute-start | bytes 245768 | tf_op jit(solution)/shard_map/ppermute | solution.py:473

commit v12 on v11

--- a/solution.py
+++ b/solution.py
@@ -247,8 +247,14 @@
     return early, late
 
 
-def table_kernel(sizes, ids_hbm, weights_hbm, after, combine_high, combine_low, ids, weights, sems):
-    exp_count, groups = sizes
+def table_kernel(
+    sizes, ids_hbm, weights_hbm, after, gate, up, _, combine_high, combine_low, buffer, ids, weights,
+    sems, sem
+):
+    exp_count, groups = sizes
+    lines = gate.shape[0] // BLOCK
+    last = READY - 1
+    fetch_rows(gate if last < lines else up, last % lines, buffer, sem)
     pairs = ((ids_hbm, ids), (weights_hbm, weights))
     copies = [pltpu.make_async_copy(a, b, sems.at[n]) for n, (a, b) in enumerate(pairs)]
     for copy in copies:
@@ -284,6 +290,7 @@
         high = table.astype(BF16)
         combine_high[order] = high
         combine_low[order] = (table - high.astype(F32)).astype(BF16)
+    await_all(buffer, sem)
 
 
 def prepare_kernel(sizes, rows, active_hbm, gate, up, after, _, mask, *rest):
@@ -293,7 +300,7 @@
     small = pltpu.make_async_copy(active_hbm, active, small_sem)
     small.start()
     lines = gate.shape[0] // BLOCK
-    for n, buffer in enumerate(buffers[1:READY], 1):
+    for n, buffer in enumerate(buffers[1 : READY - 1], 1):
         fetch_rows(gate if n < lines else up, n % lines, buffer, sems.at[n])
     small.wait()
     unit_width = mask.shape[1]
@@ -309,7 +316,7 @@
         return jnp.where(blocks == entry, 1.0, found)
 
     mask[...] = lax.fori_loop(0, active.shape[2], add_entry, jnp.zeros(mask.shape, F32))
-    for n, buffer in enumerate(buffers[1:READY], 1):
+    for n, buffer in enumerate(buffers[1 : READY - 1], 1):
         await_all(buffer, sems.at[n])
 
 
@@ -514,28 +521,38 @@
             pltpu.SemaphoreType.DMA((READY,)),
         ],
         flops=2 * tok_count * slots * features,
-        moved=(READY - 1) * piece_bytes,
+        moved=(READY - 2) * piece_bytes,
         aliases={4: 1},
     )
-    arrived = [shift(sends[d - 1], d) for d in distances(exp_count)]
+    order = list(range(exp_count - 1, 0, -1))
+    arrived = [shift(sends[d - 1], d) for d in order]
     mine = call(
-        functools.partial(join_kernel, distances(exp_count)),
+        functools.partial(join_kernel, order),
         [((batch * CAP, width), BF16)],
         [(mask, pl.ANY)] + [(v, None) for v in arrived],
         moved=1 << 20,
     )[0]
     other = swap(mine)
     padded = -(-slots // 128) * 128
-    combine_high, combine_low = call(
+    combine_high, combine_low, ready[READY - 1] = call(
         functools.partial(table_kernel, sizes),
-        [((2, tok_count, padded), BF16)] * 2,
-        [(ids, pltpu.HBM), (weights, pltpu.HBM), (mine, pl.ANY)],
+        [((2, tok_count, padded), BF16)] * 2 + [buffer],
+        [
+            (ids, pltpu.HBM),
+            (weights, pltpu.HBM),
+            (mine, pl.ANY),
+            (gate_weight, pltpu.HBM),
+            (up_weight, pltpu.HBM),
+            (ready[READY - 1], pltpu.VMEM),
+        ],
         [
             pltpu.VMEM(ids.shape, jnp.int32),
             pltpu.VMEM(weights.shape, F32),
             pltpu.SemaphoreType.DMA((2,)),
+            pltpu.SemaphoreType.DMA,
         ],
-        moved=1 << 21,
+        moved=1 << 22,
+        aliases={5: 2},
     )
     acc = pltpu.VMEM((slots, unit_width), F32)
     part = features // unit_count

time: 60.9 us -> 61.7 us (1.013)
  waiting for transfers between devices: 6.49 us -> 8.22 us
  starting transfers between devices: 18.6 us -> 17.5 us
    ppermute x10, waiting for transfers between devices: 5.64 us -> 8.21 us  [shift(): return lax.ppermute(value, ('exp', 'unit'), pairs)]
    ppermute x10, starting transfers between devices: 17.9 us -> 16.8 us  [shift(): return lax.ppermute(value, ('exp', 'unit'), pairs)]
    ppermute x3, waiting for transfers between devices: 0.84 us -> 0.01 us  [swap(): return lax.ppermute(value, 'unit', [(u, u ^ 1) for u in range(unit_count)])]
  transfers between devices with their start and end apart: 13 -> 13, of which waited for: 6 -> 5; matrix products, arithmetic and copies ran while one was open for 0% -> 0% of each run, Pallas kernels for 31% -> 30%
where the time goes in v12:
time: 61.7 us; the launch traced here: 61.4 us
  Pallas kernels  35.5 us (58%)
  starting transfers between devices  17.5 us (28%)
  waiting for transfers between devices  8.22 us (13%)
    pallas_call x10, Pallas kernels, call(): pl.pallas_call(kernel, out_shape=shapes, in_specs=specs, out_specs=[vmem]...  35.5 us
    ppermute x10, starting transfers between devices, shift(): return lax.ppermute(value, ('exp', 'unit'), pairs)  16.8 us
    ppermute x10, waiting for transfers between devices, shift(): return lax.ppermute(value, ('exp', 'unit'), pairs)  8.21 us
  transfers between devices with their start and end apart: 13, of which 5 were waited for; matrix products, arithmetic and copies ran while one was open for 0% of the time, Pallas kernels for 30%

profile of v12, /device:TPU:0, one launch (start us, length us, event | category | flops | bytes accessed | tf_op | source)
XLA Modules:
  0.0 61.4 jit_solution(13814668732300926298)
XLA Ops:
  0.0 2.4 %shard_map.82 = (bf16[40,4096]{1,0:T(8,128)(2,1)S(1)}, bf16[7,512,512]{2,1,0:T(8,128)(2,1)S(1)}, bf16[40,2048]{1,0:T(8,128)(2,1)S(1)}, bf16[40,2048]{1,0:T(8,128)(2,1)S(1)}, bf16[40,2048]{1,0:T(8,128)(2,1)S(1)}) custom-call(bf16[128,4096]{1,0:T(8,128)(2,1)} %tokens_hbm.1, f32[1,4096]{1,0:T(1,128)} %bitcast.3, s32[2,128]{1,0:T(2,128)} %bitcast.4, ...), custom_call_target="tpu_custom_call" | custom-call | flops 83886080 | bytes 5767168 | tf_op jit(solution)/shard_map/pallas_call | solution.py:447
  2.4 5.1 %collective-permute-start = (bf16[40,2048]{1,0:T(8,128)(2,1)S(1)}, bf16[40,2048]{1,0:T(8,128)(2,1)S(1)}, u32[]{:S(2)}, u32[]{:S(2)}) collective-permute-start(bf16[40,2048]{1,0:T(8,128)(2,1)S(1)} %get-tuple-element.46), channel_id=1, source_target_pairs={{0,12},{1,13},{2,14},{3,15},{4,0},{5,1},{6,2},{7,3},{8,4},{9,5},{1... | collective-permute-start | bytes 491528 | tf_op jit(solution)/shard_map/ppermute | solution.py:480
  7.5 0.0 collective-permute-start.1
  7.5 1.0 %collective-permute-start.2 = (bf16[40,2048]{1,0:T(8,128)(2,1)S(1)}, bf16[40,2048]{1,0:T(8,128)(2,1)S(1)}, u32[]{:S(2)}, u32[]{:S(2)}) collective-permute-start(bf16[40,2048]{1,0:T(8,128)(2,1)S(1)} %get-tuple-element.48), channel_id=1, source_target_pairs={{0,4},{1,5},{2,6},{3,7},{4,8},{5,9},{6,10},{7,11},{8,12},{9,13},{1... | collective-permute-start | bytes 491528 | tf_op jit(solution)/shard_map/ppermute | solution.py:480
  8.5 10.8 %shard_map.83 = (f32[8,3584]{1,0:T(8,128)S(1)}, bf16[7,512,512]{2,1,0:T(8,128)(2,1)S(1)}, bf16[7,512,512]{2,1,0:T(8,128)(2,1)S(1)}, bf16[7,512,512]{2,1,0:T(8,12...) custom-call(s32[2,8,48]{2,1,0:T(8,128)} %active_hbm.1, ...), custom_call_target="tpu_custom_call", output_to_operand_aliasing={{1}: (4, {})} | custom-call | flops 167772160 | bytes 33030144 | tf_op jit(solution)/shard_map/pallas_call | solution.py:447
  19.4 0.0 collective-permute-done.refs_0_
  19.4 2.0 %collective-permute-done.1.refs_1_ = bf16[40,2048]{1,0:T(8,128)(2,1)S(1)} collective-permute-done((bf16[40,2048]{1,0:T(8,128)(2,1)S(1)}, bf16[40,2048]{1,0:T(8,128)(2,1)S(1)}, u32[]{:S(2)}, u32[]{:S(2)}) %collective-permute-start.1) | collective-permute-done | bytes 163872 | tf_op jit(solution)/shard_map/ppermute | solution.py:480
  21.4 0.0 collective-permute-done.2.refs_2_
  21.5 0.1 collective-permute-start.3
  21.5 2.1 %shard_map.85 = (bf16[2,128,256]{2,1,0:T(8,128)(2,1)S(1)}, bf16[2,128,256]{2,1,0:T(8,128)(2,1)S(1)}, bf16[7,512,512]{2,1,0:T(8,128)(2,1)S(1)}) custom-call(s32[2,128]{1,0:T(2,128)} %bitcast.5, f32[2,128]{1,0:T(2,128)} %bitcast.6, bf16[120,2048]{1,0:T(8,128)(2,1)S(1)} %shard_map.84.after.mine, ...), custom_call_target="tpu_custom_call", output_to_operand_aliasing={{2}: (5, {})} | custom-call | bytes 4194304 | tf_op jit(solution)/shard_map/pallas_call | solution.py:447
  23.7 0.0 collective-permute-done.3.other
  23.7 13.4 %shard_map.86 = (bf16[160,3584]{1,0:T(8,128)(2,1)S(1)}, bf16[160,1024]{1,0:T(8,128)(2,1)S(1)}, bf16[7,512,512]{2,1,0:T(8,128)(2,1)S(1)}, bf16[7,512,512]{2,1,0:T...) custom-call(bf16[40,4096]{1,0:T(8,128)(2,1)S(1)} %get-tuple-element., ...), custom_call_target="tpu_custom_call", output_to_operand_aliasing={{2}: (3, {}), {3}: (4, {}), {4}: (5, {}), {5}: (6, {}), {6}... | custom-call | flops 9395240960 | bytes 36700160 | tf_op jit(solution)/shard_map/pallas_call | solution.py:447
  37.1 0.6 collective-permute-start.4
  37.7 2.0 %shard_map.89 = (bf16[160,1024]{1,0:T(8,128)(2,1)S(1)}, bf16[7,512,512]{2,1,0:T(8,128)(2,1)S(1)}) custom-call(bf16[160,3584]{1,0:T(8,128)(2,1)S(1)} %get-tuple-element.64.hidden, bf16[7,512,512]{2,1,0:T(8,128)(2,1)S(1)} %get-tuple-element.72.refs_0_, bf16[7,512,512]{2,1,0:T(8,128)(2,1)S(1)} %get-tuple-element.73.refs_1_, bf16[3584,4096]{1,0:T(8,128)(2,1)} %refs_2_.1), custom_call_target="tpu_custom_call" | custom-call | flops 1174405120 | bytes 3670016 | tf_op jit(solution)/shard_map/pallas_call | solution.py:447
  39.7 0.1 collective-permute-start.9
  39.8 0.0 collective-permute-done.4.received
  39.8 2.0 %shard_map.87 = (bf16[40,1024]{1,0:T(8,128)(2,1)S(1)}, bf16[40,1024]{1,0:T(8,128)(2,1)S(1)}, bf16[40,1024]{1,0:T(8,128)(2,1)S(1)}, bf16[40,1024]{1,0:T(8,128)(2,1)S(1)}, bf16[7,512,512]{2,1,0:T(8,128)(2,1)S(1)}) custom-call(bf16[160,3584]{1,0:T(8,128)(2,1)S(1)} %get-tuple-element.64.hidden, bf16[160,1024]{1,0:T(8,128)(2,1)S(1)} %collective-permute-done.4.received, ...), custom_call_target="tpu_custom_call" | custom-call | flops 1174405120 | bytes 3670016 | tf_op jit(solution)/shard_map/pallas_call | solution.py:447
  41.9 3.8 %collective-permute-start.5 = (bf16[40,1024]{1,0:T(8,128)(2,1)S(1)}, bf16[40,1024]{1,0:T(8,128)(2,1)S(1)}, u32[]{:S(2)}, u32[]{:S(2)}) collective-permute-start(bf16[40,1024]{1,0:T(8,128)(2,1)S(1)} %get-tuple-element.68), channel_id=1, source_target_pairs={{0,10},{1,11},{2,8},{3,9},{4,14},{5,15},{6,12},{7,13},{8,2},{9,3},... | collective-permute-start | bytes 245768 | tf_op jit(solution)/shard_map/ppermute | solution.py:480
  45.6 0.4 collective-permute-start.6
  46.1 2.5 %collective-permute-start.7 = (bf16[40,1024]{1,0:T(8,128)(2,1)S(1)}, bf16[40,1024]{1,0:T(8,128)(2,1)S(1)}, u32[]{:S(2)}, u32[]{:S(2)}) collective-permute-start(bf16[40,1024]{1,0:T(8,128)(2,1)S(1)} %get-tuple-element.70), channel_id=1, source_target_pairs={{0,6},{1,7},{2,4},{3,5},{4,10},{5,11},{6,8},{7,9},{8,14},{9,15},{1... | collective-permute-start | bytes 245768 | tf_op jit(solution)/shard_map/ppermute | solution.py:480
  48.6 0.5 collective-permute-start.8
  49.1 0.0 collective-permute-done.9.received
  49.1 1.4 %shard_map.90 = (bf16[40,1024]{1,0:T(8,128)(2,1)S(1)}, bf16[40,1024]{1,0:T(8,128)(2,1)S(1)}, bf16[40,1024]{1,0:T(8,128)(2,1)S(1)}, bf16[40,1024]{1,0:T(8,128)(2,1)S(1)}) custom-call(bf16[160,3584]{1,0:T(8,128)(2,1)S(1)} %get-tuple-element.64.hidden, bf16[160,1024]{1,0:T(8,128)(2,1)S(1)} %collective-permute-done.9.received, ...), custom_call_target="tpu_custom_call" | custom-call | flops 1174405120 | bytes 3670016 | tf_op jit(solution)/shard_map/pallas_call | solution.py:447
  50.5 0.2 collective-permute-start.10
  50.7 0.0 collective-permute-done.5.refs_0_
  50.7 2.2 %collective-permute-start.11 = (bf16[40,1024]{1,0:T(8,128)(2,1)S(1)}, bf16[40,1024]{1,0:T(8,128)(2,1)S(1)}, u32[]{:S(2)}, u32[]{:S(2)}) collective-permute-start(bf16[40,1024]{1,0:T(8,128)(2,1)S(1)} %get-tuple-element.78), channel_id=1, source_target_pairs={{0,12},{1,13},{2,14},{3,15},{4,0},{5,1},{6,2},{7,3},{8,4},{9,5},{1... | collective-permute-start | bytes 245768 | tf_op jit(solution)/shard_map/ppermute | solution.py:480
  52.9 1.1 %collective-permute-done.6.refs_1_ = bf16[40,1024]{1,0:T(8,128)(2,1)S(1)} collective-permute-done((bf16[40,1024]{1,0:T(8,128)(2,1)S(1)}, bf16[40,1024]{1,0:T(8,128)(2,1)S(1)}, u32[]{:S(2)}, u32[]{:S(2)}) %collective-permute-start.6) | collective-permute-done | bytes 81952 | tf_op jit(solution)/shard_map/ppermute | solution.py:480
  54.1 1.0 %collective-permute-start.12 = (bf16[40,1024]{1,0:T(8,128)(2,1)S(1)}, bf16[40,1024]{1,0:T(8,128)(2,1)S(1)}, u32[]{:S(2)}, u32[]{:S(2)}) collective-permute-start(bf16[40,1024]{1,0:T(8,128)(2,1)S(1)} %get-tuple-element.79), channel_id=1, source_target_pairs={{0,4},{1,5},{2,6},{3,7},{4,8},{5,9},{6,10},{7,11},{8,12},{9,13},{1... | collective-permute-start | bytes 245768 | tf_op jit(solution)/shard_map/ppermute | solution.py:480
  55.1 0.0 collective-permute-done.7.refs_2_
  55.1 0.7 %collective-permute-done.8.refs_3_ = bf16[40,1024]{1,0:T(8,128)(2,1)S(1)} collective-permute-done((bf16[40,1024]{1,0:T(8,128)(2,1)S(1)}, bf16[40,1024]{1,0:T(8,128)(2,1)S(1)}, u32[]{:S(2)}, u32[]{:S(2)}) %collective-permute-start.8) | collective-permute-done | bytes 81952 | tf_op jit(solution)/shard_map/ppermute | solution.py:480
  55.7 0.3 shard_map.88.refs_0_
  56.0 1.6 %collective-permute-done.10.refs_1_ = bf16[40,1024]{1,0:T(8,128)(2,1)S(1)} collective-permute-done((bf16[40,1024]{1,0:T(8,128)(2,1)S(1)}, bf16[40,1024]{1,0:T(8,128)(2,1)S(1)}, u32[]{:S(2)}, u32[]{:S(2)}) %collective-permute-start.10) | collective-permute-done | bytes 81952 | tf_op jit(solution)/shard_map/ppermute | solution.py:480
  57.7 0.0 collective-permute-done.11.refs_2_
  57.7 2.7 %collective-permute-done.12.refs_3_ = bf16[40,1024]{1,0:T(8,128)(2,1)S(1)} collective-permute-done((bf16[40,1024]{1,0:T(8,128)(2,1)S(1)}, bf16[40,1024]{1,0:T(8,128)(2,1)S(1)}, u32[]{:S(2)}, u32[]{:S(2)}) %collective-permute-start.12) | collective-permute-done | bytes 81952 | tf_op jit(solution)/shard_map/ppermute | solution.py:480
  60.4 1.0 %shard_map.91 = bf16[128,1024]{1,0:T(8,128)(2,1)} custom-call(bf16[2,128,256]{2,1,0:T(8,128)(2,1)S(1)} %get-tuple-element.50.high, bf16[2,128,256]{2,1,0:T(8,128)(2,1)S(1)} %get-tuple-element.51.refs_15_.low, f32[128,1024]{1,0:T(8,128)S(1)} %shard_map.88.refs_0_, bf16[40,1024]{1,0:T(8,128)(2,1)S(1)} %collective-permute-done.10.refs_1_, ...), custom_call_target="tpu_custom_call" | custom-call | flops 83886080 | bytes 1048576 | tf_op jit(solution)/shard_map/pallas_call | solution.py:447
  (1 shorter events, 0.0 us)
Async XLA Ops:
  2.4 17.0 %collective-permute-start = (bf16[40,2048]{1,0:T(8,128)(2,1)S(1)}, bf16[40,2048]{1,0:T(8,128)(2,1)S(1)}, u32[]{:S(2)}, u32[]{:S(2)}) collective-permute-start(bf16[40,2048]{1,0:T(8,128)(2,1)S(1)} %get-tuple-element.46), channel_id=1, source_target_pairs={{0,12},{1,13},{2,14},{3,15},{4,0},{5,1},{6,2},{7,3},{8,4},{9,5},{1... | collective-permute-start | bytes 491528 | tf_op jit(solution)/shard_map/ppermute | solution.py:480
  7.5 13.9 %collective-permute-start.1 = (bf16[40,2048]{1,0:T(8,128)(2,1)S(1)}, bf16[40,2048]{1,0:T(8,128)(2,1)S(1)}, u32[]{:S(2)}, u32[]{:S(2)}) collective-permute-start(bf16[40,2048]{1,0:T(8,128)(2,1)S(1)} %get-tuple-element.47), channel_id=1, source_target_pairs={{0,8},{1,9},{2,10},{3,11},{4,12},{5,13},{6,14},{7,15},{8,0},{9,1},... | collective-permute-start | bytes 491528 | tf_op jit(solution)/shard_map/ppermute | solution.py:480
  7.5 13.9 %collective-permute-start.2 = (bf16[40,2048]{1,0:T(8,128)(2,1)S(1)}, bf16[40,2048]{1,0:T(8,128)(2,1)S(1)}, u32[]{:S(2)}, u32[]{:S(2)}) collective-permute-start(bf16[40,2048]{1,0:T(8,128)(2,1)S(1)} %get-tuple-element.48), channel_id=1, source_target_pairs={{0,4},{1,5},{2,6},{3,7},{4,8},{5,9},{6,10},{7,11},{8,12},{9,13},{1... | collective-permute-start | bytes 491528 | tf_op jit(solution)/shard_map/ppermute | solution.py:480
  21.5 2.2 %collective-permute-start.3 = (bf16[120,2048]{1,0:T(8,128)(2,1)S(1)}, bf16[120,2048]{1,0:T(8,128)(2,1)S(1)}, u32[]{:S(2)}, u32[]{:S(2)}) collective-permute-start(bf16[120,2048]{1,0:T(8,128)(2,1)S(1)} %shard_map.84.after.mine), channel_id=1, source_target_pairs={{0,1},{1,0},{2,3},{3,2},{4,5},{5,4},{6,7},{7,6},{8,9},{9,8},{10,11... | collective-permute-start | bytes 1474568 | tf_op jit(solution)/shard_map/ppermute | solution.py:483
  37.1 2.7 %collective-permute-start.4 = (bf16[160,1024]{1,0:T(8,128)(2,1)S(1)}, bf16[160,1024]{1,0:T(8,128)(2,1)S(1)}, u32[]{:S(2)}, u32[]{:S(2)}) collective-permute-start(bf16[160,1024]{1,0:T(8,128)(2,1)S(1)} %get-tuple-element.65), channel_id=1, source_target_pairs={{0,1},{1,0},{2,3},{3,2},{4,5},{5,4},{6,7},{7,6},{8,9},{9,8},{10,11... | collective-permute-start | bytes 983048 | tf_op jit(solution)/shard_map/ppermute | solution.py:483
  39.7 9.4 %collective-permute-start.9 = (bf16[160,1024]{1,0:T(8,128)(2,1)S(1)}, bf16[160,1024]{1,0:T(8,128)(2,1)S(1)}, u32[]{:S(2)}, u32[]{:S(2)}) collective-permute-start(bf16[160,1024]{1,0:T(8,128)(2,1)S(1)} %get-tuple-element.74), channel_id=1, source_target_pairs={{0,1},{1,0},{2,3},{3,2},{4,5},{5,4},{6,7},{7,6},{8,9},{9,8},{10,11... | collective-permute-start | bytes 983048 | tf_op jit(solution)/shard_map/ppermute | solution.py:483
  41.9 8.8 %collective-permute-start.5 = (bf16[40,1024]{1,0:T(8,128)(2,1)S(1)}, bf16[40,1024]{1,0:T(8,128)(2,1)S(1)}, u32[]{:S(2)}, u32[]{:S(2)}) collective-permute-start(bf16[40,1024]{1,0:T(8,128)(2,1)S(1)} %get-tuple-element.68), channel_id=1, source_target_pairs={{0,10},{1,11},{2,8},{3,9},{4,14},{5,15},{6,12},{7,13},{8,2},{9,3},... | collective-permute-start | bytes 245768 | tf_op jit(solution)/shard_map/ppermute | solution.py:480
  45.6 8.4 %collective-permute-start.6 = (bf16[40,1024]{1,0:T(8,128)(2,1)S(1)}, bf16[40,1024]{1,0:T(8,128)(2,1)S(1)}, u32[]{:S(2)}, u32[]{:S(2)}) collective-permute-start(bf16[40,1024]{1,0:T(8,128)(2,1)S(1)} %get-tuple-element.69), channel_id=1, source_target_pairs={{0,14},{1,15},{2,12},{3,13},{4,2},{5,3},{6,0},{7,1},{8,6},{9,7},{1... | collective-permute-start | bytes 245768 | tf_op jit(solution)/shard_map/ppermute | solution.py:480
  46.1 9.0 %collective-permute-start.7 = (bf16[40,1024]{1,0:T(8,128)(2,1)S(1)}, bf16[40,1024]{1,0:T(8,128)(2,1)S(1)}, u32[]{:S(2)}, u32[]{:S(2)}) collective-permute-start(bf16[40,1024]{1,0:T(8,128)(2,1)S(1)} %get-tuple-element.70), channel_id=1, source_target_pairs={{0,6},{1,7},{2,4},{3,5},{4,10},{5,11},{6,8},{7,9},{8,14},{9,15},{1... | collective-permute-start | bytes 245768 | tf_op jit(solution)/shard_map/ppermute | solution.py:480
  48.6 7.2 %collective-permute-start.8 = (bf16[40,1024]{1,0:T(8,128)(2,1)S(1)}, bf16[40,1024]{1,0:T(8,128)(2,1)S(1)}, u32[]{:S(2)}, u32[]{:S(2)}) collective-permute-start(bf16[40,1024]{1,0:T(8,128)(2,1)S(1)} %get-tuple-element.71), channel_id=1, source_target_pairs={{0,2},{1,3},{2,0},{3,1},{4,6},{5,7},{6,4},{7,5},{8,10},{9,11},{10,... | collective-permute-start | bytes 245768 | tf_op jit(solution)/shard_map/ppermute | solution.py:480
  50.5 7.2 %collective-permute-start.10 = (bf16[40,1024]{1,0:T(8,128)(2,1)S(1)}, bf16[40,1024]{1,0:T(8,128)(2,1)S(1)}, u32[]{:S(2)}, u32[]{:S(2)}) collective-permute-start(bf16[40,1024]{1,0:T(8,128)(2,1)S(1)} %get-tuple-element.77), channel_id=1, source_target_pairs={{0,8},{1,9},{2,10},{3,11},{4,12},{5,13},{6,14},{7,15},{8,0},{9,1},... | collective-permute-start | bytes 245768 | tf_op jit(solution)/shard_map/ppermute | solution.py:480
  50.7 7.0 %collective-permute-start.11 = (bf16[40,1024]{1,0:T(8,128)(2,1)S(1)}, bf16[40,1024]{1,0:T(8,128)(2,1)S(1)}, u32[]{:S(2)}, u32[]{:S(2)}) collective-permute-start(bf16[40,1024]{1,0:T(8,128)(2,1)S(1)} %get-tuple-element.78), channel_id=1, source_target_pairs={{0,12},{1,13},{2,14},{3,15},{4,0},{5,1},{6,2},{7,3},{8,4},{9,5},{1... | collective-permute-start | bytes 245768 | tf_op jit(solution)/shard_map/ppermute | solution.py:480
  54.1 6.3 %collective-permute-start.12 = (bf16[40,1024]{1,0:T(8,128)(2,1)S(1)}, bf16[40,1024]{1,0:T(8,128)(2,1)S(1)}, u32[]{:S(2)}, u32[]{:S(2)}) collective-permute-start(bf16[40,1024]{1,0:T(8,128)(2,1)S(1)} %get-tuple-element.79), channel_id=1, source_target_pairs={{0,4},{1,5},{2,6},{3,7},{4,8},{5,9},{6,10},{7,11},{8,12},{9,13},{1... | collective-permute-start | bytes 245768 | tf_op jit(solution)/shard_map/ppermute | solution.py:480

commit v13 on v12

--- a/solution.py
+++ b/solution.py
@@ -524,7 +524,7 @@
         moved=(READY - 2) * piece_bytes,
         aliases={4: 1},
     )
-    order = list(range(exp_count - 1, 0, -1))
+    order = distances(exp_count)
     arrived = [shift(sends[d - 1], d) for d in order]
     mine = call(
         functools.partial(join_kernel, order),

time: 61.7 us -> 61.4 us (level)
  waiting for transfers between devices: 8.22 us -> 6.28 us
  starting transfers between devices: 17.5 us -> 19.1 us
    ppermute x10, waiting for transfers between devices: 8.21 us -> 6.27 us  [shift(): return lax.ppermute(value, ('exp', 'unit'), pairs)]
    ppermute x10, starting transfers between devices: 16.8 us -> 18.4 us  [shift(): return lax.ppermute(value, ('exp', 'unit'), pairs)]
  transfers between devices with their start and end apart: 13 -> 13, of which waited for: 5 -> 4; matrix products, arithmetic and copies ran while one was open for 0% -> 0% of each run, Pallas kernels for 30% -> 31%
where the time goes in v13:
time: 61.4 us; the launch traced here: 61.1 us
  Pallas kernels  35.5 us (58%)
  starting transfers between devices  19.1 us (31%)
  waiting for transfers between devices  6.28 us (10%)
    pallas_call x10, Pallas kernels, call(): pl.pallas_call(kernel, out_shape=shapes, in_specs=specs, out_specs=[vmem]...  35.5 us
    ppermute x10, starting transfers between devices, shift(): return lax.ppermute(value, ('exp', 'unit'), pairs)  18.4 us
    ppermute x10, waiting for transfers between devices, shift(): return lax.ppermute(value, ('exp', 'unit'), pairs)  6.27 us
  transfers between devices with their start and end apart: 13, of which 4 were waited for; matrix products, arithmetic and copies ran while one was open for 0% of the time, Pallas kernels for 31%

profile of v13, /device:TPU:0, one launch (start us, length us, event | category | flops | bytes accessed | tf_op | source)
XLA Modules:
  0.0 61.1 jit_solution(12739669350928394526)
XLA Ops:
  0.0 2.4 %shard_map.82 = (bf16[40,4096]{1,0:T(8,128)(2,1)S(1)}, bf16[7,512,512]{2,1,0:T(8,128)(2,1)S(1)}, bf16[40,2048]{1,0:T(8,128)(2,1)S(1)}, bf16[40,2048]{1,0:T(8,128)(2,1)S(1)}, bf16[40,2048]{1,0:T(8,128)(2,1)S(1)}) custom-call(bf16[128,4096]{1,0:T(8,128)(2,1)} %tokens_hbm.1, f32[1,4096]{1,0:T(1,128)} %bitcast.3, s32[2,128]{1,0:T(2,128)} %bitcast.4, ...), custom_call_target="tpu_custom_call" | custom-call | flops 83886080 | bytes 5767168 | tf_op jit(solution)/shard_map/pallas_call | solution.py:447
  2.4 4.1 %collective-permute-start = (bf16[40,2048]{1,0:T(8,128)(2,1)S(1)}, bf16[40,2048]{1,0:T(8,128)(2,1)S(1)}, u32[]{:S(2)}, u32[]{:S(2)}) collective-permute-start(bf16[40,2048]{1,0:T(8,128)(2,1)S(1)} %get-tuple-element.46), channel_id=1, source_target_pairs={{0,8},{1,9},{2,10},{3,11},{4,12},{5,13},{6,14},{7,15},{8,0},{9,1},... | collective-permute-start | bytes 491528 | tf_op jit(solution)/shard_map/ppermute | solution.py:480
  6.5 1.6 %collective-permute-start.1 = (bf16[40,2048]{1,0:T(8,128)(2,1)S(1)}, bf16[40,2048]{1,0:T(8,128)(2,1)S(1)}, u32[]{:S(2)}, u32[]{:S(2)}) collective-permute-start(bf16[40,2048]{1,0:T(8,128)(2,1)S(1)} %get-tuple-element.47), channel_id=1, source_target_pairs={{0,4},{1,5},{2,6},{3,7},{4,8},{5,9},{6,10},{7,11},{8,12},{9,13},{1... | collective-permute-start | bytes 491528 | tf_op jit(solution)/shard_map/ppermute | solution.py:480
  8.1 2.2 %collective-permute-start.2 = (bf16[40,2048]{1,0:T(8,128)(2,1)S(1)}, bf16[40,2048]{1,0:T(8,128)(2,1)S(1)}, u32[]{:S(2)}, u32[]{:S(2)}) collective-permute-start(bf16[40,2048]{1,0:T(8,128)(2,1)S(1)} %get-tuple-element.48), channel_id=1, source_target_pairs={{0,12},{1,13},{2,14},{3,15},{4,0},{5,1},{6,2},{7,3},{8,4},{9,5},{1... | collective-permute-start | bytes 491528 | tf_op jit(solution)/shard_map/ppermute | solution.py:480
  10.4 10.8 %shard_map.83 = (f32[8,3584]{1,0:T(8,128)S(1)}, bf16[7,512,512]{2,1,0:T(8,128)(2,1)S(1)}, bf16[7,512,512]{2,1,0:T(8,128)(2,1)S(1)}, bf16[7,512,512]{2,1,0:T(8,12...) custom-call(s32[2,8,48]{2,1,0:T(8,128)} %active_hbm.1, ...), custom_call_target="tpu_custom_call", output_to_operand_aliasing={{1}: (4, {})} | custom-call | flops 167772160 | bytes 33030144 | tf_op jit(solution)/shard_map/pallas_call | solution.py:447
  21.2 0.0 collective-permute-done.refs_0_
  21.2 0.0 collective-permute-done.1.refs_1_
  21.2 0.0 collective-permute-done.2.refs_2_
  21.3 0.1 collective-permute-start.3
  21.3 2.1 %shard_map.85 = (bf16[2,128,256]{2,1,0:T(8,128)(2,1)S(1)}, bf16[2,128,256]{2,1,0:T(8,128)(2,1)S(1)}, bf16[7,512,512]{2,1,0:T(8,128)(2,1)S(1)}) custom-call(s32[2,128]{1,0:T(2,128)} %bitcast.5, f32[2,128]{1,0:T(2,128)} %bitcast.6, bf16[120,2048]{1,0:T(8,128)(2,1)S(1)} %shard_map.84.after.mine, ...), custom_call_target="tpu_custom_call", output_to_operand_aliasing={{2}: (5, {})} | custom-call | bytes 4194304 | tf_op jit(solution)/shard_map/pallas_call | solution.py:447
  23.5 0.0 collective-permute-done.3.other
  23.5 13.4 %shard_map.86 = (bf16[160,3584]{1,0:T(8,128)(2,1)S(1)}, bf16[160,1024]{1,0:T(8,128)(2,1)S(1)}, bf16[7,512,512]{2,1,0:T(8,128)(2,1)S(1)}, bf16[7,512,512]{2,1,0:T...) custom-call(bf16[40,4096]{1,0:T(8,128)(2,1)S(1)} %get-tuple-element., ...), custom_call_target="tpu_custom_call", output_to_operand_aliasing={{2}: (3, {}), {3}: (4, {}), {4}: (5, {}), {5}: (6, {}), {6}... | custom-call | flops 9395240960 | bytes 36700160 | tf_op jit(solution)/shard_map/pallas_call | solution.py:447
  36.9 0.6 collective-permute-start.4
  37.5 2.0 %shard_map.89 = (bf16[160,1024]{1,0:T(8,128)(2,1)S(1)}, bf16[7,512,512]{2,1,0:T(8,128)(2,1)S(1)}) custom-call(bf16[160,3584]{1,0:T(8,128)(2,1)S(1)} %get-tuple-element.64.hidden, bf16[7,512,512]{2,1,0:T(8,128)(2,1)S(1)} %get-tuple-element.72.refs_0_, bf16[7,512,512]{2,1,0:T(8,128)(2,1)S(1)} %get-tuple-element.73.refs_1_, bf16[3584,4096]{1,0:T(8,128)(2,1)} %refs_2_.1), custom_call_target="tpu_custom_call" | custom-call | flops 1174405120 | bytes 3670016 | tf_op jit(solution)/shard_map/pallas_call | solution.py:447
  39.5 0.1 collective-permute-start.9
  39.6 0.0 collective-permute-done.4.received
  39.6 2.0 %shard_map.87 = (bf16[40,1024]{1,0:T(8,128)(2,1)S(1)}, bf16[40,1024]{1,0:T(8,128)(2,1)S(1)}, bf16[40,1024]{1,0:T(8,128)(2,1)S(1)}, bf16[40,1024]{1,0:T(8,128)(2,1)S(1)}, bf16[7,512,512]{2,1,0:T(8,128)(2,1)S(1)}) custom-call(bf16[160,3584]{1,0:T(8,128)(2,1)S(1)} %get-tuple-element.64.hidden, bf16[160,1024]{1,0:T(8,128)(2,1)S(1)} %collective-permute-done.4.received, ...), custom_call_target="tpu_custom_call" | custom-call | flops 1174405120 | bytes 3670016 | tf_op jit(solution)/shard_map/pallas_call | solution.py:447
  41.7 3.7 %collective-permute-start.5 = (bf16[40,1024]{1,0:T(8,128)(2,1)S(1)}, bf16[40,1024]{1,0:T(8,128)(2,1)S(1)}, u32[]{:S(2)}, u32[]{:S(2)}) collective-permute-start(bf16[40,1024]{1,0:T(8,128)(2,1)S(1)} %get-tuple-element.68), channel_id=1, source_target_pairs={{0,10},{1,11},{2,8},{3,9},{4,14},{5,15},{6,12},{7,13},{8,2},{9,3},... | collective-permute-start | bytes 245768 | tf_op jit(solution)/shard_map/ppermute | solution.py:480
  45.3 0.4 collective-permute-start.6
  45.7 2.5 %collective-permute-start.7 = (bf16[40,1024]{1,0:T(8,128)(2,1)S(1)}, bf16[40,1024]{1,0:T(8,128)(2,1)S(1)}, u32[]{:S(2)}, u32[]{:S(2)}) collective-permute-start(bf16[40,1024]{1,0:T(8,128)(2,1)S(1)} %get-tuple-element.70), channel_id=1, source_target_pairs={{0,6},{1,7},{2,4},{3,5},{4,10},{5,11},{6,8},{7,9},{8,14},{9,15},{1... | collective-permute-start | bytes 245768 | tf_op jit(solution)/shard_map/ppermute | solution.py:480
  48.3 0.5 collective-permute-start.8
  48.8 0.0 collective-permute-done.9.received
  48.8 1.4 %shard_map.90 = (bf16[40,1024]{1,0:T(8,128)(2,1)S(1)}, bf16[40,1024]{1,0:T(8,128)(2,1)S(1)}, bf16[40,1024]{1,0:T(8,128)(2,1)S(1)}, bf16[40,1024]{1,0:T(8,128)(2,1)S(1)}) custom-call(bf16[160,3584]{1,0:T(8,128)(2,1)S(1)} %get-tuple-element.64.hidden, bf16[160,1024]{1,0:T(8,128)(2,1)S(1)} %collective-permute-done.9.received, ...), custom_call_target="tpu_custom_call" | custom-call | flops 1174405120 | bytes 3670016 | tf_op jit(solution)/shard_map/pallas_call | solution.py:447
  50.2 0.3 collective-permute-start.10
  50.5 0.0 collective-permute-done.5.refs_0_
  50.5 2.1 %collective-permute-start.11 = (bf16[40,1024]{1,0:T(8,128)(2,1)S(1)}, bf16[40,1024]{1,0:T(8,128)(2,1)S(1)}, u32[]{:S(2)}, u32[]{:S(2)}) collective-permute-start(bf16[40,1024]{1,0:T(8,128)(2,1)S(1)} %get-tuple-element.78), channel_id=1, source_target_pairs={{0,12},{1,13},{2,14},{3,15},{4,0},{5,1},{6,2},{7,3},{8,4},{9,5},{1... | collective-permute-start | bytes 245768 | tf_op jit(solution)/shard_map/ppermute | solution.py:480
  52.6 1.1 %collective-permute-done.6.refs_1_ = bf16[40,1024]{1,0:T(8,128)(2,1)S(1)} collective-permute-done((bf16[40,1024]{1,0:T(8,128)(2,1)S(1)}, bf16[40,1024]{1,0:T(8,128)(2,1)S(1)}, u32[]{:S(2)}, u32[]{:S(2)}) %collective-permute-start.6) | collective-permute-done | bytes 81952 | tf_op jit(solution)/shard_map/ppermute | solution.py:480
  53.8 0.9 %collective-permute-start.12 = (bf16[40,1024]{1,0:T(8,128)(2,1)S(1)}, bf16[40,1024]{1,0:T(8,128)(2,1)S(1)}, u32[]{:S(2)}, u32[]{:S(2)}) collective-permute-start(bf16[40,1024]{1,0:T(8,128)(2,1)S(1)} %get-tuple-element.79), channel_id=1, source_target_pairs={{0,4},{1,5},{2,6},{3,7},{4,8},{5,9},{6,10},{7,11},{8,12},{9,13},{1... | collective-permute-start | bytes 245768 | tf_op jit(solution)/shard_map/ppermute | solution.py:480
  54.7 0.0 collective-permute-done.7.refs_2_
  54.7 0.8 %collective-permute-done.8.refs_3_ = bf16[40,1024]{1,0:T(8,128)(2,1)S(1)} collective-permute-done((bf16[40,1024]{1,0:T(8,128)(2,1)S(1)}, bf16[40,1024]{1,0:T(8,128)(2,1)S(1)}, u32[]{:S(2)}, u32[]{:S(2)}) %collective-permute-start.8) | collective-permute-done | bytes 81952 | tf_op jit(solution)/shard_map/ppermute | solution.py:480
  55.4 0.3 shard_map.88.refs_0_
  55.7 1.7 %collective-permute-done.10.refs_1_ = bf16[40,1024]{1,0:T(8,128)(2,1)S(1)} collective-permute-done((bf16[40,1024]{1,0:T(8,128)(2,1)S(1)}, bf16[40,1024]{1,0:T(8,128)(2,1)S(1)}, u32[]{:S(2)}, u32[]{:S(2)}) %collective-permute-start.10) | collective-permute-done | bytes 81952 | tf_op jit(solution)/shard_map/ppermute | solution.py:480
  57.4 0.0 collective-permute-done.11.refs_2_
  57.4 2.6 %collective-permute-done.12.refs_3_ = bf16[40,1024]{1,0:T(8,128)(2,1)S(1)} collective-permute-done((bf16[40,1024]{1,0:T(8,128)(2,1)S(1)}, bf16[40,1024]{1,0:T(8,128)(2,1)S(1)}, u32[]{:S(2)}, u32[]{:S(2)}) %collective-permute-start.12) | collective-permute-done | bytes 81952 | tf_op jit(solution)/shard_map/ppermute | solution.py:480
  60.1 1.0 %shard_map.91 = bf16[128,1024]{1,0:T(8,128)(2,1)} custom-call(bf16[2,128,256]{2,1,0:T(8,128)(2,1)S(1)} %get-tuple-element.50.high, bf16[2,128,256]{2,1,0:T(8,128)(2,1)S(1)} %get-tuple-element.51.refs_15_.low, f32[128,1024]{1,0:T(8,128)S(1)} %shard_map.88.refs_0_, bf16[40,1024]{1,0:T(8,128)(2,1)S(1)} %collective-permute-done.10.refs_1_, ...), custom_call_target="tpu_custom_call" | custom-call | flops 83886080 | bytes 1048576 | tf_op jit(solution)/shard_map/pallas_call | solution.py:447
  (1 shorter events, 0.0 us)
Async XLA Ops:
  2.4 18.8 %collective-permute-start = (bf16[40,2048]{1,0:T(8,128)(2,1)S(1)}, bf16[40,2048]{1,0:T(8,128)(2,1)S(1)}, u32[]{:S(2)}, u32[]{:S(2)}) collective-permute-start(bf16[40,2048]{1,0:T(8,128)(2,1)S(1)} %get-tuple-element.46), channel_id=1, source_target_pairs={{0,8},{1,9},{2,10},{3,11},{4,12},{5,13},{6,14},{7,15},{8,0},{9,1},... | collective-permute-start | bytes 491528 | tf_op jit(solution)/shard_map/ppermute | solution.py:480
  6.5 14.7 %collective-permute-start.1 = (bf16[40,2048]{1,0:T(8,128)(2,1)S(1)}, bf16[40,2048]{1,0:T(8,128)(2,1)S(1)}, u32[]{:S(2)}, u32[]{:S(2)}) collective-permute-start(bf16[40,2048]{1,0:T(8,128)(2,1)S(1)} %get-tuple-element.47), channel_id=1, source_target_pairs={{0,4},{1,5},{2,6},{3,7},{4,8},{5,9},{6,10},{7,11},{8,12},{9,13},{1... | collective-permute-start | bytes 491528 | tf_op jit(solution)/shard_map/ppermute | solution.py:480
  8.1 13.1 %collective-permute-start.2 = (bf16[40,2048]{1,0:T(8,128)(2,1)S(1)}, bf16[40,2048]{1,0:T(8,128)(2,1)S(1)}, u32[]{:S(2)}, u32[]{:S(2)}) collective-permute-start(bf16[40,2048]{1,0:T(8,128)(2,1)S(1)} %get-tuple-element.48), channel_id=1, source_target_pairs={{0,12},{1,13},{2,14},{3,15},{4,0},{5,1},{6,2},{7,3},{8,4},{9,5},{1... | collective-permute-start | bytes 491528 | tf_op jit(solution)/shard_map/ppermute | solution.py:480
  21.3 2.2 %collective-permute-start.3 = (bf16[120,2048]{1,0:T(8,128)(2,1)S(1)}, bf16[120,2048]{1,0:T(8,128)(2,1)S(1)}, u32[]{:S(2)}, u32[]{:S(2)}) collective-permute-start(bf16[120,2048]{1,0:T(8,128)(2,1)S(1)} %shard_map.84.after.mine), channel_id=1, source_target_pairs={{0,1},{1,0},{2,3},{3,2},{4,5},{5,4},{6,7},{7,6},{8,9},{9,8},{10,11... | collective-permute-start | bytes 1474568 | tf_op jit(solution)/shard_map/ppermute | solution.py:483
  36.9 2.7 %collective-permute-start.4 = (bf16[160,1024]{1,0:T(8,128)(2,1)S(1)}, bf16[160,1024]{1,0:T(8,128)(2,1)S(1)}, u32[]{:S(2)}, u32[]{:S(2)}) collective-permute-start(bf16[160,1024]{1,0:T(8,128)(2,1)S(1)} %get-tuple-element.65), channel_id=1, source_target_pairs={{0,1},{1,0},{2,3},{3,2},{4,5},{5,4},{6,7},{7,6},{8,9},{9,8},{10,11... | collective-permute-start | bytes 983048 | tf_op jit(solution)/shard_map/ppermute | solution.py:483
  39.5 9.3 %collective-permute-start.9 = (bf16[160,1024]{1,0:T(8,128)(2,1)S(1)}, bf16[160,1024]{1,0:T(8,128)(2,1)S(1)}, u32[]{:S(2)}, u32[]{:S(2)}) collective-permute-start(bf16[160,1024]{1,0:T(8,128)(2,1)S(1)} %get-tuple-element.74), channel_id=1, source_target_pairs={{0,1},{1,0},{2,3},{3,2},{4,5},{5,4},{6,7},{7,6},{8,9},{9,8},{10,11... | collective-permute-start | bytes 983048 | tf_op jit(solution)/shard_map/ppermute | solution.py:483
  41.7 8.8 %collective-permute-start.5 = (bf16[40,1024]{1,0:T(8,128)(2,1)S(1)}, bf16[40,1024]{1,0:T(8,128)(2,1)S(1)}, u32[]{:S(2)}, u32[]{:S(2)}) collective-permute-start(bf16[40,1024]{1,0:T(8,128)(2,1)S(1)} %get-tuple-element.68), channel_id=1, source_target_pairs={{0,10},{1,11},{2,8},{3,9},{4,14},{5,15},{6,12},{7,13},{8,2},{9,3},... | collective-permute-start | bytes 245768 | tf_op jit(solution)/shard_map/ppermute | solution.py:480
  45.3 8.4 %collective-permute-start.6 = (bf16[40,1024]{1,0:T(8,128)(2,1)S(1)}, bf16[40,1024]{1,0:T(8,128)(2,1)S(1)}, u32[]{:S(2)}, u32[]{:S(2)}) collective-permute-start(bf16[40,1024]{1,0:T(8,128)(2,1)S(1)} %get-tuple-element.69), channel_id=1, source_target_pairs={{0,14},{1,15},{2,12},{3,13},{4,2},{5,3},{6,0},{7,1},{8,6},{9,7},{1... | collective-permute-start | bytes 245768 | tf_op jit(solution)/shard_map/ppermute | solution.py:480
  45.7 8.9 %collective-permute-start.7 = (bf16[40,1024]{1,0:T(8,128)(2,1)S(1)}, bf16[40,1024]{1,0:T(8,128)(2,1)S(1)}, u32[]{:S(2)}, u32[]{:S(2)}) collective-permute-start(bf16[40,1024]{1,0:T(8,128)(2,1)S(1)} %get-tuple-element.70), channel_id=1, source_target_pairs={{0,6},{1,7},{2,4},{3,5},{4,10},{5,11},{6,8},{7,9},{8,14},{9,15},{1... | collective-permute-start | bytes 245768 | tf_op jit(solution)/shard_map/ppermute | solution.py:480
  48.3 7.2 %collective-permute-start.8 = (bf16[40,1024]{1,0:T(8,128)(2,1)S(1)}, bf16[40,1024]{1,0:T(8,128)(2,1)S(1)}, u32[]{:S(2)}, u32[]{:S(2)}) collective-permute-start(bf16[40,1024]{1,0:T(8,128)(2,1)S(1)} %get-tuple-element.71), channel_id=1, source_target_pairs={{0,2},{1,3},{2,0},{3,1},{4,6},{5,7},{6,4},{7,5},{8,10},{9,11},{10,... | collective-permute-start | bytes 245768 | tf_op jit(solution)/shard_map/ppermute | solution.py:480
  50.2 7.3 %collective-permute-start.10 = (bf16[40,1024]{1,0:T(8,128)(2,1)S(1)}, bf16[40,1024]{1,0:T(8,128)(2,1)S(1)}, u32[]{:S(2)}, u32[]{:S(2)}) collective-permute-start(bf16[40,1024]{1,0:T(8,128)(2,1)S(1)} %get-tuple-element.77), channel_id=1, source_target_pairs={{0,8},{1,9},{2,10},{3,11},{4,12},{5,13},{6,14},{7,15},{8,0},{9,1},... | collective-permute-start | bytes 245768 | tf_op jit(solution)/shard_map/ppermute | solution.py:480
  50.5 6.9 %collective-permute-start.11 = (bf16[40,1024]{1,0:T(8,128)(2,1)S(1)}, bf16[40,1024]{1,0:T(8,128)(2,1)S(1)}, u32[]{:S(2)}, u32[]{:S(2)}) collective-permute-start(bf16[40,1024]{1,0:T(8,128)(2,1)S(1)} %get-tuple-element.78), channel_id=1, source_target_pairs={{0,12},{1,13},{2,14},{3,15},{4,0},{5,1},{6,2},{7,3},{8,4},{9,5},{1... | collective-permute-start | bytes 245768 | tf_op jit(solution)/shard_map/ppermute | solution.py:480
  53.8 6.3 %collective-permute-start.12 = (bf16[40,1024]{1,0:T(8,128)(2,1)S(1)}, bf16[40,1024]{1,0:T(8,128)(2,1)S(1)}, u32[]{:S(2)}, u32[]{:S(2)}) collective-permute-start(bf16[40,1024]{1,0:T(8,128)(2,1)S(1)} %get-tuple-element.79), channel_id=1, source_target_pairs={{0,4},{1,5},{2,6},{3,7},{4,8},{5,9},{6,10},{7,11},{8,12},{9,13},{1... | collective-permute-start | bytes 245768 | tf_op jit(solution)/shard_map/ppermute | solution.py:480

commit v14 on v13

--- a/solution.py
+++ b/solution.py
@@ -17,9 +17,9 @@
 EPSILON = 1e-05
 
 BLOCK = 512
-READY = 11
-BUFFERS = 12
-LIMIT = 8
+READY = 12
+BUFFERS = 13
+LIMIT = 5
 
 F32 = jnp.float32
 BF16 = jnp.bfloat16
@@ -332,7 +332,7 @@
     refs = refs[BUFFERS:]
     up, down, mask, _, hidden, gives = [refs.pop(0) for _ in range(6)]
     buffers = [refs.pop(0) for _ in range(BUFFERS)]
-    gate_sum, up_sum, rows, sems = refs
+    total, rows, sems = refs
     half = own.shape[1] // 2
     features, unit_width = up.shape
     columns, lines = unit_width // BLOCK, features // BLOCK
@@ -362,7 +362,6 @@
             if index + n >= READY:
                 await_all(pair[n], sems.at[(index + n) % count])
         line = index % lines
-        total = gate_sum if index < lines else up_sum
         left = [rows[:, (line + n) * BLOCK : (line + n + 1) * BLOCK] for n in range(2)]
         for column in range(columns):
             cols = slice(column * BLOCK, (column + 1) * BLOCK)
@@ -370,10 +369,13 @@
             value = value + jnp.dot(left[1], pair[1][column], preferred_element_type=F32)
             if line > 0:
                 value = total[:, cols] + value
-            if index < 2 * lines - 2:
+            if line < lines - 2:
                 total[:, cols] = value
                 continue
-            value = jnp.maximum(gate_sum[:, cols], 0.0) * jnp.maximum(value, 0.0)
+            if index < lines:
+                hidden[:, cols] = jnp.maximum(value, 0.0).astype(BF16)
+                continue
+            value = hidden[:, cols].astype(F32) * jnp.maximum(value, 0.0)
             parts = []
             for d in range(exp_count):
                 parts.append(value[d * CAP : (d + 1) * CAP, :] * mask[d : d + 1, cols])
@@ -554,7 +556,6 @@
         moved=1 << 22,
         aliases={5: 2},
     )
-    acc = pltpu.VMEM((slots, unit_width), F32)
     part = features // unit_count
     hidden, first_given, *buffers = call(
         functools.partial(hidden_kernel, sizes),
@@ -564,8 +565,7 @@
         + [(up_weight, pltpu.HBM), (down_weight, pltpu.HBM), (mask, None)]
         + [(combine_low, pl.ANY)],
         [
-            acc,
-            acc,
+            pltpu.VMEM((slots, unit_width), F32),
             pltpu.VMEM((slots, features), BF16),
             pltpu.SemaphoreType.DMA((BUFFERS,)),
         ],

time: 61.4 us -> 60.7 us (0.989)
  transfers between devices with their start and end apart: 13 -> 13, of which waited for: 4 -> 5; matrix products, arithmetic and copies ran while one was open for 0% -> 0% of each run, Pallas kernels for 31% -> 33%
where the time goes in v14:
time: 60.7 us; the launch traced here: 60.4 us
  Pallas kernels  35.7 us (59%)
  starting transfers between devices  18.6 us (31%)
  waiting for transfers between devices  6 us (10%)
    pallas_call x10, Pallas kernels, call(): pl.pallas_call(kernel, out_shape=shapes, in_specs=specs, out_specs=[vmem]...  35.7 us
    ppermute x10, starting transfers between devices, shift(): return lax.ppermute(value, ('exp', 'unit'), pairs)  17.8 us
    ppermute x10, waiting for transfers between devices, shift(): return lax.ppermute(value, ('exp', 'unit'), pairs)  5.99 us
  transfers between devices with their start and end apart: 13, of which 5 were waited for; matrix products, arithmetic and copies ran while one was open for 0% of the time, Pallas kernels for 33%

profile of v14, /device:TPU:0, one launch (start us, length us, event | category | flops | bytes accessed | tf_op | source)
XLA Modules:
  0.0 60.4 jit_solution(16272335554358656758)
XLA Ops:
  0.0 2.4 %shard_map.82 = (bf16[40,4096]{1,0:T(8,128)(2,1)S(1)}, bf16[7,512,512]{2,1,0:T(8,128)(2,1)S(1)}, bf16[40,2048]{1,0:T(8,128)(2,1)S(1)}, bf16[40,2048]{1,0:T(8,128)(2,1)S(1)}, bf16[40,2048]{1,0:T(8,128)(2,1)S(1)}) custom-call(bf16[128,4096]{1,0:T(8,128)(2,1)} %tokens_hbm.1, f32[1,4096]{1,0:T(1,128)} %bitcast.3, s32[2,128]{1,0:T(2,128)} %bitcast.4, ...), custom_call_target="tpu_custom_call" | custom-call | flops 83886080 | bytes 5767168 | tf_op jit(solution)/shard_map/pallas_call | solution.py:449
  2.4 4.1 %collective-permute-start = (bf16[40,2048]{1,0:T(8,128)(2,1)S(1)}, bf16[40,2048]{1,0:T(8,128)(2,1)S(1)}, u32[]{:S(2)}, u32[]{:S(2)}) collective-permute-start(bf16[40,2048]{1,0:T(8,128)(2,1)S(1)} %get-tuple-element.47), channel_id=1, source_target_pairs={{0,8},{1,9},{2,10},{3,11},{4,12},{5,13},{6,14},{7,15},{8,0},{9,1},... | collective-permute-start | bytes 491528 | tf_op jit(solution)/shard_map/ppermute | solution.py:482
  6.5 1.6 %collective-permute-start.1 = (bf16[40,2048]{1,0:T(8,128)(2,1)S(1)}, bf16[40,2048]{1,0:T(8,128)(2,1)S(1)}, u32[]{:S(2)}, u32[]{:S(2)}) collective-permute-start(bf16[40,2048]{1,0:T(8,128)(2,1)S(1)} %get-tuple-element.48), channel_id=1, source_target_pairs={{0,4},{1,5},{2,6},{3,7},{4,8},{5,9},{6,10},{7,11},{8,12},{9,13},{1... | collective-permute-start | bytes 491528 | tf_op jit(solution)/shard_map/ppermute | solution.py:482
  8.1 2.2 %collective-permute-start.2 = (bf16[40,2048]{1,0:T(8,128)(2,1)S(1)}, bf16[40,2048]{1,0:T(8,128)(2,1)S(1)}, u32[]{:S(2)}, u32[]{:S(2)}) collective-permute-start(bf16[40,2048]{1,0:T(8,128)(2,1)S(1)} %get-tuple-element.49), channel_id=1, source_target_pairs={{0,12},{1,13},{2,14},{3,15},{4,0},{5,1},{6,2},{7,3},{8,4},{9,5},{1... | collective-permute-start | bytes 491528 | tf_op jit(solution)/shard_map/ppermute | solution.py:482
  10.4 11.9 %shard_map.83 = (f32[8,3584]{1,0:T(8,128)S(1)}, bf16[7,512,512]{2,1,0:T(8,128)(2,1)S(1)}, bf16[7,512,512]{2,1,0:T(8,128)(2,1)S(1)}, bf16[7,512,512]{2,1,0:T(8,12...) custom-call(s32[2,8,48]{2,1,0:T(8,128)} %active_hbm.1, ...), custom_call_target="tpu_custom_call", output_to_operand_aliasing={{1}: (4, {})} | custom-call | flops 167772160 | bytes 36700160 | tf_op jit(solution)/shard_map/pallas_call | solution.py:449
  22.3 0.0 collective-permute-done.refs_0_
  22.3 0.0 collective-permute-done.1.refs_1_
  22.3 0.0 collective-permute-done.2.refs_2_
  22.4 0.1 collective-permute-start.3
  22.4 2.1 %shard_map.85 = (bf16[2,128,256]{2,1,0:T(8,128)(2,1)S(1)}, bf16[2,128,256]{2,1,0:T(8,128)(2,1)S(1)}, bf16[7,512,512]{2,1,0:T(8,128)(2,1)S(1)}) custom-call(s32[2,128]{1,0:T(2,128)} %bitcast.5, f32[2,128]{1,0:T(2,128)} %bitcast.6, bf16[120,2048]{1,0:T(8,128)(2,1)S(1)} %shard_map.84.after.mine, ...), custom_call_target="tpu_custom_call", output_to_operand_aliasing={{2}: (5, {})} | custom-call | bytes 4194304 | tf_op jit(solution)/shard_map/pallas_call | solution.py:449
  24.6 0.0 collective-permute-done.3.other
  24.6 12.5 %shard_map.86 = (bf16[160,3584]{1,0:T(8,128)(2,1)S(1)}, bf16[160,1024]{1,0:T(8,128)(2,1)S(1)}, bf16[7,512,512]{2,1,0:T(8,128)(2,1)S(1)}, bf16[7,512,512]{2,1,0:T...) custom-call(bf16[40,4096]{1,0:T(8,128)(2,1)S(1)} %get-tuple-element., ...), custom_call_target="tpu_custom_call", output_to_operand_aliasing={{2}: (3, {}), {3}: (4, {}), {4}: (5, {}), {5}: (6, {}), {6}... | custom-call | flops 9395240960 | bytes 36700160 | tf_op jit(solution)/shard_map/pallas_call | solution.py:449
  37.1 0.6 collective-permute-start.4
  37.6 2.0 %shard_map.89 = (bf16[160,1024]{1,0:T(8,128)(2,1)S(1)}, bf16[7,512,512]{2,1,0:T(8,128)(2,1)S(1)}) custom-call(bf16[160,3584]{1,0:T(8,128)(2,1)S(1)} %get-tuple-element.66.hidden, bf16[7,512,512]{2,1,0:T(8,128)(2,1)S(1)} %get-tuple-element.74.refs_0_, bf16[7,512,512]{2,1,0:T(8,128)(2,1)S(1)} %get-tuple-element.75.refs_1_, bf16[3584,4096]{1,0:T(8,128)(2,1)} %refs_2_.1), custom_call_target="tpu_custom_call" | custom-call | flops 1174405120 | bytes 3670016 | tf_op jit(solution)/shard_map/pallas_call | solution.py:449
  39.7 0.1 collective-permute-start.9
  39.8 0.0 collective-permute-done.4.received
  39.8 2.0 %shard_map.87 = (bf16[40,1024]{1,0:T(8,128)(2,1)S(1)}, bf16[40,1024]{1,0:T(8,128)(2,1)S(1)}, bf16[40,1024]{1,0:T(8,128)(2,1)S(1)}, bf16[40,1024]{1,0:T(8,128)(2,1)S(1)}, bf16[7,512,512]{2,1,0:T(8,128)(2,1)S(1)}) custom-call(bf16[160,3584]{1,0:T(8,128)(2,1)S(1)} %get-tuple-element.66.hidden, bf16[160,1024]{1,0:T(8,128)(2,1)S(1)} %collective-permute-done.4.received, ...), custom_call_target="tpu_custom_call" | custom-call | flops 1174405120 | bytes 3670016 | tf_op jit(solution)/shard_map/pallas_call | solution.py:449
  41.8 2.6 %collective-permute-start.5 = (bf16[40,1024]{1,0:T(8,128)(2,1)S(1)}, bf16[40,1024]{1,0:T(8,128)(2,1)S(1)}, u32[]{:S(2)}, u32[]{:S(2)}) collective-permute-start(bf16[40,1024]{1,0:T(8,128)(2,1)S(1)} %get-tuple-element.70), channel_id=1, source_target_pairs={{0,10},{1,11},{2,8},{3,9},{4,14},{5,15},{6,12},{7,13},{8,2},{9,3},... | collective-permute-start | bytes 245768 | tf_op jit(solution)/shard_map/ppermute | solution.py:482
  44.4 0.5 collective-permute-start.6
  44.9 2.4 %collective-permute-start.7 = (bf16[40,1024]{1,0:T(8,128)(2,1)S(1)}, bf16[40,1024]{1,0:T(8,128)(2,1)S(1)}, u32[]{:S(2)}, u32[]{:S(2)}) collective-permute-start(bf16[40,1024]{1,0:T(8,128)(2,1)S(1)} %get-tuple-element.72), channel_id=1, source_target_pairs={{0,6},{1,7},{2,4},{3,5},{4,10},{5,11},{6,8},{7,9},{8,14},{9,15},{1... | collective-permute-start | bytes 245768 | tf_op jit(solution)/shard_map/ppermute | solution.py:482
  47.3 0.5 collective-permute-start.8
  47.9 0.0 collective-permute-done.9.received
  47.9 1.4 %shard_map.90 = (bf16[40,1024]{1,0:T(8,128)(2,1)S(1)}, bf16[40,1024]{1,0:T(8,128)(2,1)S(1)}, bf16[40,1024]{1,0:T(8,128)(2,1)S(1)}, bf16[40,1024]{1,0:T(8,128)(2,1)S(1)}) custom-call(bf16[160,3584]{1,0:T(8,128)(2,1)S(1)} %get-tuple-element.66.hidden, bf16[160,1024]{1,0:T(8,128)(2,1)S(1)} %collective-permute-done.9.received, ...), custom_call_target="tpu_custom_call" | custom-call | flops 1174405120 | bytes 3670016 | tf_op jit(solution)/shard_map/pallas_call | solution.py:449
  49.2 1.4 %collective-permute-start.10 = (bf16[40,1024]{1,0:T(8,128)(2,1)S(1)}, bf16[40,1024]{1,0:T(8,128)(2,1)S(1)}, u32[]{:S(2)}, u32[]{:S(2)}) collective-permute-start(bf16[40,1024]{1,0:T(8,128)(2,1)S(1)} %get-tuple-element.79), channel_id=1, source_target_pairs={{0,8},{1,9},{2,10},{3,11},{4,12},{5,13},{6,14},{7,15},{8,0},{9,1},... | collective-permute-start | bytes 245768 | tf_op jit(solution)/shard_map/ppermute | solution.py:482
  50.6 0.0 collective-permute-done.5.refs_0_
  50.6 1.1 %collective-permute-start.11 = (bf16[40,1024]{1,0:T(8,128)(2,1)S(1)}, bf16[40,1024]{1,0:T(8,128)(2,1)S(1)}, u32[]{:S(2)}, u32[]{:S(2)}) collective-permute-start(bf16[40,1024]{1,0:T(8,128)(2,1)S(1)} %get-tuple-element.80), channel_id=1, source_target_pairs={{0,12},{1,13},{2,14},{3,15},{4,0},{5,1},{6,2},{7,3},{8,4},{9,5},{1... | collective-permute-start | bytes 245768 | tf_op jit(solution)/shard_map/ppermute | solution.py:482
  51.7 1.4 %collective-permute-done.6.refs_1_ = bf16[40,1024]{1,0:T(8,128)(2,1)S(1)} collective-permute-done((bf16[40,1024]{1,0:T(8,128)(2,1)S(1)}, bf16[40,1024]{1,0:T(8,128)(2,1)S(1)}, u32[]{:S(2)}, u32[]{:S(2)}) %collective-permute-start.6) | collective-permute-done | bytes 81952 | tf_op jit(solution)/shard_map/ppermute | solution.py:482
  53.1 1.4 %collective-permute-start.12 = (bf16[40,1024]{1,0:T(8,128)(2,1)S(1)}, bf16[40,1024]{1,0:T(8,128)(2,1)S(1)}, u32[]{:S(2)}, u32[]{:S(2)}) collective-permute-start(bf16[40,1024]{1,0:T(8,128)(2,1)S(1)} %get-tuple-element.81), channel_id=1, source_target_pairs={{0,4},{1,5},{2,6},{3,7},{4,8},{5,9},{6,10},{7,11},{8,12},{9,13},{1... | collective-permute-start | bytes 245768 | tf_op jit(solution)/shard_map/ppermute | solution.py:482
  54.5 0.0 collective-permute-done.7.refs_2_
  54.5 0.3 collective-permute-done.8.refs_3_
  54.7 0.3 shard_map.88.refs_0_
  55.0 1.6 %collective-permute-done.10.refs_1_ = bf16[40,1024]{1,0:T(8,128)(2,1)S(1)} collective-permute-done((bf16[40,1024]{1,0:T(8,128)(2,1)S(1)}, bf16[40,1024]{1,0:T(8,128)(2,1)S(1)}, u32[]{:S(2)}, u32[]{:S(2)}) %collective-permute-start.10) | collective-permute-done | bytes 81952 | tf_op jit(solution)/shard_map/ppermute | solution.py:482
  56.7 0.2 collective-permute-done.11.refs_2_
  56.8 2.5 %collective-permute-done.12.refs_3_ = bf16[40,1024]{1,0:T(8,128)(2,1)S(1)} collective-permute-done((bf16[40,1024]{1,0:T(8,128)(2,1)S(1)}, bf16[40,1024]{1,0:T(8,128)(2,1)S(1)}, u32[]{:S(2)}, u32[]{:S(2)}) %collective-permute-start.12) | collective-permute-done | bytes 81952 | tf_op jit(solution)/shard_map/ppermute | solution.py:482
  59.4 1.0 %shard_map.91 = bf16[128,1024]{1,0:T(8,128)(2,1)} custom-call(bf16[2,128,256]{2,1,0:T(8,128)(2,1)S(1)} %get-tuple-element.51.high, bf16[2,128,256]{2,1,0:T(8,128)(2,1)S(1)} %get-tuple-element.52.refs_16_.low, f32[128,1024]{1,0:T(8,128)S(1)} %shard_map.88.refs_0_, bf16[40,1024]{1,0:T(8,128)(2,1)S(1)} %collective-permute-done.10.refs_1_, ...), custom_call_target="tpu_custom_call" | custom-call | flops 83886080 | bytes 1048576 | tf_op jit(solution)/shard_map/pallas_call | solution.py:449
  (1 shorter events, 0.0 us)
Async XLA Ops:
  2.4 19.9 %collective-permute-start = (bf16[40,2048]{1,0:T(8,128)(2,1)S(1)}, bf16[40,2048]{1,0:T(8,128)(2,1)S(1)}, u32[]{:S(2)}, u32[]{:S(2)}) collective-permute-start(bf16[40,2048]{1,0:T(8,128)(2,1)S(1)} %get-tuple-element.47), channel_id=1, source_target_pairs={{0,8},{1,9},{2,10},{3,11},{4,12},{5,13},{6,14},{7,15},{8,0},{9,1},... | collective-permute-start | bytes 491528 | tf_op jit(solution)/shard_map/ppermute | solution.py:482
  6.5 15.8 %collective-permute-start.1 = (bf16[40,2048]{1,0:T(8,128)(2,1)S(1)}, bf16[40,2048]{1,0:T(8,128)(2,1)S(1)}, u32[]{:S(2)}, u32[]{:S(2)}) collective-permute-start(bf16[40,2048]{1,0:T(8,128)(2,1)S(1)} %get-tuple-element.48), channel_id=1, source_target_pairs={{0,4},{1,5},{2,6},{3,7},{4,8},{5,9},{6,10},{7,11},{8,12},{9,13},{1... | collective-permute-start | bytes 491528 | tf_op jit(solution)/shard_map/ppermute | solution.py:482
  8.1 14.2 %collective-permute-start.2 = (bf16[40,2048]{1,0:T(8,128)(2,1)S(1)}, bf16[40,2048]{1,0:T(8,128)(2,1)S(1)}, u32[]{:S(2)}, u32[]{:S(2)}) collective-permute-start(bf16[40,2048]{1,0:T(8,128)(2,1)S(1)} %get-tuple-element.49), channel_id=1, source_target_pairs={{0,12},{1,13},{2,14},{3,15},{4,0},{5,1},{6,2},{7,3},{8,4},{9,5},{1... | collective-permute-start | bytes 491528 | tf_op jit(solution)/shard_map/ppermute | solution.py:482
  22.4 2.2 %collective-permute-start.3 = (bf16[120,2048]{1,0:T(8,128)(2,1)S(1)}, bf16[120,2048]{1,0:T(8,128)(2,1)S(1)}, u32[]{:S(2)}, u32[]{:S(2)}) collective-permute-start(bf16[120,2048]{1,0:T(8,128)(2,1)S(1)} %shard_map.84.after.mine), channel_id=1, source_target_pairs={{0,1},{1,0},{2,3},{3,2},{4,5},{5,4},{6,7},{7,6},{8,9},{9,8},{10,11... | collective-permute-start | bytes 1474568 | tf_op jit(solution)/shard_map/ppermute | solution.py:485
  37.1 2.7 %collective-permute-start.4 = (bf16[160,1024]{1,0:T(8,128)(2,1)S(1)}, bf16[160,1024]{1,0:T(8,128)(2,1)S(1)}, u32[]{:S(2)}, u32[]{:S(2)}) collective-permute-start(bf16[160,1024]{1,0:T(8,128)(2,1)S(1)} %get-tuple-element.67), channel_id=1, source_target_pairs={{0,1},{1,0},{2,3},{3,2},{4,5},{5,4},{6,7},{7,6},{8,9},{9,8},{10,11... | collective-permute-start | bytes 983048 | tf_op jit(solution)/shard_map/ppermute | solution.py:485
  39.7 8.2 %collective-permute-start.9 = (bf16[160,1024]{1,0:T(8,128)(2,1)S(1)}, bf16[160,1024]{1,0:T(8,128)(2,1)S(1)}, u32[]{:S(2)}, u32[]{:S(2)}) collective-permute-start(bf16[160,1024]{1,0:T(8,128)(2,1)S(1)} %get-tuple-element.76), channel_id=1, source_target_pairs={{0,1},{1,0},{2,3},{3,2},{4,5},{5,4},{6,7},{7,6},{8,9},{9,8},{10,11... | collective-permute-start | bytes 983048 | tf_op jit(solution)/shard_map/ppermute | solution.py:485
  41.8 8.8 %collective-permute-start.5 = (bf16[40,1024]{1,0:T(8,128)(2,1)S(1)}, bf16[40,1024]{1,0:T(8,128)(2,1)S(1)}, u32[]{:S(2)}, u32[]{:S(2)}) collective-permute-start(bf16[40,1024]{1,0:T(8,128)(2,1)S(1)} %get-tuple-element.70), channel_id=1, source_target_pairs={{0,10},{1,11},{2,8},{3,9},{4,14},{5,15},{6,12},{7,13},{8,2},{9,3},... | collective-permute-start | bytes 245768 | tf_op jit(solution)/shard_map/ppermute | solution.py:482
  44.4 8.7 %collective-permute-start.6 = (bf16[40,1024]{1,0:T(8,128)(2,1)S(1)}, bf16[40,1024]{1,0:T(8,128)(2,1)S(1)}, u32[]{:S(2)}, u32[]{:S(2)}) collective-permute-start(bf16[40,1024]{1,0:T(8,128)(2,1)S(1)} %get-tuple-element.71), channel_id=1, source_target_pairs={{0,14},{1,15},{2,12},{3,13},{4,2},{5,3},{6,0},{7,1},{8,6},{9,7},{1... | collective-permute-start | bytes 245768 | tf_op jit(solution)/shard_map/ppermute | solution.py:482
  44.9 9.5 %collective-permute-start.7 = (bf16[40,1024]{1,0:T(8,128)(2,1)S(1)}, bf16[40,1024]{1,0:T(8,128)(2,1)S(1)}, u32[]{:S(2)}, u32[]{:S(2)}) collective-permute-start(bf16[40,1024]{1,0:T(8,128)(2,1)S(1)} %get-tuple-element.72), channel_id=1, source_target_pairs={{0,6},{1,7},{2,4},{3,5},{4,10},{5,11},{6,8},{7,9},{8,14},{9,15},{1... | collective-permute-start | bytes 245768 | tf_op jit(solution)/shard_map/ppermute | solution.py:482
  47.3 7.4 %collective-permute-start.8 = (bf16[40,1024]{1,0:T(8,128)(2,1)S(1)}, bf16[40,1024]{1,0:T(8,128)(2,1)S(1)}, u32[]{:S(2)}, u32[]{:S(2)}) collective-permute-start(bf16[40,1024]{1,0:T(8,128)(2,1)S(1)} %get-tuple-element.73), channel_id=1, source_target_pairs={{0,2},{1,3},{2,0},{3,1},{4,6},{5,7},{6,4},{7,5},{8,10},{9,11},{10,... | collective-permute-start | bytes 245768 | tf_op jit(solution)/shard_map/ppermute | solution.py:482
  49.2 7.4 %collective-permute-start.10 = (bf16[40,1024]{1,0:T(8,128)(2,1)S(1)}, bf16[40,1024]{1,0:T(8,128)(2,1)S(1)}, u32[]{:S(2)}, u32[]{:S(2)}) collective-permute-start(bf16[40,1024]{1,0:T(8,128)(2,1)S(1)} %get-tuple-element.79), channel_id=1, source_target_pairs={{0,8},{1,9},{2,10},{3,11},{4,12},{5,13},{6,14},{7,15},{8,0},{9,1},... | collective-permute-start | bytes 245768 | tf_op jit(solution)/shard_map/ppermute | solution.py:482
  50.6 6.2 %collective-permute-start.11 = (bf16[40,1024]{1,0:T(8,128)(2,1)S(1)}, bf16[40,1024]{1,0:T(8,128)(2,1)S(1)}, u32[]{:S(2)}, u32[]{:S(2)}) collective-permute-start(bf16[40,1024]{1,0:T(8,128)(2,1)S(1)} %get-tuple-element.80), channel_id=1, source_target_pairs={{0,12},{1,13},{2,14},{3,15},{4,0},{5,1},{6,2},{7,3},{8,4},{9,5},{1... | collective-permute-start | bytes 245768 | tf_op jit(solution)/shard_map/ppermute | solution.py:482
  53.1 6.3 %collective-permute-start.12 = (bf16[40,1024]{1,0:T(8,128)(2,1)S(1)}, bf16[40,1024]{1,0:T(8,128)(2,1)S(1)}, u32[]{:S(2)}, u32[]{:S(2)}) collective-permute-start(bf16[40,1024]{1,0:T(8,128)(2,1)S(1)} %get-tuple-element.81), channel_id=1, source_target_pairs={{0,4},{1,5},{2,6},{3,7},{4,8},{5,9},{6,10},{7,11},{8,12},{9,13},{1... | collective-permute-start | bytes 245768 | tf_op jit(solution)/shard_map/ppermute | solution.py:482

commit v15 on v14

--- a/solution.py
+++ b/solution.py
@@ -401,25 +401,25 @@
     await_all(kept_weights, sem)
 
 
-def keep_kernel(sizes, ahead, hidden, received, *refs):
+def keep_kernel(sizes, offset, lacks, hidden, received, *refs):
     exp_count, groups = sizes
     refs = list(refs)
-    if ahead is not None:
-        sem, down = refs.pop(), refs.pop(0)
-        next_weights = refs[received.shape[1] // BLOCK + exp_count :]
-        for step, buffer in enumerate(next_weights, 1):
-            fetch_columns(sizes, down, ahead, True, step, buffer, sem.at[step - 1])
-    weights = refs[: received.shape[1] // BLOCK]
-    outs = refs[len(weights) : len(weights) + exp_count]
+    extra = []
+    if lacks:
+        sems, scratch, down = refs.pop(), refs.pop(), refs.pop(0)
+        extra = [scratch.at[n] for n in range(lacks)]
+    held = received.shape[1] // BLOCK - lacks
+    for n, buffer in enumerate(extra):
+        fetch_columns(sizes, down, offset, True, held + n, buffer, sems.at[n])
+    weights, outs = refs[:held] + extra, refs[held:]
     for step, buffer in enumerate(weights):
+        if step >= held:
+            await_all(buffer, sems.at[step - held])
         cols = slice(step * BLOCK, (step + 1) * BLOCK)
         value = jnp.dot(hidden[...], stacked(buffer), preferred_element_type=F32)
         value = value + received[:, cols].astype(F32)
         for d in range(exp_count):
             outs[d][:, cols] = value[d * CAP : (d + 1) * CAP, :].astype(BF16)
-    if ahead is not None:
-        for step, buffer in enumerate(next_weights, 1):
-            await_all(buffer, sem.at[step - 1])
 
 
 def combine_kernel(order, high, low, *refs):
@@ -595,20 +595,22 @@
     taken = [swap(value) for value in given]
     home = {}
     for order, offset in enumerate(offsets):
-        more = order < groups - 1
-        outs = call(
-            functools.partial(keep_kernel, sizes, offsets[order + 1] if more else None),
-            [((CAP, part), BF16)] * exp_count + [buffer] * (steps - 1 if more else 0),
+        lacks = steps - len(kept_weights[order])
+        kept = call(
+            functools.partial(keep_kernel, sizes, offset, lacks),
+            [((CAP, part), BF16)] * exp_count,
             [(hidden, None), (taken[order], None)]
-            + ([(down_weight, pltpu.HBM)] if more else [])
+            + ([(down_weight, pltpu.HBM)] if lacks else [])
             + [(v, pltpu.VMEM) for v in kept_weights[order]],
-            [pltpu.SemaphoreType.DMA((steps - 1,))] if more else [],
+            [
+                pltpu.VMEM((lacks,) + buffer[0], BF16),
+                pltpu.SemaphoreType.DMA((lacks,)),
+            ]
+            if lacks
+            else [],
             flops=2 * slots * unit_width * part,
             moved=piece_bytes,
         )
-        kept = outs[:exp_count]
-        if more:
-            kept_weights[order + 1] = list(kept_weights[order + 1]) + list(outs[exp_count:])
         for d in distances(exp_count) + [0]:
             home[offset, d] = shift(kept[d], -d, offset) if d or offset else kept[d]
     mixed = None

time: 60.7 us -> 60.1 us (level)
  waiting for transfers between devices: 6 us -> 5.09 us
  Pallas kernels: 35.7 us -> 36.4 us
    ppermute x10, waiting for transfers between devices: 5.99 us -> 5.08 us  [shift(): return lax.ppermute(value, ('exp', 'unit'), pairs)]
    pallas_call x10, Pallas kernels: 35.7 us -> 36.4 us  [call(): pl.pallas_call(kernel, out_shape=shapes, in_specs=specs, out_specs=[vmem]...]
  transfers between devices with their start and end apart: 13 -> 13, of which waited for: 5 -> 3; matrix products, arithmetic and copies ran while one was open for 0% -> 0% of each run, Pallas kernels for 33% -> 34%
where the time goes in v15:
time: 60.1 us; the launch traced here: 59.8 us
  Pallas kernels  36.4 us (61%)
  starting transfers between devices  18.1 us (30%)
  waiting for transfers between devices  5.09 us (8%)
    pallas_call x10, Pallas kernels, call(): pl.pallas_call(kernel, out_shape=shapes, in_specs=specs, out_specs=[vmem]...  36.4 us
    ppermute x10, starting transfers between devices, shift(): return lax.ppermute(value, ('exp', 'unit'), pairs)  17.4 us
    ppermute x10, waiting for transfers between devices, shift(): return lax.ppermute(value, ('exp', 'unit'), pairs)  5.08 us
  transfers between devices with their start and end apart: 13, of which 3 were waited for; matrix products, arithmetic and copies ran while one was open for 0% of the time, Pallas kernels for 34%

profile of v15, /device:TPU:0, one launch (start us, length us, event | category | flops | bytes accessed | tf_op | source)
XLA Modules:
  0.0 59.8 jit_solution(4355170089922606781)
XLA Ops:
  0.0 2.4 %shard_map.82 = (bf16[40,4096]{1,0:T(8,128)(2,1)S(1)}, bf16[7,512,512]{2,1,0:T(8,128)(2,1)S(1)}, bf16[40,2048]{1,0:T(8,128)(2,1)S(1)}, bf16[40,2048]{1,0:T(8,128)(2,1)S(1)}, bf16[40,2048]{1,0:T(8,128)(2,1)S(1)}) custom-call(bf16[128,4096]{1,0:T(8,128)(2,1)} %tokens_hbm.1, f32[1,4096]{1,0:T(1,128)} %bitcast.3, s32[2,128]{1,0:T(2,128)} %bitcast.4, ...), custom_call_target="tpu_custom_call" | custom-call | flops 83886080 | bytes 5767168 | tf_op jit(solution)/shard_map/pallas_call | solution.py:449
  2.4 4.1 %collective-permute-start = (bf16[40,2048]{1,0:T(8,128)(2,1)S(1)}, bf16[40,2048]{1,0:T(8,128)(2,1)S(1)}, u32[]{:S(2)}, u32[]{:S(2)}) collective-permute-start(bf16[40,2048]{1,0:T(8,128)(2,1)S(1)} %get-tuple-element.46), channel_id=1, source_target_pairs={{0,8},{1,9},{2,10},{3,11},{4,12},{5,13},{6,14},{7,15},{8,0},{9,1},... | collective-permute-start | bytes 491528 | tf_op jit(solution)/shard_map/ppermute | solution.py:482
  6.5 1.6 %collective-permute-start.1 = (bf16[40,2048]{1,0:T(8,128)(2,1)S(1)}, bf16[40,2048]{1,0:T(8,128)(2,1)S(1)}, u32[]{:S(2)}, u32[]{:S(2)}) collective-permute-start(bf16[40,2048]{1,0:T(8,128)(2,1)S(1)} %get-tuple-element.47), channel_id=1, source_target_pairs={{0,4},{1,5},{2,6},{3,7},{4,8},{5,9},{6,10},{7,11},{8,12},{9,13},{1... | collective-permute-start | bytes 491528 | tf_op jit(solution)/shard_map/ppermute | solution.py:482
  8.1 2.2 %collective-permute-start.2 = (bf16[40,2048]{1,0:T(8,128)(2,1)S(1)}, bf16[40,2048]{1,0:T(8,128)(2,1)S(1)}, u32[]{:S(2)}, u32[]{:S(2)}) collective-permute-start(bf16[40,2048]{1,0:T(8,128)(2,1)S(1)} %get-tuple-element.48), channel_id=1, source_target_pairs={{0,12},{1,13},{2,14},{3,15},{4,0},{5,1},{6,2},{7,3},{8,4},{9,5},{1... | collective-permute-start | bytes 491528 | tf_op jit(solution)/shard_map/ppermute | solution.py:482
  10.4 11.9 %shard_map.83 = (f32[8,3584]{1,0:T(8,128)S(1)}, bf16[7,512,512]{2,1,0:T(8,128)(2,1)S(1)}, bf16[7,512,512]{2,1,0:T(8,128)(2,1)S(1)}, bf16[7,512,512]{2,1,0:T(8,12...) custom-call(s32[2,8,48]{2,1,0:T(8,128)} %active_hbm.1, ...), custom_call_target="tpu_custom_call", output_to_operand_aliasing={{1}: (4, {})} | custom-call | flops 167772160 | bytes 36700160 | tf_op jit(solution)/shard_map/pallas_call | solution.py:449
  22.3 0.0 collective-permute-done.refs_0_
  22.3 0.0 collective-permute-done.1.refs_1_
  22.3 0.0 collective-permute-done.2.refs_2_
  22.4 0.1 collective-permute-start.3
  22.4 2.1 %shard_map.85 = (bf16[2,128,256]{2,1,0:T(8,128)(2,1)S(1)}, bf16[2,128,256]{2,1,0:T(8,128)(2,1)S(1)}, bf16[7,512,512]{2,1,0:T(8,128)(2,1)S(1)}) custom-call(s32[2,128]{1,0:T(2,128)} %bitcast.5, f32[2,128]{1,0:T(2,128)} %bitcast.6, bf16[120,2048]{1,0:T(8,128)(2,1)S(1)} %shard_map.84.after.mine, ...), custom_call_target="tpu_custom_call", output_to_operand_aliasing={{2}: (5, {})} | custom-call | bytes 4194304 | tf_op jit(solution)/shard_map/pallas_call | solution.py:449
  24.6 0.0 collective-permute-done.3.other
  24.6 12.5 %shard_map.86 = (bf16[160,3584]{1,0:T(8,128)(2,1)S(1)}, bf16[160,1024]{1,0:T(8,128)(2,1)S(1)}, bf16[7,512,512]{2,1,0:T(8,128)(2,1)S(1)}, bf16[7,512,512]{2,1,0:T...) custom-call(bf16[40,4096]{1,0:T(8,128)(2,1)S(1)} %get-tuple-element., ...), custom_call_target="tpu_custom_call", output_to_operand_aliasing={{2}: (3, {}), {3}: (4, {}), {4}: (5, {}), {5}: (6, {}), {6}... | custom-call | flops 9395240960 | bytes 36700160 | tf_op jit(solution)/shard_map/pallas_call | solution.py:449
  37.1 0.6 collective-permute-start.4
  37.6 2.0 %shard_map.89 = (bf16[160,1024]{1,0:T(8,128)(2,1)S(1)}, bf16[7,512,512]{2,1,0:T(8,128)(2,1)S(1)}) custom-call(bf16[160,3584]{1,0:T(8,128)(2,1)S(1)} %get-tuple-element.65.hidden, bf16[7,512,512]{2,1,0:T(8,128)(2,1)S(1)} %get-tuple-element.73.refs_0_, bf16[7,512,512]{2,1,0:T(8,128)(2,1)S(1)} %get-tuple-element.74.refs_1_, bf16[3584,4096]{1,0:T(8,128)(2,1)} %refs_0_.1), custom_call_target="tpu_custom_call" | custom-call | flops 1174405120 | bytes 3670016 | tf_op jit(solution)/shard_map/pallas_call | solution.py:449
  39.7 0.1 collective-permute-start.9
  39.8 0.0 collective-permute-done.4.received
  39.8 1.4 %shard_map.87 = (bf16[40,1024]{1,0:T(8,128)(2,1)S(1)}, bf16[40,1024]{1,0:T(8,128)(2,1)S(1)}, bf16[40,1024]{1,0:T(8,128)(2,1)S(1)}, bf16[40,1024]{1,0:T(8,128)(2,1)S(1)}) custom-call(bf16[160,3584]{1,0:T(8,128)(2,1)S(1)} %get-tuple-element.65.hidden, bf16[160,1024]{1,0:T(8,128)(2,1)S(1)} %collective-permute-done.4.received, ...), custom_call_target="tpu_custom_call" | custom-call | flops 1174405120 | bytes 3670016 | tf_op jit(solution)/shard_map/pallas_call | solution.py:449
  41.1 2.6 %collective-permute-start.5 = (bf16[40,1024]{1,0:T(8,128)(2,1)S(1)}, bf16[40,1024]{1,0:T(8,128)(2,1)S(1)}, u32[]{:S(2)}, u32[]{:S(2)}) collective-permute-start(bf16[40,1024]{1,0:T(8,128)(2,1)S(1)} %get-tuple-element.69), channel_id=1, source_target_pairs={{0,10},{1,11},{2,8},{3,9},{4,14},{5,15},{6,12},{7,13},{8,2},{9,3},... | collective-permute-start | bytes 245768 | tf_op jit(solution)/shard_map/ppermute | solution.py:482
  43.7 0.5 collective-permute-start.6
  44.2 2.4 %collective-permute-start.7 = (bf16[40,1024]{1,0:T(8,128)(2,1)S(1)}, bf16[40,1024]{1,0:T(8,128)(2,1)S(1)}, u32[]{:S(2)}, u32[]{:S(2)}) collective-permute-start(bf16[40,1024]{1,0:T(8,128)(2,1)S(1)} %get-tuple-element.71), channel_id=1, source_target_pairs={{0,6},{1,7},{2,4},{3,5},{4,10},{5,11},{6,8},{7,9},{8,14},{9,15},{1... | collective-permute-start | bytes 245768 | tf_op jit(solution)/shard_map/ppermute | solution.py:482
  46.6 0.5 collective-permute-start.8
  47.2 0.0 collective-permute-done.9.received
  47.2 2.8 %shard_map.90 = (bf16[40,1024]{1,0:T(8,128)(2,1)S(1)}, bf16[40,1024]{1,0:T(8,128)(2,1)S(1)}, bf16[40,1024]{1,0:T(8,128)(2,1)S(1)}, bf16[40,1024]{1,0:T(8,128)(2,1)S(1)}) custom-call(bf16[160,3584]{1,0:T(8,128)(2,1)S(1)} %get-tuple-element.65.hidden, bf16[160,1024]{1,0:T(8,128)(2,1)S(1)} %collective-permute-done.9.received, bf16[3584,4096]{1,0:T(8,128)(2,1)} %refs_0_.1, ...), custom_call_target="tpu_custom_call" | custom-call | flops 1174405120 | bytes 3670016 | tf_op jit(solution)/shard_map/pallas_call | solution.py:449
  50.0 1.4 %collective-permute-start.10 = (bf16[40,1024]{1,0:T(8,128)(2,1)S(1)}, bf16[40,1024]{1,0:T(8,128)(2,1)S(1)}, u32[]{:S(2)}, u32[]{:S(2)}) collective-permute-start(bf16[40,1024]{1,0:T(8,128)(2,1)S(1)} %get-tuple-element.77), channel_id=1, source_target_pairs={{0,8},{1,9},{2,10},{3,11},{4,12},{5,13},{6,14},{7,15},{8,0},{9,1},... | collective-permute-start | bytes 245768 | tf_op jit(solution)/shard_map/ppermute | solution.py:482
  51.4 0.0 collective-permute-done.5.refs_0_
  51.4 1.1 %collective-permute-start.11 = (bf16[40,1024]{1,0:T(8,128)(2,1)S(1)}, bf16[40,1024]{1,0:T(8,128)(2,1)S(1)}, u32[]{:S(2)}, u32[]{:S(2)}) collective-permute-start(bf16[40,1024]{1,0:T(8,128)(2,1)S(1)} %get-tuple-element.78), channel_id=1, source_target_pairs={{0,12},{1,13},{2,14},{3,15},{4,0},{5,1},{6,2},{7,3},{8,4},{9,5},{1... | collective-permute-start | bytes 245768 | tf_op jit(solution)/shard_map/ppermute | solution.py:482
  52.5 0.0 collective-permute-done.6.refs_1_
  52.5 0.9 %collective-permute-start.12 = (bf16[40,1024]{1,0:T(8,128)(2,1)S(1)}, bf16[40,1024]{1,0:T(8,128)(2,1)S(1)}, u32[]{:S(2)}, u32[]{:S(2)}) collective-permute-start(bf16[40,1024]{1,0:T(8,128)(2,1)S(1)} %get-tuple-element.79), channel_id=1, source_target_pairs={{0,4},{1,5},{2,6},{3,7},{4,8},{5,9},{6,10},{7,11},{8,12},{9,13},{1... | collective-permute-start | bytes 245768 | tf_op jit(solution)/shard_map/ppermute | solution.py:482
  53.4 0.0 collective-permute-done.7.refs_2_
  53.4 0.6 %collective-permute-done.8.refs_3_ = bf16[40,1024]{1,0:T(8,128)(2,1)S(1)} collective-permute-done((bf16[40,1024]{1,0:T(8,128)(2,1)S(1)}, bf16[40,1024]{1,0:T(8,128)(2,1)S(1)}, u32[]{:S(2)}, u32[]{:S(2)}) %collective-permute-start.8) | collective-permute-done | bytes 81952 | tf_op jit(solution)/shard_map/ppermute | solution.py:482
  54.1 0.3 shard_map.88.refs_0_
  54.3 3.4 %collective-permute-done.10.refs_1_ = bf16[40,1024]{1,0:T(8,128)(2,1)S(1)} collective-permute-done((bf16[40,1024]{1,0:T(8,128)(2,1)S(1)}, bf16[40,1024]{1,0:T(8,128)(2,1)S(1)}, u32[]{:S(2)}, u32[]{:S(2)}) %collective-permute-start.10) | collective-permute-done | bytes 81952 | tf_op jit(solution)/shard_map/ppermute | solution.py:482
  57.8 0.0 collective-permute-done.11.refs_2_
  57.8 1.0 %collective-permute-done.12.refs_3_ = bf16[40,1024]{1,0:T(8,128)(2,1)S(1)} collective-permute-done((bf16[40,1024]{1,0:T(8,128)(2,1)S(1)}, bf16[40,1024]{1,0:T(8,128)(2,1)S(1)}, u32[]{:S(2)}, u32[]{:S(2)}) %collective-permute-start.12) | collective-permute-done | bytes 81952 | tf_op jit(solution)/shard_map/ppermute | solution.py:482
  58.8 1.0 %shard_map.91 = bf16[128,1024]{1,0:T(8,128)(2,1)} custom-call(bf16[2,128,256]{2,1,0:T(8,128)(2,1)S(1)} %get-tuple-element.50.high, bf16[2,128,256]{2,1,0:T(8,128)(2,1)S(1)} %get-tuple-element.51.refs_16_.low, f32[128,1024]{1,0:T(8,128)S(1)} %shard_map.88.refs_0_, bf16[40,1024]{1,0:T(8,128)(2,1)S(1)} %collective-permute-done.10.refs_1_, ...), custom_call_target="tpu_custom_call" | custom-call | flops 83886080 | bytes 1048576 | tf_op jit(solution)/shard_map/pallas_call | solution.py:449
  (1 shorter events, 0.0 us)
Async XLA Ops:
  2.4 19.9 %collective-permute-start = (bf16[40,2048]{1,0:T(8,128)(2,1)S(1)}, bf16[40,2048]{1,0:T(8,128)(2,1)S(1)}, u32[]{:S(2)}, u32[]{:S(2)}) collective-permute-start(bf16[40,2048]{1,0:T(8,128)(2,1)S(1)} %get-tuple-element.46), channel_id=1, source_target_pairs={{0,8},{1,9},{2,10},{3,11},{4,12},{5,13},{6,14},{7,15},{8,0},{9,1},... | collective-permute-start | bytes 491528 | tf_op jit(solution)/shard_map/ppermute | solution.py:482
  6.5 15.8 %collective-permute-start.1 = (bf16[40,2048]{1,0:T(8,128)(2,1)S(1)}, bf16[40,2048]{1,0:T(8,128)(2,1)S(1)}, u32[]{:S(2)}, u32[]{:S(2)}) collective-permute-start(bf16[40,2048]{1,0:T(8,128)(2,1)S(1)} %get-tuple-element.47), channel_id=1, source_target_pairs={{0,4},{1,5},{2,6},{3,7},{4,8},{5,9},{6,10},{7,11},{8,12},{9,13},{1... | collective-permute-start | bytes 491528 | tf_op jit(solution)/shard_map/ppermute | solution.py:482
  8.1 14.2 %collective-permute-start.2 = (bf16[40,2048]{1,0:T(8,128)(2,1)S(1)}, bf16[40,2048]{1,0:T(8,128)(2,1)S(1)}, u32[]{:S(2)}, u32[]{:S(2)}) collective-permute-start(bf16[40,2048]{1,0:T(8,128)(2,1)S(1)} %get-tuple-element.48), channel_id=1, source_target_pairs={{0,12},{1,13},{2,14},{3,15},{4,0},{5,1},{6,2},{7,3},{8,4},{9,5},{1... | collective-permute-start | bytes 491528 | tf_op jit(solution)/shard_map/ppermute | solution.py:482
  22.4 2.2 %collective-permute-start.3 = (bf16[120,2048]{1,0:T(8,128)(2,1)S(1)}, bf16[120,2048]{1,0:T(8,128)(2,1)S(1)}, u32[]{:S(2)}, u32[]{:S(2)}) collective-permute-start(bf16[120,2048]{1,0:T(8,128)(2,1)S(1)} %shard_map.84.after.mine), channel_id=1, source_target_pairs={{0,1},{1,0},{2,3},{3,2},{4,5},{5,4},{6,7},{7,6},{8,9},{9,8},{10,11... | collective-permute-start | bytes 1474568 | tf_op jit(solution)/shard_map/ppermute | solution.py:485
  37.1 2.7 %collective-permute-start.4 = (bf16[160,1024]{1,0:T(8,128)(2,1)S(1)}, bf16[160,1024]{1,0:T(8,128)(2,1)S(1)}, u32[]{:S(2)}, u32[]{:S(2)}) collective-permute-start(bf16[160,1024]{1,0:T(8,128)(2,1)S(1)} %get-tuple-element.66), channel_id=1, source_target_pairs={{0,1},{1,0},{2,3},{3,2},{4,5},{5,4},{6,7},{7,6},{8,9},{9,8},{10,11... | collective-permute-start | bytes 983048 | tf_op jit(solution)/shard_map/ppermute | solution.py:485
  39.7 7.5 %collective-permute-start.9 = (bf16[160,1024]{1,0:T(8,128)(2,1)S(1)}, bf16[160,1024]{1,0:T(8,128)(2,1)S(1)}, u32[]{:S(2)}, u32[]{:S(2)}) collective-permute-start(bf16[160,1024]{1,0:T(8,128)(2,1)S(1)} %get-tuple-element.75), channel_id=1, source_target_pairs={{0,1},{1,0},{2,3},{3,2},{4,5},{5,4},{6,7},{7,6},{8,9},{9,8},{10,11... | collective-permute-start | bytes 983048 | tf_op jit(solution)/shard_map/ppermute | solution.py:485
  41.1 10.2 %collective-permute-start.5 = (bf16[40,1024]{1,0:T(8,128)(2,1)S(1)}, bf16[40,1024]{1,0:T(8,128)(2,1)S(1)}, u32[]{:S(2)}, u32[]{:S(2)}) collective-permute-start(bf16[40,1024]{1,0:T(8,128)(2,1)S(1)} %get-tuple-element.69), channel_id=1, source_target_pairs={{0,10},{1,11},{2,8},{3,9},{4,14},{5,15},{6,12},{7,13},{8,2},{9,3},... | collective-permute-start | bytes 245768 | tf_op jit(solution)/shard_map/ppermute | solution.py:482
  43.7 8.8 %collective-permute-start.6 = (bf16[40,1024]{1,0:T(8,128)(2,1)S(1)}, bf16[40,1024]{1,0:T(8,128)(2,1)S(1)}, u32[]{:S(2)}, u32[]{:S(2)}) collective-permute-start(bf16[40,1024]{1,0:T(8,128)(2,1)S(1)} %get-tuple-element.70), channel_id=1, source_target_pairs={{0,14},{1,15},{2,12},{3,13},{4,2},{5,3},{6,0},{7,1},{8,6},{9,7},{1... | collective-permute-start | bytes 245768 | tf_op jit(solution)/shard_map/ppermute | solution.py:482
  44.2 9.2 %collective-permute-start.7 = (bf16[40,1024]{1,0:T(8,128)(2,1)S(1)}, bf16[40,1024]{1,0:T(8,128)(2,1)S(1)}, u32[]{:S(2)}, u32[]{:S(2)}) collective-permute-start(bf16[40,1024]{1,0:T(8,128)(2,1)S(1)} %get-tuple-element.71), channel_id=1, source_target_pairs={{0,6},{1,7},{2,4},{3,5},{4,10},{5,11},{6,8},{7,9},{8,14},{9,15},{1... | collective-permute-start | bytes 245768 | tf_op jit(solution)/shard_map/ppermute | solution.py:482
  46.6 7.4 %collective-permute-start.8 = (bf16[40,1024]{1,0:T(8,128)(2,1)S(1)}, bf16[40,1024]{1,0:T(8,128)(2,1)S(1)}, u32[]{:S(2)}, u32[]{:S(2)}) collective-permute-start(bf16[40,1024]{1,0:T(8,128)(2,1)S(1)} %get-tuple-element.72), channel_id=1, source_target_pairs={{0,2},{1,3},{2,0},{3,1},{4,6},{5,7},{6,4},{7,5},{8,10},{9,11},{10,... | collective-permute-start | bytes 245768 | tf_op jit(solution)/shard_map/ppermute | solution.py:482
  50.0 7.8 %collective-permute-start.10 = (bf16[40,1024]{1,0:T(8,128)(2,1)S(1)}, bf16[40,1024]{1,0:T(8,128)(2,1)S(1)}, u32[]{:S(2)}, u32[]{:S(2)}) collective-permute-start(bf16[40,1024]{1,0:T(8,128)(2,1)S(1)} %get-tuple-element.77), channel_id=1, source_target_pairs={{0,8},{1,9},{2,10},{3,11},{4,12},{5,13},{6,14},{7,15},{8,0},{9,1},... | collective-permute-start | bytes 245768 | tf_op jit(solution)/shard_map/ppermute | solution.py:482
  51.4 6.4 %collective-permute-start.11 = (bf16[40,1024]{1,0:T(8,128)(2,1)S(1)}, bf16[40,1024]{1,0:T(8,128)(2,1)S(1)}, u32[]{:S(2)}, u32[]{:S(2)}) collective-permute-start(bf16[40,1024]{1,0:T(8,128)(2,1)S(1)} %get-tuple-element.78), channel_id=1, source_target_pairs={{0,12},{1,13},{2,14},{3,15},{4,0},{5,1},{6,2},{7,3},{8,4},{9,5},{1... | collective-permute-start | bytes 245768 | tf_op jit(solution)/shard_map/ppermute | solution.py:482
  52.5 6.3 %collective-permute-start.12 = (bf16[40,1024]{1,0:T(8,128)(2,1)S(1)}, bf16[40,1024]{1,0:T(8,128)(2,1)S(1)}, u32[]{:S(2)}, u32[]{:S(2)}) collective-permute-start(bf16[40,1024]{1,0:T(8,128)(2,1)S(1)} %get-tuple-element.79), channel_id=1, source_target_pairs={{0,4},{1,5},{2,6},{3,7},{4,8},{5,9},{6,10},{7,11},{8,12},{9,13},{1... | collective-permute-start | bytes 245768 | tf_op jit(solution)/shard_map/ppermute | solution.py:482

commit v16 on v15

--- a/solution.py
+++ b/solution.py
@@ -526,7 +526,7 @@
         moved=(READY - 2) * piece_bytes,
         aliases={4: 1},
     )
-    order = distances(exp_count)
+    order = list(range(1, exp_count))
     arrived = [shift(sends[d - 1], d) for d in order]
     mine = call(
         functools.partial(join_kernel, order),

time: 60.1 us -> 60.8 us (1.012)
  transfers between devices with their start and end apart: 13 -> 13, of which waited for: 3 -> 2; matrix products, arithmetic and copies ran while one was open for 0% -> 0% of each run, Pallas kernels for 34% -> 34%
where the time goes in v16:
time: 60.8 us; the launch traced here: 60.5 us
  Pallas kernels  36.4 us (60%)
  starting transfers between devices  18.5 us (30%)
  waiting for transfers between devices  5.44 us (9%)
    pallas_call x10, Pallas kernels, call(): pl.pallas_call(kernel, out_shape=shapes, in_specs=specs, out_specs=[vmem]...  36.4 us
    ppermute x10, starting transfers between devices, shift(): return lax.ppermute(value, ('exp', 'unit'), pairs)  17.7 us
    ppermute x10, waiting for transfers between devices, shift(): return lax.ppermute(value, ('exp', 'unit'), pairs)  5.43 us
  transfers between devices with their start and end apart: 13, of which 2 were waited for; matrix products, arithmetic and copies ran while one was open for 0% of the time, Pallas kernels for 34%

profile of v16, /device:TPU:0, one launch (start us, length us, event | category | flops | bytes accessed | tf_op | source)
XLA Modules:
  0.0 60.5 jit_solution(3810965720925946469)
XLA Ops:
  0.0 2.4 %shard_map.82 = (bf16[40,4096]{1,0:T(8,128)(2,1)S(1)}, bf16[7,512,512]{2,1,0:T(8,128)(2,1)S(1)}, bf16[40,2048]{1,0:T(8,128)(2,1)S(1)}, bf16[40,2048]{1,0:T(8,128)(2,1)S(1)}, bf16[40,2048]{1,0:T(8,128)(2,1)S(1)}) custom-call(bf16[128,4096]{1,0:T(8,128)(2,1)} %tokens_hbm.1, f32[1,4096]{1,0:T(1,128)} %bitcast.3, s32[2,128]{1,0:T(2,128)} %bitcast.4, ...), custom_call_target="tpu_custom_call" | custom-call | flops 83886080 | bytes 5767168 | tf_op jit(solution)/shard_map/pallas_call | solution.py:449
  2.4 3.1 %collective-permute-start = (bf16[40,2048]{1,0:T(8,128)(2,1)S(1)}, bf16[40,2048]{1,0:T(8,128)(2,1)S(1)}, u32[]{:S(2)}, u32[]{:S(2)}) collective-permute-start(bf16[40,2048]{1,0:T(8,128)(2,1)S(1)} %get-tuple-element.46), channel_id=1, source_target_pairs={{0,4},{1,5},{2,6},{3,7},{4,8},{5,9},{6,10},{7,11},{8,12},{9,13},{1... | collective-permute-start | bytes 491528 | tf_op jit(solution)/shard_map/ppermute | solution.py:482
  5.5 2.6 %collective-permute-start.1 = (bf16[40,2048]{1,0:T(8,128)(2,1)S(1)}, bf16[40,2048]{1,0:T(8,128)(2,1)S(1)}, u32[]{:S(2)}, u32[]{:S(2)}) collective-permute-start(bf16[40,2048]{1,0:T(8,128)(2,1)S(1)} %get-tuple-element.47), channel_id=1, source_target_pairs={{0,8},{1,9},{2,10},{3,11},{4,12},{5,13},{6,14},{7,15},{8,0},{9,1},... | collective-permute-start | bytes 491528 | tf_op jit(solution)/shard_map/ppermute | solution.py:482
  8.1 1.3 %collective-permute-start.2 = (bf16[40,2048]{1,0:T(8,128)(2,1)S(1)}, bf16[40,2048]{1,0:T(8,128)(2,1)S(1)}, u32[]{:S(2)}, u32[]{:S(2)}) collective-permute-start(bf16[40,2048]{1,0:T(8,128)(2,1)S(1)} %get-tuple-element.48), channel_id=1, source_target_pairs={{0,12},{1,13},{2,14},{3,15},{4,0},{5,1},{6,2},{7,3},{8,4},{9,5},{1... | collective-permute-start | bytes 491528 | tf_op jit(solution)/shard_map/ppermute | solution.py:482
  9.4 11.9 %shard_map.83 = (f32[8,3584]{1,0:T(8,128)S(1)}, bf16[7,512,512]{2,1,0:T(8,128)(2,1)S(1)}, bf16[7,512,512]{2,1,0:T(8,128)(2,1)S(1)}, bf16[7,512,512]{2,1,0:T(8,12...) custom-call(s32[2,8,48]{2,1,0:T(8,128)} %active_hbm.1, ...), custom_call_target="tpu_custom_call", output_to_operand_aliasing={{1}: (4, {})} | custom-call | flops 167772160 | bytes 36700160 | tf_op jit(solution)/shard_map/pallas_call | solution.py:449
  21.4 0.0 collective-permute-done.refs_0_
  21.4 0.0 collective-permute-done.1.refs_1_
  21.4 0.0 collective-permute-done.2.refs_2_
  21.5 0.1 collective-permute-start.3
  21.5 2.1 %shard_map.85 = (bf16[2,128,256]{2,1,0:T(8,128)(2,1)S(1)}, bf16[2,128,256]{2,1,0:T(8,128)(2,1)S(1)}, bf16[7,512,512]{2,1,0:T(8,128)(2,1)S(1)}) custom-call(s32[2,128]{1,0:T(2,128)} %bitcast.5, f32[2,128]{1,0:T(2,128)} %bitcast.6, bf16[120,2048]{1,0:T(8,128)(2,1)S(1)} %shard_map.84.after.mine, ...), custom_call_target="tpu_custom_call", output_to_operand_aliasing={{2}: (5, {})} | custom-call | bytes 4194304 | tf_op jit(solution)/shard_map/pallas_call | solution.py:449
  23.7 0.0 collective-permute-done.3.other
  23.7 12.5 %shard_map.86 = (bf16[160,3584]{1,0:T(8,128)(2,1)S(1)}, bf16[160,1024]{1,0:T(8,128)(2,1)S(1)}, bf16[7,512,512]{2,1,0:T(8,128)(2,1)S(1)}, bf16[7,512,512]{2,1,0:T...) custom-call(bf16[40,4096]{1,0:T(8,128)(2,1)S(1)} %get-tuple-element., ...), custom_call_target="tpu_custom_call", output_to_operand_aliasing={{2}: (3, {}), {3}: (4, {}), {4}: (5, {}), {5}: (6, {}), {6}... | custom-call | flops 9395240960 | bytes 36700160 | tf_op jit(solution)/shard_map/pallas_call | solution.py:449
  36.2 0.6 collective-permute-start.4
  36.7 2.0 %shard_map.89 = (bf16[160,1024]{1,0:T(8,128)(2,1)S(1)}, bf16[7,512,512]{2,1,0:T(8,128)(2,1)S(1)}) custom-call(bf16[160,3584]{1,0:T(8,128)(2,1)S(1)} %get-tuple-element.65.hidden, bf16[7,512,512]{2,1,0:T(8,128)(2,1)S(1)} %get-tuple-element.73.refs_0_, bf16[7,512,512]{2,1,0:T(8,128)(2,1)S(1)} %get-tuple-element.74.refs_1_, bf16[3584,4096]{1,0:T(8,128)(2,1)} %refs_0_.1), custom_call_target="tpu_custom_call" | custom-call | flops 1174405120 | bytes 3670016 | tf_op jit(solution)/shard_map/pallas_call | solution.py:449
  38.8 0.1 collective-permute-start.9
  38.9 0.0 collective-permute-done.4.received
  38.9 1.4 %shard_map.87 = (bf16[40,1024]{1,0:T(8,128)(2,1)S(1)}, bf16[40,1024]{1,0:T(8,128)(2,1)S(1)}, bf16[40,1024]{1,0:T(8,128)(2,1)S(1)}, bf16[40,1024]{1,0:T(8,128)(2,1)S(1)}) custom-call(bf16[160,3584]{1,0:T(8,128)(2,1)S(1)} %get-tuple-element.65.hidden, bf16[160,1024]{1,0:T(8,128)(2,1)S(1)} %collective-permute-done.4.received, ...), custom_call_target="tpu_custom_call" | custom-call | flops 1174405120 | bytes 3670016 | tf_op jit(solution)/shard_map/pallas_call | solution.py:449
  40.2 1.4 %collective-permute-start.5 = (bf16[40,1024]{1,0:T(8,128)(2,1)S(1)}, bf16[40,1024]{1,0:T(8,128)(2,1)S(1)}, u32[]{:S(2)}, u32[]{:S(2)}) collective-permute-start(bf16[40,1024]{1,0:T(8,128)(2,1)S(1)} %get-tuple-element.69), channel_id=1, source_target_pairs={{0,10},{1,11},{2,8},{3,9},{4,14},{5,15},{6,12},{7,13},{8,2},{9,3},... | collective-permute-start | bytes 245768 | tf_op jit(solution)/shard_map/ppermute | solution.py:482
  41.6 3.4 %collective-permute-start.6 = (bf16[40,1024]{1,0:T(8,128)(2,1)S(1)}, bf16[40,1024]{1,0:T(8,128)(2,1)S(1)}, u32[]{:S(2)}, u32[]{:S(2)}) collective-permute-start(bf16[40,1024]{1,0:T(8,128)(2,1)S(1)} %get-tuple-element.70), channel_id=1, source_target_pairs={{0,14},{1,15},{2,12},{3,13},{4,2},{5,3},{6,0},{7,1},{8,6},{9,7},{1... | collective-permute-start | bytes 245768 | tf_op jit(solution)/shard_map/ppermute | solution.py:482
  45.0 0.0 collective-permute-start.7
  45.0 1.5 %collective-permute-start.8 = (bf16[40,1024]{1,0:T(8,128)(2,1)S(1)}, bf16[40,1024]{1,0:T(8,128)(2,1)S(1)}, u32[]{:S(2)}, u32[]{:S(2)}) collective-permute-start(bf16[40,1024]{1,0:T(8,128)(2,1)S(1)} %get-tuple-element.72), channel_id=1, source_target_pairs={{0,2},{1,3},{2,0},{3,1},{4,6},{5,7},{6,4},{7,5},{8,10},{9,11},{10,... | collective-permute-start | bytes 245768 | tf_op jit(solution)/shard_map/ppermute | solution.py:482
  46.5 0.0 collective-permute-done.9.received
  46.5 2.8 %shard_map.90 = (bf16[40,1024]{1,0:T(8,128)(2,1)S(1)}, bf16[40,1024]{1,0:T(8,128)(2,1)S(1)}, bf16[40,1024]{1,0:T(8,128)(2,1)S(1)}, bf16[40,1024]{1,0:T(8,128)(2,1)S(1)}) custom-call(bf16[160,3584]{1,0:T(8,128)(2,1)S(1)} %get-tuple-element.65.hidden, bf16[160,1024]{1,0:T(8,128)(2,1)S(1)} %collective-permute-done.9.received, bf16[3584,4096]{1,0:T(8,128)(2,1)} %refs_0_.1, ...), custom_call_target="tpu_custom_call" | custom-call | flops 1174405120 | bytes 3670016 | tf_op jit(solution)/shard_map/pallas_call | solution.py:449
  49.3 1.2 %collective-permute-start.10 = (bf16[40,1024]{1,0:T(8,128)(2,1)S(1)}, bf16[40,1024]{1,0:T(8,128)(2,1)S(1)}, u32[]{:S(2)}, u32[]{:S(2)}) collective-permute-start(bf16[40,1024]{1,0:T(8,128)(2,1)S(1)} %get-tuple-element.77), channel_id=1, source_target_pairs={{0,8},{1,9},{2,10},{3,11},{4,12},{5,13},{6,14},{7,15},{8,0},{9,1},... | collective-permute-start | bytes 245768 | tf_op jit(solution)/shard_map/ppermute | solution.py:482
  50.5 0.0 collective-permute-done.5.refs_0_
  50.5 2.7 %collective-permute-start.11 = (bf16[40,1024]{1,0:T(8,128)(2,1)S(1)}, bf16[40,1024]{1,0:T(8,128)(2,1)S(1)}, u32[]{:S(2)}, u32[]{:S(2)}) collective-permute-start(bf16[40,1024]{1,0:T(8,128)(2,1)S(1)} %get-tuple-element.78), channel_id=1, source_target_pairs={{0,12},{1,13},{2,14},{3,15},{4,0},{5,1},{6,2},{7,3},{8,4},{9,5},{1... | collective-permute-start | bytes 245768 | tf_op jit(solution)/shard_map/ppermute | solution.py:482
  53.2 0.0 collective-permute-done.6.refs_1_
  53.2 0.5 collective-permute-start.12
  53.8 0.0 collective-permute-done.7.refs_2_
  53.8 0.0 collective-permute-done.8.refs_3_
  53.8 0.3 shard_map.88.refs_0_
  54.1 2.2 %collective-permute-done.10.refs_1_ = bf16[40,1024]{1,0:T(8,128)(2,1)S(1)} collective-permute-done((bf16[40,1024]{1,0:T(8,128)(2,1)S(1)}, bf16[40,1024]{1,0:T(8,128)(2,1)S(1)}, u32[]{:S(2)}, u32[]{:S(2)}) %collective-permute-start.10) | collective-permute-done | bytes 81952 | tf_op jit(solution)/shard_map/ppermute | solution.py:482
  56.3 0.0 collective-permute-done.11.refs_2_
  56.3 3.1 %collective-permute-done.12.refs_3_ = bf16[40,1024]{1,0:T(8,128)(2,1)S(1)} collective-permute-done((bf16[40,1024]{1,0:T(8,128)(2,1)S(1)}, bf16[40,1024]{1,0:T(8,128)(2,1)S(1)}, u32[]{:S(2)}, u32[]{:S(2)}) %collective-permute-start.12) | collective-permute-done | bytes 81952 | tf_op jit(solution)/shard_map/ppermute | solution.py:482
  59.5 1.0 %shard_map.91 = bf16[128,1024]{1,0:T(8,128)(2,1)} custom-call(bf16[2,128,256]{2,1,0:T(8,128)(2,1)S(1)} %get-tuple-element.50.high, bf16[2,128,256]{2,1,0:T(8,128)(2,1)S(1)} %get-tuple-element.51.refs_16_.low, f32[128,1024]{1,0:T(8,128)S(1)} %shard_map.88.refs_0_, bf16[40,1024]{1,0:T(8,128)(2,1)S(1)} %collective-permute-done.10.refs_1_, ...), custom_call_target="tpu_custom_call" | custom-call | flops 83886080 | bytes 1048576 | tf_op jit(solution)/shard_map/pallas_call | solution.py:449
  (1 shorter events, 0.0 us)
Async XLA Ops:
  2.4 19.0 %collective-permute-start = (bf16[40,2048]{1,0:T(8,128)(2,1)S(1)}, bf16[40,2048]{1,0:T(8,128)(2,1)S(1)}, u32[]{:S(2)}, u32[]{:S(2)}) collective-permute-start(bf16[40,2048]{1,0:T(8,128)(2,1)S(1)} %get-tuple-element.46), channel_id=1, source_target_pairs={{0,4},{1,5},{2,6},{3,7},{4,8},{5,9},{6,10},{7,11},{8,12},{9,13},{1... | collective-permute-start | bytes 491528 | tf_op jit(solution)/shard_map/ppermute | solution.py:482
  5.5 15.9 %collective-permute-start.1 = (bf16[40,2048]{1,0:T(8,128)(2,1)S(1)}, bf16[40,2048]{1,0:T(8,128)(2,1)S(1)}, u32[]{:S(2)}, u32[]{:S(2)}) collective-permute-start(bf16[40,2048]{1,0:T(8,128)(2,1)S(1)} %get-tuple-element.47), channel_id=1, source_target_pairs={{0,8},{1,9},{2,10},{3,11},{4,12},{5,13},{6,14},{7,15},{8,0},{9,1},... | collective-permute-start | bytes 491528 | tf_op jit(solution)/shard_map/ppermute | solution.py:482
  8.1 13.3 %collective-permute-start.2 = (bf16[40,2048]{1,0:T(8,128)(2,1)S(1)}, bf16[40,2048]{1,0:T(8,128)(2,1)S(1)}, u32[]{:S(2)}, u32[]{:S(2)}) collective-permute-start(bf16[40,2048]{1,0:T(8,128)(2,1)S(1)} %get-tuple-element.48), channel_id=1, source_target_pairs={{0,12},{1,13},{2,14},{3,15},{4,0},{5,1},{6,2},{7,3},{8,4},{9,5},{1... | collective-permute-start | bytes 491528 | tf_op jit(solution)/shard_map/ppermute | solution.py:482
  21.5 2.2 %collective-permute-start.3 = (bf16[120,2048]{1,0:T(8,128)(2,1)S(1)}, bf16[120,2048]{1,0:T(8,128)(2,1)S(1)}, u32[]{:S(2)}, u32[]{:S(2)}) collective-permute-start(bf16[120,2048]{1,0:T(8,128)(2,1)S(1)} %shard_map.84.after.mine), channel_id=1, source_target_pairs={{0,1},{1,0},{2,3},{3,2},{4,5},{5,4},{6,7},{7,6},{8,9},{9,8},{10,11... | collective-permute-start | bytes 1474568 | tf_op jit(solution)/shard_map/ppermute | solution.py:485
  36.2 2.7 %collective-permute-start.4 = (bf16[160,1024]{1,0:T(8,128)(2,1)S(1)}, bf16[160,1024]{1,0:T(8,128)(2,1)S(1)}, u32[]{:S(2)}, u32[]{:S(2)}) collective-permute-start(bf16[160,1024]{1,0:T(8,128)(2,1)S(1)} %get-tuple-element.66), channel_id=1, source_target_pairs={{0,1},{1,0},{2,3},{3,2},{4,5},{5,4},{6,7},{7,6},{8,9},{9,8},{10,11... | collective-permute-start | bytes 983048 | tf_op jit(solution)/shard_map/ppermute | solution.py:485
  38.8 7.7 %collective-permute-start.9 = (bf16[160,1024]{1,0:T(8,128)(2,1)S(1)}, bf16[160,1024]{1,0:T(8,128)(2,1)S(1)}, u32[]{:S(2)}, u32[]{:S(2)}) collective-permute-start(bf16[160,1024]{1,0:T(8,128)(2,1)S(1)} %get-tuple-element.75), channel_id=1, source_target_pairs={{0,1},{1,0},{2,3},{3,2},{4,5},{5,4},{6,7},{7,6},{8,9},{9,8},{10,11... | collective-permute-start | bytes 983048 | tf_op jit(solution)/shard_map/ppermute | solution.py:485
  40.2 10.2 %collective-permute-start.5 = (bf16[40,1024]{1,0:T(8,128)(2,1)S(1)}, bf16[40,1024]{1,0:T(8,128)(2,1)S(1)}, u32[]{:S(2)}, u32[]{:S(2)}) collective-permute-start(bf16[40,1024]{1,0:T(8,128)(2,1)S(1)} %get-tuple-element.69), channel_id=1, source_target_pairs={{0,10},{1,11},{2,8},{3,9},{4,14},{5,15},{6,12},{7,13},{8,2},{9,3},... | collective-permute-start | bytes 245768 | tf_op jit(solution)/shard_map/ppermute | solution.py:482
  41.6 11.6 %collective-permute-start.6 = (bf16[40,1024]{1,0:T(8,128)(2,1)S(1)}, bf16[40,1024]{1,0:T(8,128)(2,1)S(1)}, u32[]{:S(2)}, u32[]{:S(2)}) collective-permute-start(bf16[40,1024]{1,0:T(8,128)(2,1)S(1)} %get-tuple-element.70), channel_id=1, source_target_pairs={{0,14},{1,15},{2,12},{3,13},{4,2},{5,3},{6,0},{7,1},{8,6},{9,7},{1... | collective-permute-start | bytes 245768 | tf_op jit(solution)/shard_map/ppermute | solution.py:482
  45.0 8.8 %collective-permute-start.7 = (bf16[40,1024]{1,0:T(8,128)(2,1)S(1)}, bf16[40,1024]{1,0:T(8,128)(2,1)S(1)}, u32[]{:S(2)}, u32[]{:S(2)}) collective-permute-start(bf16[40,1024]{1,0:T(8,128)(2,1)S(1)} %get-tuple-element.71), channel_id=1, source_target_pairs={{0,6},{1,7},{2,4},{3,5},{4,10},{5,11},{6,8},{7,9},{8,14},{9,15},{1... | collective-permute-start | bytes 245768 | tf_op jit(solution)/shard_map/ppermute | solution.py:482
  45.0 8.8 %collective-permute-start.8 = (bf16[40,1024]{1,0:T(8,128)(2,1)S(1)}, bf16[40,1024]{1,0:T(8,128)(2,1)S(1)}, u32[]{:S(2)}, u32[]{:S(2)}) collective-permute-start(bf16[40,1024]{1,0:T(8,128)(2,1)S(1)} %get-tuple-element.72), channel_id=1, source_target_pairs={{0,2},{1,3},{2,0},{3,1},{4,6},{5,7},{6,4},{7,5},{8,10},{9,11},{10,... | collective-permute-start | bytes 245768 | tf_op jit(solution)/shard_map/ppermute | solution.py:482
  49.3 7.0 %collective-permute-start.10 = (bf16[40,1024]{1,0:T(8,128)(2,1)S(1)}, bf16[40,1024]{1,0:T(8,128)(2,1)S(1)}, u32[]{:S(2)}, u32[]{:S(2)}) collective-permute-start(bf16[40,1024]{1,0:T(8,128)(2,1)S(1)} %get-tuple-element.77), channel_id=1, source_target_pairs={{0,8},{1,9},{2,10},{3,11},{4,12},{5,13},{6,14},{7,15},{8,0},{9,1},... | collective-permute-start | bytes 245768 | tf_op jit(solution)/shard_map/ppermute | solution.py:482
  50.5 5.8 %collective-permute-start.11 = (bf16[40,1024]{1,0:T(8,128)(2,1)S(1)}, bf16[40,1024]{1,0:T(8,128)(2,1)S(1)}, u32[]{:S(2)}, u32[]{:S(2)}) collective-permute-start(bf16[40,1024]{1,0:T(8,128)(2,1)S(1)} %get-tuple-element.78), channel_id=1, source_target_pairs={{0,12},{1,13},{2,14},{3,15},{4,0},{5,1},{6,2},{7,3},{8,4},{9,5},{1... | collective-permute-start | bytes 245768 | tf_op jit(solution)/shard_map/ppermute | solution.py:482
  53.2 6.3 %collective-permute-start.12 = (bf16[40,1024]{1,0:T(8,128)(2,1)S(1)}, bf16[40,1024]{1,0:T(8,128)(2,1)S(1)}, u32[]{:S(2)}, u32[]{:S(2)}) collective-permute-start(bf16[40,1024]{1,0:T(8,128)(2,1)S(1)} %get-tuple-element.79), channel_id=1, source_target_pairs={{0,4},{1,5},{2,6},{3,7},{4,8},{5,9},{6,10},{7,11},{8,12},{9,13},{1... | collective-permute-start | bytes 245768 | tf_op jit(solution)/shard_map/ppermute | solution.py:482
